TPU v7x, 128 devices: a whole 4x4x4 slice. The times are simulated.
128 devices in a mesh: ctx: 16 (over y, z_hi, core), tp: 8 (over x, z_lo).
Axes of the slice: x: 4, y: 4, z: 4 (z_hi: 2, z_lo: 2; z = z_hi * 2 + z_lo), core: 2. Of those that a mesh axis runs over, the one named last changes fastest.
Arguments:
- query: bfloat16 [4096, 5120], P('ctx', 'tp'), may hold values from -6 to 6
- key_projected: bfloat16 [4096, 1024], P('ctx', 'tp'), may hold values from -6 to 6
- value: bfloat16 [4096, 1024], P('ctx', 'tp'), may hold values from -6 to 6
- attention_output: bfloat16 [4096, 5120], P('ctx', 'tp'), may hold values from -6 to 6
- output_gradient: bfloat16 [4096, 5120], P('ctx', 'tp'), may hold values from -6 to 6
- lse: float32 [40, 4096], P('tp', 'ctx'), may hold values from 4 to 7
- block_mask: int32 [32, 32], replicated, may hold values from 0 to 1, as said below
- positions: int32 [4096], P('ctx'), may hold values from 0 to 1023, as said below
- segments: int32 [4096], replicated, may hold values from 0 to 63, as said below
- w_query: bfloat16 [5120, 5120], P(None, 'tp'), may hold values from -0.078125 to 0.078125
- key_weight: bfloat16 [5120, 1024], P(None, 'tp'), may hold values from -0.078125 to 0.078125
- value_weight: bfloat16 [5120, 1024], P(None, 'tp'), may hold values from -0.078125 to 0.078125
Outputs:
- input_grad_t: bfloat16 [5120, 4096], P('tp', 'ctx')
Inputs may be any that keep to these rules, and one draw needn't show every extreme that they name: block_mask[a, b] is 1 exactly when tile b is tile a or an ancestor of tile a in a forest of tiles in which every tile's parent is an earlier tile. `positions`: a token's position is 128 times its tile's number of ancestors plus its offset from the first token of its segment within the tile. `segments`: never falling along the tokens; one segment a tile, except that a tile that is no other tile's ancestor may hold two, the second beginning inside it.
All inputs are finite; a program needn't handle non-finite values.
Results may differ from a plain program's by a relative error of at most 0.0065.
The roundings to bfloat16 on the way count: a program that leaves them out, or rounds other values in their place, can miss the bound.
Values may be sent and summed in bfloat16 or wider, within the bound.
No kernel may reach another device: no remote copies, remote signals or barrier semaphores. Data moves between devices by JAX's collectives and lax.ppermute only.
A program may use at most 128 MiB of HBM per device.

v0:
```python
import jax
import jax.numpy as jnp
from jax import lax
from jax.sharding import PartitionSpec as P

QUERY_HEADS = 40
KEY_VALUE_HEADS = 8
HEAD_SIZE = 128
TILE = 128


rope_base = 1000000.0


def rope_tables(positions, head_dim):
    half = head_dim // 2
    exponent = jnp.arange(half).astype(jnp.float32) * (2.0 / head_dim)
    inverse = jnp.power(jnp.float32(rope_base), -exponent)
    angles = positions.astype(jnp.float32)[:, None] * inverse[None, :]
    cosine_table = jnp.cos(angles)
    sine_table = jnp.sin(angles)
    return (
        jnp.concatenate([cosine_table, cosine_table], 1),
        jnp.concatenate([sine_table, sine_table], 1),
    )


def rotate_forward(values, cosine_table, sine_table):
    half = values.shape[-1] // 2
    turned = jnp.concatenate([-values[..., half:], values[..., :half]], -1)
    return values * cosine_table[:, None, :] + turned * sine_table[:, None, :]


def unrotate_halves(grads, cosine_table, sine_table):
    half = grads.shape[-1] // 2
    scaled = grads * sine_table[:, None, :]
    turned = jnp.concatenate([scaled[..., half:], -scaled[..., :half]], -1)
    return grads * cosine_table[:, None, :] + turned


def block_size(tile):
    for multiple in (4, 2, 1):
        return multiple * tile
    return tile


def pair_mask(block_mask, segments, q_start, q_count, k_start, k_count, tile):
    q_start = jnp.asarray(q_start)
    k_start = jnp.asarray(k_start)
    table = lax.dynamic_slice(
        block_mask, (q_start // tile, k_start // tile), (q_count // tile, k_count // tile)
    )
    needed = jnp.any(table > 0)
    wide = (
        jnp.broadcast_to(
            table[:, None, :, None], (q_count // tile, tile, k_count // tile, tile)
        ).reshape(q_count, k_count)
        > 0
    )
    q_index = q_start + jnp.arange(q_count)
    k_index = k_start + jnp.arange(k_count)
    seg_query = lax.dynamic_slice_in_dim(segments, q_start, q_count)
    seg_key = lax.dynamic_slice_in_dim(segments, k_start, k_count)
    same_tile = q_index[:, None] // tile == k_index[None, :] // tile
    inner = (k_index[None, :] <= q_index[:, None]) & (seg_query[:, None] == seg_key[None, :])
    return (wide & (jnp.logical_not(same_tile) | inner), needed)


def score_grads(query_blk, grad_blk, lse_blk, delta_blk, key_blk, value_blk, allowed, logit_scale):
    scores = (
        jnp.einsum("tkgd,skd->tkgs", query_blk, key_blk, preferred_element_type=jnp.float32)
        * logit_scale
    )
    probs = jnp.where(allowed[:, None, None, :], jnp.exp(scores - lse_blk[..., None]), 0.0)
    dprobs = jnp.einsum("tkgd,skd->tkgs", grad_blk, value_blk, preferred_element_type=jnp.float32)
    dscore = probs * (dprobs - delta_blk[..., None])
    return (probs.astype(jnp.bfloat16), dscore.astype(jnp.bfloat16))


def local(
    query,
    key_projected,
    value,
    attention_output,
    output_gradient,
    lse,
    block_mask,
    positions,
    segments,
    w_query,
    key_weight,
    value_weight,
):
    tok_rows = query.shape[0]
    kv_local = key_projected.shape[1] // HEAD_SIZE
    query_groups = QUERY_HEADS // KEY_VALUE_HEADS
    heads_local = kv_local * query_groups
    logit_scale = HEAD_SIZE ** (-0.5)
    q_start = lax.axis_index("ctx") * tok_rows
    cosine_table, sine_table = rope_tables(positions, HEAD_SIZE)
    query_rotated = rotate_forward(
        query.astype(jnp.float32).reshape(tok_rows, heads_local, HEAD_SIZE),
        cosine_table,
        sine_table,
    ).astype(jnp.bfloat16)
    query_four = query_rotated.reshape(tok_rows, kv_local, query_groups, HEAD_SIZE)
    key_rotated = rotate_forward(
        key_projected.astype(jnp.float32).reshape(tok_rows, kv_local, HEAD_SIZE),
        cosine_table,
        sine_table,
    ).astype(jnp.bfloat16)
    grad_four = output_gradient.reshape(tok_rows, kv_local, query_groups, HEAD_SIZE)
    row_dot_delta = jnp.sum(
        grad_four.astype(jnp.float32)
        * attention_output.reshape(tok_rows, kv_local, query_groups, HEAD_SIZE).astype(jnp.float32),
        -1,
    )
    row_logsumexp = lse.T.reshape(tok_rows, kv_local, query_groups)
    key_whole, value_whole = (
        lax.all_gather(
            key_rotated.reshape(tok_rows, kv_local * HEAD_SIZE), "ctx", axis=0, tiled=True
        ),
        lax.all_gather(value, "ctx", axis=0, tiled=True),
    )
    key_total = key_whole.shape[0]
    key_step = block_size(TILE)
    query_empty = jnp.zeros((tok_rows, kv_local, query_groups, HEAD_SIZE), jnp.float32)

    def all_terms(accum, index):
        k_start = index * key_step
        key_blk = lax.dynamic_slice_in_dim(key_whole, k_start, key_step, 0).reshape(
            key_step, kv_local, HEAD_SIZE
        )
        value_blk = lax.dynamic_slice_in_dim(value_whole, k_start, key_step, 0).reshape(
            key_step, kv_local, HEAD_SIZE
        )
        allowed, needed = pair_mask(
            block_mask, segments, q_start, tok_rows, k_start, key_step, TILE
        )
        probs_bf, dscore_bf = score_grads(
            query_four,
            grad_four,
            row_logsumexp,
            row_dot_delta,
            key_blk,
            value_blk,
            allowed,
            logit_scale,
        )
        query_sum = accum + jnp.einsum(
            "tkgs,skd->tkgd", dscore_bf, key_blk, preferred_element_type=jnp.float32
        )
        key_part = jnp.einsum(
            "tkgs,tkgd->skd", dscore_bf, query_four, preferred_element_type=jnp.float32
        )
        value_part = jnp.einsum(
            "tkgs,tkgd->skd", probs_bf, grad_four, preferred_element_type=jnp.float32
        )
        stacked = jnp.concatenate(
            [
                key_part.reshape(key_step, kv_local * HEAD_SIZE),
                value_part.reshape(key_step, kv_local * HEAD_SIZE),
            ],
            1,
        )
        return (query_sum, stacked)

    query_acc, blocks = lax.scan(all_terms, query_empty, jnp.arange(key_total // key_step))
    terms = blocks.reshape(key_total, 2 * kv_local * HEAD_SIZE)
    summed = lax.psum_scatter(terms, "ctx", scatter_dimension=0, tiled=True)
    key_rot_grad = (
        summed[:, : kv_local * HEAD_SIZE].reshape(tok_rows, kv_local, HEAD_SIZE) * logit_scale
    )
    value_gradient = summed[:, kv_local * HEAD_SIZE :].reshape(tok_rows, kv_local, HEAD_SIZE)
    query_rot_grad = (query_acc * logit_scale).reshape(tok_rows, heads_local, HEAD_SIZE)
    query_grad = (
        unrotate_halves(query_rot_grad, cosine_table, sine_table)
        .astype(jnp.bfloat16)
        .reshape(tok_rows, heads_local * HEAD_SIZE)
    )
    key_gradient = (
        unrotate_halves(key_rot_grad, cosine_table, sine_table)
        .astype(jnp.bfloat16)
        .reshape(tok_rows, kv_local * HEAD_SIZE)
    )
    value_grad_bf = value_gradient.astype(jnp.bfloat16).reshape(tok_rows, kv_local * HEAD_SIZE)
    contract = (((1,), (1,)), ((), ()))
    result = lax.dot_general(w_query, query_grad, contract, preferred_element_type=jnp.float32)
    result = result + lax.dot_general(
        key_weight, key_gradient, contract, preferred_element_type=jnp.float32
    )
    result = result + lax.dot_general(
        value_weight, value_grad_bf, contract, preferred_element_type=jnp.float32
    )
    return lax.psum_scatter(result, "tp", scatter_dimension=0, tiled=True).astype(jnp.bfloat16)


def solution(mesh):
    in_specs = (
        P("ctx", "tp"),
        P("ctx", "tp"),
        P("ctx", "tp"),
        P("ctx", "tp"),
        P("ctx", "tp"),
        P("tp", "ctx"),
        P(),
        P("ctx"),
        P(),
        P(None, "tp"),
        P(None, "tp"),
        P(None, "tp"),
    )
    out_specs = P("tp", "ctx")
    return jax.shard_map(local, mesh=mesh, in_specs=in_specs, out_specs=out_specs, check_vma=False)
```

profile of v0, /device:TPU:0, one launch (start us, length us, event | category | flops | bytes accessed | tf_op | source)
XLA Modules:
  0.0 400.1 jit_solution(8950835141512801970)
XLA Ops:
  10.0 1.6 pad_maximum_fusion.1
  12.0 0.9 copy.40
  12.9 1.1 copy.36
  14.1 2.0 copy.41
  16.9 1.2 multiply_reduce_fusion
  18.3 39.1 %all-gather.5.cloned.1.call-done = bf16[4096,128]{1,0:T(8,128)(2,1)} async-done(((bf16[256,128]{1,0:T(8,128)(2,1)}), bf16[4096,128]{1,0:T(8,128)(2,1)}) %all-gather.5.cloned.1.call-update) | async-done | bytes 1048592 | tf_op jit(solution)/shard_map/all_gather | solution.py:123
  57.4 46.1 %all-gather.3.cloned.1.call-done = bf16[4096,128]{1,0:T(8,128)(2,1)} async-done(((bf16[256,128]{1,0:T(8,128)(2,1)}), bf16[4096,128]{1,0:T(8,128)(2,1)}) %all-gather.3.cloned.1.call-update) | async-done | bytes 1048592 | tf_op jit(solution)/shard_map/all_gather | solution.py:120
  103.5 92.3 %while.16 = (s32[]{:T(128)}, f32[256,1,5,128]{0,3,2,1:T(8,128)S(1)}, f32[8,512,256]{2,1,0:T(8,128)}, s32[8]{0:T(128)S(1)}, bf16[4096,128]{1,0:T(8,128)(2,1)}, /*...) while((s32[]{:T(128)}, ...), condition=%wide.region_2.3_spmd.clone, body=%wide.region_1.2_spmd.clone.sunk | while | flops 846802944 | bytes 19434012 | solution.py:168
  107.0 1.4 fusion.77
  108.4 1.7 fusion.80
  110.1 2.0 fusion.78
  112.6 1.4 fusion.79
  118.5 1.4 fusion.77
  119.9 1.7 fusion.80
  121.6 2.0 fusion.78
  124.1 1.4 fusion.79
  130.0 1.4 fusion.77
  131.4 1.7 fusion.80
  133.1 2.0 fusion.78
  135.7 1.4 fusion.79
  141.6 1.4 fusion.77
  143.0 1.7 fusion.80
  144.7 2.0 fusion.78
  147.2 1.4 fusion.79
  153.1 1.4 fusion.77
  154.5 1.7 fusion.80
  156.2 2.0 fusion.78
  158.7 1.4 fusion.79
  164.6 1.4 fusion.77
  166.0 1.7 fusion.80
  167.7 2.0 fusion.78
  170.2 1.4 fusion.79
  176.2 1.4 fusion.77
  177.6 1.7 fusion.80
  179.3 2.0 fusion.78
  181.8 1.4 fusion.79
  187.7 1.4 fusion.77
  189.1 1.7 fusion.80
  190.8 2.0 fusion.78
  193.4 1.4 fusion.79
  197.7 7.5 %fusion.46 = f32[256,5120]{1,0:T(8,128)} fusion(bf16[256,640]{0,1:T(8,128)(2,1)S(1)} %fusion.34, bf16[5120,640]{1,0:T(8,128)(2,1)} %param.23), kind=kOutput, calls=%fused_computation.91 | convolution fusion | flops 1677721600 | bytes 12124160 | tf_op jit(solution)/shard_map/dot_general | solution.py:188
  205.3 69.7 %reduce-scatter.3.cloned.1.call-done = f32[256,256]{1,0:T(8,128)} async-done(((f32[4096,256]{1,0:T(8,128)}), f32[256,256]{1,0:T(8,128)}) %reduce-scatter.3.cloned.1.call-update) | async-done | bytes 262160 | tf_op jit(solution)/shard_map/reduce_scatter | solution.py:170
  275.0 1.0 multiply_bitcast_fusion
  276.2 3.6 convolution_add_fusion.1
  279.8 3.2 fusion.31
  282.9 108.6 %reduce-scatter.5.cloned.1.call-done = f32[640,256]{0,1:T(8,128)} async-done(((f32[5120,256]{0,1:T(8,128)}), f32[640,256]{0,1:T(8,128)}) %reduce-scatter.5.cloned.1.call-update) | async-done | bytes 655376 | tf_op jit(solution)/shard_map/reduce_scatter | solution.py:195
  391.6 1.1 convert_element_type.93
  392.7 0.9 copy.45
  (145 shorter events, 42.4 us)
Async XLA Ops:
  6.5 269.6 %copy-start = (bf16[5120,128]{1,0:T(8,128)(2,1)S(1)}, bf16[5120,128]{1,0:T(8,128)(2,1)}, u32[]{:S(2)}) copy-start(bf16[5120,128]{1,0:T(8,128)(2,1)} %param.24) | copy-start | bytes 3932164
  6.5 5.5 %copy-start.9 = (bf16[256,640]{1,0:T(8,128)(2,1)S(1)}, bf16[256,640]{1,0:T(8,128)(2,1)}, u32[]{:S(2)}) copy-start(bf16[256,640]{1,0:T(8,128)(2,1)} %param.18) | copy-start | bytes 983044
  6.5 50.8 %all-gather.5.cloned.1.call-start = ((), (), s32[]{:S(2)}) async-start(), calls=%async_computation.3 | async-start | bytes 1114112 | tf_op jit(solution)/shard_map/all_gather | solution.py:123
  7.3 96.3 %all-gather.3.cloned.1.call-start = ((), (), s32[]{:S(2)}) async-start(), calls=%async_computation.2 | async-start | bytes 1114112 | tf_op jit(solution)/shard_map/all_gather | solution.py:120
  9.4 0.7 copy-start.2
  11.7 263.3 %reduce-scatter.3.cloned.1.call-start = ((), (), s32[]{:S(2)}) async-start(), calls=%async_computation.4 | async-start | bytes 4456448 | tf_op jit(solution)/shard_map/reduce_scatter | solution.py:170
  11.9 6.4 %copy-start.4 = (f32[256,128]{0,1:T(8,128)}, f32[256,128]{0,1:T(8,128)S(1)}, u32[]{:S(2)}) copy-start(f32[256,128]{0,1:T(8,128)S(1)} %copy.37) | copy-start | bytes 393220
  12.0 6.3 %copy-start.6 = (f32[256,128]{0,1:T(8,128)}, f32[256,128]{0,1:T(8,128)S(1)}, u32[]{:S(2)}) copy-start(f32[256,128]{0,1:T(8,128)S(1)} %copy.39) | copy-start | bytes 393220
  14.1 89.4 %copy-start.10 = (f32[5,256]{1,0:T(8,128)S(1)}, f32[5,256]{1,0:T(8,128)}, u32[]{:S(2)}) copy-start(f32[5,256]{1,0:T(8,128)} %param.19) | copy-start | bytes 15364
  195.8 0.9 copy-start.7
  195.8 195.7 %reduce-scatter.5.cloned.1.call-start = ((), (), s32[]{:S(2)}) async-start(), calls=%async_computation.5 | async-start | bytes 5898240 | tf_op jit(solution)/shard_map/reduce_scatter | solution.py:195
  196.7 0.9 copy-start.5
  197.7 77.3 %copy-start.3 = (f32[256,64]{1,0:T(8,128)S(1)}, f32[256,64]{1,0:T(8,128)}, u32[]{:S(2)}) copy-start(f32[256,64]{1,0:T(8,128)} %copy-done.2) | copy-start | bytes 196612
  276.1 3.6 copy-start.1
  276.1 3.6 copy-start.8
Sparse Core Ops, SparseCore 0:
  9.8 47.5 all-gather.4
  59.8 43.6 all-gather.2
  196.0 79.0 reduce-scatter.2
  283.1 108.4 reduce-scatter.4
where the time goes:
time: 403 us; the launch traced here: 400 us
  waiting for transfers between devices  264 us (66%)
  matrix products  69.8 us (17%)
  local copies, waits for them, and re-layouts  30.3 us (8%)
  other arithmetic  16.7 us (4%)
  between operations  13.4 us (3%)
  loops' own time  5.49 us (1%)
    reduce_scatter x1, waiting for transfers between devices, local(): lax.psum_scatter(result, 'tp', scatter_dimension=0, tiled=True)  109 us
    reduce_scatter x1, waiting for transfers between devices, local(): summed = lax.psum_scatter(terms, 'ctx', scatter_dimension=0, tiled=True)  69.7 us
    all_gather x1, waiting for transfers between devices, local(): lax.all_gather(key_rotated.reshape(tok_rows, kv_local * HEAD_SIZE), 'ctx'...  46.1 us
    all_gather x1, waiting for transfers between devices, local(): lax.all_gather(value, 'ctx', axis=0, tiled=True)  39.1 us
    dot_general x8, matrix products, score_grads(): jnp.einsum('tkgd,skd->tkgs', grad_blk, value_blk, preferred_element_type=...  15.6 us
    dot_general x8, matrix products, all_terms(): jnp.einsum('tkgs,tkgd->skd', probs_bf, grad_four, preferred_element_type=...  13.5 us
    dot_general x8, matrix products, score_grads(): jnp.einsum('tkgd,skd->tkgs', query_blk, key_blk, preferred_element_type=j...  11.1 us
    dot_general x8, matrix products, all_terms(): jnp.einsum('tkgs,skd->tkgd', dscore_bf, key_blk, preferred_element_type=j...  10.9 us
  transfers between devices with their start and end apart: 4, of which 4 were waited for; matrix products, arithmetic and copies ran while one was open for 5% of the time, Pallas kernels for 0%

commit v1 on v0

v1 whole, which is shorter than its diff:
```python
import numpy as np
import jax
import jax.numpy as jnp
from jax import lax
from jax.experimental import pallas as pl
from jax.experimental.pallas import tpu as pltpu
from jax.sharding import Mesh, PartitionSpec as P

HEAD = 128
TILE = 128
GROUPS = 5
TOK = 256
TILES = 32
ROWS = GROUPS * TILE
SCALE = HEAD**-0.5
ROPE_BASE = 1000000.0
CTX = ("y", "zh", "core")
TP = ("x", "zl")
SLOTS = ((0, 0), (0, 1), (1, 0), (3, 0), (2, 0), (1, 1), (3, 1), (2, 1))

f32 = jnp.float32
bf16 = jnp.bfloat16


def shift(x, axes, sizes, offs):
    perm = []
    for source in np.ndindex(*sizes):
        dest = tuple((a + o) % s for a, o, s in zip(source, offs, sizes))
        perm.append(
            (int(np.ravel_multi_index(source, sizes)), int(np.ravel_multi_index(dest, sizes)))
        )
    return lax.ppermute(x, axes, perm)


def shift_y(x, k):
    return shift(x, ("y",), (4,), (k % 4,))


def swap_zh(x):
    return shift(x, ("zh",), (2,), (1,))


def swap_core(x):
    return shift(x, ("core",), (2,), (1,))


def rope_tables(positions):
    half = HEAD // 2
    exponent = jnp.arange(half).astype(f32) * (2.0 / HEAD)
    inverse = jnp.power(f32(ROPE_BASE), -exponent)
    angles = positions.astype(f32)[:, None] * inverse[None, :]
    cosine, sine = jnp.cos(angles), jnp.sin(angles)
    return jnp.concatenate([cosine, cosine], 1), jnp.concatenate([sine, sine], 1)


def half_sign(shape, axis):
    return jnp.where(lax.broadcasted_iota(jnp.int32, shape, axis) < HEAD // 2, -1.0, 1.0).astype(f32)


def prep_kernel(query, grad, att, cos, sin, q_rows, q_cols, g_rows, g_cols, delta):
    sign = half_sign((TILE, HEAD), 1)
    for t in range(2):
        tok = pl.ds(t * TILE, TILE)
        c, s = cos[tok, :], sin[tok, :] * sign
        for h in range(GROUPS):
            feat = pl.ds(h * HEAD, HEAD)
            lane = pl.ds(h * TILE, TILE)
            x = query[tok, feat].astype(f32)
            rot = (x * c + pltpu.roll(x, HEAD // 2, 1) * s).astype(bf16)
            q_rows[t, lane, :] = rot
            q_cols[t, :, lane] = rot.T
            g = grad[tok, feat]
            g_rows[t, lane, :] = g
            g_cols[t, :, lane] = g.T
            prod = g.astype(f32) * att[tok, feat].astype(f32)
            delta[t, :, lane] = jnp.sum(prod.T, axis=0, keepdims=True)


def attention_kernel(
    mask, info, seg, lse, delta, cos, sin, q_rows, q_cols, g_rows, g_cols, kv_mine, kv_other,
    dkv_mine, dkv_other, qg, kv, dkv, acc, dq, sem,
):
    first = pltpu.make_async_copy(kv_mine, kv.at[pl.ds(0, 8 * TOK)], sem.at[0])
    second = pltpu.make_async_copy(kv_other, kv.at[pl.ds(8 * TOK, 8 * TOK)], sem.at[1])
    first.start()
    second.start()
    dq[...] = jnp.zeros_like(dq)
    first.wait()
    second.wait()
    q_tile = info[TILES]

    def pair(t, start, allowed):
        keys = kv[pl.ds(start, TILE), :HEAD]
        vals = kv[pl.ds(start, TILE), HEAD:]
        keys_t = keys.T
        scores = jnp.dot(keys, q_cols[t], preferred_element_type=f32)
        probs = jnp.exp(scores * SCALE - lse[t])
        if allowed is not None:
            probs = jnp.where(allowed, probs, 0.0)
        dprobs = jnp.dot(vals, g_cols[t], preferred_element_type=f32)
        dscore = (probs * (dprobs - delta[t])).astype(bf16)
        probs = probs.astype(bf16)
        dq[t] += jnp.dot(keys_t, dscore, preferred_element_type=f32)
        acc[:, :HEAD] += jnp.dot(dscore, q_rows[t], preferred_element_type=f32)
        acc[:, HEAD:] += jnp.dot(probs, g_rows[t], preferred_element_type=f32)

    def step(j, carry):
        tile = info[j]
        need0 = mask[q_tile, tile] > 0
        need1 = mask[q_tile + 1, tile] > 0
        start = pl.multiple_of(j * TILE, TILE)

        @pl.when(need0 | need1)
        def _():
            acc[...] = jnp.zeros_like(acc)
            for t, need in ((0, need0), (1, need1)):
                diagonal = need & (tile == q_tile + t)

                @pl.when(need & jnp.logical_not(diagonal))
                def _():
                    pair(t, start, None)

                @pl.when(diagonal)
                def _():
                    row = jnp.broadcast_to(seg[t], (TILE, TILE))
                    causal = lax.broadcasted_iota(jnp.int32, (TILE, TILE), 0) <= (
                        lax.broadcasted_iota(jnp.int32, (TILE, TILE), 1)
                    )
                    one = jnp.where((row.T == row) & causal, 1.0, 0.0)
                    pair(t, start, jnp.concatenate([one] * GROUPS, 1) > 0.5)

            dkv[pl.ds(start, TILE), :] = acc[...].astype(bf16)

        @pl.when(jnp.logical_not(need0 | need1))
        def _():
            dkv[pl.ds(start, TILE), :] = jnp.zeros((TILE, 2 * HEAD), bf16)

        return carry

    lax.fori_loop(0, TILES, step, 0)
    first = pltpu.make_async_copy(dkv.at[pl.ds(0, 8 * TOK)], dkv_mine, sem.at[0])
    second = pltpu.make_async_copy(dkv.at[pl.ds(8 * TOK, 8 * TOK)], dkv_other, sem.at[1])
    second.start()
    first.start()
    sign = half_sign((HEAD, TILE), 0)
    for t in range(2):
        tok = pl.ds(t * TILE, TILE)
        c, s = cos[tok, :].T, sin[tok, :].T
        for h in range(GROUPS):
            g = dq[t, :, pl.ds(h * TILE, TILE)] * SCALE
            u = g * s
            half = HEAD // 2
            turned = jnp.concatenate([u[half:], -u[:half]], 0)
            qg[pl.ds(h * HEAD, HEAD), tok] = (g * c + turned).astype(bf16)
    first.wait()
    second.wait()


def vmem(n):
    return [pl.BlockSpec(memory_space=pltpu.VMEM)] * n


def prep(query, grad, att, cos, sin):
    s = jax.ShapeDtypeStruct
    return pl.pallas_call(
        prep_kernel,
        out_shape=(
            s((2, ROWS, HEAD), bf16),
            s((2, HEAD, ROWS), bf16),
            s((2, ROWS, HEAD), bf16),
            s((2, HEAD, ROWS), bf16),
            s((2, 1, ROWS), f32),
        ),
        in_specs=vmem(5),
        out_specs=tuple(vmem(5)),
        compiler_params=pltpu.CompilerParams(vmem_limit_bytes=32 << 20),
        cost_estimate=pl.CostEstimate(flops=10000000, bytes_accessed=3000000, transcendentals=0),
        name="prep",
    )(query, grad, att, cos, sin)


def attention(mask, info, seg, lse, delta, cos, sin, q_rows, q_cols, g_rows, g_cols, mine, other):
    s = jax.ShapeDtypeStruct
    smem = [pl.BlockSpec(memory_space=pltpu.SMEM)] * 2
    hbm = [pl.BlockSpec(memory_space=pl.ANY)] * 2
    return pl.pallas_call(
        attention_kernel,
        out_shape=(
            s((8 * TOK, 2 * HEAD), bf16),
            s((8 * TOK, 2 * HEAD), bf16),
            s((ROWS, TOK), bf16),
        ),
        in_specs=smem + vmem(9) + hbm,
        out_specs=tuple(hbm + vmem(1)),
        scratch_shapes=[
            pltpu.VMEM((16 * TOK, 2 * HEAD), bf16),
            pltpu.VMEM((16 * TOK, 2 * HEAD), bf16),
            pltpu.VMEM((TILE, 2 * HEAD), f32),
            pltpu.VMEM((2, HEAD, ROWS), f32),
            pltpu.SemaphoreType.DMA((2,)),
        ],
        compiler_params=pltpu.CompilerParams(vmem_limit_bytes=48 << 20),
        cost_estimate=pl.CostEstimate(
            flops=2000000000, bytes_accessed=8000000, transcendentals=1000000
        ),
        name="attention",
    )(mask, info, seg, lse, delta, cos, sin, q_rows, q_cols, g_rows, g_cols, mine, other)


def local(
    query, key, value, att, grad, lse, block_mask, positions, segments, w_query, key_weight,
    value_weight,
):
    y, zh, core = lax.axis_index("y"), lax.axis_index("zh"), lax.axis_index("core")
    me = lax.axis_index(CTX)
    cos, sin = rope_tables(positions)
    half = HEAD // 2
    key_f = key.astype(f32)
    turned = jnp.concatenate([-key_f[:, half:], key_f[:, :half]], 1)
    key_rot = (key_f * cos + turned * sin).astype(bf16)
    block = jnp.concatenate([key_rot, value], 1)

    across = swap_zh(block)
    near = [shift_y(block, k) for k in (1, 3, 2)]
    far = [shift_y(across, k) for k in (1, 3, 2)]
    q_rows, q_cols, g_rows, g_cols, delta = prep(query, grad, att, cos, sin)
    mine = jnp.concatenate([block, across] + near + far, 0)
    other = swap_core(mine)

    owners = [
        ((y - dy) % 4) * 4 + ((zh - dz) % 2) * 2 + (core + dc) % 2
        for dc in (0, 1)
        for dy, dz in SLOTS
    ]
    tiles = (2 * jnp.stack(owners)[:, None] + jnp.arange(2)[None, :]).reshape(-1)
    info = jnp.concatenate([tiles, 2 * me[None]]).astype(jnp.int32)
    seg = lax.dynamic_slice_in_dim(segments, me * TOK, TOK).astype(f32).reshape(2, 1, TILE)
    lse_rows = lse.reshape(GROUPS, 2, TILE).transpose(1, 0, 2).reshape(2, 1, ROWS)
    dkv_mine, dkv_other, query_grad = attention(
        block_mask, info, seg, lse_rows, delta, cos, sin, q_rows, q_cols, g_rows, g_cols, mine, other
    )

    summed = dkv_mine.astype(f32) + swap_core(dkv_other).astype(f32)
    parts = lax.optimization_barrier(summed.astype(bf16)).reshape(8, TOK, 2 * HEAD)
    far = [shift_y(parts[5 + i], -k) for i, k in enumerate((1, 3, 2))]
    near = [shift_y(parts[2 + i], -k) for i, k in enumerate((1, 3, 2))]
    across = parts[1].astype(f32) + sum(p.astype(f32) for p in far)
    across = swap_zh(lax.optimization_barrier(across.astype(bf16)))
    total = parts[0].astype(f32) + across.astype(f32) + sum(p.astype(f32) for p in near)

    key_rot_grad = total[:, :HEAD] * SCALE
    u = key_rot_grad * sin
    key_grad = (
        key_rot_grad * cos + jnp.concatenate([u[:, half:], -u[:, :half]], 1)
    ).astype(bf16)
    value_grad = total[:, HEAD:].astype(bf16)

    result = jnp.dot(w_query, query_grad, preferred_element_type=f32)
    contract = (((1,), (1,)), ((), ()))
    result = result + lax.dot_general(key_weight, key_grad, contract, preferred_element_type=f32)
    result = result + lax.dot_general(
        value_weight, value_grad, contract, preferred_element_type=f32
    )
    send = lax.optimization_barrier(result.astype(bf16)).reshape(8, 640, TOK)
    got = lax.all_to_all(send, TP, 0, 0)
    return jnp.sum(got.astype(f32), 0).astype(bf16)


def solution(mesh):
    fine = Mesh(mesh.devices.reshape(4, 2, 2, 4, 2), ("y", "zh", "core", "x", "zl"))
    in_specs = (
        P(CTX, TP),
        P(CTX, TP),
        P(CTX, TP),
        P(CTX, TP),
        P(CTX, TP),
        P(TP, CTX),
        P(),
        P(CTX),
        P(),
        P(None, TP),
        P(None, TP),
        P(None, TP),
    )
    return jax.shard_map(
        local, mesh=fine, in_specs=in_specs, out_specs=P(TP, CTX), check_vma=False
    )
```

time: 403 us -> 109 us (0.27)
  waiting for transfers between devices: 264 us -> 14 us
  matrix products: 69.8 us -> 7.08 us
  blocking collectives: 0 us -> 36.3 us
  starting transfers between devices: 0.12 us -> 29.3 us
  local copies, waits for them, and re-layouts: 30.3 us -> 7.51 us
  between operations: 13.4 us -> 0.19 us
  other arithmetic: 16.7 us -> 8.37 us
  Pallas kernels: 0 us -> 5.81 us
  loops' own time: 5.49 us -> 0 us
    reduce_scatter x2 -> x0, waiting for transfers between devices: 178 us -> none  [the longest x1 109 us: local(): lax.psum_scatter(result, 'tp', scatter_dimension=0, tiled=True)]
    all_gather x2 -> x0, waiting for transfers between devices: 85.2 us -> none  [the longest x1 46.1 us: local(): lax.all_gather(key_rotated.reshape(tok_rows, kv_local * HEAD_SIZE), 'ctx'...]
    dot_general x43 -> x3, matrix products: 69.8 us -> 7.08 us  [the longest x1 5.33 us: local(): result = jnp.dot(w_query, query_grad, preferred_element_type=f32)]
    all_to_all x0 -> x1, blocking collectives: none -> 36.3 us  [local(): got = lax.all_to_all(send, TP, 0, 0)]
    ppermute x0 -> x16, starting transfers between devices: none -> 29.3 us  [shift(): return lax.ppermute(x, axes, perm)]
    ppermute x0 -> x16, waiting for transfers between devices: none -> 14 us  [shift(): return lax.ppermute(x, axes, perm)]
    dynamic_slice x17 -> x0, local copies, waits for them, and re-layouts: 11.5 us -> none  [the longest x8 6.07 us: pair_mask(): seg_key = lax.dynamic_slice_in_dim(segments, k_start, k_count)]
    dynamic_update_slice x16 -> x0, local copies, waits for them, and re-layouts: 8.37 us -> none  [local(): lax.scan(all_terms, query_empty, jnp.arange(key_total // key_step))]
  transfers between devices with their start and end apart: 4 -> 16, of which waited for: 4 -> 6; matrix products, arithmetic and copies ran while one was open for 5% -> 5% of each run, Pallas kernels for 0% -> 1%
where the time goes in v1:
time: 109 us
  blocking collectives  36.3 us (33%)
  starting transfers between devices  29.3 us (27%)
  waiting for transfers between devices  14 us (13%)
  other arithmetic  8.37 us (8%)
  local copies, waits for them, and re-layouts  7.51 us (7%)
  matrix products  7.08 us (6%)
  Pallas kernels  5.81 us (5%)
    all_to_all x1, blocking collectives, local(): got = lax.all_to_all(send, TP, 0, 0)  36.3 us
    ppermute x16, starting transfers between devices, shift(): return lax.ppermute(x, axes, perm)  29.3 us
    ppermute x16, waiting for transfers between devices, shift(): return lax.ppermute(x, axes, perm)  14 us
    dot_general x1, matrix products, local(): result = jnp.dot(w_query, query_grad, preferred_element_type=f32)  5.33 us
    pallas_call x1, Pallas kernels, attention(): pl.pallas_call(attention_kernel, out_shape=(s((8 * TOK, 2 * HEAD), bf16),...  4.99 us
    unnamed x20, local copies, waits for them, and re-layouts  4.45 us
    reduce_sum x1, other arithmetic, local(): return jnp.sum(got.astype(f32), 0).astype(bf16)  2.22 us
  transfers between devices with their start and end apart: 16, of which 6 were waited for; matrix products, arithmetic and copies ran while one was open for 5% of the time, Pallas kernels for 1%

profile of v1, /device:TPU:0, one launch (start us, length us, event | category | flops | bytes accessed | tf_op | source)
XLA Modules:
  0.0 108.6 jit_solution(9158886562133260998)
XLA Ops:
  0.0 1.0 slice.66
  1.0 0.9 convert_element_type.73
  1.9 0.7 convert_element_type.71
  2.6 0.5 multiply_sine_fusion
  3.1 1.0 fusion.4
  4.1 1.5 %pad_maximum_fusion.2 = (bf16[256,256]{1,0:T(8,128)(2,1)S(1)}, bf16[2048,256]{1,0:T(8,128)(2,1)}) fusion(bf16[256,128]{1,0:T(8,128)(2,1)} %param.14, bf16[256,128]{1,0:T(8,128)(2,1)S(1)} %get-tuple-element.31), kind=kLoop, calls=%fused_computation.19 | loop fusion | flops 262143 | bytes 393216 | tf_op jit(solution)/shard_map/concatenate | solution.py:221
  5.6 4.0 %collective-permute-start = (bf16[256,256]{1,0:T(8,128)(2,1)S(1)}, bf16[256,256]{1,0:T(8,128)(2,1)S(1)}, u32[]{:S(2)}, u32[]{:S(2)}) collective-permute-start(bf16[256,256]{1,0:T(8,128)(2,1)S(1)} %get-tuple-element.29), channel_id=1, source_target_pairs={{0,16},{16,0},{1,17},{17,1},{2,18},{18,2},{3,19},{19,3},{4,20},{20... | collective-permute-start | bytes 393224 | tf_op jit(solution)/shard_map/ppermute | solution.py:32
  9.6 1.6 %collective-permute-start.1 = (bf16[256,256]{1,0:T(8,128)(2,1)S(1)}, bf16[256,256]{1,0:T(8,128)(2,1)S(1)}, u32[]{:S(2)}, u32[]{:S(2)}) collective-permute-start(bf16[256,256]{1,0:T(8,128)(2,1)S(1)} %get-tuple-element.29), channel_id=1, source_target_pairs={{0,32},{32,64},{64,96},{96,0},{1,33},{33,65},{65,97},{97,1},{2,34}... | collective-permute-start | bytes 393224 | tf_op jit(solution)/shard_map/ppermute | solution.py:32
  11.2 1.7 %collective-permute-start.2 = (bf16[256,256]{1,0:T(8,128)(2,1)S(1)}, bf16[256,256]{1,0:T(8,128)(2,1)S(1)}, u32[]{:S(2)}, u32[]{:S(2)}) collective-permute-start(bf16[256,256]{1,0:T(8,128)(2,1)S(1)} %get-tuple-element.29), channel_id=1, source_target_pairs={{0,96},{32,0},{64,32},{96,64},{1,97},{33,1},{65,33},{97,65},{2,98}... | collective-permute-start | bytes 393224 | tf_op jit(solution)/shard_map/ppermute | solution.py:32
  12.9 2.0 %collective-permute-start.3 = (bf16[256,256]{1,0:T(8,128)(2,1)S(1)}, bf16[256,256]{1,0:T(8,128)(2,1)S(1)}, u32[]{:S(2)}, u32[]{:S(2)}) collective-permute-start(bf16[256,256]{1,0:T(8,128)(2,1)S(1)} %get-tuple-element.29), channel_id=1, source_target_pairs={{0,64},{32,96},{64,0},{96,32},{1,65},{33,97},{65,1},{97,33},{2,66}... | collective-permute-start | bytes 393224 | tf_op jit(solution)/shard_map/ppermute | solution.py:32
  14.8 1.5 %collective-permute-start.6 = (bf16[256,256]{1,0:T(8,128)(2,1)S(1)}, bf16[256,256]{1,0:T(8,128)(2,1)S(1)}, u32[]{:S(2)}, u32[]{:S(2)}) collective-permute-start(bf16[256,256]{1,0:T(8,128)(2,1)S(1)} %collective-permute-done), channel_id=1, source_target_pairs={{0,64},{32,96},{64,0},{96,32},{1,65},{33,97},{65,1},{97,33},{2,66}... | collective-permute-start | bytes 393224 | tf_op jit(solution)/shard_map/ppermute | solution.py:32
  16.4 1.8 %collective-permute-start.5 = (bf16[256,256]{1,0:T(8,128)(2,1)S(1)}, bf16[256,256]{1,0:T(8,128)(2,1)S(1)}, u32[]{:S(2)}, u32[]{:S(2)}) collective-permute-start(bf16[256,256]{1,0:T(8,128)(2,1)S(1)} %collective-permute-done), channel_id=1, source_target_pairs={{0,96},{32,0},{64,32},{96,64},{1,97},{33,1},{65,33},{97,65},{2,98}... | collective-permute-start | bytes 393224 | tf_op jit(solution)/shard_map/ppermute | solution.py:32
  18.2 0.7 constant_dynamic-update-slice_fusion.6
  18.9 0.2 collective-permute-start.4
  19.1 0.7 constant_dynamic-update-slice_fusion.5
  19.7 0.7 constant_dynamic-update-slice_fusion.4
  20.4 0.6 collective-permute-done.3
  21.0 0.7 constant_dynamic-update-slice_fusion.3
  21.6 3.8 %collective-permute-done.4 = bf16[256,256]{1,0:T(8,128)(2,1)S(1)} collective-permute-done((bf16[256,256]{1,0:T(8,128)(2,1)S(1)}, bf16[256,256]{1,0:T(8,128)(2,1)S(1)}, u32[]{:S(2)}, u32[]{:S(2)}) %collective-permute-start.4) | collective-permute-done | bytes 131104 | tf_op jit(solution)/shard_map/ppermute | solution.py:32
  25.5 0.7 constant_dynamic-update-slice_fusion.2
  26.1 0.7 constant_dynamic-update-slice_fusion.1
  26.8 0.7 constant_dynamic-update-slice_fusion.kv_mine
  27.5 0.1 stack.67
  27.8 0.8 prep.1
  28.7 0.8 dynamic-slice_convert_fusion
  29.4 1.0 collective-permute-done.7.kv_other
  30.4 5.0 %attention.1 = (bf16[2048,256]{1,0:T(8,128)(2,1)S(1)}, bf16[2048,256]{1,0:T(8,128)(2,1)S(1)}, bf16[640,256]{1,0:T(8,128)(2,1)S(1)}) custom-call(s32[32,32]{1,0:T(8,128)S(1)} %copy-done.4, s32[33]{0:T(128)S(1)} %pad_add_fusion.info, f32[2,1,128]{2,1,0:T(1,128)S(1)} %bitcast.31, f32[2,1,640]{2,1,0:T(1,128)S(1)} %reshape.177.lse, ...), custom_call_target="tpu_custom_call" | custom-call | flops 2000000000 | bytes 8000000 | tf_op jit(solution)/shard_map/attention/pallas_call | solution.py:186
  35.4 2.2 %collective-permute-start.8 = (bf16[2048,256]{1,0:T(8,128)(2,1)S(1)}, bf16[2048,256]{1,0:T(8,128)(2,1)S(1)}, u32[]{:S(2)}, u32[]{:S(2)}) collective-permute-start(bf16[2048,256]{1,0:T(8,128)(2,1)S(1)} %get-tuple-element.20), channel_id=1, source_target_pairs={{0,8},{8,0},{1,9},{9,1},{2,10},{10,2},{3,11},{11,3},{4,12},{12,4},... | collective-permute-start | bytes 3145736 | tf_op jit(solution)/shard_map/ppermute | solution.py:32
  37.7 2.3 %collective-permute-done.8 = bf16[2048,256]{1,0:T(8,128)(2,1)S(1)} collective-permute-done((bf16[2048,256]{1,0:T(8,128)(2,1)S(1)}, bf16[2048,256]{1,0:T(8,128)(2,1)S(1)}, u32[]{:S(2)}, u32[]{:S(2)}) %collective-permute-start.8) | collective-permute-done | bytes 1048608 | tf_op jit(solution)/shard_map/ppermute | solution.py:32
  40.0 0.3 add_convert_fusion
  40.3 1.5 %collective-permute-start.9 = (bf16[256,256]{1,0:T(8,128)(2,1)S(1)}, bf16[256,256]{1,0:T(8,128)(2,1)S(1)}, u32[]{:S(2)}, u32[]{:S(2)}) collective-permute-start(bf16[256,256]{1,0:T(8,128)(2,1)S(1)} %get-tuple-element.21), channel_id=1, source_target_pairs={{0,96},{32,0},{64,32},{96,64},{1,97},{33,1},{65,33},{97,65},{2,98}... | collective-permute-start | bytes 393224 | tf_op jit(solution)/shard_map/ppermute | solution.py:32
  41.8 0.8 collective-permute-start.11
  42.6 0.5 collective-permute-start.10
  43.1 3.5 %collective-permute-start.15 = (bf16[256,256]{1,0:T(8,128)(2,1)S(1)}, bf16[256,256]{1,0:T(8,128)(2,1)S(1)}, u32[]{:S(2)}, u32[]{:S(2)}) collective-permute-start(bf16[256,256]{1,0:T(8,128)(2,1)S(1)} %get-tuple-element.22), channel_id=1, source_target_pairs={{0,64},{32,96},{64,0},{96,32},{1,65},{33,97},{65,1},{97,33},{2,66}... | collective-permute-start | bytes 393224 | tf_op jit(solution)/shard_map/ppermute | solution.py:32
  46.6 0.1 collective-permute-start.14
  46.7 3.1 %collective-permute-start.13 = (bf16[256,256]{1,0:T(8,128)(2,1)S(1)}, bf16[256,256]{1,0:T(8,128)(2,1)S(1)}, u32[]{:S(2)}, u32[]{:S(2)}) collective-permute-start(bf16[256,256]{1,0:T(8,128)(2,1)S(1)} %get-tuple-element.24), channel_id=1, source_target_pairs={{0,96},{32,0},{64,32},{96,64},{1,97},{33,1},{65,33},{97,65},{2,98}... | collective-permute-start | bytes 393224 | tf_op jit(solution)/shard_map/ppermute | solution.py:32
  49.8 2.8 %collective-permute-done.10 = bf16[256,256]{1,0:T(8,128)(2,1)S(1)} collective-permute-done((bf16[256,256]{1,0:T(8,128)(2,1)S(1)}, bf16[256,256]{1,0:T(8,128)(2,1)S(1)}, u32[]{:S(2)}, u32[]{:S(2)}) %collective-permute-start.10) | collective-permute-done | bytes 131104 | tf_op jit(solution)/shard_map/ppermute | solution.py:32
  52.6 4.9 %collective-permute-start.12 = (bf16[256,256]{1,0:T(8,128)(2,1)S(1)}, bf16[256,256]{1,0:T(8,128)(2,1)S(1)}, u32[]{:S(2)}, u32[]{:S(2)}) collective-permute-start(bf16[256,256]{1,0:T(8,128)(2,1)S(1)} %add_convert_fusion.1), channel_id=1, source_target_pairs={{0,16},{16,0},{1,17},{17,1},{2,18},{18,2},{3,19},{19,3},{4,20},{20... | collective-permute-start | bytes 393224 | tf_op jit(solution)/shard_map/ppermute | solution.py:32
  57.6 3.5 %collective-permute-done.12 = bf16[256,256]{1,0:T(8,128)(2,1)S(1)} collective-permute-done((bf16[256,256]{1,0:T(8,128)(2,1)S(1)}, bf16[256,256]{1,0:T(8,128)(2,1)S(1)}, u32[]{:S(2)}, u32[]{:S(2)}) %collective-permute-start.12) | collective-permute-done | bytes 131104 | tf_op jit(solution)/shard_map/ppermute | solution.py:32
  61.1 0.1 fusion.6
  61.3 0.8 fusion.9
  62.2 0.5 copy-done.5
  62.6 0.9 fusion.7
  63.5 5.3 %fusion.2 = bf16[5120,256]{0,1:T(8,128)(2,1)S(1)} fusion(f32[256,5120]{1,0:T(8,128)S(1)} %fusion.9, f32[256,5120]{1,0:T(8,128)S(1)} %fusion.7, bf16[640,256]{1,0:T(8,128)(2,1)S(1)} %get-tuple-element.18, bf16[5120,640]{1,0:T(8,128)(2,1)} %param.21), kind=kOutput, calls=%fused_computation.3 | convolution fusion | flops 1681653760 | bytes 19988480 | tf_op jit(solution)/shard_map/dot_general | solution.py:258
  68.9 0.2 copy.24
  69.1 36.3 %all_to_all.5 = bf16[8,640,256]{1,2,0:T(8,128)(2,1)} all-to-all(bf16[8,640,256]{1,2,0:T(8,128)(2,1)S(1)} %bitcast.33), channel_id=1, replica_groups=mesh['y'=4,'zh'=2,'core'=2,'x'=4,'zl'=2] {'x','zl'}, dimensions={0} | all-to-all | bytes 5242880 | tf_op jit(solution)/shard_map/all_to_all | solution.py:265
  105.4 2.2 %reduce_sum.12 = bf16[640,256]{0,1:T(8,128)(2,1)S(1)} reduce(bf16[8,640,256]{1,2,0:T(8,128)(2,1)} %all_to_all.5, bf16[]{:T(256)} %constant.167.clone.1), dimensions={0}, to_apply=%region_0.1 | reduce | flops 1146880 | bytes 2949122 | tf_op jit(solution)/shard_map/reduce_sum | solution.py:266
  107.6 0.9 copy.20
  (34 shorter events, 0.7 us)
Async XLA Ops:
  0.0 61.3 %copy-start = (bf16[5120,128]{1,0:T(8,128)(2,1)S(1)}, bf16[5120,128]{1,0:T(8,128)(2,1)}, u32[]{:S(2)}) copy-start(bf16[5120,128]{1,0:T(8,128)(2,1)} %param.23) | copy-start | bytes 3932164
  0.0 27.4 %copy-start.6 = (f32[5,256]{1,0:T(8,128)S(1)}, f32[5,256]{1,0:T(8,128)}, u32[]{:S(2)}) copy-start(f32[5,256]{1,0:T(8,128)} %param.17) | copy-start | bytes 15364
  0.0 27.7 %copy-start.2 = (bf16[256,640]{1,0:T(8,128)(2,1)S(1)}, bf16[256,640]{1,0:T(8,128)(2,1)}, u32[]{:S(2)}) copy-start(bf16[256,640]{1,0:T(8,128)(2,1)} %grad.1) | copy-start | bytes 983044
  0.0 27.7 %copy-start.3 = (bf16[256,640]{1,0:T(8,128)(2,1)S(1)}, bf16[256,640]{1,0:T(8,128)(2,1)}, u32[]{:S(2)}) copy-start(bf16[256,640]{1,0:T(8,128)(2,1)} %att.1) | copy-start | bytes 983044
  0.0 27.7 %copy-start.1 = (bf16[256,640]{1,0:T(8,128)(2,1)S(1)}, bf16[256,640]{1,0:T(8,128)(2,1)}, u32[]{:S(2)}) copy-start(bf16[256,640]{1,0:T(8,128)(2,1)} %query.1) | copy-start | bytes 983044
  2.6 27.9 %copy-start.4 = (s32[32,32]{1,0:T(8,128)S(1)}, s32[32,32]{1,0:T(8,128)}, u32[]{:S(2)}) copy-start(s32[32,32]{1,0:T(8,128)} %mask.1) | copy-start | bytes 12292
  5.6 9.2 %collective-permute-start = (bf16[256,256]{1,0:T(8,128)(2,1)S(1)}, bf16[256,256]{1,0:T(8,128)(2,1)S(1)}, u32[]{:S(2)}, u32[]{:S(2)}) collective-permute-start(bf16[256,256]{1,0:T(8,128)(2,1)S(1)} %get-tuple-element.29), channel_id=1, source_target_pairs={{0,16},{16,0},{1,17},{17,1},{2,18},{18,2},{3,19},{19,3},{4,20},{20... | collective-permute-start | bytes 393224 | tf_op jit(solution)/shard_map/ppermute | solution.py:32
  9.6 9.2 %collective-permute-start.1 = (bf16[256,256]{1,0:T(8,128)(2,1)S(1)}, bf16[256,256]{1,0:T(8,128)(2,1)S(1)}, u32[]{:S(2)}, u32[]{:S(2)}) collective-permute-start(bf16[256,256]{1,0:T(8,128)(2,1)S(1)} %get-tuple-element.29), channel_id=1, source_target_pairs={{0,32},{32,64},{64,96},{96,0},{1,33},{33,65},{65,97},{97,1},{2,34}... | collective-permute-start | bytes 393224 | tf_op jit(solution)/shard_map/ppermute | solution.py:32
  11.2 8.6 %collective-permute-start.2 = (bf16[256,256]{1,0:T(8,128)(2,1)S(1)}, bf16[256,256]{1,0:T(8,128)(2,1)S(1)}, u32[]{:S(2)}, u32[]{:S(2)}) collective-permute-start(bf16[256,256]{1,0:T(8,128)(2,1)S(1)} %get-tuple-element.29), channel_id=1, source_target_pairs={{0,96},{32,0},{64,32},{96,64},{1,97},{33,1},{65,33},{97,65},{2,98}... | collective-permute-start | bytes 393224 | tf_op jit(solution)/shard_map/ppermute | solution.py:32
  12.9 8.1 %collective-permute-start.3 = (bf16[256,256]{1,0:T(8,128)(2,1)S(1)}, bf16[256,256]{1,0:T(8,128)(2,1)S(1)}, u32[]{:S(2)}, u32[]{:S(2)}) collective-permute-start(bf16[256,256]{1,0:T(8,128)(2,1)S(1)} %get-tuple-element.29), channel_id=1, source_target_pairs={{0,64},{32,96},{64,0},{96,32},{1,65},{33,97},{65,1},{97,33},{2,66}... | collective-permute-start | bytes 393224 | tf_op jit(solution)/shard_map/ppermute | solution.py:32
  14.8 11.9 %collective-permute-start.6 = (bf16[256,256]{1,0:T(8,128)(2,1)S(1)}, bf16[256,256]{1,0:T(8,128)(2,1)S(1)}, u32[]{:S(2)}, u32[]{:S(2)}) collective-permute-start(bf16[256,256]{1,0:T(8,128)(2,1)S(1)} %collective-permute-done), channel_id=1, source_target_pairs={{0,64},{32,96},{64,0},{96,32},{1,65},{33,97},{65,1},{97,33},{2,66}... | collective-permute-start | bytes 393224 | tf_op jit(solution)/shard_map/ppermute | solution.py:32
  16.4 9.7 %collective-permute-start.5 = (bf16[256,256]{1,0:T(8,128)(2,1)S(1)}, bf16[256,256]{1,0:T(8,128)(2,1)S(1)}, u32[]{:S(2)}, u32[]{:S(2)}) collective-permute-start(bf16[256,256]{1,0:T(8,128)(2,1)S(1)} %collective-permute-done), channel_id=1, source_target_pairs={{0,96},{32,0},{64,32},{96,64},{1,97},{33,1},{65,33},{97,65},{2,98}... | collective-permute-start | bytes 393224 | tf_op jit(solution)/shard_map/ppermute | solution.py:32
  18.9 6.6 %collective-permute-start.4 = (bf16[256,256]{1,0:T(8,128)(2,1)S(1)}, bf16[256,256]{1,0:T(8,128)(2,1)S(1)}, u32[]{:S(2)}, u32[]{:S(2)}) collective-permute-start(bf16[256,256]{1,0:T(8,128)(2,1)S(1)} %collective-permute-done), channel_id=1, source_target_pairs={{0,32},{32,64},{64,96},{96,0},{1,33},{33,65},{65,97},{97,1},{2,34}... | collective-permute-start | bytes 393224 | tf_op jit(solution)/shard_map/ppermute | solution.py:32
  27.4 3.0 %collective-permute-start.7 = (bf16[2048,256]{1,0:T(8,128)(2,1)}, bf16[2048,256]{1,0:T(8,128)(2,1)}, u32[]{:S(2)}, u32[]{:S(2)}) collective-permute-start(bf16[2048,256]{1,0:T(8,128)(2,1)} %constant_dynamic-update-slice_fusion.kv_mine), channel_id=1, source_target_pairs={{0,8},{8,0},{1,9},{9,1},{2,10},{10,2},{3,11},{11,3},{4,12},{12,4},... | collective-permute-start | bytes 3145736 | tf_op jit(solution)/shard_map/ppermute | solution.py:32
  35.4 4.5 %collective-permute-start.8 = (bf16[2048,256]{1,0:T(8,128)(2,1)S(1)}, bf16[2048,256]{1,0:T(8,128)(2,1)S(1)}, u32[]{:S(2)}, u32[]{:S(2)}) collective-permute-start(bf16[2048,256]{1,0:T(8,128)(2,1)S(1)} %get-tuple-element.20), channel_id=1, source_target_pairs={{0,8},{8,0},{1,9},{9,1},{2,10},{10,2},{3,11},{11,3},{4,12},{12,4},... | collective-permute-start | bytes 3145736 | tf_op jit(solution)/shard_map/ppermute | solution.py:32
  40.3 6.4 %collective-permute-start.9 = (bf16[256,256]{1,0:T(8,128)(2,1)S(1)}, bf16[256,256]{1,0:T(8,128)(2,1)S(1)}, u32[]{:S(2)}, u32[]{:S(2)}) collective-permute-start(bf16[256,256]{1,0:T(8,128)(2,1)S(1)} %get-tuple-element.21), channel_id=1, source_target_pairs={{0,96},{32,0},{64,32},{96,64},{1,97},{33,1},{65,33},{97,65},{2,98}... | collective-permute-start | bytes 393224 | tf_op jit(solution)/shard_map/ppermute | solution.py:32
  41.8 8.0 %collective-permute-start.11 = (bf16[256,256]{1,0:T(8,128)(2,1)S(1)}, bf16[256,256]{1,0:T(8,128)(2,1)S(1)}, u32[]{:S(2)}, u32[]{:S(2)}) collective-permute-start(bf16[256,256]{1,0:T(8,128)(2,1)S(1)} %get-tuple-element.25), channel_id=1, source_target_pairs={{0,64},{32,96},{64,0},{96,32},{1,65},{33,97},{65,1},{97,33},{2,66}... | collective-permute-start | bytes 393224 | tf_op jit(solution)/shard_map/ppermute | solution.py:32
  42.6 10.0 %collective-permute-start.10 = (bf16[256,256]{1,0:T(8,128)(2,1)S(1)}, bf16[256,256]{1,0:T(8,128)(2,1)S(1)}, u32[]{:S(2)}, u32[]{:S(2)}) collective-permute-start(bf16[256,256]{1,0:T(8,128)(2,1)S(1)} %get-tuple-element.26), channel_id=1, source_target_pairs={{0,32},{32,64},{64,96},{96,0},{1,33},{33,65},{65,97},{97,1},{2,34}... | collective-permute-start | bytes 393224 | tf_op jit(solution)/shard_map/ppermute | solution.py:32
  43.1 14.5 %collective-permute-start.15 = (bf16[256,256]{1,0:T(8,128)(2,1)S(1)}, bf16[256,256]{1,0:T(8,128)(2,1)S(1)}, u32[]{:S(2)}, u32[]{:S(2)}) collective-permute-start(bf16[256,256]{1,0:T(8,128)(2,1)S(1)} %get-tuple-element.22), channel_id=1, source_target_pairs={{0,64},{32,96},{64,0},{96,32},{1,65},{33,97},{65,1},{97,33},{2,66}... | collective-permute-start | bytes 393224 | tf_op jit(solution)/shard_map/ppermute | solution.py:32
  46.6 11.0 %collective-permute-start.14 = (bf16[256,256]{1,0:T(8,128)(2,1)S(1)}, bf16[256,256]{1,0:T(8,128)(2,1)S(1)}, u32[]{:S(2)}, u32[]{:S(2)}) collective-permute-start(bf16[256,256]{1,0:T(8,128)(2,1)S(1)} %get-tuple-element.23), channel_id=1, source_target_pairs={{0,32},{32,64},{64,96},{96,0},{1,33},{33,65},{65,97},{97,1},{2,34}... | collective-permute-start | bytes 393224 | tf_op jit(solution)/shard_map/ppermute | solution.py:32
  46.7 10.8 %collective-permute-start.13 = (bf16[256,256]{1,0:T(8,128)(2,1)S(1)}, bf16[256,256]{1,0:T(8,128)(2,1)S(1)}, u32[]{:S(2)}, u32[]{:S(2)}) collective-permute-start(bf16[256,256]{1,0:T(8,128)(2,1)S(1)} %get-tuple-element.24), channel_id=1, source_target_pairs={{0,96},{32,0},{64,32},{96,64},{1,97},{33,1},{65,33},{97,65},{2,98}... | collective-permute-start | bytes 393224 | tf_op jit(solution)/shard_map/ppermute | solution.py:32
  52.6 8.4 %collective-permute-start.12 = (bf16[256,256]{1,0:T(8,128)(2,1)S(1)}, bf16[256,256]{1,0:T(8,128)(2,1)S(1)}, u32[]{:S(2)}, u32[]{:S(2)}) collective-permute-start(bf16[256,256]{1,0:T(8,128)(2,1)S(1)} %add_convert_fusion.1), channel_id=1, source_target_pairs={{0,16},{16,0},{1,17},{17,1},{2,18},{18,2},{3,19},{19,3},{4,20},{20... | collective-permute-start | bytes 393224 | tf_op jit(solution)/shard_map/ppermute | solution.py:32
  61.3 1.3 %copy-start.5 = (bf16[5120,128]{1,0:T(8,128)(2,1)S(1)}, bf16[5120,128]{1,0:T(8,128)(2,1)}, u32[]{:S(2)}) copy-start(bf16[5120,128]{1,0:T(8,128)(2,1)} %param.22) | copy-start | bytes 3932164

commit v2 on v1

--- a/solution.py
+++ b/solution.py
@@ -16,7 +16,6 @@
 ROPE_BASE = 1000000.0
 CTX = ("y", "zh", "core")
 TP = ("x", "zl")
-SLOTS = ((0, 0), (0, 1), (1, 0), (3, 0), (2, 0), (1, 1), (3, 1), (2, 1))
 
 f32 = jnp.float32
 bf16 = jnp.bfloat16
@@ -44,17 +43,25 @@
     return shift(x, ("core",), (2,), (1,))
 
 
-def rope_tables(positions):
-    half = HEAD // 2
-    exponent = jnp.arange(half).astype(f32) * (2.0 / HEAD)
-    inverse = jnp.power(f32(ROPE_BASE), -exponent)
-    angles = positions.astype(f32)[:, None] * inverse[None, :]
-    cosine, sine = jnp.cos(angles), jnp.sin(angles)
-    return jnp.concatenate([cosine, cosine], 1), jnp.concatenate([sine, sine], 1)
+INVERSE = np.power(np.float64(ROPE_BASE), -np.arange(HEAD // 2) * (2.0 / HEAD)).astype(np.float32)
 
 
 def half_sign(shape, axis):
     return jnp.where(lax.broadcasted_iota(jnp.int32, shape, axis) < HEAD // 2, -1.0, 1.0).astype(f32)
+
+
+def block_kernel(key, value, positions, inverse, cos, sin, block):
+    sign = half_sign((TILE, HEAD), 1)
+    for t in range(2):
+        tok = pl.ds(t * TILE, TILE)
+        place = jnp.broadcast_to(positions[t], (TILE, TILE)).T
+        angles = place * inverse[...]
+        c, s = jnp.cos(angles), jnp.sin(angles)
+        cos[tok, :] = c
+        sin[tok, :] = s
+        x = key[tok, :].astype(f32)
+        block[tok, :HEAD] = (x * c + pltpu.roll(x, HEAD // 2, 1) * (s * sign)).astype(bf16)
+        block[tok, HEAD:] = value[tok, :]
 
 
 def prep_kernel(query, grad, att, cos, sin, q_rows, q_cols, g_rows, g_cols, delta):
@@ -87,7 +94,8 @@
     dq[...] = jnp.zeros_like(dq)
     first.wait()
     second.wait()
-    q_tile = info[TILES]
+    me = info[0]
+    q_tile = 2 * me
 
     def pair(t, start, allowed):
         keys = kv[pl.ds(start, TILE), :HEAD]
@@ -105,7 +113,11 @@
         acc[:, HEAD:] += jnp.dot(probs, g_rows[t], preferred_element_type=f32)
 
     def step(j, carry):
-        tile = info[j]
+        slot = lax.shift_right_logical(j, 1)
+        back_y = (lax.shift_right_logical(me, 2) - slot) & 3
+        back_rest = (me ^ (lax.shift_right_logical(slot, 1) & 2)) & 2
+        back_core = (me ^ lax.shift_right_logical(slot, 3)) & 1
+        tile = 2 * (4 * back_y + back_rest + back_core) + (j & 1)
         need0 = mask[q_tile, tile] > 0
         need1 = mask[q_tile + 1, tile] > 0
         start = pl.multiple_of(j * TILE, TILE)
@@ -207,63 +219,118 @@
     )(mask, info, seg, lse, delta, cos, sin, q_rows, q_cols, g_rows, g_cols, mine, other)
 
 
+def make_block(key, value, positions):
+    s = jax.ShapeDtypeStruct
+    inverse = jnp.asarray(np.concatenate([INVERSE, INVERSE])[None, :])
+    return pl.pallas_call(
+        block_kernel,
+        out_shape=(s((TOK, HEAD), f32), s((TOK, HEAD), f32), s((TOK, 2 * HEAD), bf16)),
+        in_specs=vmem(4),
+        out_specs=tuple(vmem(3)),
+        cost_estimate=pl.CostEstimate(flops=5000000, bytes_accessed=700000, transcendentals=60000),
+        name="block",
+    )(key, value, positions.astype(f32).reshape(2, 1, TILE), inverse)
+
+
+WIDTH = 5120
+STEP_ROWS = 640
+
+
+def project_kernel(
+    own, across, near1, near2, near3, cos, sin, qg, wq, wk, wv, out, kg, vg
+):
+    @pl.when(pl.program_id(0) == 0)
+    def _():
+        total = own[...].astype(f32) + across[...].astype(f32)
+        total += near1[...].astype(f32) + near2[...].astype(f32) + near3[...].astype(f32)
+        sign = half_sign((TOK, HEAD), 1)
+        g = total[:, :HEAD] * SCALE
+        key_grad = g * cos[...] - pltpu.roll(g * sin[...], HEAD // 2, 1) * sign
+        kg[...] = key_grad.T.astype(bf16)
+        vg[...] = total[:, HEAD:].T.astype(bf16)
+
+    result = jnp.dot(wq[...], qg[...], preferred_element_type=f32)
+    result += jnp.dot(wk[...], kg[...], preferred_element_type=f32)
+    result += jnp.dot(wv[...], vg[...], preferred_element_type=f32)
+    out[...] = result.astype(bf16)
+
+
+def project(own, across, near, cos, sin, qg, wq, wk, wv):
+    def whole(shape):
+        return pl.BlockSpec(shape, lambda i: (0, 0))
+
+    def rows(width):
+        return pl.BlockSpec((STEP_ROWS, width), lambda i: (i, 0))
+
+    return pl.pallas_call(
+        project_kernel,
+        grid=(WIDTH // STEP_ROWS,),
+        out_shape=jax.ShapeDtypeStruct((WIDTH, TOK), bf16),
+        in_specs=[whole((TOK, 2 * HEAD))] * 5
+        + [whole((TOK, HEAD))] * 2
+        + [whole((ROWS, TOK)), rows(ROWS), rows(HEAD), rows(HEAD)],
+        out_specs=rows(TOK),
+        scratch_shapes=[pltpu.VMEM((HEAD, TOK), bf16), pltpu.VMEM((HEAD, TOK), bf16)],
+        compiler_params=pltpu.CompilerParams(vmem_limit_bytes=32 << 20),
+        cost_estimate=pl.CostEstimate(
+            flops=2350000000, bytes_accessed=12000000, transcendentals=0
+        ),
+        name="project",
+    )(own, across, *near, cos, sin, qg, wq, wk, wv)
+
+
+def last_kernel(parts, out):
+    total = parts[0].astype(f32)
+    for i in range(1, 8):
+        total += parts[i].astype(f32)
+    out[...] = total.astype(bf16)
+
+
+def last_sum(parts):
+    return pl.pallas_call(
+        last_kernel,
+        grid=(5,),
+        out_shape=jax.ShapeDtypeStruct((640, TOK), bf16),
+        in_specs=[pl.BlockSpec((8, 128, TOK), lambda i: (0, i, 0))],
+        out_specs=pl.BlockSpec((128, TOK), lambda i: (i, 0)),
+        cost_estimate=pl.CostEstimate(flops=1300000, bytes_accessed=3000000, transcendentals=0),
+        name="last_sum",
+    )(parts)
+
+
 def local(
     query, key, value, att, grad, lse, block_mask, positions, segments, w_query, key_weight,
     value_weight,
 ):
-    y, zh, core = lax.axis_index("y"), lax.axis_index("zh"), lax.axis_index("core")
     me = lax.axis_index(CTX)
-    cos, sin = rope_tables(positions)
-    half = HEAD // 2
-    key_f = key.astype(f32)
-    turned = jnp.concatenate([-key_f[:, half:], key_f[:, :half]], 1)
-    key_rot = (key_f * cos + turned * sin).astype(bf16)
-    block = jnp.concatenate([key_rot, value], 1)
+    cos, sin, block = make_block(key, value, positions)
 
     across = swap_zh(block)
-    near = [shift_y(block, k) for k in (1, 3, 2)]
-    far = [shift_y(across, k) for k in (1, 3, 2)]
-    q_rows, q_cols, g_rows, g_cols, delta = prep(query, grad, att, cos, sin)
-    mine = jnp.concatenate([block, across] + near + far, 0)
-    other = swap_core(mine)
-
-    owners = [
-        ((y - dy) % 4) * 4 + ((zh - dz) % 2) * 2 + (core + dc) % 2
-        for dc in (0, 1)
-        for dy, dz in SLOTS
-    ]
-    tiles = (2 * jnp.stack(owners)[:, None] + jnp.arange(2)[None, :]).reshape(-1)
-    info = jnp.concatenate([tiles, 2 * me[None]]).astype(jnp.int32)
+    near = [shift_y(block, k) for k in (1, 2, 3)]
+    info = me.reshape(1)
     seg = lax.dynamic_slice_in_dim(segments, me * TOK, TOK).astype(f32).reshape(2, 1, TILE)
     lse_rows = lse.reshape(GROUPS, 2, TILE).transpose(1, 0, 2).reshape(2, 1, ROWS)
+    ready = (info, seg, lse_rows, *prep(query, grad, att, cos, sin))
+    across, ready = lax.optimization_barrier((across, ready))
+    info, seg, lse_rows, q_rows, q_cols, g_rows, g_cols, delta = ready
+    far = [shift_y(across, k) for k in (1, 2, 3)]
+    mine = jnp.concatenate([block] + near + [across] + far, 0)
+    other = swap_core(mine)
+
     dkv_mine, dkv_other, query_grad = attention(
         block_mask, info, seg, lse_rows, delta, cos, sin, q_rows, q_cols, g_rows, g_cols, mine, other
     )
 
     summed = dkv_mine.astype(f32) + swap_core(dkv_other).astype(f32)
     parts = lax.optimization_barrier(summed.astype(bf16)).reshape(8, TOK, 2 * HEAD)
-    far = [shift_y(parts[5 + i], -k) for i, k in enumerate((1, 3, 2))]
-    near = [shift_y(parts[2 + i], -k) for i, k in enumerate((1, 3, 2))]
-    across = parts[1].astype(f32) + sum(p.astype(f32) for p in far)
+    far = [shift_y(parts[4 + k], -k) for k in (1, 2, 3)]
+    near = [shift_y(parts[k], -k) for k in (1, 2, 3)]
+    across = parts[4].astype(f32) + sum(p.astype(f32) for p in far)
     across = swap_zh(lax.optimization_barrier(across.astype(bf16)))
-    total = parts[0].astype(f32) + across.astype(f32) + sum(p.astype(f32) for p in near)
-
-    key_rot_grad = total[:, :HEAD] * SCALE
-    u = key_rot_grad * sin
-    key_grad = (
-        key_rot_grad * cos + jnp.concatenate([u[:, half:], -u[:, :half]], 1)
-    ).astype(bf16)
-    value_grad = total[:, HEAD:].astype(bf16)
-
-    result = jnp.dot(w_query, query_grad, preferred_element_type=f32)
-    contract = (((1,), (1,)), ((), ()))
-    result = result + lax.dot_general(key_weight, key_grad, contract, preferred_element_type=f32)
-    result = result + lax.dot_general(
-        value_weight, value_grad, contract, preferred_element_type=f32
+    send = project(
+        parts[0], across, near, cos, sin, query_grad, w_query, key_weight, value_weight
     )
-    send = lax.optimization_barrier(result.astype(bf16)).reshape(8, 640, TOK)
-    got = lax.all_to_all(send, TP, 0, 0)
-    return jnp.sum(got.astype(f32), 0).astype(bf16)
+    return last_sum(lax.all_to_all(send.reshape(8, 640, TOK), TP, 0, 0))
 
 
 def solution(mesh):

time: 109 us -> 107 us (0.982)
  the two profiles are of different devices: /device:TPU:0 before, /device:TPU:24 now
where the time goes in v2:
time: 107 us
  blocking collectives  36.5 us (34%)
  starting transfers between devices  27.8 us (26%)
  waiting for transfers between devices  17.3 us (16%)
  Pallas kernels  15.8 us (15%)
  local copies, waits for them, and re-layouts  6.55 us (6%)
  other arithmetic  2.39 us (2%)
    all_to_all x1, blocking collectives, local(): return last_sum(lax.all_to_all(send.reshape(8, 640, TOK), TP, 0, 0))  36.5 us
    ppermute x16, starting transfers between devices, shift(): return lax.ppermute(x, axes, perm)  27.8 us
    ppermute x16, waiting for transfers between devices, shift(): return lax.ppermute(x, axes, perm)  17.3 us
    unnamed x31, local copies, waits for them, and re-layouts  5.77 us
    pallas_call x1, Pallas kernels, project(): pl.pallas_call(project_kernel, grid=(WIDTH // STEP_ROWS,), out_shape=jax....  4.95 us
    pallas_call x1, Pallas kernels, last_sum(): pl.pallas_call(last_kernel, grid=(5,), out_shape=jax.ShapeDtypeStruct((64...  4.12 us
    pallas_call x1, Pallas kernels, attention(): pl.pallas_call(attention_kernel, out_shape=(s((8 * TOK, 2 * HEAD), bf16),...  3.79 us
    pallas_call x1, Pallas kernels, make_block(): pl.pallas_call(block_kernel, out_shape=(s((TOK, HEAD), f32), s((TOK, HEAD...  2.17 us
  transfers between devices with their start and end apart: 16, of which 8 were waited for; matrix products, arithmetic and copies ran while one was open for 2% of the time, Pallas kernels for 1%

profile of v2, /device:TPU:24, one launch (start us, length us, event | category | flops | bytes accessed | tf_op | source)
XLA Modules:
  0.0 106.6 jit_solution(1848496363403340324)
XLA Ops:
  0.0 1.3 %convert_element_type.30 = f32[256]{0:T(256)} convert(s32[256]{0:T(256)} %param.20) | non-fusion elementwise | flops 256 | bytes 2048 | tf_op jit(solution)/shard_map/convert_element_type | solution.py:232
  1.3 2.2 %block.1 = (f32[256,128]{1,0:T(8,128)}, f32[256,128]{1,0:T(8,128)}, bf16[256,256]{1,0:T(8,128)(2,1)}) custom-call(bf16[256,128]{1,0:T(8,128)(2,1)} %key.1, bf16[256,128]{1,0:T(8,128)(2,1)} %value.1, f32[2,1,128]{2,1,0:T(1,128)} %bitcast.12, f32[1,128]{1,0:T(1,128)} %constant.27.clone.inverse), custom_call_target="tpu_custom_call" | custom-call | flops 5000000 | bytes 700000 | tf_op jit(solution)/shard_map/block/pallas_call | solution.py:225
  3.4 0.7 collective-permute-start.3
  4.2 0.9 collective-permute-start.2
  5.0 2.3 %collective-permute-start.1 = (bf16[256,256]{1,0:T(8,128)(2,1)}, bf16[256,256]{1,0:T(8,128)(2,1)S(1)}, u32[]{:S(2)}, u32[]{:S(2)}) collective-permute-start(bf16[256,256]{1,0:T(8,128)(2,1)} %get-tuple-element.25), channel_id=1, source_target_pairs={{0,32},{32,64},{64,96},{96,0},{1,33},{33,65},{65,97},{97,1},{2,34}... | collective-permute-start | bytes 393224 | tf_op jit(solution)/shard_map/ppermute | solution.py:31
  7.3 3.9 %collective-permute-start = (bf16[256,256]{1,0:T(8,128)(2,1)}, bf16[256,256]{1,0:T(8,128)(2,1)S(1)}, u32[]{:S(2)}, u32[]{:S(2)}) collective-permute-start(bf16[256,256]{1,0:T(8,128)(2,1)} %get-tuple-element.25), channel_id=1, source_target_pairs={{0,16},{16,0},{1,17},{17,1},{2,18},{18,2},{3,19},{19,3},{4,20},{20... | collective-permute-start | bytes 393224 | tf_op jit(solution)/shard_map/ppermute | solution.py:31
  11.2 0.9 constant_dynamic-update-slice_fusion.7
  12.1 0.8 dynamic-slice_convert_fusion
  12.9 0.7 reshape.39
  13.6 0.9 copy-done.2
  14.5 0.9 copy-done.4
  15.4 1.0 copy-done.6
  16.4 1.0 copy-done.7
  17.4 1.0 copy-done.8
  18.3 0.8 prep.1
  19.2 0.0 collective-permute-done
  19.2 0.3 collective-permute-start.6
  19.5 2.2 %collective-permute-start.5 = (bf16[256,256]{1,0:T(8,128)(2,1)S(1)}, bf16[256,256]{1,0:T(8,128)(2,1)S(1)}, u32[]{:S(2)}, u32[]{:S(2)}) collective-permute-start(bf16[256,256]{1,0:T(8,128)(2,1)S(1)} %collective-permute-done), channel_id=1, source_target_pairs={{0,64},{32,96},{64,0},{96,32},{1,65},{33,97},{65,1},{97,33},{2,66}... | collective-permute-start | bytes 393224 | tf_op jit(solution)/shard_map/ppermute | solution.py:31
  21.7 0.0 collective-permute-done.1
  21.7 2.5 %collective-permute-start.4 = (bf16[256,256]{1,0:T(8,128)(2,1)S(1)}, bf16[256,256]{1,0:T(8,128)(2,1)S(1)}, u32[]{:S(2)}, u32[]{:S(2)}) collective-permute-start(bf16[256,256]{1,0:T(8,128)(2,1)S(1)} %collective-permute-done), channel_id=1, source_target_pairs={{0,32},{32,64},{64,96},{96,0},{1,33},{33,65},{65,97},{97,1},{2,34}... | collective-permute-start | bytes 393224 | tf_op jit(solution)/shard_map/ppermute | solution.py:31
  24.2 0.0 collective-permute-done.2
  24.2 0.0 collective-permute-done.3
  24.3 3.7 %collective-permute-done.4 = bf16[256,256]{1,0:T(8,128)(2,1)S(1)} collective-permute-done((bf16[256,256]{1,0:T(8,128)(2,1)S(1)}, bf16[256,256]{1,0:T(8,128)(2,1)S(1)}, u32[]{:S(2)}, u32[]{:S(2)}) %collective-permute-start.4) | collective-permute-done | bytes 131104 | tf_op jit(solution)/shard_map/ppermute | solution.py:31
  28.0 0.0 collective-permute-done.5
  28.0 0.1 collective-permute-start.7
  28.1 0.0 slice-start
  28.1 0.0 slice-start.1
  28.2 2.6 %collective-permute-done.7.kv_other = bf16[2048,256]{1,0:T(8,128)(2,1)S(1)} collective-permute-done((bf16[2048,256]{1,0:T(8,128)(2,1)S(1)}, bf16[2048,256]{1,0:T(8,128)(2,1)S(1)}, u32[]{:S(2)}, u32[]{:S(2)}) %collective-permute-start.7) | collective-permute-done | bytes 1048608 | tf_op jit(solution)/shard_map/ppermute | solution.py:31
  30.8 3.8 %attention.1 = (bf16[2048,256]{1,0:T(8,128)(2,1)S(1)}, bf16[2048,256]{1,0:T(8,128)(2,1)S(1)}, bf16[640,256]{1,0:T(8,128)(2,1)S(1)}) custom-call(s32[32,32]{1,0:T(8,128)S(1)} %copy-done.9, s32[1]{0:T(128)} %bitcast.1.info, f32[2,1,128]{2,1,0:T(1,128)S(1)} %bitcast.10, f32[2,1,640]{2,1,0:T(1,128)S(1)} %copy.16.lse, f32[2,1,640]{2,1,0:T(1,128)S(1)} %get-tuple-element.36.delta, ...), custom_call_target="tpu_custom_call" | custom-call | flops 2000000000 | bytes 8000000 | tf_op jit(solution)/shard_map/attention/pallas_call | solution.py:198
  34.6 2.2 %collective-permute-start.8 = (bf16[2048,256]{1,0:T(8,128)(2,1)S(1)}, bf16[2048,256]{1,0:T(8,128)(2,1)S(1)}, u32[]{:S(2)}, u32[]{:S(2)}) collective-permute-start(bf16[2048,256]{1,0:T(8,128)(2,1)S(1)} %get-tuple-element.43), channel_id=1, source_target_pairs={{0,8},{8,0},{1,9},{9,1},{2,10},{10,2},{3,11},{11,3},{4,12},{12,4},... | collective-permute-start | bytes 3145736 | tf_op jit(solution)/shard_map/ppermute | solution.py:31
  36.8 2.3 %collective-permute-done.8 = bf16[2048,256]{1,0:T(8,128)(2,1)S(1)} collective-permute-done((bf16[2048,256]{1,0:T(8,128)(2,1)S(1)}, bf16[2048,256]{1,0:T(8,128)(2,1)S(1)}, u32[]{:S(2)}, u32[]{:S(2)}) %collective-permute-start.8) | collective-permute-done | bytes 1048608 | tf_op jit(solution)/shard_map/ppermute | solution.py:31
  39.1 0.3 add_convert_fusion
  39.4 0.1 fusion
  39.5 2.7 %collective-permute-start.11 = (bf16[256,256]{1,0:T(8,128)(2,1)S(1)}, bf16[256,256]{1,0:T(8,128)(2,1)S(1)}, u32[]{:S(2)}, u32[]{:S(2)}) collective-permute-start(bf16[256,256]{1,0:T(8,128)(2,1)S(1)} %get-tuple-element.48), channel_id=1, source_target_pairs={{0,32},{32,64},{64,96},{96,0},{1,33},{33,65},{65,97},{97,1},{2,34}... | collective-permute-start | bytes 393224 | tf_op jit(solution)/shard_map/ppermute | solution.py:31
  42.2 1.1 %collective-permute-start.10 = (bf16[256,256]{1,0:T(8,128)(2,1)S(1)}, bf16[256,256]{1,0:T(8,128)(2,1)S(1)}, u32[]{:S(2)}, u32[]{:S(2)}) collective-permute-start(bf16[256,256]{1,0:T(8,128)(2,1)S(1)} %get-tuple-element.49), channel_id=1, source_target_pairs={{0,64},{32,96},{64,0},{96,32},{1,65},{33,97},{65,1},{97,33},{2,66}... | collective-permute-start | bytes 393224 | tf_op jit(solution)/shard_map/ppermute | solution.py:31
  43.4 3.2 %collective-permute-start.15 = (bf16[256,256]{1,0:T(8,128)(2,1)S(1)}, bf16[256,256]{1,0:T(8,128)(2,1)S(1)}, u32[]{:S(2)}, u32[]{:S(2)}) collective-permute-start(bf16[256,256]{1,0:T(8,128)(2,1)S(1)} %get-tuple-element.45), channel_id=1, source_target_pairs={{0,32},{32,64},{64,96},{96,0},{1,33},{33,65},{65,97},{97,1},{2,34}... | collective-permute-start | bytes 393224 | tf_op jit(solution)/shard_map/ppermute | solution.py:31
  46.6 1.2 %collective-permute-start.14 = (bf16[256,256]{1,0:T(8,128)(2,1)S(1)}, bf16[256,256]{1,0:T(8,128)(2,1)S(1)}, u32[]{:S(2)}, u32[]{:S(2)}) collective-permute-start(bf16[256,256]{1,0:T(8,128)(2,1)S(1)} %get-tuple-element.46), channel_id=1, source_target_pairs={{0,64},{32,96},{64,0},{96,32},{1,65},{33,97},{65,1},{97,33},{2,66}... | collective-permute-start | bytes 393224 | tf_op jit(solution)/shard_map/ppermute | solution.py:31
  47.8 0.9 collective-permute-done.11
  48.7 1.4 %collective-permute-done.10 = bf16[256,256]{1,0:T(8,128)(2,1)S(1)} collective-permute-done((bf16[256,256]{1,0:T(8,128)(2,1)S(1)}, bf16[256,256]{1,0:T(8,128)(2,1)S(1)}, u32[]{:S(2)}, u32[]{:S(2)}) %collective-permute-start.10) | collective-permute-done | bytes 131104 | tf_op jit(solution)/shard_map/ppermute | solution.py:31
  50.1 2.9 %collective-permute-done.9 = bf16[256,256]{1,0:T(8,128)(2,1)S(1)} collective-permute-done((bf16[256,256]{1,0:T(8,128)(2,1)S(1)}, bf16[256,256]{1,0:T(8,128)(2,1)S(1)}, u32[]{:S(2)}, u32[]{:S(2)}) %collective-permute-start.9) | collective-permute-done | bytes 131104 | tf_op jit(solution)/shard_map/ppermute | solution.py:31
  53.0 0.1 add_convert_fusion.1
  53.1 4.5 %collective-permute-start.12 = (bf16[256,256]{1,0:T(8,128)(2,1)S(1)}, bf16[256,256]{1,0:T(8,128)(2,1)S(1)}, u32[]{:S(2)}, u32[]{:S(2)}) collective-permute-start(bf16[256,256]{1,0:T(8,128)(2,1)S(1)} %add_convert_fusion.1), channel_id=1, source_target_pairs={{0,16},{16,0},{1,17},{17,1},{2,18},{18,2},{3,19},{19,3},{4,20},{20... | collective-permute-start | bytes 393224 | tf_op jit(solution)/shard_map/ppermute | solution.py:31
  57.6 0.0 collective-permute-done.14.near2
  57.6 0.1 collective-permute-done.13.near1
  57.6 3.4 %collective-permute-done.12.across = bf16[256,256]{1,0:T(8,128)(2,1)S(1)} collective-permute-done((bf16[256,256]{1,0:T(8,128)(2,1)S(1)}, bf16[256,256]{1,0:T(8,128)(2,1)S(1)}, u32[]{:S(2)}, u32[]{:S(2)}) %collective-permute-start.12) | collective-permute-done | bytes 131104 | tf_op jit(solution)/shard_map/ppermute | solution.py:31
  61.1 4.9 %project.1 = bf16[5120,256]{1,0:T(8,128)(2,1)S(1)} custom-call(bf16[256,256]{1,0:T(8,128)(2,1)S(1)} %get-tuple-element.51.own, bf16[256,256]{1,0:T(8,128)(2,1)S(1)} %collective-permute-done.12.across, bf16[256,256]{1,0:T(8,128)(2,1)S(1)} %collective-permute-done.13.near1, bf16[256,256]{1,0:T(8,128)(2,1)S(1)} %collective-permute-done.14.near2, ...), custom_call_target="tpu_custom_call" | custom-call | flops 2350000128 | bytes 12000000 | tf_op jit(solution)/shard_map/project/pallas_call | solution.py:265
  66.0 36.5 %all_to_all.5.parts = bf16[8,640,256]{2,1,0:T(8,128)(2,1)} all-to-all(bf16[8,640,256]{2,1,0:T(8,128)(2,1)S(1)} %bitcast.7), channel_id=1, replica_groups=mesh['y'=4,'zh'=2,'core'=2,'x'=4,'zl'=2] {'x','zl'}, dimensions={0} | all-to-all | bytes 5242880 | tf_op jit(solution)/shard_map/all_to_all | solution.py:333
  102.5 4.1 %last_sum.1 = bf16[640,256]{1,0:T(8,128)(2,1)} custom-call(bf16[8,640,256]{2,1,0:T(8,128)(2,1)} %all_to_all.5.parts), custom_call_target="tpu_custom_call" | custom-call | flops 1300000 | bytes 3000000 | tf_op jit(solution)/shard_map/last_sum/pallas_call | solution.py:290
  (30 shorter events, 0.1 us)
Async XLA Ops:
  0.0 30.8 %copy-start.9 = (s32[32,32]{1,0:T(8,128)S(1)}, s32[32,32]{1,0:T(8,128)}, u32[]{:S(2)}) copy-start(s32[32,32]{1,0:T(8,128)} %mask.1) | copy-start | bytes 12292
  3.4 27.3 %copy-start.3 = (f32[256,128]{1,0:T(8,128)S(1)}, f32[256,128]{1,0:T(8,128)}, u32[]{:S(2)}) copy-start(f32[256,128]{1,0:T(8,128)} %get-tuple-element.26.cos) | copy-start | bytes 393220
  3.4 27.3 %copy-start.5 = (f32[256,128]{1,0:T(8,128)S(1)}, f32[256,128]{1,0:T(8,128)}, u32[]{:S(2)}) copy-start(f32[256,128]{1,0:T(8,128)} %get-tuple-element.27.sin) | copy-start | bytes 393220
  3.4 20.8 %collective-permute-start.3 = (bf16[256,256]{1,0:T(8,128)(2,1)}, bf16[256,256]{1,0:T(8,128)(2,1)S(1)}, u32[]{:S(2)}, u32[]{:S(2)}) collective-permute-start(bf16[256,256]{1,0:T(8,128)(2,1)} %get-tuple-element.25), channel_id=1, source_target_pairs={{0,96},{32,0},{64,32},{96,64},{1,97},{33,1},{65,33},{97,65},{2,98}... | collective-permute-start | bytes 393224 | tf_op jit(solution)/shard_map/ppermute | solution.py:31
  4.2 20.0 %collective-permute-start.2 = (bf16[256,256]{1,0:T(8,128)(2,1)}, bf16[256,256]{1,0:T(8,128)(2,1)S(1)}, u32[]{:S(2)}, u32[]{:S(2)}) collective-permute-start(bf16[256,256]{1,0:T(8,128)(2,1)} %get-tuple-element.25), channel_id=1, source_target_pairs={{0,64},{32,96},{64,0},{96,32},{1,65},{33,97},{65,1},{97,33},{2,66}... | collective-permute-start | bytes 393224 | tf_op jit(solution)/shard_map/ppermute | solution.py:31
  5.0 16.6 %collective-permute-start.1 = (bf16[256,256]{1,0:T(8,128)(2,1)}, bf16[256,256]{1,0:T(8,128)(2,1)S(1)}, u32[]{:S(2)}, u32[]{:S(2)}) collective-permute-start(bf16[256,256]{1,0:T(8,128)(2,1)} %get-tuple-element.25), channel_id=1, source_target_pairs={{0,32},{32,64},{64,96},{96,0},{1,33},{33,65},{65,97},{97,1},{2,34}... | collective-permute-start | bytes 393224 | tf_op jit(solution)/shard_map/ppermute | solution.py:31
  7.3 11.9 %collective-permute-start = (bf16[256,256]{1,0:T(8,128)(2,1)}, bf16[256,256]{1,0:T(8,128)(2,1)S(1)}, u32[]{:S(2)}, u32[]{:S(2)}) collective-permute-start(bf16[256,256]{1,0:T(8,128)(2,1)} %get-tuple-element.25), channel_id=1, source_target_pairs={{0,16},{16,0},{1,17},{17,1},{2,18},{18,2},{3,19},{19,3},{4,20},{20... | collective-permute-start | bytes 393224 | tf_op jit(solution)/shard_map/ppermute | solution.py:31
  13.6 0.9 copy-start.2
  14.5 0.9 copy-start.4
  15.4 1.0 copy-start.6
  16.4 1.0 copy-start.7
  17.4 1.0 copy-start.8
  19.2 8.8 %collective-permute-start.6 = (bf16[256,256]{1,0:T(8,128)(2,1)S(1)}, bf16[256,256]{1,0:T(8,128)(2,1)S(1)}, u32[]{:S(2)}, u32[]{:S(2)}) collective-permute-start(bf16[256,256]{1,0:T(8,128)(2,1)S(1)} %collective-permute-done), channel_id=1, source_target_pairs={{0,96},{32,0},{64,32},{96,64},{1,97},{33,1},{65,33},{97,65},{2,98}... | collective-permute-start | bytes 393224 | tf_op jit(solution)/shard_map/ppermute | solution.py:31
  19.5 8.5 %collective-permute-start.5 = (bf16[256,256]{1,0:T(8,128)(2,1)S(1)}, bf16[256,256]{1,0:T(8,128)(2,1)S(1)}, u32[]{:S(2)}, u32[]{:S(2)}) collective-permute-start(bf16[256,256]{1,0:T(8,128)(2,1)S(1)} %collective-permute-done), channel_id=1, source_target_pairs={{0,64},{32,96},{64,0},{96,32},{1,65},{33,97},{65,1},{97,33},{2,66}... | collective-permute-start | bytes 393224 | tf_op jit(solution)/shard_map/ppermute | solution.py:31
  21.7 6.3 %collective-permute-start.4 = (bf16[256,256]{1,0:T(8,128)(2,1)S(1)}, bf16[256,256]{1,0:T(8,128)(2,1)S(1)}, u32[]{:S(2)}, u32[]{:S(2)}) collective-permute-start(bf16[256,256]{1,0:T(8,128)(2,1)S(1)} %collective-permute-done), channel_id=1, source_target_pairs={{0,32},{32,64},{64,96},{96,0},{1,33},{33,65},{65,97},{97,1},{2,34}... | collective-permute-start | bytes 393224 | tf_op jit(solution)/shard_map/ppermute | solution.py:31
  28.0 2.7 %collective-permute-start.7 = (bf16[2048,256]{1,0:T(8,128)(2,1)S(1)}, bf16[2048,256]{1,0:T(8,128)(2,1)S(1)}, u32[]{:S(2)}, u32[]{:S(2)}) collective-permute-start(bf16[2048,256]{1,0:T(8,128)(2,1)S(1)} %constant_dynamic-update-slice_fusion.kv_mine), channel_id=1, source_target_pairs={{0,8},{8,0},{1,9},{9,1},{2,10},{10,2},{3,11},{11,3},{4,12},{12,4},... | collective-permute-start | bytes 3145736 | tf_op jit(solution)/shard_map/ppermute | solution.py:31
  28.1 32.9 %slice-start = ((s8[6553600]{0:T(1024)(128)(4,1)}), s8[4194304]{0:T(1024)(128)(4,1)S(1)}, s32[]{:S(2)}) async-start(s8[6553600]{0:T(1024)(128)(4,1)} %bitcast.8), calls=%async_computation.1 | async-start | bytes 8388608
  28.1 32.9 %slice-start.1 = ((s8[6553600]{0:T(1024)(128)(4,1)}), s8[2359296]{0:T(1024)(128)(4,1)S(1)}, s32[]{:S(2)}) async-start(s8[6553600]{0:T(1024)(128)(4,1)} %bitcast.8), calls=%async_computation.2 | async-start | bytes 4718592
  34.6 4.5 %collective-permute-start.8 = (bf16[2048,256]{1,0:T(8,128)(2,1)S(1)}, bf16[2048,256]{1,0:T(8,128)(2,1)S(1)}, u32[]{:S(2)}, u32[]{:S(2)}) collective-permute-start(bf16[2048,256]{1,0:T(8,128)(2,1)S(1)} %get-tuple-element.43), channel_id=1, source_target_pairs={{0,8},{8,0},{1,9},{9,1},{2,10},{10,2},{3,11},{11,3},{4,12},{12,4},... | collective-permute-start | bytes 3145736 | tf_op jit(solution)/shard_map/ppermute | solution.py:31
  39.1 21.9 %copy-start = (bf16[5120,128]{1,0:T(8,128)(2,1)S(1)}, bf16[5120,128]{1,0:T(8,128)(2,1)}, u32[]{:S(2)}) copy-start(bf16[5120,128]{1,0:T(8,128)(2,1)} %wk.1) | copy-start | bytes 3932164
  39.1 21.9 %copy-start.1 = (bf16[5120,128]{1,0:T(8,128)(2,1)S(1)}, bf16[5120,128]{1,0:T(8,128)(2,1)}, u32[]{:S(2)}) copy-start(bf16[5120,128]{1,0:T(8,128)(2,1)} %wv.1) | copy-start | bytes 3932164
  39.5 9.2 %collective-permute-start.11 = (bf16[256,256]{1,0:T(8,128)(2,1)S(1)}, bf16[256,256]{1,0:T(8,128)(2,1)S(1)}, u32[]{:S(2)}, u32[]{:S(2)}) collective-permute-start(bf16[256,256]{1,0:T(8,128)(2,1)S(1)} %get-tuple-element.48), channel_id=1, source_target_pairs={{0,32},{32,64},{64,96},{96,0},{1,33},{33,65},{65,97},{97,1},{2,34}... | collective-permute-start | bytes 393224 | tf_op jit(solution)/shard_map/ppermute | solution.py:31
  42.2 7.9 %collective-permute-start.10 = (bf16[256,256]{1,0:T(8,128)(2,1)S(1)}, bf16[256,256]{1,0:T(8,128)(2,1)S(1)}, u32[]{:S(2)}, u32[]{:S(2)}) collective-permute-start(bf16[256,256]{1,0:T(8,128)(2,1)S(1)} %get-tuple-element.49), channel_id=1, source_target_pairs={{0,64},{32,96},{64,0},{96,32},{1,65},{33,97},{65,1},{97,33},{2,66}... | collective-permute-start | bytes 393224 | tf_op jit(solution)/shard_map/ppermute | solution.py:31
  43.3 9.6 %collective-permute-start.9 = (bf16[256,256]{1,0:T(8,128)(2,1)S(1)}, bf16[256,256]{1,0:T(8,128)(2,1)S(1)}, u32[]{:S(2)}, u32[]{:S(2)}) collective-permute-start(bf16[256,256]{1,0:T(8,128)(2,1)S(1)} %get-tuple-element.50), channel_id=1, source_target_pairs={{0,96},{32,0},{64,32},{96,64},{1,97},{33,1},{65,33},{97,65},{2,98}... | collective-permute-start | bytes 393224 | tf_op jit(solution)/shard_map/ppermute | solution.py:31
  43.4 14.2 %collective-permute-start.15 = (bf16[256,256]{1,0:T(8,128)(2,1)S(1)}, bf16[256,256]{1,0:T(8,128)(2,1)S(1)}, u32[]{:S(2)}, u32[]{:S(2)}) collective-permute-start(bf16[256,256]{1,0:T(8,128)(2,1)S(1)} %get-tuple-element.45), channel_id=1, source_target_pairs={{0,32},{32,64},{64,96},{96,0},{1,33},{33,65},{65,97},{97,1},{2,34}... | collective-permute-start | bytes 393224 | tf_op jit(solution)/shard_map/ppermute | solution.py:31
  46.6 11.0 %collective-permute-start.14 = (bf16[256,256]{1,0:T(8,128)(2,1)S(1)}, bf16[256,256]{1,0:T(8,128)(2,1)S(1)}, u32[]{:S(2)}, u32[]{:S(2)}) collective-permute-start(bf16[256,256]{1,0:T(8,128)(2,1)S(1)} %get-tuple-element.46), channel_id=1, source_target_pairs={{0,64},{32,96},{64,0},{96,32},{1,65},{33,97},{65,1},{97,33},{2,66}... | collective-permute-start | bytes 393224 | tf_op jit(solution)/shard_map/ppermute | solution.py:31
  48.7 8.9 %collective-permute-start.13 = (bf16[256,256]{1,0:T(8,128)(2,1)S(1)}, bf16[256,256]{1,0:T(8,128)(2,1)S(1)}, u32[]{:S(2)}, u32[]{:S(2)}) collective-permute-start(bf16[256,256]{1,0:T(8,128)(2,1)S(1)} %get-tuple-element.47), channel_id=1, source_target_pairs={{0,96},{32,0},{64,32},{96,64},{1,97},{33,1},{65,33},{97,65},{2,98}... | collective-permute-start | bytes 393224 | tf_op jit(solution)/shard_map/ppermute | solution.py:31
  53.1 8.0 %collective-permute-start.12 = (bf16[256,256]{1,0:T(8,128)(2,1)S(1)}, bf16[256,256]{1,0:T(8,128)(2,1)S(1)}, u32[]{:S(2)}, u32[]{:S(2)}) collective-permute-start(bf16[256,256]{1,0:T(8,128)(2,1)S(1)} %add_convert_fusion.1), channel_id=1, source_target_pairs={{0,16},{16,0},{1,17},{17,1},{2,18},{18,2},{3,19},{19,3},{4,20},{20... | collective-permute-start | bytes 393224 | tf_op jit(solution)/shard_map/ppermute | solution.py:31

commit v3 on v2

v3 whole, which is shorter than its diff:
```python
import numpy as np
import jax
import jax.numpy as jnp
from jax import lax
from jax.experimental import pallas as pl
from jax.experimental.pallas import tpu as pltpu
from jax.sharding import Mesh, PartitionSpec as P

HEAD = 128
TILE = 128
GROUPS = 5
TOK = 256
TILES = 32
ROWS = GROUPS * TILE
SCALE = HEAD**-0.5
ROPE_BASE = 1000000.0
CTX = ("y", "zh", "core")
TP = ("x", "zl")

f32 = jnp.float32
bf16 = jnp.bfloat16


def shift(x, axes, sizes, offs):
    perm = []
    for source in np.ndindex(*sizes):
        dest = tuple((a + o) % s for a, o, s in zip(source, offs, sizes))
        perm.append(
            (int(np.ravel_multi_index(source, sizes)), int(np.ravel_multi_index(dest, sizes)))
        )
    return lax.ppermute(x, axes, perm)


def shift_y(x, k):
    return shift(x, ("y",), (4,), (k % 4,))


def swap_zh(x):
    return shift(x, ("zh",), (2,), (1,))


def swap_core(x):
    return shift(x, ("core",), (2,), (1,))


INVERSE = np.power(np.float64(ROPE_BASE), -np.arange(HEAD // 2) * (2.0 / HEAD)).astype(np.float32)


def half_sign(shape, axis):
    return jnp.where(lax.broadcasted_iota(jnp.int32, shape, axis) < HEAD // 2, -1.0, 1.0).astype(f32)


def block_kernel(key, value, positions, inverse, cos, sin, block):
    sign = half_sign((TILE, HEAD), 1)
    for t in range(2):
        tok = pl.ds(t * TILE, TILE)
        place = jnp.broadcast_to(positions[t].astype(f32), (TILE, TILE)).T
        angles = place * inverse[...]
        c, s = jnp.cos(angles), jnp.sin(angles)
        cos[tok, :] = c
        sin[tok, :] = s
        x = key[tok, :].astype(f32)
        block[tok, :HEAD] = (x * c + pltpu.roll(x, HEAD // 2, 1) * (s * sign)).astype(bf16)
        block[tok, HEAD:] = value[tok, :]


def prep_kernel(joined, cos, sin, block, q_rows, q_cols, g_rows, g_cols, delta, again):
    again[...] = block[...]
    sign = half_sign((TILE, HEAD), 1)
    for t in range(2):
        tok = pl.ds(t * TILE, TILE)
        c, s = cos[tok, :], sin[tok, :] * sign
        for h in range(GROUPS):
            feat = pl.ds(h * HEAD, HEAD)
            lane = pl.ds(h * TILE, TILE)
            x = joined[tok, feat].astype(f32)
            rot = (x * c + pltpu.roll(x, HEAD // 2, 1) * s).astype(bf16)
            q_rows[t, lane, :] = rot
            q_cols[t, :, lane] = rot.T
            g = joined[tok, pl.ds(ROWS + h * HEAD, HEAD)]
            g_rows[t, lane, :] = g
            g_cols[t, :, lane] = g.T
            prod = g.astype(f32) * joined[tok, pl.ds(2 * ROWS + h * HEAD, HEAD)].astype(f32)
            delta[t, :, lane] = jnp.sum(prod.T, axis=0, keepdims=True)


def attention_kernel(
    mask, info, seg, lse, delta, cos, sin, q_rows, q_cols, g_rows, g_cols, kv_mine, kv_other,
    dkv_mine, dkv_other, qg, acc, dq, lse_rows,
):
    dq[...] = jnp.zeros_like(dq)
    for t in range(2):
        for h in range(GROUPS):
            lse_rows[t, :, pl.ds(h * TILE, TILE)] = lse[h : h + 1, t * TILE : (t + 1) * TILE]
    me = info[0]
    q_tile = 2 * me

    def pair(t, keys, vals, allowed):
        keys_t = keys.T
        scores = jnp.dot(keys, q_cols[t], preferred_element_type=f32)
        probs = jnp.exp(scores * SCALE - lse_rows[t])
        if allowed is not None:
            probs = jnp.where(allowed, probs, 0.0)
        dprobs = jnp.dot(vals, g_cols[t], preferred_element_type=f32)
        dscore = (probs * (dprobs - delta[t])).astype(bf16)
        probs = probs.astype(bf16)
        dq[t] += jnp.dot(keys_t, dscore, preferred_element_type=f32)
        acc[:, :HEAD] += jnp.dot(dscore, q_rows[t], preferred_element_type=f32)
        acc[:, HEAD:] += jnp.dot(probs, g_rows[t], preferred_element_type=f32)

    def tiles_of(kv, dkv, away):
        def step(j, carry):
            slot = lax.shift_right_logical(j, 1)
            back_y = (lax.shift_right_logical(me, 2) - slot) & 3
            back_zh = (me ^ (lax.shift_right_logical(slot, 1) & 2)) & 2
            tile = 2 * (4 * back_y + back_zh + ((me ^ away) & 1)) + (j & 1)
            need0 = mask[q_tile, tile] > 0
            need1 = mask[q_tile + 1, tile] > 0
            here = pl.ds(pl.multiple_of(j * TILE, TILE), TILE)

            @pl.when(need0 | need1)
            def _():
                acc[...] = jnp.zeros_like(acc)
                keys, vals = kv[here, :HEAD], kv[here, HEAD:]
                for t, need in ((0, need0), (1, need1)):
                    diagonal = need & (tile == q_tile + t)

                    @pl.when(need & jnp.logical_not(diagonal))
                    def _():
                        pair(t, keys, vals, None)

                    if away == 0:

                        @pl.when(diagonal)
                        def _():
                            row = jnp.broadcast_to(seg[tile], (TILE, TILE)).astype(f32)
                            causal = lax.broadcasted_iota(jnp.int32, (TILE, TILE), 0) <= (
                                lax.broadcasted_iota(jnp.int32, (TILE, TILE), 1)
                            )
                            one = jnp.where((row.T == row) & causal, 1.0, 0.0)
                            pair(t, keys, vals, jnp.concatenate([one] * GROUPS, 1) > 0.5)

                dkv[here, :] = acc[...].astype(bf16)

            @pl.when(jnp.logical_not(need0 | need1))
            def _():
                dkv[here, :] = jnp.zeros((TILE, 2 * HEAD), bf16)

            return carry

        lax.fori_loop(0, TILES // 2, step, 0)

    tiles_of(kv_mine, dkv_mine, 0)
    tiles_of(kv_other, dkv_other, 1)
    for t in range(2):
        tok = pl.ds(t * TILE, TILE)
        c, s = cos[tok, :].T, sin[tok, :].T
        for h in range(GROUPS):
            g = dq[t, :, pl.ds(h * TILE, TILE)] * SCALE
            u = g * s
            half = HEAD // 2
            turned = jnp.concatenate([u[half:], -u[:half]], 0)
            qg[pl.ds(h * HEAD, HEAD), tok] = (g * c + turned).astype(bf16)


def vmem(n):
    return [pl.BlockSpec(memory_space=pltpu.VMEM)] * n


def prep(joined, cos, sin, block):
    s = jax.ShapeDtypeStruct
    return pl.pallas_call(
        prep_kernel,
        out_shape=(
            s((2, ROWS, HEAD), bf16),
            s((2, HEAD, ROWS), bf16),
            s((2, ROWS, HEAD), bf16),
            s((2, HEAD, ROWS), bf16),
            s((2, 1, ROWS), f32),
            s((TOK, 2 * HEAD), bf16),
        ),
        in_specs=vmem(4),
        out_specs=tuple(vmem(6)),
        compiler_params=pltpu.CompilerParams(vmem_limit_bytes=32 << 20),
        cost_estimate=pl.CostEstimate(flops=10000000, bytes_accessed=3000000, transcendentals=0),
        name="prep",
    )(joined, cos, sin, block)


def attention(mask, info, seg, lse, delta, cos, sin, q_rows, q_cols, g_rows, g_cols, mine, other):
    s = jax.ShapeDtypeStruct
    smem = [pl.BlockSpec(memory_space=pltpu.SMEM)] * 2
    return pl.pallas_call(
        attention_kernel,
        out_shape=(
            s((8 * TOK, 2 * HEAD), bf16),
            s((8 * TOK, 2 * HEAD), bf16),
            s((ROWS, TOK), bf16),
        ),
        in_specs=smem + vmem(11),
        out_specs=tuple(vmem(3)),
        scratch_shapes=[
            pltpu.VMEM((TILE, 2 * HEAD), f32),
            pltpu.VMEM((2, HEAD, ROWS), f32),
            pltpu.VMEM((2, 1, ROWS), f32),
        ],
        compiler_params=pltpu.CompilerParams(vmem_limit_bytes=48 << 20),
        cost_estimate=pl.CostEstimate(
            flops=2000000000, bytes_accessed=8000000, transcendentals=1000000
        ),
        name="attention",
    )(mask, info, seg, lse, delta, cos, sin, q_rows, q_cols, g_rows, g_cols, mine, other)


def make_block(key, value, positions):
    s = jax.ShapeDtypeStruct
    inverse = jnp.asarray(np.concatenate([INVERSE, INVERSE])[None, :])
    return pl.pallas_call(
        block_kernel,
        out_shape=(s((TOK, HEAD), f32), s((TOK, HEAD), f32), s((TOK, 2 * HEAD), bf16)),
        in_specs=vmem(4),
        out_specs=tuple(vmem(3)),
        cost_estimate=pl.CostEstimate(flops=5000000, bytes_accessed=700000, transcendentals=60000),
        name="block",
    )(key, value, positions.reshape(2, 1, TILE), inverse)


WIDTH = 5120
STEP_ROWS = 640


def project_kernel(
    own, across, near1, near2, near3, cos, sin, qg, wq, wk, wv, out, kg, vg
):
    total = own[...].astype(f32) + across[...].astype(f32)
    total += near1[...].astype(f32) + near2[...].astype(f32) + near3[...].astype(f32)
    sign = half_sign((TOK, HEAD), 1)
    g = total[:, :HEAD] * SCALE
    key_grad = g * cos[...] - pltpu.roll(g * sin[...], HEAD // 2, 1) * sign
    kg[...] = key_grad.T.astype(bf16)
    vg[...] = total[:, HEAD:].T.astype(bf16)

    def step(i, carry):
        rows = pl.ds(pl.multiple_of(i * STEP_ROWS, STEP_ROWS), STEP_ROWS)
        result = jnp.dot(wq[rows, :], qg[...], preferred_element_type=f32)
        result += jnp.dot(wk[rows, :], kg[...], preferred_element_type=f32)
        result += jnp.dot(wv[rows, :], vg[...], preferred_element_type=f32)
        out[rows, :] = result.astype(bf16)
        return carry

    lax.fori_loop(0, WIDTH // STEP_ROWS, step, 0)


def project(own, across, near, cos, sin, qg, wq, wk, wv):
    return pl.pallas_call(
        project_kernel,
        out_shape=jax.ShapeDtypeStruct((WIDTH, TOK), bf16),
        in_specs=vmem(11),
        out_specs=vmem(1)[0],
        scratch_shapes=[pltpu.VMEM((HEAD, TOK), bf16), pltpu.VMEM((HEAD, TOK), bf16)],
        compiler_params=pltpu.CompilerParams(vmem_limit_bytes=40 << 20),
        cost_estimate=pl.CostEstimate(
            flops=2350000000, bytes_accessed=12000000, transcendentals=0
        ),
        name="project",
    )(own, across, *near, cos, sin, qg, wq, wk, wv)


def last_kernel(parts, out):
    def step(i, carry):
        rows = pl.ds(pl.multiple_of(i * TILE, TILE), TILE)
        total = parts[0, rows, :].astype(f32)
        for k in range(1, 8):
            total += parts[k, rows, :].astype(f32)
        out[rows, :] = total.astype(bf16)
        return carry

    lax.fori_loop(0, 5, step, 0)


def last_sum(parts):
    return pl.pallas_call(
        last_kernel,
        out_shape=jax.ShapeDtypeStruct((640, TOK), bf16),
        in_specs=vmem(1),
        out_specs=vmem(1)[0],
        compiler_params=pltpu.CompilerParams(vmem_limit_bytes=16 << 20),
        cost_estimate=pl.CostEstimate(flops=1300000, bytes_accessed=3000000, transcendentals=0),
        name="last_sum",
    )(parts)


def local(
    query, key, value, att, grad, lse, block_mask, positions, segments, w_query, key_weight,
    value_weight,
):
    me = lax.axis_index(CTX)
    cos, sin, block = make_block(key, value, positions)

    across = swap_zh(block)
    q_rows, q_cols, g_rows, g_cols, delta, again = prep(
        jnp.concatenate([query, grad, att], 1), cos, sin, block
    )
    near = [shift_y(again, k) for k in (1, 2, 3)]
    far = [shift_y(across, k) for k in (1, 2, 3)]
    mine = jnp.concatenate([block] + near + [across] + far, 0)
    other = swap_core(mine)

    dkv_mine, dkv_other, query_grad = attention(
        block_mask, me.reshape(1), segments.reshape(TILES, 1, TILE), lse, delta, cos, sin, q_rows,
        q_cols, g_rows, g_cols, mine, other,
    )

    summed = dkv_mine.astype(f32) + swap_core(dkv_other).astype(f32)
    parts = lax.optimization_barrier(summed.astype(bf16)).reshape(8, TOK, 2 * HEAD)
    far = [shift_y(parts[4 + k], -k) for k in (1, 2, 3)]
    across = parts[4].astype(f32) + sum(p.astype(f32) for p in far)
    across, rest = lax.optimization_barrier(
        (across.astype(bf16), (parts[1], parts[2], parts[3]))
    )
    near = [shift_y(rest[k - 1], -k) for k in (1, 2, 3)]
    across = swap_zh(across)
    send = project(
        parts[0], across, near, cos, sin, query_grad, w_query, key_weight, value_weight
    )
    return last_sum(lax.all_to_all(send.reshape(8, 640, TOK), TP, 0, 0))


def solution(mesh):
    fine = Mesh(mesh.devices.reshape(4, 2, 2, 4, 2), ("y", "zh", "core", "x", "zl"))
    in_specs = (
        P(CTX, TP),
        P(CTX, TP),
        P(CTX, TP),
        P(CTX, TP),
        P(CTX, TP),
        P(TP, CTX),
        P(),
        P(CTX),
        P(),
        P(None, TP),
        P(None, TP),
        P(None, TP),
    )
    return jax.shard_map(
        local, mesh=fine, in_specs=in_specs, out_specs=P(TP, CTX), check_vma=False
    )
```

time: 107 us -> 106 us (level)
  the two profiles are of different devices: /device:TPU:24 before, /device:TPU:0 now
where the time goes in v3:
time: 106 us
  blocking collectives  36.8 us (35%)
  starting transfers between devices  26.9 us (25%)
  waiting for transfers between devices  26.7 us (25%)
  Pallas kernels  12.4 us (12%)
  other arithmetic  1.61 us (2%)
  local copies, waits for them, and re-layouts  1.32 us (1%)
    all_to_all x1, blocking collectives, local(): return last_sum(lax.all_to_all(send.reshape(8, 640, TOK), TP, 0, 0))  36.8 us
    ppermute x16, starting transfers between devices, shift(): return lax.ppermute(x, axes, perm)  26.9 us
    ppermute x16, waiting for transfers between devices, shift(): return lax.ppermute(x, axes, perm)  26.7 us
    pallas_call x1, Pallas kernels, project(): pl.pallas_call(project_kernel, out_shape=jax.ShapeDtypeStruct((WIDTH, TOK...  4.87 us
    pallas_call x1, Pallas kernels, attention(): pl.pallas_call(attention_kernel, out_shape=(s((8 * TOK, 2 * HEAD), bf16),...  3.49 us
    pallas_call x1, Pallas kernels, make_block(): pl.pallas_call(block_kernel, out_shape=(s((TOK, HEAD), f32), s((TOK, HEAD...  2.17 us
  transfers between devices with their start and end apart: 16, of which 10 were waited for; matrix products, arithmetic and copies ran while one was open for 1% of the time, Pallas kernels for 1%

profile of v3, /device:TPU:0, one launch (start us, length us, event | category | flops | bytes accessed | tf_op | source)
XLA Modules:
  0.0 106.0 jit_solution(10277516521911722379)
XLA Ops:
  0.0 2.2 %block.1 = (f32[256,128]{1,0:T(8,128)}, f32[256,128]{1,0:T(8,128)}, bf16[256,256]{1,0:T(8,128)(2,1)}) custom-call(bf16[256,128]{1,0:T(8,128)(2,1)} %key.1, bf16[256,128]{1,0:T(8,128)(2,1)} %value.1, s32[2,1,128]{2,1,0:T(1,128)} %bitcast.8, f32[1,128]{1,0:T(1,128)} %constant.21.clone.inverse), custom_call_target="tpu_custom_call" | custom-call | flops 5000000 | bytes 700000 | tf_op jit(solution)/shard_map/block/pallas_call | solution.py:218
  2.2 4.0 %collective-permute-start.3 = (bf16[256,256]{1,0:T(8,128)(2,1)}, bf16[256,256]{1,0:T(8,128)(2,1)S(1)}, u32[]{:S(2)}, u32[]{:S(2)}) collective-permute-start(bf16[256,256]{1,0:T(8,128)(2,1)} %get-tuple-element.23.block), channel_id=1, source_target_pairs={{0,16},{16,0},{1,17},{17,1},{2,18},{18,2},{3,19},{19,3},{4,20},{20... | collective-permute-start | bytes 393224 | tf_op jit(solution)/shard_map/ppermute | solution.py:31
  6.2 1.2 %pad_maximum_fusion.joined = bf16[256,1920]{1,0:T(8,128)(2,1)S(1)} fusion(bf16[256,640]{1,0:T(8,128)(2,1)} %param.16, bf16[256,640]{1,0:T(8,128)(2,1)} %param.17, bf16[256,640]{1,0:T(8,128)(2,1)} %param.13), kind=kLoop, calls=%fused_computation.1 | loop fusion | flops 2949120 | bytes 1966080 | tf_op jit(solution)/shard_map/concatenate | solution.py:302
  7.5 0.0 copy-start.7
  7.5 0.0 copy-start.8
  7.5 0.0 copy-start.9
  7.5 0.8 prep.1
  8.4 0.0 copy-start.5
  8.4 1.6 %collective-permute-start = (bf16[256,256]{1,0:T(8,128)(2,1)S(1)}, bf16[256,256]{1,0:T(8,128)(2,1)S(1)}, u32[]{:S(2)}, u32[]{:S(2)}) collective-permute-start(bf16[256,256]{1,0:T(8,128)(2,1)S(1)} %get-tuple-element.29), channel_id=1, source_target_pairs={{0,32},{32,64},{64,96},{96,0},{1,33},{33,65},{65,97},{97,1},{2,34}... | collective-permute-start | bytes 393224 | tf_op jit(solution)/shard_map/ppermute | solution.py:31
  10.0 1.7 %collective-permute-start.2 = (bf16[256,256]{1,0:T(8,128)(2,1)S(1)}, bf16[256,256]{1,0:T(8,128)(2,1)S(1)}, u32[]{:S(2)}, u32[]{:S(2)}) collective-permute-start(bf16[256,256]{1,0:T(8,128)(2,1)S(1)} %get-tuple-element.29), channel_id=1, source_target_pairs={{0,96},{32,0},{64,32},{96,64},{1,97},{33,1},{65,33},{97,65},{2,98}... | collective-permute-start | bytes 393224 | tf_op jit(solution)/shard_map/ppermute | solution.py:31
  11.7 2.0 %collective-permute-start.1 = (bf16[256,256]{1,0:T(8,128)(2,1)S(1)}, bf16[256,256]{1,0:T(8,128)(2,1)S(1)}, u32[]{:S(2)}, u32[]{:S(2)}) collective-permute-start(bf16[256,256]{1,0:T(8,128)(2,1)S(1)} %get-tuple-element.29), channel_id=1, source_target_pairs={{0,64},{32,96},{64,0},{96,32},{1,65},{33,97},{65,1},{97,33},{2,66}... | collective-permute-start | bytes 393224 | tf_op jit(solution)/shard_map/ppermute | solution.py:31
  13.7 0.0 collective-permute-done.3
  13.7 1.1 %collective-permute-start.6 = (bf16[256,256]{1,0:T(8,128)(2,1)S(1)}, bf16[256,256]{1,0:T(8,128)(2,1)S(1)}, u32[]{:S(2)}, u32[]{:S(2)}) collective-permute-start(bf16[256,256]{1,0:T(8,128)(2,1)S(1)} %collective-permute-done.3), channel_id=1, source_target_pairs={{0,96},{32,0},{64,32},{96,64},{1,97},{33,1},{65,33},{97,65},{2,98}... | collective-permute-start | bytes 393224 | tf_op jit(solution)/shard_map/ppermute | solution.py:31
  14.8 1.7 %collective-permute-start.5 = (bf16[256,256]{1,0:T(8,128)(2,1)S(1)}, bf16[256,256]{1,0:T(8,128)(2,1)S(1)}, u32[]{:S(2)}, u32[]{:S(2)}) collective-permute-start(bf16[256,256]{1,0:T(8,128)(2,1)S(1)} %collective-permute-done.3), channel_id=1, source_target_pairs={{0,64},{32,96},{64,0},{96,32},{1,65},{33,97},{65,1},{97,33},{2,66}... | collective-permute-start | bytes 393224 | tf_op jit(solution)/shard_map/ppermute | solution.py:31
  16.5 0.0 collective-permute-done
  16.5 0.2 collective-permute-start.4
  16.7 3.1 %collective-permute-done.1 = bf16[256,256]{1,0:T(8,128)(2,1)S(1)} collective-permute-done((bf16[256,256]{1,0:T(8,128)(2,1)S(1)}, bf16[256,256]{1,0:T(8,128)(2,1)S(1)}, u32[]{:S(2)}, u32[]{:S(2)}) %collective-permute-start.1) | collective-permute-done | bytes 131104 | tf_op jit(solution)/shard_map/ppermute | solution.py:31
  19.8 0.0 collective-permute-done.2
  19.9 4.4 %collective-permute-done.4 = bf16[256,256]{1,0:T(8,128)(2,1)S(1)} collective-permute-done((bf16[256,256]{1,0:T(8,128)(2,1)S(1)}, bf16[256,256]{1,0:T(8,128)(2,1)S(1)}, u32[]{:S(2)}, u32[]{:S(2)}) %collective-permute-start.4) | collective-permute-done | bytes 131104 | tf_op jit(solution)/shard_map/ppermute | solution.py:31
  24.3 0.0 collective-permute-done.5
  24.4 0.1 collective-permute-start.7
  24.5 2.6 %collective-permute-done.7.kv_other = bf16[2048,256]{1,0:T(8,128)(2,1)S(1)} collective-permute-done((bf16[2048,256]{1,0:T(8,128)(2,1)S(1)}, bf16[2048,256]{1,0:T(8,128)(2,1)S(1)}, u32[]{:S(2)}, u32[]{:S(2)}) %collective-permute-start.7) | collective-permute-done | bytes 1048608 | tf_op jit(solution)/shard_map/ppermute | solution.py:31
  27.1 0.0 copy-start.6
  27.1 1.1 %copy-done.6 = bf16[2,128,640]{2,1,0:T(8,128)(2,1)S(1)} copy-done((bf16[2,128,640]{2,1,0:T(8,128)(2,1)S(1)}, bf16[2,128,640]{2,1,0:T(8,128)(2,1)}, u32[]{:S(2)}) %copy-start.6) | copy-done | bytes 327704
  28.2 3.5 %attention.1 = (bf16[2048,256]{1,0:T(8,128)(2,1)S(1)}, bf16[2048,256]{1,0:T(8,128)(2,1)S(1)}, bf16[640,256]{1,0:T(8,128)(2,1)S(1)}) custom-call(s32[32,32]{1,0:T(8,128)S(1)} %copy-done.7, s32[1]{0:T(128)} %bitcast.info, s32[32,1,128]{2,1,0:T(1,128)S(1)} %bitcast.7, f32[5,256]{1,0:T(8,128)S(1)} %copy-done.9, f32[2,1,640]{2,1,0:T(1,128)S(1)} %get-tuple-element.24.delta, ...), custom_call_target="tpu_custom_call" | custom-call | flops 2000000000 | bytes 8000000 | tf_op jit(solution)/shard_map/attention/pallas_call | solution.py:193
  31.7 2.2 %collective-permute-start.8 = (bf16[2048,256]{1,0:T(8,128)(2,1)S(1)}, bf16[2048,256]{1,0:T(8,128)(2,1)S(1)}, u32[]{:S(2)}, u32[]{:S(2)}) collective-permute-start(bf16[2048,256]{1,0:T(8,128)(2,1)S(1)} %get-tuple-element.31), channel_id=1, source_target_pairs={{0,8},{8,0},{1,9},{9,1},{2,10},{10,2},{3,11},{11,3},{4,12},{12,4},... | collective-permute-start | bytes 3145736 | tf_op jit(solution)/shard_map/ppermute | solution.py:31
  34.0 2.3 %collective-permute-done.8 = bf16[2048,256]{1,0:T(8,128)(2,1)S(1)} collective-permute-done((bf16[2048,256]{1,0:T(8,128)(2,1)S(1)}, bf16[2048,256]{1,0:T(8,128)(2,1)S(1)}, u32[]{:S(2)}, u32[]{:S(2)}) %collective-permute-start.8) | collective-permute-done | bytes 1048608 | tf_op jit(solution)/shard_map/ppermute | solution.py:31
  36.3 0.3 add_convert_fusion
  36.6 0.0 copy-start
  36.6 0.1 fusion
  36.6 1.2 %collective-permute-start.11 = (bf16[256,256]{1,0:T(8,128)(2,1)S(1)}, bf16[256,256]{1,0:T(8,128)(2,1)S(1)}, u32[]{:S(2)}, u32[]{:S(2)}) collective-permute-start(bf16[256,256]{1,0:T(8,128)(2,1)S(1)} %get-tuple-element.40), channel_id=1, source_target_pairs={{0,32},{32,64},{64,96},{96,0},{1,33},{33,65},{65,97},{97,1},{2,34}... | collective-permute-start | bytes 393224 | tf_op jit(solution)/shard_map/ppermute | solution.py:31
  37.9 2.3 %collective-permute-start.10 = (bf16[256,256]{1,0:T(8,128)(2,1)S(1)}, bf16[256,256]{1,0:T(8,128)(2,1)S(1)}, u32[]{:S(2)}, u32[]{:S(2)}) collective-permute-start(bf16[256,256]{1,0:T(8,128)(2,1)S(1)} %get-tuple-element.41), channel_id=1, source_target_pairs={{0,64},{32,96},{64,0},{96,32},{1,65},{33,97},{65,1},{97,33},{2,66}... | collective-permute-start | bytes 393224 | tf_op jit(solution)/shard_map/ppermute | solution.py:31
  40.2 0.6 collective-permute-start.9
  40.8 3.1 %collective-permute-done.11 = bf16[256,256]{1,0:T(8,128)(2,1)S(1)} collective-permute-done((bf16[256,256]{1,0:T(8,128)(2,1)S(1)}, bf16[256,256]{1,0:T(8,128)(2,1)S(1)}, u32[]{:S(2)}, u32[]{:S(2)}) %collective-permute-start.11) | collective-permute-done | bytes 131104 | tf_op jit(solution)/shard_map/ppermute | solution.py:31
  44.0 2.8 %collective-permute-done.10 = bf16[256,256]{1,0:T(8,128)(2,1)S(1)} collective-permute-done((bf16[256,256]{1,0:T(8,128)(2,1)S(1)}, bf16[256,256]{1,0:T(8,128)(2,1)S(1)}, u32[]{:S(2)}, u32[]{:S(2)}) %collective-permute-start.10) | collective-permute-done | bytes 131104 | tf_op jit(solution)/shard_map/ppermute | solution.py:31
  46.8 0.3 collective-permute-done.9
  47.1 0.1 add_convert_fusion.1
  47.2 4.5 %collective-permute-start.12 = (bf16[256,256]{1,0:T(8,128)(2,1)S(1)}, bf16[256,256]{1,0:T(8,128)(2,1)S(1)}, u32[]{:S(2)}, u32[]{:S(2)}) collective-permute-start(bf16[256,256]{1,0:T(8,128)(2,1)S(1)} %add_convert_fusion.1), channel_id=1, source_target_pairs={{0,16},{16,0},{1,17},{17,1},{2,18},{18,2},{3,19},{19,3},{4,20},{20... | collective-permute-start | bytes 393224 | tf_op jit(solution)/shard_map/ppermute | solution.py:31
  51.6 2.7 %collective-permute-start.13 = (bf16[256,256]{1,0:T(8,128)(2,1)S(1)}, bf16[256,256]{1,0:T(8,128)(2,1)S(1)}, u32[]{:S(2)}, u32[]{:S(2)}) collective-permute-start(bf16[256,256]{1,0:T(8,128)(2,1)S(1)} %get-tuple-element.33), channel_id=1, source_target_pairs={{0,96},{32,0},{64,32},{96,64},{1,97},{33,1},{65,33},{97,65},{2,98}... | collective-permute-start | bytes 393224 | tf_op jit(solution)/shard_map/ppermute | solution.py:31
  54.3 0.3 collective-permute-start.14
  54.6 0.5 collective-permute-start.15
  55.1 0.0 collective-permute-done.12.across
  55.1 4.6 %collective-permute-done.13.near1 = bf16[256,256]{1,0:T(8,128)(2,1)S(1)} collective-permute-done((bf16[256,256]{1,0:T(8,128)(2,1)S(1)}, bf16[256,256]{1,0:T(8,128)(2,1)S(1)}, u32[]{:S(2)}, u32[]{:S(2)}) %collective-permute-start.13) | collective-permute-done | bytes 131104 | tf_op jit(solution)/shard_map/ppermute | solution.py:31
  59.8 2.4 %collective-permute-done.14.near2 = bf16[256,256]{1,0:T(8,128)(2,1)S(1)} collective-permute-done((bf16[256,256]{1,0:T(8,128)(2,1)S(1)}, bf16[256,256]{1,0:T(8,128)(2,1)S(1)}, u32[]{:S(2)}, u32[]{:S(2)}) %collective-permute-start.14) | collective-permute-done | bytes 131104 | tf_op jit(solution)/shard_map/ppermute | solution.py:31
  62.1 1.1 %collective-permute-done.15.near3 = bf16[256,256]{1,0:T(8,128)(2,1)S(1)} collective-permute-done((bf16[256,256]{1,0:T(8,128)(2,1)S(1)}, bf16[256,256]{1,0:T(8,128)(2,1)S(1)}, u32[]{:S(2)}, u32[]{:S(2)}) %collective-permute-start.15) | collective-permute-done | bytes 131104 | tf_op jit(solution)/shard_map/ppermute | solution.py:31
  63.3 4.9 %project.1 = bf16[5120,256]{1,0:T(8,128)(2,1)S(1)} custom-call(bf16[256,256]{1,0:T(8,128)(2,1)S(1)} %get-tuple-element.43.own, bf16[256,256]{1,0:T(8,128)(2,1)S(1)} %collective-permute-done.12.across, bf16[256,256]{1,0:T(8,128)(2,1)S(1)} %collective-permute-done.13.near1, bf16[256,256]{1,0:T(8,128)(2,1)S(1)} %collective-permute-done.14.near2, ...), custom_call_target="tpu_custom_call" | custom-call | flops 2350000128 | bytes 12000000 | tf_op jit(solution)/shard_map/project/pallas_call | solution.py:255
  68.1 36.8 %all_to_all.5.parts = bf16[8,640,256]{2,1,0:T(8,128)(2,1)S(1)} all-to-all(bf16[8,640,256]{2,1,0:T(8,128)(2,1)S(1)} %bitcast.4), channel_id=1, replica_groups=mesh['y'=4,'zh'=2,'core'=2,'x'=4,'zl'=2] {'x','zl'}, dimensions={0} | all-to-all | bytes 5242880 | tf_op jit(solution)/shard_map/all_to_all | solution.py:326
  104.9 1.1 %last_sum.1 = bf16[640,256]{1,0:T(8,128)(2,1)} custom-call(bf16[8,640,256]{2,1,0:T(8,128)(2,1)S(1)} %all_to_all.5.parts), custom_call_target="tpu_custom_call" | custom-call | flops 1300000 | bytes 3000000 | tf_op jit(solution)/shard_map/last_sum/pallas_call | solution.py:282
  (27 shorter events, 0.1 us)
Async XLA Ops:
  2.2 5.3 %copy-start.2 = (f32[256,128]{1,0:T(8,128)S(1)}, f32[256,128]{1,0:T(8,128)}, u32[]{:S(2)}) copy-start(f32[256,128]{1,0:T(8,128)} %get-tuple-element.21.cos) | copy-start | bytes 393220
  2.2 5.3 %copy-start.3 = (f32[256,128]{1,0:T(8,128)S(1)}, f32[256,128]{1,0:T(8,128)}, u32[]{:S(2)}) copy-start(f32[256,128]{1,0:T(8,128)} %get-tuple-element.22.sin) | copy-start | bytes 393220
  2.2 5.4 %copy-start.4 = (bf16[256,256]{1,0:T(8,128)(2,1)S(1)}, bf16[256,256]{1,0:T(8,128)(2,1)}, u32[]{:S(2)}) copy-start(bf16[256,256]{1,0:T(8,128)(2,1)} %get-tuple-element.23.block) | copy-start | bytes 393220
  2.2 11.5 %collective-permute-start.3 = (bf16[256,256]{1,0:T(8,128)(2,1)}, bf16[256,256]{1,0:T(8,128)(2,1)S(1)}, u32[]{:S(2)}, u32[]{:S(2)}) collective-permute-start(bf16[256,256]{1,0:T(8,128)(2,1)} %get-tuple-element.23.block), channel_id=1, source_target_pairs={{0,16},{16,0},{1,17},{17,1},{2,18},{18,2},{3,19},{19,3},{4,20},{20... | collective-permute-start | bytes 393224 | tf_op jit(solution)/shard_map/ppermute | solution.py:31
  7.5 19.6 %copy-start.7 = (s32[32,32]{1,0:T(8,128)S(1)}, s32[32,32]{1,0:T(8,128)}, u32[]{:S(2)}) copy-start(s32[32,32]{1,0:T(8,128)} %mask.1) | copy-start | bytes 12292
  7.5 19.6 %copy-start.8 = (s32[4096]{0:T(1024)S(1)}, s32[4096]{0:T(1024)}, u32[]{:S(2)}) copy-start(s32[4096]{0:T(1024)} %param.21) | copy-start | bytes 49156
  7.5 19.6 %copy-start.9 = (f32[5,256]{1,0:T(8,128)S(1)}, f32[5,256]{1,0:T(8,128)}, u32[]{:S(2)}) copy-start(f32[5,256]{1,0:T(8,128)} %lse.1) | copy-start | bytes 15364
  8.4 16.0 %copy-start.5 = (bf16[2,128,640]{2,1,0:T(8,128)(2,1)}, bf16[2,128,640]{2,1,0:T(8,128)(2,1)S(1)}, u32[]{:S(2)}) copy-start(bf16[2,128,640]{2,1,0:T(8,128)(2,1)S(1)} %get-tuple-element.28.g_cols) | copy-start | bytes 983044
  8.4 8.1 %collective-permute-start = (bf16[256,256]{1,0:T(8,128)(2,1)S(1)}, bf16[256,256]{1,0:T(8,128)(2,1)S(1)}, u32[]{:S(2)}, u32[]{:S(2)}) collective-permute-start(bf16[256,256]{1,0:T(8,128)(2,1)S(1)} %get-tuple-element.29), channel_id=1, source_target_pairs={{0,32},{32,64},{64,96},{96,0},{1,33},{33,65},{65,97},{97,1},{2,34}... | collective-permute-start | bytes 393224 | tf_op jit(solution)/shard_map/ppermute | solution.py:31
  10.0 9.8 %collective-permute-start.2 = (bf16[256,256]{1,0:T(8,128)(2,1)S(1)}, bf16[256,256]{1,0:T(8,128)(2,1)S(1)}, u32[]{:S(2)}, u32[]{:S(2)}) collective-permute-start(bf16[256,256]{1,0:T(8,128)(2,1)S(1)} %get-tuple-element.29), channel_id=1, source_target_pairs={{0,96},{32,0},{64,32},{96,64},{1,97},{33,1},{65,33},{97,65},{2,98}... | collective-permute-start | bytes 393224 | tf_op jit(solution)/shard_map/ppermute | solution.py:31
  11.7 8.1 %collective-permute-start.1 = (bf16[256,256]{1,0:T(8,128)(2,1)S(1)}, bf16[256,256]{1,0:T(8,128)(2,1)S(1)}, u32[]{:S(2)}, u32[]{:S(2)}) collective-permute-start(bf16[256,256]{1,0:T(8,128)(2,1)S(1)} %get-tuple-element.29), channel_id=1, source_target_pairs={{0,64},{32,96},{64,0},{96,32},{1,65},{33,97},{65,1},{97,33},{2,66}... | collective-permute-start | bytes 393224 | tf_op jit(solution)/shard_map/ppermute | solution.py:31
  13.7 10.6 %collective-permute-start.6 = (bf16[256,256]{1,0:T(8,128)(2,1)S(1)}, bf16[256,256]{1,0:T(8,128)(2,1)S(1)}, u32[]{:S(2)}, u32[]{:S(2)}) collective-permute-start(bf16[256,256]{1,0:T(8,128)(2,1)S(1)} %collective-permute-done.3), channel_id=1, source_target_pairs={{0,96},{32,0},{64,32},{96,64},{1,97},{33,1},{65,33},{97,65},{2,98}... | collective-permute-start | bytes 393224 | tf_op jit(solution)/shard_map/ppermute | solution.py:31
  14.8 9.5 %collective-permute-start.5 = (bf16[256,256]{1,0:T(8,128)(2,1)S(1)}, bf16[256,256]{1,0:T(8,128)(2,1)S(1)}, u32[]{:S(2)}, u32[]{:S(2)}) collective-permute-start(bf16[256,256]{1,0:T(8,128)(2,1)S(1)} %collective-permute-done.3), channel_id=1, source_target_pairs={{0,64},{32,96},{64,0},{96,32},{1,65},{33,97},{65,1},{97,33},{2,66}... | collective-permute-start | bytes 393224 | tf_op jit(solution)/shard_map/ppermute | solution.py:31
  16.5 7.8 %collective-permute-start.4 = (bf16[256,256]{1,0:T(8,128)(2,1)S(1)}, bf16[256,256]{1,0:T(8,128)(2,1)S(1)}, u32[]{:S(2)}, u32[]{:S(2)}) collective-permute-start(bf16[256,256]{1,0:T(8,128)(2,1)S(1)} %collective-permute-done.3), channel_id=1, source_target_pairs={{0,32},{32,64},{64,96},{96,0},{1,33},{33,65},{65,97},{97,1},{2,34}... | collective-permute-start | bytes 393224 | tf_op jit(solution)/shard_map/ppermute | solution.py:31
  24.4 2.7 %collective-permute-start.7 = (bf16[2048,256]{1,0:T(8,128)(2,1)S(1)}, bf16[2048,256]{1,0:T(8,128)(2,1)S(1)}, u32[]{:S(2)}, u32[]{:S(2)}) collective-permute-start(bf16[2048,256]{1,0:T(8,128)(2,1)S(1)} %constant_dynamic-update-slice_fusion.kv_mine), channel_id=1, source_target_pairs={{0,8},{8,0},{1,9},{9,1},{2,10},{10,2},{3,11},{11,3},{4,12},{12,4},... | collective-permute-start | bytes 3145736 | tf_op jit(solution)/shard_map/ppermute | solution.py:31
  27.1 36.1 %slice-start = ((s8[6553600]{0:T(1024)(128)(4,1)}), s8[4194304]{0:T(1024)(128)(4,1)S(1)}, s32[]{:S(2)}) async-start(s8[6553600]{0:T(1024)(128)(4,1)} %bitcast.5), calls=%async_computation.1 | async-start | bytes 8388608
  27.1 1.1 %copy-start.6 = (bf16[2,128,640]{2,1,0:T(8,128)(2,1)S(1)}, bf16[2,128,640]{2,1,0:T(8,128)(2,1)}, u32[]{:S(2)}) copy-start(bf16[2,128,640]{2,1,0:T(8,128)(2,1)} %copy-done.5) | copy-start | bytes 983044
  28.2 35.0 %slice-start.1 = ((s8[6553600]{0:T(1024)(128)(4,1)}), s8[2359296]{0:T(1024)(128)(4,1)S(1)}, s32[]{:S(2)}) async-start(s8[6553600]{0:T(1024)(128)(4,1)} %bitcast.5), calls=%async_computation.2 | async-start | bytes 4718592
  31.7 4.5 %collective-permute-start.8 = (bf16[2048,256]{1,0:T(8,128)(2,1)S(1)}, bf16[2048,256]{1,0:T(8,128)(2,1)S(1)}, u32[]{:S(2)}, u32[]{:S(2)}) collective-permute-start(bf16[2048,256]{1,0:T(8,128)(2,1)S(1)} %get-tuple-element.31), channel_id=1, source_target_pairs={{0,8},{8,0},{1,9},{9,1},{2,10},{10,2},{3,11},{11,3},{4,12},{12,4},... | collective-permute-start | bytes 3145736 | tf_op jit(solution)/shard_map/ppermute | solution.py:31
  36.2 27.0 %copy-start.1 = (bf16[5120,128]{1,0:T(8,128)(2,1)S(1)}, bf16[5120,128]{1,0:T(8,128)(2,1)}, u32[]{:S(2)}) copy-start(bf16[5120,128]{1,0:T(8,128)(2,1)} %wv.1) | copy-start | bytes 3932164
  36.6 26.7 %copy-start = (bf16[5120,128]{1,0:T(8,128)(2,1)S(1)}, bf16[5120,128]{1,0:T(8,128)(2,1)}, u32[]{:S(2)}) copy-start(bf16[5120,128]{1,0:T(8,128)(2,1)} %wk.1) | copy-start | bytes 3932164
  36.6 7.4 %collective-permute-start.11 = (bf16[256,256]{1,0:T(8,128)(2,1)S(1)}, bf16[256,256]{1,0:T(8,128)(2,1)S(1)}, u32[]{:S(2)}, u32[]{:S(2)}) collective-permute-start(bf16[256,256]{1,0:T(8,128)(2,1)S(1)} %get-tuple-element.40), channel_id=1, source_target_pairs={{0,32},{32,64},{64,96},{96,0},{1,33},{33,65},{65,97},{97,1},{2,34}... | collective-permute-start | bytes 393224 | tf_op jit(solution)/shard_map/ppermute | solution.py:31
  37.9 8.9 %collective-permute-start.10 = (bf16[256,256]{1,0:T(8,128)(2,1)S(1)}, bf16[256,256]{1,0:T(8,128)(2,1)S(1)}, u32[]{:S(2)}, u32[]{:S(2)}) collective-permute-start(bf16[256,256]{1,0:T(8,128)(2,1)S(1)} %get-tuple-element.41), channel_id=1, source_target_pairs={{0,64},{32,96},{64,0},{96,32},{1,65},{33,97},{65,1},{97,33},{2,66}... | collective-permute-start | bytes 393224 | tf_op jit(solution)/shard_map/ppermute | solution.py:31
  40.2 6.9 %collective-permute-start.9 = (bf16[256,256]{1,0:T(8,128)(2,1)S(1)}, bf16[256,256]{1,0:T(8,128)(2,1)S(1)}, u32[]{:S(2)}, u32[]{:S(2)}) collective-permute-start(bf16[256,256]{1,0:T(8,128)(2,1)S(1)} %get-tuple-element.42), channel_id=1, source_target_pairs={{0,96},{32,0},{64,32},{96,64},{1,97},{33,1},{65,33},{97,65},{2,98}... | collective-permute-start | bytes 393224 | tf_op jit(solution)/shard_map/ppermute | solution.py:31
  47.2 8.0 %collective-permute-start.12 = (bf16[256,256]{1,0:T(8,128)(2,1)S(1)}, bf16[256,256]{1,0:T(8,128)(2,1)S(1)}, u32[]{:S(2)}, u32[]{:S(2)}) collective-permute-start(bf16[256,256]{1,0:T(8,128)(2,1)S(1)} %add_convert_fusion.1), channel_id=1, source_target_pairs={{0,16},{16,0},{1,17},{17,1},{2,18},{18,2},{3,19},{19,3},{4,20},{20... | collective-permute-start | bytes 393224 | tf_op jit(solution)/shard_map/ppermute | solution.py:31
  51.6 8.1 %collective-permute-start.13 = (bf16[256,256]{1,0:T(8,128)(2,1)S(1)}, bf16[256,256]{1,0:T(8,128)(2,1)S(1)}, u32[]{:S(2)}, u32[]{:S(2)}) collective-permute-start(bf16[256,256]{1,0:T(8,128)(2,1)S(1)} %get-tuple-element.33), channel_id=1, source_target_pairs={{0,96},{32,0},{64,32},{96,64},{1,97},{33,1},{65,33},{97,65},{2,98}... | collective-permute-start | bytes 393224 | tf_op jit(solution)/shard_map/ppermute | solution.py:31
  54.3 7.8 %collective-permute-start.14 = (bf16[256,256]{1,0:T(8,128)(2,1)S(1)}, bf16[256,256]{1,0:T(8,128)(2,1)S(1)}, u32[]{:S(2)}, u32[]{:S(2)}) collective-permute-start(bf16[256,256]{1,0:T(8,128)(2,1)S(1)} %get-tuple-element.34), channel_id=1, source_target_pairs={{0,64},{32,96},{64,0},{96,32},{1,65},{33,97},{65,1},{97,33},{2,66}... | collective-permute-start | bytes 393224 | tf_op jit(solution)/shard_map/ppermute | solution.py:31
  54.6 8.6 %collective-permute-start.15 = (bf16[256,256]{1,0:T(8,128)(2,1)S(1)}, bf16[256,256]{1,0:T(8,128)(2,1)S(1)}, u32[]{:S(2)}, u32[]{:S(2)}) collective-permute-start(bf16[256,256]{1,0:T(8,128)(2,1)S(1)} %get-tuple-element.35), channel_id=1, source_target_pairs={{0,32},{32,64},{64,96},{96,0},{1,33},{33,65},{65,97},{97,1},{2,34}... | collective-permute-start | bytes 393224 | tf_op jit(solution)/shard_map/ppermute | solution.py:31

commit v4 on v3

--- a/solution.py
+++ b/solution.py
@@ -1,3 +1,5 @@
+import functools
+
 import numpy as np
 import jax
 import jax.numpy as jnp
@@ -64,8 +66,7 @@
         block[tok, HEAD:] = value[tok, :]
 
 
-def prep_kernel(joined, cos, sin, block, q_rows, q_cols, g_rows, g_cols, delta, again):
-    again[...] = block[...]
+def prep_kernel(joined, cos, sin, q_rows, q_cols, g_rows, g_cols, delta):
     sign = half_sign((TILE, HEAD), 1)
     for t in range(2):
         tok = pl.ds(t * TILE, TILE)
@@ -84,16 +85,24 @@
             delta[t, :, lane] = jnp.sum(prod.T, axis=0, keepdims=True)
 
 
-def attention_kernel(
-    mask, info, seg, lse, delta, cos, sin, q_rows, q_cols, g_rows, g_cols, kv_mine, kv_other,
-    dkv_mine, dkv_other, qg, acc, dq, lse_rows,
-):
-    dq[...] = jnp.zeros_like(dq)
+EARLY = 5
+
+
+def attention_kernel(early, *refs):
+    mask, info, seg, lse, delta, q_rows, q_cols, g_rows, g_cols, kv_mine, kv_other = refs[:11]
+    if early:
+        dkv_mine, dkv_other, dq, acc, lse_rows = refs[11:]
+        dq[...] = jnp.zeros_like(dq)
+    else:
+        dq_in, cos, sin, dkv_mine, dkv_other, qg, acc, lse_rows, dq = refs[11:]
+        dq[...] = dq_in[...]
     for t in range(2):
         for h in range(GROUPS):
             lse_rows[t, :, pl.ds(h * TILE, TILE)] = lse[h : h + 1, t * TILE : (t + 1) * TILE]
     me = info[0]
     q_tile = 2 * me
+    first_slot = 0 if early else EARLY
+    slots = EARLY if early else 8 - EARLY
 
     def pair(t, keys, vals, allowed):
         keys_t = keys.T
@@ -110,7 +119,7 @@
 
     def tiles_of(kv, dkv, away):
         def step(j, carry):
-            slot = lax.shift_right_logical(j, 1)
+            slot = lax.shift_right_logical(j, 1) + first_slot
             back_y = (lax.shift_right_logical(me, 2) - slot) & 3
             back_zh = (me ^ (lax.shift_right_logical(slot, 1) & 2)) & 2
             tile = 2 * (4 * back_y + back_zh + ((me ^ away) & 1)) + (j & 1)
@@ -129,7 +138,7 @@
                     def _():
                         pair(t, keys, vals, None)
 
-                    if away == 0:
+                    if early and away == 0:
 
                         @pl.when(diagonal)
                         def _():
@@ -148,10 +157,12 @@
 
             return carry
 
-        lax.fori_loop(0, TILES // 2, step, 0)
+        lax.fori_loop(0, 2 * slots, step, 0)
 
     tiles_of(kv_mine, dkv_mine, 0)
     tiles_of(kv_other, dkv_other, 1)
+    if early:
+        return
     for t in range(2):
         tok = pl.ds(t * TILE, TILE)
         c, s = cos[tok, :].T, sin[tok, :].T
@@ -167,7 +178,7 @@
     return [pl.BlockSpec(memory_space=pltpu.VMEM)] * n
 
 
-def prep(joined, cos, sin, block):
+def prep(joined, cos, sin):
     s = jax.ShapeDtypeStruct
     return pl.pallas_call(
         prep_kernel,
@@ -177,39 +188,34 @@
             s((2, ROWS, HEAD), bf16),
             s((2, HEAD, ROWS), bf16),
             s((2, 1, ROWS), f32),
-            s((TOK, 2 * HEAD), bf16),
         ),
-        in_specs=vmem(4),
-        out_specs=tuple(vmem(6)),
+        in_specs=vmem(3),
+        out_specs=tuple(vmem(5)),
         compiler_params=pltpu.CompilerParams(vmem_limit_bytes=32 << 20),
-        cost_estimate=pl.CostEstimate(flops=10000000, bytes_accessed=3000000, transcendentals=0),
+        cost_estimate=pl.CostEstimate(flops=1000000, bytes_accessed=10000, transcendentals=0),
         name="prep",
-    )(joined, cos, sin, block)
-
-
-def attention(mask, info, seg, lse, delta, cos, sin, q_rows, q_cols, g_rows, g_cols, mine, other):
+    )(joined, cos, sin)
+
+
+def attention(early, mask, info, *operands):
     s = jax.ShapeDtypeStruct
-    smem = [pl.BlockSpec(memory_space=pltpu.SMEM)] * 2
-    return pl.pallas_call(
-        attention_kernel,
+    rows = (EARLY if early else 8 - EARLY) * TOK
+    dq = (2, HEAD, ROWS)
+    scratch = [pltpu.VMEM((TILE, 2 * HEAD), f32), pltpu.VMEM((2, 1, ROWS), f32)]
+    return pl.pallas_call(
+        functools.partial(attention_kernel, early),
         out_shape=(
-            s((8 * TOK, 2 * HEAD), bf16),
-            s((8 * TOK, 2 * HEAD), bf16),
-            s((ROWS, TOK), bf16),
+            s((rows, 2 * HEAD), bf16),
+            s((rows, 2 * HEAD), bf16),
+            s(dq, f32) if early else s((ROWS, TOK), bf16),
         ),
-        in_specs=smem + vmem(11),
+        in_specs=[pl.BlockSpec(memory_space=pltpu.SMEM)] * 2 + vmem(len(operands)),
         out_specs=tuple(vmem(3)),
-        scratch_shapes=[
-            pltpu.VMEM((TILE, 2 * HEAD), f32),
-            pltpu.VMEM((2, HEAD, ROWS), f32),
-            pltpu.VMEM((2, 1, ROWS), f32),
-        ],
-        compiler_params=pltpu.CompilerParams(vmem_limit_bytes=48 << 20),
-        cost_estimate=pl.CostEstimate(
-            flops=2000000000, bytes_accessed=8000000, transcendentals=1000000
-        ),
-        name="attention",
-    )(mask, info, seg, lse, delta, cos, sin, q_rows, q_cols, g_rows, g_cols, mine, other)
+        scratch_shapes=scratch if early else scratch + [pltpu.VMEM(dq, f32)],
+        compiler_params=pltpu.CompilerParams(vmem_limit_bytes=32 << 20),
+        cost_estimate=pl.CostEstimate(flops=1000000, bytes_accessed=10000, transcendentals=0),
+        name="early" if early else "late",
+    )(mask, info, *operands)
 
 
 def make_block(key, value, positions):
@@ -225,26 +231,55 @@
     )(key, value, positions.reshape(2, 1, TILE), inverse)
 
 
+def combine_kernel(early_mine, early_other, late_mine, late_other, own, across, *parts):
+    def early(k):
+        rows = pl.ds(k * TOK, TOK)
+        return early_mine[rows, :].astype(f32) + early_other[rows, :].astype(f32)
+
+    own[...] = early(0)
+    across[...] = early(4)
+    for k in range(3):
+        rows = pl.ds(k * TOK, TOK)
+        parts[k][:TOK, :] = early(k + 1).astype(bf16)
+        late = late_mine[rows, :].astype(f32) + late_other[rows, :].astype(f32)
+        parts[k][TOK:, :] = late.astype(bf16)
+
+
+def combine(early_mine, early_other, late_mine, late_other):
+    s = jax.ShapeDtypeStruct
+    return pl.pallas_call(
+        combine_kernel,
+        out_shape=(
+            [s((TOK, 2 * HEAD), f32)] * 2 + [s((2 * TOK, 2 * HEAD), bf16)] * 3
+        ),
+        in_specs=vmem(4),
+        out_specs=vmem(5),
+        cost_estimate=pl.CostEstimate(flops=1000000, bytes_accessed=10000, transcendentals=0),
+        name="combine",
+    )(early_mine, early_other, late_mine, late_other)
+
+
 WIDTH = 5120
 STEP_ROWS = 640
 
 
 def project_kernel(
-    own, across, near1, near2, near3, cos, sin, qg, wq, wk, wv, out, kg, vg
+    own, across, near1, near2, near3, cos, sin, qg, wq, wk, wv, out, grads
 ):
     total = own[...].astype(f32) + across[...].astype(f32)
-    total += near1[...].astype(f32) + near2[...].astype(f32) + near3[...].astype(f32)
+    for near in (near1, near2, near3):
+        total += near[:TOK, :].astype(f32)
     sign = half_sign((TOK, HEAD), 1)
     g = total[:, :HEAD] * SCALE
     key_grad = g * cos[...] - pltpu.roll(g * sin[...], HEAD // 2, 1) * sign
-    kg[...] = key_grad.T.astype(bf16)
-    vg[...] = total[:, HEAD:].T.astype(bf16)
+    grads[:ROWS, :] = qg[...]
+    grads[ROWS : ROWS + HEAD, :] = key_grad.T.astype(bf16)
+    grads[ROWS + HEAD :, :] = total[:, HEAD:].T.astype(bf16)
 
     def step(i, carry):
         rows = pl.ds(pl.multiple_of(i * STEP_ROWS, STEP_ROWS), STEP_ROWS)
-        result = jnp.dot(wq[rows, :], qg[...], preferred_element_type=f32)
-        result += jnp.dot(wk[rows, :], kg[...], preferred_element_type=f32)
-        result += jnp.dot(wv[rows, :], vg[...], preferred_element_type=f32)
+        weights = jnp.concatenate([wq[rows, :], wk[rows, :], wv[rows, :]], 1)
+        result = jnp.dot(weights, grads[...], preferred_element_type=f32)
         out[rows, :] = result.astype(bf16)
         return carry
 
@@ -257,7 +292,7 @@
         out_shape=jax.ShapeDtypeStruct((WIDTH, TOK), bf16),
         in_specs=vmem(11),
         out_specs=vmem(1)[0],
-        scratch_shapes=[pltpu.VMEM((HEAD, TOK), bf16), pltpu.VMEM((HEAD, TOK), bf16)],
+        scratch_shapes=[pltpu.VMEM((ROWS + 2 * HEAD, TOK), bf16)],
         compiler_params=pltpu.CompilerParams(vmem_limit_bytes=40 << 20),
         cost_estimate=pl.CostEstimate(
             flops=2350000000, bytes_accessed=12000000, transcendentals=0
@@ -298,31 +333,33 @@
     cos, sin, block = make_block(key, value, positions)
 
     across = swap_zh(block)
-    q_rows, q_cols, g_rows, g_cols, delta, again = prep(
-        jnp.concatenate([query, grad, att], 1), cos, sin, block
-    )
+    joined = jnp.concatenate([query, grad, att], 1)
+    joined, again = lax.optimization_barrier((joined, block))
     near = [shift_y(again, k) for k in (1, 2, 3)]
+    across, joined = lax.optimization_barrier((across, joined))
     far = [shift_y(across, k) for k in (1, 2, 3)]
-    mine = jnp.concatenate([block] + near + [across] + far, 0)
-    other = swap_core(mine)
-
-    dkv_mine, dkv_other, query_grad = attention(
-        block_mask, me.reshape(1), segments.reshape(TILES, 1, TILE), lse, delta, cos, sin, q_rows,
-        q_cols, g_rows, g_cols, mine, other,
-    )
-
-    summed = dkv_mine.astype(f32) + swap_core(dkv_other).astype(f32)
-    parts = lax.optimization_barrier(summed.astype(bf16)).reshape(8, TOK, 2 * HEAD)
-    far = [shift_y(parts[4 + k], -k) for k in (1, 2, 3)]
-    across = parts[4].astype(f32) + sum(p.astype(f32) for p in far)
-    across, rest = lax.optimization_barrier(
-        (across.astype(bf16), (parts[1], parts[2], parts[3]))
-    )
-    near = [shift_y(rest[k - 1], -k) for k in (1, 2, 3)]
-    across = swap_zh(across)
-    send = project(
-        parts[0], across, near, cos, sin, query_grad, w_query, key_weight, value_weight
-    )
+    ready, near = lax.optimization_barrier((prep(joined, cos, sin), near))
+    q_rows, q_cols, g_rows, g_cols, delta = ready
+    common = (
+        block_mask, me.reshape(1), segments.reshape(TILES, 1, TILE), lse, delta, q_rows, q_cols,
+        g_rows, g_cols,
+    )
+
+    mine = jnp.concatenate([block] + near + [across], 0)
+    early_mine, early_other, dq = attention(True, *common, mine, swap_core(mine))
+    dq, far = lax.optimization_barrier((dq, far))
+    mine = jnp.concatenate(far, 0)
+    late_mine, late_other, query_grad = attention(
+        False, *common, mine, swap_core(mine), dq, cos, sin
+    )
+
+    own, across, *parts = combine(
+        early_mine, swap_core(early_other), late_mine, swap_core(late_other)
+    )
+    got = [shift_y(parts[k - 1], -k) for k in (1, 2, 3)]
+    across = across + sum(p[TOK:].astype(f32) for p in got)
+    across = swap_zh(lax.optimization_barrier(across.astype(bf16)))
+    send = project(own, across, got, cos, sin, query_grad, w_query, key_weight, value_weight)
     return last_sum(lax.all_to_all(send.reshape(8, 640, TOK), TP, 0, 0))
 
 

time: 106 us -> 110 us (1.038)
  starting transfers between devices: 26.9 us -> 18.3 us
  waiting for transfers between devices: 26.7 us -> 32.5 us
  local copies, waits for them, and re-layouts: 1.32 us -> 5.43 us
  Pallas kernels: 12.4 us -> 15.3 us
    ppermute x16 -> x15, starting transfers between devices: 26.9 us -> 18.3 us  [shift(): return lax.ppermute(x, axes, perm)]
    ppermute x16 -> x15, waiting for transfers between devices: 26.7 us -> 32.5 us  [shift(): return lax.ppermute(x, axes, perm)]
    unnamed x31 -> x34, local copies, waits for them, and re-layouts: 1.24 us -> 5.41 us
    pallas_call x1 -> x3, Pallas kernels: 3.49 us -> 6.95 us  [the longest x2 4.37 us: attention(): pl.pallas_call(functools.partial(attention_kernel, early), out_shape=(s((...]
  transfers between devices with their start and end apart: 16 -> 15, of which waited for: 10 -> 12; matrix products, arithmetic and copies ran while one was open for 1% -> 1% of each run, Pallas kernels for 1% -> 5%
where the time goes in v4:
time: 110 us; the launch traced here: 111 us
  blocking collectives  36.6 us (33%)
  waiting for transfers between devices  32.5 us (30%)
  starting transfers between devices  18.3 us (17%)
  Pallas kernels  15.3 us (14%)
  local copies, waits for them, and re-layouts  5.43 us (5%)
  other arithmetic  2.26 us (2%)
    all_to_all x1, blocking collectives, local(): return last_sum(lax.all_to_all(send.reshape(8, 640, TOK), TP, 0, 0))  36.6 us
    ppermute x15, waiting for transfers between devices, shift(): return lax.ppermute(x, axes, perm)  32.5 us
    ppermute x15, starting transfers between devices, shift(): return lax.ppermute(x, axes, perm)  18.3 us
    unnamed x34, local copies, waits for them, and re-layouts  5.41 us
    pallas_call x2, Pallas kernels, attention(): pl.pallas_call(functools.partial(attention_kernel, early), out_shape=(s((...  4.37 us
    pallas_call x1, Pallas kernels, project(): pl.pallas_call(project_kernel, out_shape=jax.ShapeDtypeStruct((WIDTH, TOK...  4.24 us
    pallas_call x1, Pallas kernels, combine(): pl.pallas_call(combine_kernel, out_shape=[s((TOK, 2 * HEAD), f32)] * 2 +...  2.58 us
  transfers between devices with their start and end apart: 15, of which 12 were waited for; matrix products, arithmetic and copies ran while one was open for 1% of the time, Pallas kernels for 5%

profile of v4, /device:TPU:0, one launch (start us, length us, event | category | flops | bytes accessed | tf_op | source)
XLA Modules:
  0.0 110.5 jit_solution(12636744205788779517)
XLA Ops:
  0.0 2.2 %block.1 = (f32[256,128]{1,0:T(8,128)}, f32[256,128]{1,0:T(8,128)}, bf16[256,256]{1,0:T(8,128)(2,1)}) custom-call(bf16[256,128]{1,0:T(8,128)(2,1)} %key.1, bf16[256,128]{1,0:T(8,128)(2,1)} %value.1, s32[2,1,128]{2,1,0:T(1,128)} %bitcast.7, f32[1,128]{1,0:T(1,128)} %constant.21.clone.inverse), custom_call_target="tpu_custom_call" | custom-call | flops 5000000 | bytes 700000 | tf_op jit(solution)/shard_map/block/pallas_call | solution.py:224
  2.2 0.0 copy-start.8
  2.2 0.0 copy-start.9
  2.2 0.0 copy-start.10
  2.2 4.0 %collective-permute-start = (bf16[256,256]{1,0:T(8,128)(2,1)}, bf16[256,256]{1,0:T(8,128)(2,1)S(1)}, u32[]{:S(2)}, u32[]{:S(2)}) collective-permute-start(bf16[256,256]{1,0:T(8,128)(2,1)} %get-tuple-element.50), channel_id=1, source_target_pairs={{0,16},{16,0},{1,17},{17,1},{2,18},{18,2},{3,19},{19,3},{4,20},{20... | collective-permute-start | bytes 393224 | tf_op jit(solution)/shard_map/ppermute | solution.py:33
  6.3 1.2 %pad_maximum_fusion.joined = bf16[256,1920]{1,0:T(8,128)(2,1)S(1)} fusion(bf16[256,640]{1,0:T(8,128)(2,1)} %param.16, bf16[256,640]{1,0:T(8,128)(2,1)} %param.17, bf16[256,640]{1,0:T(8,128)(2,1)} %param.13), kind=kLoop, calls=%fused_computation | loop fusion | flops 2949120 | bytes 1966080 | tf_op jit(solution)/shard_map/concatenate | solution.py:336
  7.5 3.1 %collective-permute-start.3 = (bf16[256,256]{1,0:T(8,128)(2,1)S(1)}, bf16[256,256]{1,0:T(8,128)(2,1)S(1)}, u32[]{:S(2)}, u32[]{:S(2)}) collective-permute-start(bf16[256,256]{1,0:T(8,128)(2,1)S(1)} %copy-done.13), channel_id=1, source_target_pairs={{0,96},{32,0},{64,32},{96,64},{1,97},{33,1},{65,33},{97,65},{2,98}... | collective-permute-start | bytes 393224 | tf_op jit(solution)/shard_map/ppermute | solution.py:33
  10.6 0.6 collective-permute-start.2
  11.2 1.0 collective-permute-start.1
  12.2 0.0 collective-permute-done
  12.2 0.8 prep.1
  13.1 2.8 %collective-permute-done.3 = bf16[256,256]{1,0:T(8,128)(2,1)S(1)} collective-permute-done((bf16[256,256]{1,0:T(8,128)(2,1)S(1)}, bf16[256,256]{1,0:T(8,128)(2,1)S(1)}, u32[]{:S(2)}, u32[]{:S(2)}) %collective-permute-start.3) | collective-permute-done | bytes 131104 | tf_op jit(solution)/shard_map/ppermute | solution.py:33
  15.9 2.3 %collective-permute-done.2 = bf16[256,256]{1,0:T(8,128)(2,1)S(1)} collective-permute-done((bf16[256,256]{1,0:T(8,128)(2,1)S(1)}, bf16[256,256]{1,0:T(8,128)(2,1)S(1)}, u32[]{:S(2)}, u32[]{:S(2)}) %collective-permute-start.2) | collective-permute-done | bytes 131104 | tf_op jit(solution)/shard_map/ppermute | solution.py:33
  18.2 1.4 %collective-permute-done.1 = bf16[256,256]{1,0:T(8,128)(2,1)S(1)} collective-permute-done((bf16[256,256]{1,0:T(8,128)(2,1)S(1)}, bf16[256,256]{1,0:T(8,128)(2,1)S(1)}, u32[]{:S(2)}, u32[]{:S(2)}) %collective-permute-start.1) | collective-permute-done | bytes 131104 | tf_op jit(solution)/shard_map/ppermute | solution.py:33
  19.7 0.1 collective-permute-start.4
  19.8 0.6 collective-permute-start.8
  20.4 0.6 collective-permute-start.7
  21.0 0.9 collective-permute-start.6
  21.9 0.0 collective-permute-done.4.refs_10_
  21.9 0.0 copy-done.10
  21.9 3.0 %early.1 = (bf16[1280,256]{1,0:T(8,128)(2,1)S(1)}, bf16[1280,256]{1,0:T(8,128)(2,1)S(1)}, f32[2,128,640]{2,1,0:T(8,128)S(1)}) custom-call(s32[32,32]{1,0:T(8,128)S(1)} %copy-done.8, s32[1]{0:T(128)} %bitcast.refs_1_, s32[32,1,128]{2,1,0:T(1,128)S(1)} %bitcast.5, f32[5,256]{1,0:T(8,128)S(1)} %copy-done.10, f32[2,1,640]{2,1,0:T(1,128)S(1)} %get-tuple-element.51.refs_4_, ...), custom_call_target="tpu_custom_call" | custom-call | flops 1000000 | bytes 10000 | tf_op jit(solution)/shard_map/early/pallas_call | solution.py:205
  24.9 1.2 %collective-permute-done.8 = bf16[256,256]{1,0:T(8,128)(2,1)S(1)} collective-permute-done((bf16[256,256]{1,0:T(8,128)(2,1)S(1)}, bf16[256,256]{1,0:T(8,128)(2,1)S(1)}, u32[]{:S(2)}, u32[]{:S(2)}) %collective-permute-start.8) | collective-permute-done | bytes 131104 | tf_op jit(solution)/shard_map/ppermute | solution.py:33
  26.1 2.1 %collective-permute-done.7 = bf16[256,256]{1,0:T(8,128)(2,1)S(1)} collective-permute-done((bf16[256,256]{1,0:T(8,128)(2,1)S(1)}, bf16[256,256]{1,0:T(8,128)(2,1)S(1)}, u32[]{:S(2)}, u32[]{:S(2)}) %collective-permute-start.7) | collective-permute-done | bytes 131104 | tf_op jit(solution)/shard_map/ppermute | solution.py:33
  28.2 2.0 %collective-permute-done.6 = bf16[256,256]{1,0:T(8,128)(2,1)S(1)} collective-permute-done((bf16[256,256]{1,0:T(8,128)(2,1)S(1)}, bf16[256,256]{1,0:T(8,128)(2,1)S(1)}, u32[]{:S(2)}, u32[]{:S(2)}) %collective-permute-start.6) | collective-permute-done | bytes 131104 | tf_op jit(solution)/shard_map/ppermute | solution.py:33
  30.3 0.1 collective-permute-start.9
  30.4 0.5 collective-permute-start.5
  30.9 1.2 %collective-permute-done.9.refs_10_ = bf16[768,256]{1,0:T(8,128)(2,1)S(1)} collective-permute-done((bf16[768,256]{1,0:T(8,128)(2,1)S(1)}, bf16[768,256]{1,0:T(8,128)(2,1)S(1)}, u32[]{:S(2)}, u32[]{:S(2)}) %collective-permute-start.9) | collective-permute-done | bytes 393248 | tf_op jit(solution)/shard_map/ppermute | solution.py:33
  32.1 1.4 %late.1 = (bf16[768,256]{1,0:T(8,128)(2,1)S(1)}, bf16[768,256]{1,0:T(8,128)(2,1)S(1)}, bf16[640,256]{1,0:T(8,128)(2,1)S(1)}) custom-call(s32[32,32]{1,0:T(8,128)S(1)} %copy-done.8, s32[1]{0:T(128)} %bitcast.refs_1_, s32[32,1,128]{2,1,0:T(1,128)S(1)} %bitcast.6, f32[5,256]{1,0:T(8,128)S(1)} %copy-done.10, f32[2,1,640]{2,1,0:T(1,128)S(1)} %get-tuple-element.51.refs_4_, ...), custom_call_target="tpu_custom_call" | custom-call | flops 1000000 | bytes 10000 | tf_op jit(solution)/shard_map/late/pallas_call | solution.py:205
  33.5 0.7 copy-done.6
  34.3 0.1 collective-permute-start.10
  34.4 0.0 collective-permute-done.5.early_other
  34.4 1.6 %collective-permute-done.10.late_other = bf16[768,256]{1,0:T(8,128)(2,1)S(1)} collective-permute-done((bf16[768,256]{1,0:T(8,128)(2,1)S(1)}, bf16[768,256]{1,0:T(8,128)(2,1)S(1)}, u32[]{:S(2)}, u32[]{:S(2)}) %collective-permute-start.10) | collective-permute-done | bytes 393248 | tf_op jit(solution)/shard_map/ppermute | solution.py:33
  36.0 0.7 copy-done.12
  36.7 2.6 %combine.1 = (f32[256,256]{1,0:T(8,128)}, f32[256,256]{1,0:T(8,128)}, bf16[512,256]{1,0:T(8,128)(2,1)}, bf16[512,256]{1,0:T(8,128)(2,1)}, bf16[512,256]{1,0:T(8,128)(2,1)}) custom-call(bf16[1280,256]{1,0:T(8,128)(2,1)} %copy-done.5, bf16[1280,256]{1,0:T(8,128)(2,1)} %copy-done.11, bf16[768,256]{1,0:T(8,128)(2,1)} %copy-done.6, bf16[768,256]{1,0:T(8,128)(2,1)} %copy-done.12), custom_call_target="tpu_custom_call" | custom-call | flops 1000000 | bytes 10000 | tf_op jit(solution)/shard_map/combine/pallas_call | solution.py:250
  39.3 0.9 collective-permute-start.11
  40.2 0.3 collective-permute-start.12
  40.5 1.0 collective-permute-start.13
  41.5 7.2 %collective-permute-done.11.near1 = bf16[512,256]{1,0:T(8,128)(2,1)S(1)} collective-permute-done((bf16[512,256]{1,0:T(8,128)(2,1)}, bf16[512,256]{1,0:T(8,128)(2,1)S(1)}, u32[]{:S(2)}, u32[]{:S(2)}) %collective-permute-start.11) | collective-permute-done | bytes 262176 | tf_op jit(solution)/shard_map/ppermute | solution.py:33
  48.7 2.5 %collective-permute-done.12.near2 = bf16[512,256]{1,0:T(8,128)(2,1)S(1)} collective-permute-done((bf16[512,256]{1,0:T(8,128)(2,1)}, bf16[512,256]{1,0:T(8,128)(2,1)S(1)}, u32[]{:S(2)}, u32[]{:S(2)}) %collective-permute-start.12) | collective-permute-done | bytes 262176 | tf_op jit(solution)/shard_map/ppermute | solution.py:33
  51.2 4.4 %collective-permute-done.13.near3 = bf16[512,256]{1,0:T(8,128)(2,1)S(1)} collective-permute-done((bf16[512,256]{1,0:T(8,128)(2,1)}, bf16[512,256]{1,0:T(8,128)(2,1)S(1)}, u32[]{:S(2)}, u32[]{:S(2)}) %collective-permute-start.13) | collective-permute-done | bytes 262176 | tf_op jit(solution)/shard_map/ppermute | solution.py:33
  55.6 1.0 add_convert_fusion
  56.6 4.5 %collective-permute-start.14 = (bf16[256,256]{1,0:T(8,128)(2,1)S(1)}, bf16[256,256]{1,0:T(8,128)(2,1)S(1)}, u32[]{:S(2)}, u32[]{:S(2)}) collective-permute-start(bf16[256,256]{1,0:T(8,128)(2,1)S(1)} %add_convert_fusion), channel_id=1, source_target_pairs={{0,16},{16,0},{1,17},{17,1},{2,18},{18,2},{3,19},{19,3},{4,20},{20... | collective-permute-start | bytes 393224 | tf_op jit(solution)/shard_map/ppermute | solution.py:33
  61.1 3.7 %collective-permute-done.14.across = bf16[256,256]{1,0:T(8,128)(2,1)S(1)} collective-permute-done((bf16[256,256]{1,0:T(8,128)(2,1)S(1)}, bf16[256,256]{1,0:T(8,128)(2,1)S(1)}, u32[]{:S(2)}, u32[]{:S(2)}) %collective-permute-start.14) | collective-permute-done | bytes 131104 | tf_op jit(solution)/shard_map/ppermute | solution.py:33
  64.8 2.9 %copy-done = bf16[5120,640]{1,0:T(8,128)(2,1)S(1)} copy-done((bf16[5120,640]{1,0:T(8,128)(2,1)S(1)}, bf16[5120,640]{1,0:T(8,128)(2,1)}, u32[]{:S(2)}) %copy-start) | copy-done | bytes 6553624
  67.6 0.9 copy-done.7
  68.6 4.2 %project.1 = bf16[5120,256]{1,0:T(8,128)(2,1)S(1)} custom-call(f32[256,256]{1,0:T(8,128)S(1)} %copy-done.7, bf16[256,256]{1,0:T(8,128)(2,1)S(1)} %collective-permute-done.14.across, bf16[512,256]{1,0:T(8,128)(2,1)S(1)} %collective-permute-done.11.near1, bf16[512,256]{1,0:T(8,128)(2,1)S(1)} %collective-permute-done.12.near2, ...), custom_call_target="tpu_custom_call" | custom-call | flops 2350000128 | bytes 12000000 | tf_op jit(solution)/shard_map/project/pallas_call | solution.py:290
  72.8 36.6 %all_to_all.5.parts = bf16[8,640,256]{2,1,0:T(8,128)(2,1)S(1)} all-to-all(bf16[8,640,256]{2,1,0:T(8,128)(2,1)S(1)} %bitcast.4), channel_id=1, replica_groups=mesh['y'=4,'zh'=2,'core'=2,'x'=4,'zl'=2] {'x','zl'}, dimensions={0} | all-to-all | bytes 5242880 | tf_op jit(solution)/shard_map/all_to_all | solution.py:363
  109.4 1.1 last_sum.1
  (28 shorter events, 0.1 us)
Async XLA Ops:
  2.2 5.3 %copy-start.13 = (bf16[256,256]{1,0:T(8,128)(2,1)S(1)}, bf16[256,256]{1,0:T(8,128)(2,1)}, u32[]{:S(2)}) copy-start(bf16[256,256]{1,0:T(8,128)(2,1)} %get-tuple-element.50) | copy-start | bytes 393220
  2.2 10.1 %copy-start.3 = (f32[256,128]{1,0:T(8,128)S(1)}, f32[256,128]{1,0:T(8,128)}, u32[]{:S(2)}) copy-start(f32[256,128]{1,0:T(8,128)} %get-tuple-element.43.cos.refs_12_) | copy-start | bytes 393220
  2.2 10.1 %copy-start.4 = (f32[256,128]{1,0:T(8,128)S(1)}, f32[256,128]{1,0:T(8,128)}, u32[]{:S(2)}) copy-start(f32[256,128]{1,0:T(8,128)} %get-tuple-element.44.sin.refs_13_) | copy-start | bytes 393220
  2.2 19.7 %copy-start.8 = (s32[32,32]{1,0:T(8,128)S(1)}, s32[32,32]{1,0:T(8,128)}, u32[]{:S(2)}) copy-start(s32[32,32]{1,0:T(8,128)} %refs_0_.3) | copy-start | bytes 12292
  2.2 19.7 %copy-start.9 = (s32[4096]{0:T(1024)S(1)}, s32[4096]{0:T(1024)}, u32[]{:S(2)}) copy-start(s32[4096]{0:T(1024)} %param.21) | copy-start | bytes 49156
  2.2 19.7 %copy-start.10 = (f32[5,256]{1,0:T(8,128)S(1)}, f32[5,256]{1,0:T(8,128)}, u32[]{:S(2)}) copy-start(f32[5,256]{1,0:T(8,128)} %refs_3_.3) | copy-start | bytes 15364
  2.2 10.0 %collective-permute-start = (bf16[256,256]{1,0:T(8,128)(2,1)}, bf16[256,256]{1,0:T(8,128)(2,1)S(1)}, u32[]{:S(2)}, u32[]{:S(2)}) collective-permute-start(bf16[256,256]{1,0:T(8,128)(2,1)} %get-tuple-element.50), channel_id=1, source_target_pairs={{0,16},{16,0},{1,17},{17,1},{2,18},{18,2},{3,19},{19,3},{4,20},{20... | collective-permute-start | bytes 393224 | tf_op jit(solution)/shard_map/ppermute | solution.py:33
  7.5 8.4 %collective-permute-start.3 = (bf16[256,256]{1,0:T(8,128)(2,1)S(1)}, bf16[256,256]{1,0:T(8,128)(2,1)S(1)}, u32[]{:S(2)}, u32[]{:S(2)}) collective-permute-start(bf16[256,256]{1,0:T(8,128)(2,1)S(1)} %copy-done.13), channel_id=1, source_target_pairs={{0,96},{32,0},{64,32},{96,64},{1,97},{33,1},{65,33},{97,65},{2,98}... | collective-permute-start | bytes 393224 | tf_op jit(solution)/shard_map/ppermute | solution.py:33
  10.6 7.6 %collective-permute-start.2 = (bf16[256,256]{1,0:T(8,128)(2,1)S(1)}, bf16[256,256]{1,0:T(8,128)(2,1)S(1)}, u32[]{:S(2)}, u32[]{:S(2)}) collective-permute-start(bf16[256,256]{1,0:T(8,128)(2,1)S(1)} %copy-done.13), channel_id=1, source_target_pairs={{0,64},{32,96},{64,0},{96,32},{1,65},{33,97},{65,1},{97,33},{2,66}... | collective-permute-start | bytes 393224 | tf_op jit(solution)/shard_map/ppermute | solution.py:33
  11.2 8.4 %collective-permute-start.1 = (bf16[256,256]{1,0:T(8,128)(2,1)S(1)}, bf16[256,256]{1,0:T(8,128)(2,1)S(1)}, u32[]{:S(2)}, u32[]{:S(2)}) collective-permute-start(bf16[256,256]{1,0:T(8,128)(2,1)S(1)} %copy-done.13), channel_id=1, source_target_pairs={{0,32},{32,64},{64,96},{96,0},{1,33},{33,65},{65,97},{97,1},{2,34}... | collective-permute-start | bytes 393224 | tf_op jit(solution)/shard_map/ppermute | solution.py:33
  19.7 2.2 %collective-permute-start.4 = (bf16[1280,256]{1,0:T(8,128)(2,1)S(1)}, bf16[1280,256]{1,0:T(8,128)(2,1)S(1)}, u32[]{:S(2)}, u32[]{:S(2)}) collective-permute-start(bf16[1280,256]{1,0:T(8,128)(2,1)S(1)} %constant_dynamic-update-slice_fusion.refs_9_), channel_id=1, source_target_pairs={{0,8},{8,0},{1,9},{9,1},{2,10},{10,2},{3,11},{11,3},{4,12},{12,4},... | collective-permute-start | bytes 1966088 | tf_op jit(solution)/shard_map/ppermute | solution.py:33
  19.8 6.4 %collective-permute-start.8 = (bf16[256,256]{1,0:T(8,128)(2,1)S(1)}, bf16[256,256]{1,0:T(8,128)(2,1)S(1)}, u32[]{:S(2)}, u32[]{:S(2)}) collective-permute-start(bf16[256,256]{1,0:T(8,128)(2,1)S(1)} %collective-permute-done), channel_id=1, source_target_pairs={{0,96},{32,0},{64,32},{96,64},{1,97},{33,1},{65,33},{97,65},{2,98}... | collective-permute-start | bytes 393224 | tf_op jit(solution)/shard_map/ppermute | solution.py:33
  20.4 7.8 %collective-permute-start.7 = (bf16[256,256]{1,0:T(8,128)(2,1)S(1)}, bf16[256,256]{1,0:T(8,128)(2,1)S(1)}, u32[]{:S(2)}, u32[]{:S(2)}) collective-permute-start(bf16[256,256]{1,0:T(8,128)(2,1)S(1)} %collective-permute-done), channel_id=1, source_target_pairs={{0,64},{32,96},{64,0},{96,32},{1,65},{33,97},{65,1},{97,33},{2,66}... | collective-permute-start | bytes 393224 | tf_op jit(solution)/shard_map/ppermute | solution.py:33
  21.0 9.2 %collective-permute-start.6 = (bf16[256,256]{1,0:T(8,128)(2,1)S(1)}, bf16[256,256]{1,0:T(8,128)(2,1)S(1)}, u32[]{:S(2)}, u32[]{:S(2)}) collective-permute-start(bf16[256,256]{1,0:T(8,128)(2,1)S(1)} %collective-permute-done), channel_id=1, source_target_pairs={{0,32},{32,64},{64,96},{96,0},{1,33},{33,65},{65,97},{97,1},{2,34}... | collective-permute-start | bytes 393224 | tf_op jit(solution)/shard_map/ppermute | solution.py:33
  24.9 5.4 %copy-start.5 = (bf16[1280,256]{1,0:T(8,128)(2,1)}, bf16[1280,256]{1,0:T(8,128)(2,1)S(1)}, u32[]{:S(2)}) copy-start(bf16[1280,256]{1,0:T(8,128)(2,1)S(1)} %get-tuple-element.60.early_mine) | copy-start | bytes 1966084
  30.3 1.8 %collective-permute-start.9 = (bf16[768,256]{1,0:T(8,128)(2,1)S(1)}, bf16[768,256]{1,0:T(8,128)(2,1)S(1)}, u32[]{:S(2)}, u32[]{:S(2)}) collective-permute-start(bf16[768,256]{1,0:T(8,128)(2,1)S(1)} %constant_dynamic-update-slice_fusion.5.refs_9_), channel_id=1, source_target_pairs={{0,8},{8,0},{1,9},{9,1},{2,10},{10,2},{3,11},{11,3},{4,12},{12,4},... | collective-permute-start | bytes 1179656 | tf_op jit(solution)/shard_map/ppermute | solution.py:33
  30.4 4.0 %collective-permute-start.5 = (bf16[1280,256]{1,0:T(8,128)(2,1)S(1)}, bf16[1280,256]{1,0:T(8,128)(2,1)S(1)}, u32[]{:S(2)}, u32[]{:S(2)}) collective-permute-start(bf16[1280,256]{1,0:T(8,128)(2,1)S(1)} %get-tuple-element.61), channel_id=1, source_target_pairs={{0,8},{8,0},{1,9},{9,1},{2,10},{10,2},{3,11},{11,3},{4,12},{12,4},... | collective-permute-start | bytes 1966088 | tf_op jit(solution)/shard_map/ppermute | solution.py:33
  33.5 0.7 copy-start.6
  34.3 30.5 %copy-start.1 = (bf16[5120,128]{1,0:T(8,128)(2,1)S(1)}, bf16[5120,128]{1,0:T(8,128)(2,1)}, u32[]{:S(2)}) copy-start(bf16[5120,128]{1,0:T(8,128)(2,1)} %wk.1) | copy-start | bytes 3932164
  34.3 30.5 %copy-start.2 = (bf16[5120,128]{1,0:T(8,128)(2,1)S(1)}, bf16[5120,128]{1,0:T(8,128)(2,1)}, u32[]{:S(2)}) copy-start(bf16[5120,128]{1,0:T(8,128)(2,1)} %wv.1) | copy-start | bytes 3932164
  34.3 1.7 %collective-permute-start.10 = (bf16[768,256]{1,0:T(8,128)(2,1)S(1)}, bf16[768,256]{1,0:T(8,128)(2,1)S(1)}, u32[]{:S(2)}, u32[]{:S(2)}) collective-permute-start(bf16[768,256]{1,0:T(8,128)(2,1)S(1)} %get-tuple-element.68), channel_id=1, source_target_pairs={{0,8},{8,0},{1,9},{9,1},{2,10},{10,2},{3,11},{11,3},{4,12},{12,4},... | collective-permute-start | bytes 1179656 | tf_op jit(solution)/shard_map/ppermute | solution.py:33
  34.4 1.6 %copy-start.11 = (bf16[1280,256]{1,0:T(8,128)(2,1)}, bf16[1280,256]{1,0:T(8,128)(2,1)S(1)}, u32[]{:S(2)}) copy-start(bf16[1280,256]{1,0:T(8,128)(2,1)S(1)} %collective-permute-done.5.early_other) | copy-start | bytes 1966084
  36.0 0.8 copy-start.12
  39.3 9.4 %collective-permute-start.11 = (bf16[512,256]{1,0:T(8,128)(2,1)}, bf16[512,256]{1,0:T(8,128)(2,1)S(1)}, u32[]{:S(2)}, u32[]{:S(2)}) collective-permute-start(bf16[512,256]{1,0:T(8,128)(2,1)} %get-tuple-element.71), channel_id=1, source_target_pairs={{0,96},{32,0},{64,32},{96,64},{1,97},{33,1},{65,33},{97,65},{2,98}... | collective-permute-start | bytes 786440 | tf_op jit(solution)/shard_map/ppermute | solution.py:33
  40.2 11.0 %collective-permute-start.12 = (bf16[512,256]{1,0:T(8,128)(2,1)}, bf16[512,256]{1,0:T(8,128)(2,1)S(1)}, u32[]{:S(2)}, u32[]{:S(2)}) collective-permute-start(bf16[512,256]{1,0:T(8,128)(2,1)} %get-tuple-element.72), channel_id=1, source_target_pairs={{0,64},{32,96},{64,0},{96,32},{1,65},{33,97},{65,1},{97,33},{2,66}... | collective-permute-start | bytes 786440 | tf_op jit(solution)/shard_map/ppermute | solution.py:33
  40.5 15.1 %collective-permute-start.13 = (bf16[512,256]{1,0:T(8,128)(2,1)}, bf16[512,256]{1,0:T(8,128)(2,1)S(1)}, u32[]{:S(2)}, u32[]{:S(2)}) collective-permute-start(bf16[512,256]{1,0:T(8,128)(2,1)} %get-tuple-element.73), channel_id=1, source_target_pairs={{0,32},{32,64},{64,96},{96,0},{1,33},{33,65},{65,97},{97,1},{2,34}... | collective-permute-start | bytes 786440 | tf_op jit(solution)/shard_map/ppermute | solution.py:33
  56.6 8.1 %collective-permute-start.14 = (bf16[256,256]{1,0:T(8,128)(2,1)S(1)}, bf16[256,256]{1,0:T(8,128)(2,1)S(1)}, u32[]{:S(2)}, u32[]{:S(2)}) collective-permute-start(bf16[256,256]{1,0:T(8,128)(2,1)S(1)} %add_convert_fusion), channel_id=1, source_target_pairs={{0,16},{16,0},{1,17},{17,1},{2,18},{18,2},{3,19},{19,3},{4,20},{20... | collective-permute-start | bytes 393224 | tf_op jit(solution)/shard_map/ppermute | solution.py:33
  64.8 2.9 %copy-start = (bf16[5120,640]{1,0:T(8,128)(2,1)S(1)}, bf16[5120,640]{1,0:T(8,128)(2,1)}, u32[]{:S(2)}) copy-start(bf16[5120,640]{1,0:T(8,128)(2,1)} %wq.1) | copy-start | bytes 19660804
  67.6 0.9 copy-start.7

commit v5 on v3

--- a/solution.py
+++ b/solution.py
@@ -64,8 +64,7 @@
         block[tok, HEAD:] = value[tok, :]
 
 
-def prep_kernel(joined, cos, sin, block, q_rows, q_cols, g_rows, g_cols, delta, again):
-    again[...] = block[...]
+def prep_kernel(joined, cos, sin, q_rows, q_cols, g_rows, g_cols, delta):
     sign = half_sign((TILE, HEAD), 1)
     for t in range(2):
         tok = pl.ds(t * TILE, TILE)
@@ -84,9 +83,13 @@
             delta[t, :, lane] = jnp.sum(prod.T, axis=0, keepdims=True)
 
 
+EARLY = 5
+
+
 def attention_kernel(
-    mask, info, seg, lse, delta, cos, sin, q_rows, q_cols, g_rows, g_cols, kv_mine, kv_other,
-    dkv_mine, dkv_other, qg, acc, dq, lse_rows,
+    mask, info, seg, lse, delta, cos, sin, q_rows, q_cols, g_rows, g_cols,
+    early_mine, early_other, late_mine, late_other,
+    d_early_mine, d_early_other, d_late_mine, d_late_other, qg, acc, dq, lse_rows,
 ):
     dq[...] = jnp.zeros_like(dq)
     for t in range(2):
@@ -108,9 +111,9 @@
         acc[:, :HEAD] += jnp.dot(dscore, q_rows[t], preferred_element_type=f32)
         acc[:, HEAD:] += jnp.dot(probs, g_rows[t], preferred_element_type=f32)
 
-    def tiles_of(kv, dkv, away):
+    def tiles_of(kv, dkv, away, first_slot, slots):
         def step(j, carry):
-            slot = lax.shift_right_logical(j, 1)
+            slot = lax.shift_right_logical(j, 1) + first_slot
             back_y = (lax.shift_right_logical(me, 2) - slot) & 3
             back_zh = (me ^ (lax.shift_right_logical(slot, 1) & 2)) & 2
             tile = 2 * (4 * back_y + back_zh + ((me ^ away) & 1)) + (j & 1)
@@ -129,7 +132,7 @@
                     def _():
                         pair(t, keys, vals, None)
 
-                    if away == 0:
+                    if away == 0 and first_slot == 0:
 
                         @pl.when(diagonal)
                         def _():
@@ -148,10 +151,12 @@
 
             return carry
 
-        lax.fori_loop(0, TILES // 2, step, 0)
-
-    tiles_of(kv_mine, dkv_mine, 0)
-    tiles_of(kv_other, dkv_other, 1)
+        lax.fori_loop(0, 2 * slots, step, 0)
+
+    tiles_of(early_mine, d_early_mine, 0, 0, EARLY)
+    tiles_of(early_other, d_early_other, 1, 0, EARLY)
+    tiles_of(late_mine, d_late_mine, 0, EARLY, 8 - EARLY)
+    tiles_of(late_other, d_late_other, 1, EARLY, 8 - EARLY)
     for t in range(2):
         tok = pl.ds(t * TILE, TILE)
         c, s = cos[tok, :].T, sin[tok, :].T
@@ -167,7 +172,7 @@
     return [pl.BlockSpec(memory_space=pltpu.VMEM)] * n
 
 
-def prep(joined, cos, sin, block):
+def prep(joined, cos, sin):
     s = jax.ShapeDtypeStruct
     return pl.pallas_call(
         prep_kernel,
@@ -177,39 +182,34 @@
             s((2, ROWS, HEAD), bf16),
             s((2, HEAD, ROWS), bf16),
             s((2, 1, ROWS), f32),
-            s((TOK, 2 * HEAD), bf16),
         ),
-        in_specs=vmem(4),
-        out_specs=tuple(vmem(6)),
-        compiler_params=pltpu.CompilerParams(vmem_limit_bytes=32 << 20),
-        cost_estimate=pl.CostEstimate(flops=10000000, bytes_accessed=3000000, transcendentals=0),
+        in_specs=vmem(3),
+        out_specs=tuple(vmem(5)),
+        compiler_params=pltpu.CompilerParams(vmem_limit_bytes=12 << 20),
+        cost_estimate=pl.CostEstimate(flops=1000000, bytes_accessed=10000, transcendentals=0),
         name="prep",
-    )(joined, cos, sin, block)
-
-
-def attention(mask, info, seg, lse, delta, cos, sin, q_rows, q_cols, g_rows, g_cols, mine, other):
+    )(joined, cos, sin)
+
+
+def attention(mask, info, *operands):
     s = jax.ShapeDtypeStruct
-    smem = [pl.BlockSpec(memory_space=pltpu.SMEM)] * 2
+    early, late = (s((n * TOK, 2 * HEAD), bf16) for n in (EARLY, 8 - EARLY))
     return pl.pallas_call(
         attention_kernel,
-        out_shape=(
-            s((8 * TOK, 2 * HEAD), bf16),
-            s((8 * TOK, 2 * HEAD), bf16),
-            s((ROWS, TOK), bf16),
-        ),
-        in_specs=smem + vmem(11),
-        out_specs=tuple(vmem(3)),
+        out_shape=(early, early, late, late, s((ROWS, TOK), bf16)),
+        in_specs=[pl.BlockSpec(memory_space=pltpu.SMEM)] * 2 + vmem(len(operands)),
+        out_specs=tuple(vmem(5)),
         scratch_shapes=[
             pltpu.VMEM((TILE, 2 * HEAD), f32),
             pltpu.VMEM((2, HEAD, ROWS), f32),
             pltpu.VMEM((2, 1, ROWS), f32),
         ],
-        compiler_params=pltpu.CompilerParams(vmem_limit_bytes=48 << 20),
+        compiler_params=pltpu.CompilerParams(vmem_limit_bytes=16 << 20),
         cost_estimate=pl.CostEstimate(
             flops=2000000000, bytes_accessed=8000000, transcendentals=1000000
         ),
         name="attention",
-    )(mask, info, seg, lse, delta, cos, sin, q_rows, q_cols, g_rows, g_cols, mine, other)
+    )(mask, info, *operands)
 
 
 def make_block(key, value, positions):
@@ -230,21 +230,22 @@
 
 
 def project_kernel(
-    own, across, near1, near2, near3, cos, sin, qg, wq, wk, wv, out, kg, vg
+    own, across, near1, near2, near3, cos, sin, qg, wq, wk, wv, out, grads
 ):
     total = own[...].astype(f32) + across[...].astype(f32)
-    total += near1[...].astype(f32) + near2[...].astype(f32) + near3[...].astype(f32)
+    for near in (near1, near2, near3):
+        total += near[...].astype(f32)
     sign = half_sign((TOK, HEAD), 1)
     g = total[:, :HEAD] * SCALE
     key_grad = g * cos[...] - pltpu.roll(g * sin[...], HEAD // 2, 1) * sign
-    kg[...] = key_grad.T.astype(bf16)
-    vg[...] = total[:, HEAD:].T.astype(bf16)
+    grads[:ROWS, :] = qg[...]
+    grads[ROWS : ROWS + HEAD, :] = key_grad.T.astype(bf16)
+    grads[ROWS + HEAD :, :] = total[:, HEAD:].T.astype(bf16)
 
     def step(i, carry):
         rows = pl.ds(pl.multiple_of(i * STEP_ROWS, STEP_ROWS), STEP_ROWS)
-        result = jnp.dot(wq[rows, :], qg[...], preferred_element_type=f32)
-        result += jnp.dot(wk[rows, :], kg[...], preferred_element_type=f32)
-        result += jnp.dot(wv[rows, :], vg[...], preferred_element_type=f32)
+        weights = jnp.concatenate([wq[rows, :], wk[rows, :], wv[rows, :]], 1)
+        result = jnp.dot(weights, grads[...], preferred_element_type=f32)
         out[rows, :] = result.astype(bf16)
         return carry
 
@@ -257,8 +258,8 @@
         out_shape=jax.ShapeDtypeStruct((WIDTH, TOK), bf16),
         in_specs=vmem(11),
         out_specs=vmem(1)[0],
-        scratch_shapes=[pltpu.VMEM((HEAD, TOK), bf16), pltpu.VMEM((HEAD, TOK), bf16)],
-        compiler_params=pltpu.CompilerParams(vmem_limit_bytes=40 << 20),
+        scratch_shapes=[pltpu.VMEM((ROWS + 2 * HEAD, TOK), bf16)],
+        compiler_params=pltpu.CompilerParams(vmem_limit_bytes=16 << 20),
         cost_estimate=pl.CostEstimate(
             flops=2350000000, bytes_accessed=12000000, transcendentals=0
         ),
@@ -298,31 +299,31 @@
     cos, sin, block = make_block(key, value, positions)
 
     across = swap_zh(block)
-    q_rows, q_cols, g_rows, g_cols, delta, again = prep(
-        jnp.concatenate([query, grad, att], 1), cos, sin, block
+    joined = jnp.concatenate([query, grad, att], 1)
+    joined, again = lax.optimization_barrier((joined, block))
+    near = [shift_y(again, k) for k in (1, 2, 3)]
+    across, joined = lax.optimization_barrier((across, joined))
+    far = [shift_y(across, k) for k in (1, 2, 3)]
+    q_rows, q_cols, g_rows, g_cols, delta = prep(joined, cos, sin)
+    early = jnp.concatenate([block] + near + [across], 0)
+    late = jnp.concatenate(far, 0)
+
+    early_mine, early_other, late_mine, late_other, query_grad = attention(
+        block_mask, me.reshape(1), segments.reshape(TILES, 1, TILE), lse, delta, cos, sin, q_rows,
+        q_cols, g_rows, g_cols, early, swap_core(early), late, swap_core(late),
     )
-    near = [shift_y(again, k) for k in (1, 2, 3)]
-    far = [shift_y(across, k) for k in (1, 2, 3)]
-    mine = jnp.concatenate([block] + near + [across] + far, 0)
-    other = swap_core(mine)
-
-    dkv_mine, dkv_other, query_grad = attention(
-        block_mask, me.reshape(1), segments.reshape(TILES, 1, TILE), lse, delta, cos, sin, q_rows,
-        q_cols, g_rows, g_cols, mine, other,
-    )
-
-    summed = dkv_mine.astype(f32) + swap_core(dkv_other).astype(f32)
-    parts = lax.optimization_barrier(summed.astype(bf16)).reshape(8, TOK, 2 * HEAD)
-    far = [shift_y(parts[4 + k], -k) for k in (1, 2, 3)]
-    across = parts[4].astype(f32) + sum(p.astype(f32) for p in far)
-    across, rest = lax.optimization_barrier(
-        (across.astype(bf16), (parts[1], parts[2], parts[3]))
-    )
-    near = [shift_y(rest[k - 1], -k) for k in (1, 2, 3)]
-    across = swap_zh(across)
-    send = project(
-        parts[0], across, near, cos, sin, query_grad, w_query, key_weight, value_weight
-    )
+
+    late = late_mine.astype(f32) + swap_core(late_other).astype(f32)
+    early = early_mine.astype(f32) + swap_core(early_other).astype(f32)
+    own, across = early[:TOK], early[4 * TOK :]
+    parts = [early[k * TOK : (k + 1) * TOK].astype(bf16) for k in (1, 2, 3)]
+    parts += [late[k * TOK : (k + 1) * TOK].astype(bf16) for k in range(3)]
+    own, across, parts = lax.optimization_barrier((own, across, parts))
+    far = [shift_y(parts[2 + k], -k) for k in (1, 2, 3)]
+    near = [shift_y(parts[k - 1], -k) for k in (1, 2, 3)]
+    across = across + sum(p.astype(f32) for p in far)
+    across = swap_zh(lax.optimization_barrier(across.astype(bf16)))
+    send = project(own, across, near, cos, sin, query_grad, w_query, key_weight, value_weight)
     return last_sum(lax.all_to_all(send.reshape(8, 640, TOK), TP, 0, 0))
 
 

time: 106 us -> 96.6 us (0.911)
  waiting for transfers between devices: 26.7 us -> 19 us
  local copies, waits for them, and re-layouts: 1.32 us -> 0.23 us
    ppermute x16 -> x18, waiting for transfers between devices: 26.7 us -> 19 us  [shift(): return lax.ppermute(x, axes, perm)]
    unnamed x31 -> x26, local copies, waits for them, and re-layouts: 1.24 us -> 0.11 us
    ppermute x16 -> x18, starting transfers between devices: 26.9 us -> 26.8 us  [shift(): return lax.ppermute(x, axes, perm)]
  transfers between devices with their start and end apart: 16 -> 18, of which waited for: 10 -> 10; matrix products, arithmetic and copies ran while one was open for 1% -> 2% of each run, Pallas kernels for 1% -> 1%
where the time goes in v5:
time: 96.6 us; the launch traced here: 96.3 us
  blocking collectives  36.5 us (38%)
  starting transfers between devices  26.8 us (28%)
  waiting for transfers between devices  19 us (20%)
  Pallas kernels  11.9 us (12%)
  other arithmetic  1.62 us (2%)
    all_to_all x1, blocking collectives, local(): return last_sum(lax.all_to_all(send.reshape(8, 640, TOK), TP, 0, 0))  36.5 us
    ppermute x18, starting transfers between devices, shift(): return lax.ppermute(x, axes, perm)  26.8 us
    ppermute x18, waiting for transfers between devices, shift(): return lax.ppermute(x, axes, perm)  19 us
    pallas_call x1, Pallas kernels, project(): pl.pallas_call(project_kernel, out_shape=jax.ShapeDtypeStruct((WIDTH, TOK...  4.24 us
    pallas_call x1, Pallas kernels, attention(): pl.pallas_call(attention_kernel, out_shape=(early, early, late, late, s((...  3.57 us
    pallas_call x1, Pallas kernels, make_block(): pl.pallas_call(block_kernel, out_shape=(s((TOK, HEAD), f32), s((TOK, HEAD...  2.18 us
  transfers between devices with their start and end apart: 18, of which 10 were waited for; matrix products, arithmetic and copies ran while one was open for 2% of the time, Pallas kernels for 1%

profile of v5, /device:TPU:0, one launch (start us, length us, event | category | flops | bytes accessed | tf_op | source)
XLA Modules:
  0.0 96.3 jit_solution(3518282799556774576)
XLA Ops:
  0.0 2.2 %block.1 = (f32[256,128]{1,0:T(8,128)}, f32[256,128]{1,0:T(8,128)}, bf16[256,256]{1,0:T(8,128)(2,1)}) custom-call(bf16[256,128]{1,0:T(8,128)(2,1)} %key.1, bf16[256,128]{1,0:T(8,128)(2,1)} %value.1, s32[2,1,128]{2,1,0:T(1,128)} %bitcast.8, f32[1,128]{1,0:T(1,128)} %constant.21.clone.inverse), custom_call_target="tpu_custom_call" | custom-call | flops 5000000 | bytes 700000 | tf_op jit(solution)/shard_map/block/pallas_call | solution.py:218
  2.2 4.0 %collective-permute-start = (bf16[256,256]{1,0:T(8,128)(2,1)}, bf16[256,256]{1,0:T(8,128)(2,1)S(1)}, u32[]{:S(2)}, u32[]{:S(2)}) collective-permute-start(bf16[256,256]{1,0:T(8,128)(2,1)} %get-tuple-element.40), channel_id=1, source_target_pairs={{0,16},{16,0},{1,17},{17,1},{2,18},{18,2},{3,19},{19,3},{4,20},{20... | collective-permute-start | bytes 393224 | tf_op jit(solution)/shard_map/ppermute | solution.py:31
  6.2 1.2 %pad_maximum_fusion.joined = bf16[256,1920]{1,0:T(8,128)(2,1)S(1)} fusion(bf16[256,640]{1,0:T(8,128)(2,1)} %param.16, bf16[256,640]{1,0:T(8,128)(2,1)} %param.17, bf16[256,640]{1,0:T(8,128)(2,1)} %param.13), kind=kLoop, calls=%fused_computation.1 | loop fusion | flops 2949120 | bytes 1966080 | tf_op jit(solution)/shard_map/concatenate | solution.py:302
  7.5 0.0 copy-start.4
  7.5 0.0 copy-start.5
  7.5 0.0 copy-start.6
  7.5 1.6 %collective-permute-start.1 = (bf16[256,256]{1,0:T(8,128)(2,1)S(1)}, bf16[256,256]{1,0:T(8,128)(2,1)S(1)}, u32[]{:S(2)}, u32[]{:S(2)}) collective-permute-start(bf16[256,256]{1,0:T(8,128)(2,1)S(1)} %copy-done.7), channel_id=1, source_target_pairs={{0,32},{32,64},{64,96},{96,0},{1,33},{33,65},{65,97},{97,1},{2,34}... | collective-permute-start | bytes 393224 | tf_op jit(solution)/shard_map/ppermute | solution.py:31
  9.2 1.7 %collective-permute-start.3 = (bf16[256,256]{1,0:T(8,128)(2,1)S(1)}, bf16[256,256]{1,0:T(8,128)(2,1)S(1)}, u32[]{:S(2)}, u32[]{:S(2)}) collective-permute-start(bf16[256,256]{1,0:T(8,128)(2,1)S(1)} %copy-done.7), channel_id=1, source_target_pairs={{0,96},{32,0},{64,32},{96,64},{1,97},{33,1},{65,33},{97,65},{2,98}... | collective-permute-start | bytes 393224 | tf_op jit(solution)/shard_map/ppermute | solution.py:31
  10.8 2.0 %collective-permute-start.2 = (bf16[256,256]{1,0:T(8,128)(2,1)S(1)}, bf16[256,256]{1,0:T(8,128)(2,1)S(1)}, u32[]{:S(2)}, u32[]{:S(2)}) collective-permute-start(bf16[256,256]{1,0:T(8,128)(2,1)S(1)} %copy-done.7), channel_id=1, source_target_pairs={{0,64},{32,96},{64,0},{96,32},{1,65},{33,97},{65,1},{97,33},{2,66}... | collective-permute-start | bytes 393224 | tf_op jit(solution)/shard_map/ppermute | solution.py:31
  12.8 0.0 collective-permute-done
  12.8 1.1 %collective-permute-start.7 = (bf16[256,256]{1,0:T(8,128)(2,1)S(1)}, bf16[256,256]{1,0:T(8,128)(2,1)S(1)}, u32[]{:S(2)}, u32[]{:S(2)}) collective-permute-start(bf16[256,256]{1,0:T(8,128)(2,1)S(1)} %collective-permute-done), channel_id=1, source_target_pairs={{0,96},{32,0},{64,32},{96,64},{1,97},{33,1},{65,33},{97,65},{2,98}... | collective-permute-start | bytes 393224 | tf_op jit(solution)/shard_map/ppermute | solution.py:31
  14.0 1.7 %collective-permute-start.6 = (bf16[256,256]{1,0:T(8,128)(2,1)S(1)}, bf16[256,256]{1,0:T(8,128)(2,1)S(1)}, u32[]{:S(2)}, u32[]{:S(2)}) collective-permute-start(bf16[256,256]{1,0:T(8,128)(2,1)S(1)} %collective-permute-done), channel_id=1, source_target_pairs={{0,64},{32,96},{64,0},{96,32},{1,65},{33,97},{65,1},{97,33},{2,66}... | collective-permute-start | bytes 393224 | tf_op jit(solution)/shard_map/ppermute | solution.py:31
  15.7 0.2 collective-permute-start.5
  15.9 3.1 %collective-permute-done.2 = bf16[256,256]{1,0:T(8,128)(2,1)S(1)} collective-permute-done((bf16[256,256]{1,0:T(8,128)(2,1)S(1)}, bf16[256,256]{1,0:T(8,128)(2,1)S(1)}, u32[]{:S(2)}, u32[]{:S(2)}) %collective-permute-start.2) | collective-permute-done | bytes 131104 | tf_op jit(solution)/shard_map/ppermute | solution.py:31
  19.0 0.1 collective-permute-start.4
  19.1 4.3 %collective-permute-done.5 = bf16[256,256]{1,0:T(8,128)(2,1)S(1)} collective-permute-done((bf16[256,256]{1,0:T(8,128)(2,1)S(1)}, bf16[256,256]{1,0:T(8,128)(2,1)S(1)}, u32[]{:S(2)}, u32[]{:S(2)}) %collective-permute-start.5) | collective-permute-done | bytes 131104 | tf_op jit(solution)/shard_map/ppermute | solution.py:31
  23.5 0.0 collective-permute-done.6
  23.5 0.0 collective-permute-done.7
  23.5 0.1 collective-permute-start.8
  23.6 0.8 prep.1
  24.5 0.9 collective-permute-done.8.late_other
  25.3 0.0 slice-start
  25.4 3.6 %attention.1 = (bf16[1280,256]{1,0:T(8,128)(2,1)S(1)}, bf16[1280,256]{1,0:T(8,128)(2,1)S(1)}, bf16[768,256]{1,0:T(8,128)(2,1)S(1)}, bf16[768,256]{1,0:T(8,128)(2,1)S(1)}, bf16[640,256]{1,0:T(8,128)(2,1)S(1)}) custom-call(s32[32,32]{1,0:T(8,128)S(1)} %copy-done.4, s32[1]{0:T(128)} %bitcast.info, s32[32,1,128]{2,1,0:T(1,128)S(1)} %bitcast.7, ...), custom_call_target="tpu_custom_call" | custom-call | flops 2000000000 | bytes 8000000 | tf_op jit(solution)/shard_map/attention/pallas_call | solution.py:197
  28.9 2.2 %collective-permute-start.10 = (bf16[768,256]{1,0:T(8,128)(2,1)S(1)}, bf16[768,256]{1,0:T(8,128)(2,1)S(1)}, u32[]{:S(2)}, u32[]{:S(2)}) collective-permute-start(bf16[768,256]{1,0:T(8,128)(2,1)S(1)} %get-tuple-element.45), channel_id=1, source_target_pairs={{0,8},{8,0},{1,9},{9,1},{2,10},{10,2},{3,11},{11,3},{4,12},{12,4},... | collective-permute-start | bytes 1179656 | tf_op jit(solution)/shard_map/ppermute | solution.py:31
  31.1 0.1 collective-permute-start.9
  31.2 1.3 %collective-permute-done.10 = bf16[768,256]{1,0:T(8,128)(2,1)S(1)} collective-permute-done((bf16[768,256]{1,0:T(8,128)(2,1)S(1)}, bf16[768,256]{1,0:T(8,128)(2,1)S(1)}, u32[]{:S(2)}, u32[]{:S(2)}) %collective-permute-start.10) | collective-permute-done | bytes 393248 | tf_op jit(solution)/shard_map/ppermute | solution.py:31
  32.5 0.1 add_convert_fusion
  32.6 0.8 collective-permute-done.9
  33.4 0.2 fusion
  33.6 0.0 copy-start
  33.6 0.0 copy-start.1
  33.7 2.1 %collective-permute-start.11 = (bf16[256,256]{1,0:T(8,128)(2,1)S(1)}, bf16[256,256]{1,0:T(8,128)(2,1)S(1)}, u32[]{:S(2)}, u32[]{:S(2)}) collective-permute-start(bf16[256,256]{1,0:T(8,128)(2,1)S(1)} %get-tuple-element.48), channel_id=1, source_target_pairs={{0,96},{32,0},{64,32},{96,64},{1,97},{33,1},{65,33},{97,65},{2,98}... | collective-permute-start | bytes 393224 | tf_op jit(solution)/shard_map/ppermute | solution.py:31
  35.8 1.2 %collective-permute-start.12 = (bf16[256,256]{1,0:T(8,128)(2,1)S(1)}, bf16[256,256]{1,0:T(8,128)(2,1)S(1)}, u32[]{:S(2)}, u32[]{:S(2)}) collective-permute-start(bf16[256,256]{1,0:T(8,128)(2,1)S(1)} %get-tuple-element.49), channel_id=1, source_target_pairs={{0,64},{32,96},{64,0},{96,32},{1,65},{33,97},{65,1},{97,33},{2,66}... | collective-permute-start | bytes 393224 | tf_op jit(solution)/shard_map/ppermute | solution.py:31
  37.0 0.0 collective-permute-start.13
  37.0 3.2 %collective-permute-start.15 = (bf16[256,256]{1,0:T(8,128)(2,1)S(1)}, bf16[256,256]{1,0:T(8,128)(2,1)S(1)}, u32[]{:S(2)}, u32[]{:S(2)}) collective-permute-start(bf16[256,256]{1,0:T(8,128)(2,1)S(1)} %get-tuple-element.51), channel_id=1, source_target_pairs={{0,96},{32,0},{64,32},{96,64},{1,97},{33,1},{65,33},{97,65},{2,98}... | collective-permute-start | bytes 393224 | tf_op jit(solution)/shard_map/ppermute | solution.py:31
  40.2 1.1 %collective-permute-start.16 = (bf16[256,256]{1,0:T(8,128)(2,1)S(1)}, bf16[256,256]{1,0:T(8,128)(2,1)S(1)}, u32[]{:S(2)}, u32[]{:S(2)}) collective-permute-start(bf16[256,256]{1,0:T(8,128)(2,1)S(1)} %get-tuple-element.52), channel_id=1, source_target_pairs={{0,64},{32,96},{64,0},{96,32},{1,65},{33,97},{65,1},{97,33},{2,66}... | collective-permute-start | bytes 393224 | tf_op jit(solution)/shard_map/ppermute | solution.py:31
  41.3 0.6 collective-permute-done.11
  42.0 0.0 collective-permute-start.17
  42.0 1.7 %collective-permute-done.12 = bf16[256,256]{1,0:T(8,128)(2,1)S(1)} collective-permute-done((bf16[256,256]{1,0:T(8,128)(2,1)S(1)}, bf16[256,256]{1,0:T(8,128)(2,1)S(1)}, u32[]{:S(2)}, u32[]{:S(2)}) %collective-permute-start.12) | collective-permute-done | bytes 131104 | tf_op jit(solution)/shard_map/ppermute | solution.py:31
  43.6 2.9 %collective-permute-done.13 = bf16[256,256]{1,0:T(8,128)(2,1)S(1)} collective-permute-done((bf16[256,256]{1,0:T(8,128)(2,1)S(1)}, bf16[256,256]{1,0:T(8,128)(2,1)S(1)}, u32[]{:S(2)}, u32[]{:S(2)}) %collective-permute-start.13) | collective-permute-done | bytes 131104 | tf_op jit(solution)/shard_map/ppermute | solution.py:31
  46.6 0.1 add_convert_fusion.1
  46.6 4.3 %collective-permute-start.14 = (bf16[256,256]{1,0:T(8,128)(2,1)S(1)}, bf16[256,256]{1,0:T(8,128)(2,1)S(1)}, u32[]{:S(2)}, u32[]{:S(2)}) collective-permute-start(bf16[256,256]{1,0:T(8,128)(2,1)S(1)} %add_convert_fusion.1), channel_id=1, source_target_pairs={{0,16},{16,0},{1,17},{17,1},{2,18},{18,2},{3,19},{19,3},{4,20},{20... | collective-permute-start | bytes 393224 | tf_op jit(solution)/shard_map/ppermute | solution.py:31
  50.9 0.0 collective-permute-done.15.near1
  51.0 0.2 collective-permute-done.17.near3
  51.2 3.2 %collective-permute-done.14.across = bf16[256,256]{1,0:T(8,128)(2,1)S(1)} collective-permute-done((bf16[256,256]{1,0:T(8,128)(2,1)S(1)}, bf16[256,256]{1,0:T(8,128)(2,1)S(1)}, u32[]{:S(2)}, u32[]{:S(2)}) %collective-permute-start.14) | collective-permute-done | bytes 131104 | tf_op jit(solution)/shard_map/ppermute | solution.py:31
  54.5 4.2 %project.1 = bf16[5120,256]{1,0:T(8,128)(2,1)S(1)} custom-call(f32[256,256]{1,0:T(8,128)S(1)} %get-tuple-element.46.own, bf16[256,256]{1,0:T(8,128)(2,1)S(1)} %collective-permute-done.14.across, bf16[256,256]{1,0:T(8,128)(2,1)S(1)} %collective-permute-done.15.near1, bf16[256,256]{1,0:T(8,128)(2,1)S(1)} %collective-permute-done.16.near2, ...), custom_call_target="tpu_custom_call" | custom-call | flops 2350000128 | bytes 12000000 | tf_op jit(solution)/shard_map/project/pallas_call | solution.py:256
  58.7 36.5 %all_to_all.5.parts = bf16[8,640,256]{2,1,0:T(8,128)(2,1)S(1)} all-to-all(bf16[8,640,256]{2,1,0:T(8,128)(2,1)S(1)} %bitcast.4), channel_id=1, replica_groups=mesh['y'=4,'zh'=2,'core'=2,'x'=4,'zl'=2] {'x','zl'}, dimensions={0} | all-to-all | bytes 5242880 | tf_op jit(solution)/shard_map/all_to_all | solution.py:327
  95.2 1.1 %last_sum.1 = bf16[640,256]{1,0:T(8,128)(2,1)} custom-call(bf16[8,640,256]{2,1,0:T(8,128)(2,1)S(1)} %all_to_all.5.parts), custom_call_target="tpu_custom_call" | custom-call | flops 1300000 | bytes 3000000 | tf_op jit(solution)/shard_map/last_sum/pallas_call | solution.py:283
  (30 shorter events, 0.2 us)
Async XLA Ops:
  2.2 5.3 %copy-start.7 = (bf16[256,256]{1,0:T(8,128)(2,1)S(1)}, bf16[256,256]{1,0:T(8,128)(2,1)}, u32[]{:S(2)}) copy-start(bf16[256,256]{1,0:T(8,128)(2,1)} %get-tuple-element.40) | copy-start | bytes 393220
  2.2 21.4 %copy-start.2 = (f32[256,128]{1,0:T(8,128)S(1)}, f32[256,128]{1,0:T(8,128)}, u32[]{:S(2)}) copy-start(f32[256,128]{1,0:T(8,128)} %get-tuple-element.33.cos) | copy-start | bytes 393220
  2.2 21.4 %copy-start.3 = (f32[256,128]{1,0:T(8,128)S(1)}, f32[256,128]{1,0:T(8,128)}, u32[]{:S(2)}) copy-start(f32[256,128]{1,0:T(8,128)} %get-tuple-element.34.sin) | copy-start | bytes 393220
  2.2 10.6 %collective-permute-start = (bf16[256,256]{1,0:T(8,128)(2,1)}, bf16[256,256]{1,0:T(8,128)(2,1)S(1)}, u32[]{:S(2)}, u32[]{:S(2)}) collective-permute-start(bf16[256,256]{1,0:T(8,128)(2,1)} %get-tuple-element.40), channel_id=1, source_target_pairs={{0,16},{16,0},{1,17},{17,1},{2,18},{18,2},{3,19},{19,3},{4,20},{20... | collective-permute-start | bytes 393224 | tf_op jit(solution)/shard_map/ppermute | solution.py:31
  7.5 17.8 %copy-start.4 = (s32[32,32]{1,0:T(8,128)S(1)}, s32[32,32]{1,0:T(8,128)}, u32[]{:S(2)}) copy-start(s32[32,32]{1,0:T(8,128)} %mask.1) | copy-start | bytes 12292
  7.5 17.8 %copy-start.5 = (s32[4096]{0:T(1024)S(1)}, s32[4096]{0:T(1024)}, u32[]{:S(2)}) copy-start(s32[4096]{0:T(1024)} %param.21) | copy-start | bytes 49156
  7.5 17.8 %copy-start.6 = (f32[5,256]{1,0:T(8,128)S(1)}, f32[5,256]{1,0:T(8,128)}, u32[]{:S(2)}) copy-start(f32[5,256]{1,0:T(8,128)} %lse.1) | copy-start | bytes 15364
  7.5 8.1 %collective-permute-start.1 = (bf16[256,256]{1,0:T(8,128)(2,1)S(1)}, bf16[256,256]{1,0:T(8,128)(2,1)S(1)}, u32[]{:S(2)}, u32[]{:S(2)}) collective-permute-start(bf16[256,256]{1,0:T(8,128)(2,1)S(1)} %copy-done.7), channel_id=1, source_target_pairs={{0,32},{32,64},{64,96},{96,0},{1,33},{33,65},{65,97},{97,1},{2,34}... | collective-permute-start | bytes 393224 | tf_op jit(solution)/shard_map/ppermute | solution.py:31
  9.2 9.8 %collective-permute-start.3 = (bf16[256,256]{1,0:T(8,128)(2,1)S(1)}, bf16[256,256]{1,0:T(8,128)(2,1)S(1)}, u32[]{:S(2)}, u32[]{:S(2)}) collective-permute-start(bf16[256,256]{1,0:T(8,128)(2,1)S(1)} %copy-done.7), channel_id=1, source_target_pairs={{0,96},{32,0},{64,32},{96,64},{1,97},{33,1},{65,33},{97,65},{2,98}... | collective-permute-start | bytes 393224 | tf_op jit(solution)/shard_map/ppermute | solution.py:31
  10.8 8.1 %collective-permute-start.2 = (bf16[256,256]{1,0:T(8,128)(2,1)S(1)}, bf16[256,256]{1,0:T(8,128)(2,1)S(1)}, u32[]{:S(2)}, u32[]{:S(2)}) collective-permute-start(bf16[256,256]{1,0:T(8,128)(2,1)S(1)} %copy-done.7), channel_id=1, source_target_pairs={{0,64},{32,96},{64,0},{96,32},{1,65},{33,97},{65,1},{97,33},{2,66}... | collective-permute-start | bytes 393224 | tf_op jit(solution)/shard_map/ppermute | solution.py:31
  12.8 10.6 %collective-permute-start.7 = (bf16[256,256]{1,0:T(8,128)(2,1)S(1)}, bf16[256,256]{1,0:T(8,128)(2,1)S(1)}, u32[]{:S(2)}, u32[]{:S(2)}) collective-permute-start(bf16[256,256]{1,0:T(8,128)(2,1)S(1)} %collective-permute-done), channel_id=1, source_target_pairs={{0,96},{32,0},{64,32},{96,64},{1,97},{33,1},{65,33},{97,65},{2,98}... | collective-permute-start | bytes 393224 | tf_op jit(solution)/shard_map/ppermute | solution.py:31
  14.0 9.5 %collective-permute-start.6 = (bf16[256,256]{1,0:T(8,128)(2,1)S(1)}, bf16[256,256]{1,0:T(8,128)(2,1)S(1)}, u32[]{:S(2)}, u32[]{:S(2)}) collective-permute-start(bf16[256,256]{1,0:T(8,128)(2,1)S(1)} %collective-permute-done), channel_id=1, source_target_pairs={{0,64},{32,96},{64,0},{96,32},{1,65},{33,97},{65,1},{97,33},{2,66}... | collective-permute-start | bytes 393224 | tf_op jit(solution)/shard_map/ppermute | solution.py:31
  15.7 7.8 %collective-permute-start.5 = (bf16[256,256]{1,0:T(8,128)(2,1)S(1)}, bf16[256,256]{1,0:T(8,128)(2,1)S(1)}, u32[]{:S(2)}, u32[]{:S(2)}) collective-permute-start(bf16[256,256]{1,0:T(8,128)(2,1)S(1)} %collective-permute-done), channel_id=1, source_target_pairs={{0,32},{32,64},{64,96},{96,0},{1,33},{33,65},{65,97},{97,1},{2,34}... | collective-permute-start | bytes 393224 | tf_op jit(solution)/shard_map/ppermute | solution.py:31
  19.0 6.3 %collective-permute-start.4 = (bf16[1280,256]{1,0:T(8,128)(2,1)S(1)}, bf16[1280,256]{1,0:T(8,128)(2,1)S(1)}, u32[]{:S(2)}, u32[]{:S(2)}) collective-permute-start(bf16[1280,256]{1,0:T(8,128)(2,1)S(1)} %constant_dynamic-update-slice_fusion.early_mine), channel_id=1, source_target_pairs={{0,8},{8,0},{1,9},{9,1},{2,10},{10,2},{3,11},{11,3},{4,12},{12,4},... | collective-permute-start | bytes 1966088 | tf_op jit(solution)/shard_map/ppermute | solution.py:31
  23.5 1.8 %collective-permute-start.8 = (bf16[768,256]{1,0:T(8,128)(2,1)S(1)}, bf16[768,256]{1,0:T(8,128)(2,1)S(1)}, u32[]{:S(2)}, u32[]{:S(2)}) collective-permute-start(bf16[768,256]{1,0:T(8,128)(2,1)S(1)} %constant_dynamic-update-slice_fusion.5.late_mine), channel_id=1, source_target_pairs={{0,8},{8,0},{1,9},{9,1},{2,10},{10,2},{3,11},{11,3},{4,12},{12,4},... | collective-permute-start | bytes 1179656 | tf_op jit(solution)/shard_map/ppermute | solution.py:31
  25.3 29.1 %slice-start = ((s8[6553600]{0:T(1024)(128)(4,1)}), s8[4194304]{0:T(1024)(128)(4,1)S(1)}, s32[]{:S(2)}) async-start(s8[6553600]{0:T(1024)(128)(4,1)} %bitcast.5), calls=%async_computation.1 | async-start | bytes 8388608
  28.9 3.5 %collective-permute-start.10 = (bf16[768,256]{1,0:T(8,128)(2,1)S(1)}, bf16[768,256]{1,0:T(8,128)(2,1)S(1)}, u32[]{:S(2)}, u32[]{:S(2)}) collective-permute-start(bf16[768,256]{1,0:T(8,128)(2,1)S(1)} %get-tuple-element.45), channel_id=1, source_target_pairs={{0,8},{8,0},{1,9},{9,1},{2,10},{10,2},{3,11},{11,3},{4,12},{12,4},... | collective-permute-start | bytes 1179656 | tf_op jit(solution)/shard_map/ppermute | solution.py:31
  31.1 2.3 %collective-permute-start.9 = (bf16[1280,256]{1,0:T(8,128)(2,1)S(1)}, bf16[1280,256]{1,0:T(8,128)(2,1)S(1)}, u32[]{:S(2)}, u32[]{:S(2)}) collective-permute-start(bf16[1280,256]{1,0:T(8,128)(2,1)S(1)} %get-tuple-element.43), channel_id=1, source_target_pairs={{0,8},{8,0},{1,9},{9,1},{2,10},{10,2},{3,11},{11,3},{4,12},{12,4},... | collective-permute-start | bytes 1966088 | tf_op jit(solution)/shard_map/ppermute | solution.py:31
  32.5 21.9 %slice-start.1 = ((s8[6553600]{0:T(1024)(128)(4,1)}), s8[2359296]{0:T(1024)(128)(4,1)S(1)}, s32[]{:S(2)}) async-start(s8[6553600]{0:T(1024)(128)(4,1)} %bitcast.5), calls=%async_computation.2 | async-start | bytes 4718592
  33.6 20.8 %copy-start = (bf16[5120,128]{1,0:T(8,128)(2,1)S(1)}, bf16[5120,128]{1,0:T(8,128)(2,1)}, u32[]{:S(2)}) copy-start(bf16[5120,128]{1,0:T(8,128)(2,1)} %wk.1) | copy-start | bytes 3932164
  33.6 20.8 %copy-start.1 = (bf16[5120,128]{1,0:T(8,128)(2,1)S(1)}, bf16[5120,128]{1,0:T(8,128)(2,1)}, u32[]{:S(2)}) copy-start(bf16[5120,128]{1,0:T(8,128)(2,1)} %wv.1) | copy-start | bytes 3932164
  33.7 8.3 %collective-permute-start.11 = (bf16[256,256]{1,0:T(8,128)(2,1)S(1)}, bf16[256,256]{1,0:T(8,128)(2,1)S(1)}, u32[]{:S(2)}, u32[]{:S(2)}) collective-permute-start(bf16[256,256]{1,0:T(8,128)(2,1)S(1)} %get-tuple-element.48), channel_id=1, source_target_pairs={{0,96},{32,0},{64,32},{96,64},{1,97},{33,1},{65,33},{97,65},{2,98}... | collective-permute-start | bytes 393224 | tf_op jit(solution)/shard_map/ppermute | solution.py:31
  35.8 7.9 %collective-permute-start.12 = (bf16[256,256]{1,0:T(8,128)(2,1)S(1)}, bf16[256,256]{1,0:T(8,128)(2,1)S(1)}, u32[]{:S(2)}, u32[]{:S(2)}) collective-permute-start(bf16[256,256]{1,0:T(8,128)(2,1)S(1)} %get-tuple-element.49), channel_id=1, source_target_pairs={{0,64},{32,96},{64,0},{96,32},{1,65},{33,97},{65,1},{97,33},{2,66}... | collective-permute-start | bytes 393224 | tf_op jit(solution)/shard_map/ppermute | solution.py:31
  37.0 9.6 %collective-permute-start.13 = (bf16[256,256]{1,0:T(8,128)(2,1)S(1)}, bf16[256,256]{1,0:T(8,128)(2,1)S(1)}, u32[]{:S(2)}, u32[]{:S(2)}) collective-permute-start(bf16[256,256]{1,0:T(8,128)(2,1)S(1)} %get-tuple-element.50), channel_id=1, source_target_pairs={{0,32},{32,64},{64,96},{96,0},{1,33},{33,65},{65,97},{97,1},{2,34}... | collective-permute-start | bytes 393224 | tf_op jit(solution)/shard_map/ppermute | solution.py:31
  37.0 14.0 %collective-permute-start.15 = (bf16[256,256]{1,0:T(8,128)(2,1)S(1)}, bf16[256,256]{1,0:T(8,128)(2,1)S(1)}, u32[]{:S(2)}, u32[]{:S(2)}) collective-permute-start(bf16[256,256]{1,0:T(8,128)(2,1)S(1)} %get-tuple-element.51), channel_id=1, source_target_pairs={{0,96},{32,0},{64,32},{96,64},{1,97},{33,1},{65,33},{97,65},{2,98}... | collective-permute-start | bytes 393224 | tf_op jit(solution)/shard_map/ppermute | solution.py:31
  40.2 10.7 %collective-permute-start.16 = (bf16[256,256]{1,0:T(8,128)(2,1)S(1)}, bf16[256,256]{1,0:T(8,128)(2,1)S(1)}, u32[]{:S(2)}, u32[]{:S(2)}) collective-permute-start(bf16[256,256]{1,0:T(8,128)(2,1)S(1)} %get-tuple-element.52), channel_id=1, source_target_pairs={{0,64},{32,96},{64,0},{96,32},{1,65},{33,97},{65,1},{97,33},{2,66}... | collective-permute-start | bytes 393224 | tf_op jit(solution)/shard_map/ppermute | solution.py:31
  42.0 9.2 %collective-permute-start.17 = (bf16[256,256]{1,0:T(8,128)(2,1)S(1)}, bf16[256,256]{1,0:T(8,128)(2,1)S(1)}, u32[]{:S(2)}, u32[]{:S(2)}) collective-permute-start(bf16[256,256]{1,0:T(8,128)(2,1)S(1)} %get-tuple-element.53), channel_id=1, source_target_pairs={{0,32},{32,64},{64,96},{96,0},{1,33},{33,65},{65,97},{97,1},{2,34}... | collective-permute-start | bytes 393224 | tf_op jit(solution)/shard_map/ppermute | solution.py:31
  46.6 7.8 %collective-permute-start.14 = (bf16[256,256]{1,0:T(8,128)(2,1)S(1)}, bf16[256,256]{1,0:T(8,128)(2,1)S(1)}, u32[]{:S(2)}, u32[]{:S(2)}) collective-permute-start(bf16[256,256]{1,0:T(8,128)(2,1)S(1)} %add_convert_fusion.1), channel_id=1, source_target_pairs={{0,16},{16,0},{1,17},{17,1},{2,18},{18,2},{3,19},{19,3},{4,20},{20... | collective-permute-start | bytes 393224 | tf_op jit(solution)/shard_map/ppermute | solution.py:31

commit v6 on v5

--- a/solution.py
+++ b/solution.py
@@ -14,6 +14,7 @@
 ROWS = GROUPS * TILE
 SCALE = HEAD**-0.5
 ROPE_BASE = 1000000.0
+LOG2E = 1.4426950408889634
 CTX = ("y", "zh", "core")
 TP = ("x", "zl")
 
@@ -89,74 +90,137 @@
 def attention_kernel(
     mask, info, seg, lse, delta, cos, sin, q_rows, q_cols, g_rows, g_cols,
     early_mine, early_other, late_mine, late_other,
-    d_early_mine, d_early_other, d_late_mine, d_late_other, qg, acc, dq, lse_rows,
+    d_early_mine, d_early_other, d_late_mine, d_late_other, qg,
+    kv, dkv, dq, lse_rows, lists, counts, flags,
 ):
     dq[...] = jnp.zeros_like(dq)
     for t in range(2):
         for h in range(GROUPS):
-            lse_rows[t, :, pl.ds(h * TILE, TILE)] = lse[h : h + 1, t * TILE : (t + 1) * TILE]
+            row = lse[h : h + 1, t * TILE : (t + 1) * TILE]
+            lse_rows[t, :, pl.ds(h * TILE, TILE)] = row * LOG2E
     me = info[0]
     q_tile = 2 * me
-
-    def pair(t, keys, vals, allowed):
-        keys_t = keys.T
+    groups = (
+        (early_mine, d_early_mine, 0, 0, EARLY),
+        (early_other, d_early_other, 1, 0, EARLY),
+        (late_mine, d_late_mine, 0, EARLY, 8 - EARLY),
+        (late_other, d_late_other, 1, EARLY, 8 - EARLY),
+    )
+    starts = (0, 2 * EARLY, 4 * EARLY, 4 * EARLY + 2 * (8 - EARLY))
+
+    def needs(j, away, first_slot):
+        slot = lax.shift_right_logical(j, 1) + first_slot
+        back_y = (lax.shift_right_logical(me, 2) - slot) & 3
+        back_zh = (me ^ (lax.shift_right_logical(slot, 1) & 2)) & 2
+        tile = 2 * (4 * back_y + back_zh + ((me ^ away) & 1)) + (j & 1)
+        return mask[q_tile, tile] > 0, mask[q_tile + 1, tile] > 0
+
+    for t in range(2):
+        lists[t, 0] = t
+        counts[t] = 1
+    kv[pl.ds(TILES * TILE, TILE), :] = jnp.zeros((TILE, 2 * HEAD), bf16)
+    dkv[pl.ds(TILES * TILE, TILE), :] = jnp.zeros((TILE, 2 * HEAD), f32)
+    for (source, dest, away, first_slot, slots), start in zip(groups, starts):
+
+        def collect(j, carry):
+            needed = needs(j, away, first_slot)
+            flags[start + j] = jnp.where(needed[0] | needed[1], 1, 0)
+            here = pl.ds(pl.multiple_of(j * TILE, TILE), TILE)
+            there = pl.ds(pl.multiple_of((start + j) * TILE, TILE), TILE)
+
+            @pl.when(needed[0] | needed[1])
+            def _():
+                kv[there, :] = source[here, :]
+                dkv[there, :] = jnp.zeros((TILE, 2 * HEAD), f32)
+
+            @pl.when(jnp.logical_not(needed[0] | needed[1]))
+            def _():
+                dest[here, :] = jnp.zeros((TILE, 2 * HEAD), bf16)
+
+            for t in range(2):
+                add = needed[t]
+                if start == 0:
+                    add = add & (j != t)
+
+                @pl.when(add)
+                def _():
+                    count = counts[t]
+                    lists[t, count] = start + j
+                    counts[t] = count + 1
+
+            return carry
+
+        lax.fori_loop(0, 2 * slots, collect, 0)
+
+    def two_tiles(t, first, second, allowed):
+        ones = pl.ds(pl.multiple_of(first * TILE, TILE), TILE)
+        twos = pl.ds(pl.multiple_of(second * TILE, TILE), TILE)
+        keys = jnp.concatenate([kv[ones, :HEAD], kv[twos, :HEAD]], 0)
+        vals = jnp.concatenate([kv[ones, HEAD:], kv[twos, HEAD:]], 0)
         scores = jnp.dot(keys, q_cols[t], preferred_element_type=f32)
-        probs = jnp.exp(scores * SCALE - lse_rows[t])
+        probs = jnp.exp2(scores * (SCALE * LOG2E) - lse_rows[t])
         if allowed is not None:
-            probs = jnp.where(allowed, probs, 0.0)
+            probs = jnp.concatenate([jnp.where(allowed, probs[:TILE], 0.0), probs[TILE:]], 0)
         dprobs = jnp.dot(vals, g_cols[t], preferred_element_type=f32)
         dscore = (probs * (dprobs - delta[t])).astype(bf16)
         probs = probs.astype(bf16)
-        dq[t] += jnp.dot(keys_t, dscore, preferred_element_type=f32)
-        acc[:, :HEAD] += jnp.dot(dscore, q_rows[t], preferred_element_type=f32)
-        acc[:, HEAD:] += jnp.dot(probs, g_rows[t], preferred_element_type=f32)
-
-    def tiles_of(kv, dkv, away, first_slot, slots):
-        def step(j, carry):
-            slot = lax.shift_right_logical(j, 1) + first_slot
-            back_y = (lax.shift_right_logical(me, 2) - slot) & 3
-            back_zh = (me ^ (lax.shift_right_logical(slot, 1) & 2)) & 2
-            tile = 2 * (4 * back_y + back_zh + ((me ^ away) & 1)) + (j & 1)
-            need0 = mask[q_tile, tile] > 0
-            need1 = mask[q_tile + 1, tile] > 0
-            here = pl.ds(pl.multiple_of(j * TILE, TILE), TILE)
-
-            @pl.when(need0 | need1)
+        dkeys = jnp.dot(dscore, q_rows[t], preferred_element_type=f32)
+        dvals = jnp.dot(probs, g_rows[t], preferred_element_type=f32)
+        dqs = jnp.dot(keys.T, dscore, preferred_element_type=f32)
+        return t, ones, twos, dkeys, dvals, dqs
+
+    def add(t, ones, twos, dkeys, dvals, dqs):
+        dq[t] += dqs
+        dkv[ones, :HEAD] += dkeys[:TILE]
+        dkv[ones, HEAD:] += dvals[:TILE]
+        dkv[twos, :HEAD] += dkeys[TILE:]
+        dkv[twos, HEAD:] += dvals[TILE:]
+
+    most = jnp.maximum(counts[0], counts[1])
+
+    def fill(i, carry):
+        for t in range(2):
+
+            @pl.when(i >= counts[t])
             def _():
-                acc[...] = jnp.zeros_like(acc)
-                keys, vals = kv[here, :HEAD], kv[here, HEAD:]
-                for t, need in ((0, need0), (1, need1)):
-                    diagonal = need & (tile == q_tile + t)
-
-                    @pl.when(need & jnp.logical_not(diagonal))
-                    def _():
-                        pair(t, keys, vals, None)
-
-                    if away == 0 and first_slot == 0:
-
-                        @pl.when(diagonal)
-                        def _():
-                            row = jnp.broadcast_to(seg[tile], (TILE, TILE)).astype(f32)
-                            causal = lax.broadcasted_iota(jnp.int32, (TILE, TILE), 0) <= (
-                                lax.broadcasted_iota(jnp.int32, (TILE, TILE), 1)
-                            )
-                            one = jnp.where((row.T == row) & causal, 1.0, 0.0)
-                            pair(t, keys, vals, jnp.concatenate([one] * GROUPS, 1) > 0.5)
-
-                dkv[here, :] = acc[...].astype(bf16)
-
-            @pl.when(jnp.logical_not(need0 | need1))
+                lists[t, i] = TILES
+
+        return carry
+
+    lax.fori_loop(jnp.minimum(counts[0], counts[1]), most + 1, fill, 0)
+    causal = lax.broadcasted_iota(jnp.int32, (TILE, TILE), 0) <= (
+        lax.broadcasted_iota(jnp.int32, (TILE, TILE), 1)
+    )
+    terms = []
+    for t in range(2):
+        row = jnp.broadcast_to(seg[q_tile + t], (TILE, TILE)).astype(f32)
+        listed = jnp.where(mask[q_tile + t, q_tile + t] > 0, 1.0, 0.0)
+        one = jnp.where((row.T == row) & causal, 1.0, 0.0) * listed
+        terms.append(two_tiles(t, t, lists[t, 1], jnp.concatenate([one] * GROUPS, 1) > 0.5))
+    for term in terms:
+        add(*term)
+
+    def rest(i, carry):
+        terms = [two_tiles(t, lists[t, 2 * i], lists[t, 2 * i + 1], None) for t in range(2)]
+        for term in terms:
+            add(*term)
+        return carry
+
+    lax.fori_loop(1, lax.shift_right_logical(most + 1, 1), rest, 0)
+
+    for (source, dest, away, first_slot, slots), start in zip(groups, starts):
+
+        def give(j, carry):
+            @pl.when(flags[start + j] > 0)
             def _():
-                dkv[here, :] = jnp.zeros((TILE, 2 * HEAD), bf16)
+                here = pl.ds(pl.multiple_of(j * TILE, TILE), TILE)
+                there = pl.ds(pl.multiple_of((start + j) * TILE, TILE), TILE)
+                dest[here, :] = dkv[there, :].astype(bf16)
 
             return carry
 
-        lax.fori_loop(0, 2 * slots, step, 0)
-
-    tiles_of(early_mine, d_early_mine, 0, 0, EARLY)
-    tiles_of(early_other, d_early_other, 1, 0, EARLY)
-    tiles_of(late_mine, d_late_mine, 0, EARLY, 8 - EARLY)
-    tiles_of(late_other, d_late_other, 1, EARLY, 8 - EARLY)
+        lax.fori_loop(0, 2 * slots, give, 0)
+
     for t in range(2):
         tok = pl.ds(t * TILE, TILE)
         c, s = cos[tok, :].T, sin[tok, :].T
@@ -200,9 +264,13 @@
         in_specs=[pl.BlockSpec(memory_space=pltpu.SMEM)] * 2 + vmem(len(operands)),
         out_specs=tuple(vmem(5)),
         scratch_shapes=[
-            pltpu.VMEM((TILE, 2 * HEAD), f32),
+            pltpu.VMEM(((TILES + 1) * TILE, 2 * HEAD), bf16),
+            pltpu.VMEM(((TILES + 1) * TILE, 2 * HEAD), f32),
             pltpu.VMEM((2, HEAD, ROWS), f32),
             pltpu.VMEM((2, 1, ROWS), f32),
+            pltpu.SMEM((2, TILES + 1), jnp.int32),
+            pltpu.SMEM((2,), jnp.int32),
+            pltpu.SMEM((TILES,), jnp.int32),
         ],
         compiler_params=pltpu.CompilerParams(vmem_limit_bytes=16 << 20),
         cost_estimate=pl.CostEstimate(

time: 96.6 us -> 94.1 us (0.974)
  starting transfers between devices: 26.8 us -> 24 us
    ppermute x18, starting transfers between devices: 26.8 us -> 24 us  [shift(): return lax.ppermute(x, axes, perm)]
  transfers between devices with their start and end apart: 18 -> 18, of which waited for: 10 -> 11; matrix products, arithmetic and copies ran while one was open for 2% -> 2% of each run, Pallas kernels for 1% -> 1%
where the time goes in v6:
time: 94.1 us; the launch traced here: 93.9 us
  blocking collectives  35.9 us (38%)
  starting transfers between devices  24 us (26%)
  waiting for transfers between devices  19.8 us (21%)
  Pallas kernels  12 us (13%)
  other arithmetic  1.62 us (2%)
    all_to_all x1, blocking collectives, local(): return last_sum(lax.all_to_all(send.reshape(8, 640, TOK), TP, 0, 0))  35.9 us
    ppermute x18, starting transfers between devices, shift(): return lax.ppermute(x, axes, perm)  24 us
    ppermute x18, waiting for transfers between devices, shift(): return lax.ppermute(x, axes, perm)  19.8 us
    pallas_call x1, Pallas kernels, project(): pl.pallas_call(project_kernel, out_shape=jax.ShapeDtypeStruct((WIDTH, TOK...  4.24 us
    pallas_call x1, Pallas kernels, attention(): pl.pallas_call(attention_kernel, out_shape=(early, early, late, late, s((...  3.72 us
    pallas_call x1, Pallas kernels, make_block(): pl.pallas_call(block_kernel, out_shape=(s((TOK, HEAD), f32), s((TOK, HEAD...  2.18 us
  transfers between devices with their start and end apart: 18, of which 11 were waited for; matrix products, arithmetic and copies ran while one was open for 2% of the time, Pallas kernels for 1%

profile of v6, /device:TPU:0, one launch (start us, length us, event | category | flops | bytes accessed | tf_op | source)
XLA Modules:
  0.0 93.9 jit_solution(17440266444300389670)
XLA Ops:
  0.0 2.2 %block.1 = (f32[256,128]{1,0:T(8,128)}, f32[256,128]{1,0:T(8,128)}, bf16[256,256]{1,0:T(8,128)(2,1)}) custom-call(bf16[256,128]{1,0:T(8,128)(2,1)} %key.1, bf16[256,128]{1,0:T(8,128)(2,1)} %value.1, s32[2,1,128]{2,1,0:T(1,128)} %bitcast.8, f32[1,128]{1,0:T(1,128)} %constant.21.clone.inverse), custom_call_target="tpu_custom_call" | custom-call | flops 5000000 | bytes 700000 | tf_op jit(solution)/shard_map/block/pallas_call | solution.py:286
  2.2 4.0 %collective-permute-start = (bf16[256,256]{1,0:T(8,128)(2,1)}, bf16[256,256]{1,0:T(8,128)(2,1)S(1)}, u32[]{:S(2)}, u32[]{:S(2)}) collective-permute-start(bf16[256,256]{1,0:T(8,128)(2,1)} %get-tuple-element.40), channel_id=1, source_target_pairs={{0,16},{16,0},{1,17},{17,1},{2,18},{18,2},{3,19},{19,3},{4,20},{20... | collective-permute-start | bytes 393224 | tf_op jit(solution)/shard_map/ppermute | solution.py:32
  6.2 1.2 %pad_maximum_fusion.joined = bf16[256,1920]{1,0:T(8,128)(2,1)S(1)} fusion(bf16[256,640]{1,0:T(8,128)(2,1)} %param.16, bf16[256,640]{1,0:T(8,128)(2,1)} %param.17, bf16[256,640]{1,0:T(8,128)(2,1)} %param.13), kind=kLoop, calls=%fused_computation.1 | loop fusion | flops 2949120 | bytes 1966080 | tf_op jit(solution)/shard_map/concatenate | solution.py:370
  7.5 0.0 copy-start.4
  7.5 0.0 copy-start.5
  7.5 0.0 copy-start.6
  7.5 1.6 %collective-permute-start.1 = (bf16[256,256]{1,0:T(8,128)(2,1)S(1)}, bf16[256,256]{1,0:T(8,128)(2,1)S(1)}, u32[]{:S(2)}, u32[]{:S(2)}) collective-permute-start(bf16[256,256]{1,0:T(8,128)(2,1)S(1)} %copy-done.7), channel_id=1, source_target_pairs={{0,32},{32,64},{64,96},{96,0},{1,33},{33,65},{65,97},{97,1},{2,34}... | collective-permute-start | bytes 393224 | tf_op jit(solution)/shard_map/ppermute | solution.py:32
  9.2 1.7 %collective-permute-start.3 = (bf16[256,256]{1,0:T(8,128)(2,1)S(1)}, bf16[256,256]{1,0:T(8,128)(2,1)S(1)}, u32[]{:S(2)}, u32[]{:S(2)}) collective-permute-start(bf16[256,256]{1,0:T(8,128)(2,1)S(1)} %copy-done.7), channel_id=1, source_target_pairs={{0,96},{32,0},{64,32},{96,64},{1,97},{33,1},{65,33},{97,65},{2,98}... | collective-permute-start | bytes 393224 | tf_op jit(solution)/shard_map/ppermute | solution.py:32
  10.8 2.0 %collective-permute-start.2 = (bf16[256,256]{1,0:T(8,128)(2,1)S(1)}, bf16[256,256]{1,0:T(8,128)(2,1)S(1)}, u32[]{:S(2)}, u32[]{:S(2)}) collective-permute-start(bf16[256,256]{1,0:T(8,128)(2,1)S(1)} %copy-done.7), channel_id=1, source_target_pairs={{0,64},{32,96},{64,0},{96,32},{1,65},{33,97},{65,1},{97,33},{2,66}... | collective-permute-start | bytes 393224 | tf_op jit(solution)/shard_map/ppermute | solution.py:32
  12.8 0.0 collective-permute-done
  12.8 1.1 %collective-permute-start.7 = (bf16[256,256]{1,0:T(8,128)(2,1)S(1)}, bf16[256,256]{1,0:T(8,128)(2,1)S(1)}, u32[]{:S(2)}, u32[]{:S(2)}) collective-permute-start(bf16[256,256]{1,0:T(8,128)(2,1)S(1)} %collective-permute-done), channel_id=1, source_target_pairs={{0,96},{32,0},{64,32},{96,64},{1,97},{33,1},{65,33},{97,65},{2,98}... | collective-permute-start | bytes 393224 | tf_op jit(solution)/shard_map/ppermute | solution.py:32
  14.0 1.7 %collective-permute-start.6 = (bf16[256,256]{1,0:T(8,128)(2,1)S(1)}, bf16[256,256]{1,0:T(8,128)(2,1)S(1)}, u32[]{:S(2)}, u32[]{:S(2)}) collective-permute-start(bf16[256,256]{1,0:T(8,128)(2,1)S(1)} %collective-permute-done), channel_id=1, source_target_pairs={{0,64},{32,96},{64,0},{96,32},{1,65},{33,97},{65,1},{97,33},{2,66}... | collective-permute-start | bytes 393224 | tf_op jit(solution)/shard_map/ppermute | solution.py:32
  15.7 0.2 collective-permute-start.5
  15.9 3.1 %collective-permute-done.2 = bf16[256,256]{1,0:T(8,128)(2,1)S(1)} collective-permute-done((bf16[256,256]{1,0:T(8,128)(2,1)S(1)}, bf16[256,256]{1,0:T(8,128)(2,1)S(1)}, u32[]{:S(2)}, u32[]{:S(2)}) %collective-permute-start.2) | collective-permute-done | bytes 131104 | tf_op jit(solution)/shard_map/ppermute | solution.py:32
  19.0 0.1 collective-permute-start.4
  19.1 4.3 %collective-permute-done.5 = bf16[256,256]{1,0:T(8,128)(2,1)S(1)} collective-permute-done((bf16[256,256]{1,0:T(8,128)(2,1)S(1)}, bf16[256,256]{1,0:T(8,128)(2,1)S(1)}, u32[]{:S(2)}, u32[]{:S(2)}) %collective-permute-start.5) | collective-permute-done | bytes 131104 | tf_op jit(solution)/shard_map/ppermute | solution.py:32
  23.5 0.0 collective-permute-done.6
  23.5 0.0 collective-permute-done.7
  23.5 0.1 collective-permute-start.8
  23.6 0.8 prep.1
  24.5 0.9 collective-permute-done.8.late_other
  25.3 0.0 slice-start
  25.4 3.7 %attention.1 = (bf16[1280,256]{1,0:T(8,128)(2,1)S(1)}, bf16[1280,256]{1,0:T(8,128)(2,1)S(1)}, bf16[768,256]{1,0:T(8,128)(2,1)S(1)}, bf16[768,256]{1,0:T(8,128)(2,1)S(1)}, bf16[640,256]{1,0:T(8,128)(2,1)S(1)}) custom-call(s32[32,32]{1,0:T(8,128)S(1)} %copy-done.4, s32[1]{0:T(128)} %bitcast.info, s32[32,1,128]{2,1,0:T(1,128)S(1)} %bitcast.7, ...), custom_call_target="tpu_custom_call" | custom-call | flops 2000000000 | bytes 8000000 | tf_op jit(solution)/shard_map/attention/pallas_call | solution.py:261
  29.1 1.3 %collective-permute-start.10 = (bf16[768,256]{1,0:T(8,128)(2,1)S(1)}, bf16[768,256]{1,0:T(8,128)(2,1)S(1)}, u32[]{:S(2)}, u32[]{:S(2)}) collective-permute-start(bf16[768,256]{1,0:T(8,128)(2,1)S(1)} %get-tuple-element.45), channel_id=1, source_target_pairs={{0,8},{8,0},{1,9},{9,1},{2,10},{10,2},{3,11},{11,3},{4,12},{12,4},... | collective-permute-start | bytes 1179656 | tf_op jit(solution)/shard_map/ppermute | solution.py:32
  30.4 0.1 collective-permute-start.9
  30.5 1.3 %collective-permute-done.10 = bf16[768,256]{1,0:T(8,128)(2,1)S(1)} collective-permute-done((bf16[768,256]{1,0:T(8,128)(2,1)S(1)}, bf16[768,256]{1,0:T(8,128)(2,1)S(1)}, u32[]{:S(2)}, u32[]{:S(2)}) %collective-permute-start.10) | collective-permute-done | bytes 393248 | tf_op jit(solution)/shard_map/ppermute | solution.py:32
  31.7 0.1 add_convert_fusion
  31.9 0.8 collective-permute-done.9
  32.7 0.2 fusion
  32.9 0.0 copy-start
  32.9 0.0 copy-start.1
  33.0 2.1 %collective-permute-start.11 = (bf16[256,256]{1,0:T(8,128)(2,1)S(1)}, bf16[256,256]{1,0:T(8,128)(2,1)S(1)}, u32[]{:S(2)}, u32[]{:S(2)}) collective-permute-start(bf16[256,256]{1,0:T(8,128)(2,1)S(1)} %get-tuple-element.48), channel_id=1, source_target_pairs={{0,96},{32,0},{64,32},{96,64},{1,97},{33,1},{65,33},{97,65},{2,98}... | collective-permute-start | bytes 393224 | tf_op jit(solution)/shard_map/ppermute | solution.py:32
  35.0 1.2 %collective-permute-start.12 = (bf16[256,256]{1,0:T(8,128)(2,1)S(1)}, bf16[256,256]{1,0:T(8,128)(2,1)S(1)}, u32[]{:S(2)}, u32[]{:S(2)}) collective-permute-start(bf16[256,256]{1,0:T(8,128)(2,1)S(1)} %get-tuple-element.49), channel_id=1, source_target_pairs={{0,64},{32,96},{64,0},{96,32},{1,65},{33,97},{65,1},{97,33},{2,66}... | collective-permute-start | bytes 393224 | tf_op jit(solution)/shard_map/ppermute | solution.py:32
  36.2 0.0 collective-permute-start.13
  36.2 3.2 %collective-permute-start.15 = (bf16[256,256]{1,0:T(8,128)(2,1)S(1)}, bf16[256,256]{1,0:T(8,128)(2,1)S(1)}, u32[]{:S(2)}, u32[]{:S(2)}) collective-permute-start(bf16[256,256]{1,0:T(8,128)(2,1)S(1)} %get-tuple-element.51), channel_id=1, source_target_pairs={{0,96},{32,0},{64,32},{96,64},{1,97},{33,1},{65,33},{97,65},{2,98}... | collective-permute-start | bytes 393224 | tf_op jit(solution)/shard_map/ppermute | solution.py:32
  39.5 1.1 %collective-permute-start.16 = (bf16[256,256]{1,0:T(8,128)(2,1)S(1)}, bf16[256,256]{1,0:T(8,128)(2,1)S(1)}, u32[]{:S(2)}, u32[]{:S(2)}) collective-permute-start(bf16[256,256]{1,0:T(8,128)(2,1)S(1)} %get-tuple-element.52), channel_id=1, source_target_pairs={{0,64},{32,96},{64,0},{96,32},{1,65},{33,97},{65,1},{97,33},{2,66}... | collective-permute-start | bytes 393224 | tf_op jit(solution)/shard_map/ppermute | solution.py:32
  40.6 0.6 collective-permute-done.11
  41.2 0.0 collective-permute-start.17
  41.2 1.7 %collective-permute-done.12 = bf16[256,256]{1,0:T(8,128)(2,1)S(1)} collective-permute-done((bf16[256,256]{1,0:T(8,128)(2,1)S(1)}, bf16[256,256]{1,0:T(8,128)(2,1)S(1)}, u32[]{:S(2)}, u32[]{:S(2)}) %collective-permute-start.12) | collective-permute-done | bytes 131104 | tf_op jit(solution)/shard_map/ppermute | solution.py:32
  42.9 2.9 %collective-permute-done.13 = bf16[256,256]{1,0:T(8,128)(2,1)S(1)} collective-permute-done((bf16[256,256]{1,0:T(8,128)(2,1)S(1)}, bf16[256,256]{1,0:T(8,128)(2,1)S(1)}, u32[]{:S(2)}, u32[]{:S(2)}) %collective-permute-start.13) | collective-permute-done | bytes 131104 | tf_op jit(solution)/shard_map/ppermute | solution.py:32
  45.8 0.1 add_convert_fusion.1
  45.8 2.5 %collective-permute-start.14 = (bf16[256,256]{1,0:T(8,128)(2,1)S(1)}, bf16[256,256]{1,0:T(8,128)(2,1)S(1)}, u32[]{:S(2)}, u32[]{:S(2)}) collective-permute-start(bf16[256,256]{1,0:T(8,128)(2,1)S(1)} %add_convert_fusion.1), channel_id=1, source_target_pairs={{0,16},{16,0},{1,17},{17,1},{2,18},{18,2},{3,19},{19,3},{4,20},{20... | collective-permute-start | bytes 393224 | tf_op jit(solution)/shard_map/ppermute | solution.py:32
  48.3 0.2 collective-permute-done.16.near2
  48.5 1.9 %collective-permute-done.17.near3 = bf16[256,256]{1,0:T(8,128)(2,1)S(1)} collective-permute-done((bf16[256,256]{1,0:T(8,128)(2,1)S(1)}, bf16[256,256]{1,0:T(8,128)(2,1)S(1)}, u32[]{:S(2)}, u32[]{:S(2)}) %collective-permute-start.17) | collective-permute-done | bytes 131104 | tf_op jit(solution)/shard_map/ppermute | solution.py:32
  50.4 2.2 %collective-permute-done.14.across = bf16[256,256]{1,0:T(8,128)(2,1)S(1)} collective-permute-done((bf16[256,256]{1,0:T(8,128)(2,1)S(1)}, bf16[256,256]{1,0:T(8,128)(2,1)S(1)}, u32[]{:S(2)}, u32[]{:S(2)}) %collective-permute-start.14) | collective-permute-done | bytes 131104 | tf_op jit(solution)/shard_map/ppermute | solution.py:32
  52.7 4.2 %project.1 = bf16[5120,256]{1,0:T(8,128)(2,1)S(1)} custom-call(f32[256,256]{1,0:T(8,128)S(1)} %get-tuple-element.46.own, bf16[256,256]{1,0:T(8,128)(2,1)S(1)} %collective-permute-done.14.across, bf16[256,256]{1,0:T(8,128)(2,1)S(1)} %collective-permute-done.15.near1, bf16[256,256]{1,0:T(8,128)(2,1)S(1)} %collective-permute-done.16.near2, ...), custom_call_target="tpu_custom_call" | custom-call | flops 2350000128 | bytes 12000000 | tf_op jit(solution)/shard_map/project/pallas_call | solution.py:324
  56.9 35.9 %all_to_all.5.parts = bf16[8,640,256]{2,1,0:T(8,128)(2,1)S(1)} all-to-all(bf16[8,640,256]{2,1,0:T(8,128)(2,1)S(1)} %bitcast.4), channel_id=1, replica_groups=mesh['y'=4,'zh'=2,'core'=2,'x'=4,'zl'=2] {'x','zl'}, dimensions={0} | all-to-all | bytes 5242880 | tf_op jit(solution)/shard_map/all_to_all | solution.py:395
  92.8 1.1 %last_sum.1 = bf16[640,256]{1,0:T(8,128)(2,1)} custom-call(bf16[8,640,256]{2,1,0:T(8,128)(2,1)S(1)} %all_to_all.5.parts), custom_call_target="tpu_custom_call" | custom-call | flops 1300000 | bytes 3000000 | tf_op jit(solution)/shard_map/last_sum/pallas_call | solution.py:351
  (30 shorter events, 0.2 us)
Async XLA Ops:
  2.2 5.3 %copy-start.7 = (bf16[256,256]{1,0:T(8,128)(2,1)S(1)}, bf16[256,256]{1,0:T(8,128)(2,1)}, u32[]{:S(2)}) copy-start(bf16[256,256]{1,0:T(8,128)(2,1)} %get-tuple-element.40) | copy-start | bytes 393220
  2.2 21.4 %copy-start.2 = (f32[256,128]{1,0:T(8,128)S(1)}, f32[256,128]{1,0:T(8,128)}, u32[]{:S(2)}) copy-start(f32[256,128]{1,0:T(8,128)} %get-tuple-element.33.cos) | copy-start | bytes 393220
  2.2 21.4 %copy-start.3 = (f32[256,128]{1,0:T(8,128)S(1)}, f32[256,128]{1,0:T(8,128)}, u32[]{:S(2)}) copy-start(f32[256,128]{1,0:T(8,128)} %get-tuple-element.34.sin) | copy-start | bytes 393220
  2.2 10.6 %collective-permute-start = (bf16[256,256]{1,0:T(8,128)(2,1)}, bf16[256,256]{1,0:T(8,128)(2,1)S(1)}, u32[]{:S(2)}, u32[]{:S(2)}) collective-permute-start(bf16[256,256]{1,0:T(8,128)(2,1)} %get-tuple-element.40), channel_id=1, source_target_pairs={{0,16},{16,0},{1,17},{17,1},{2,18},{18,2},{3,19},{19,3},{4,20},{20... | collective-permute-start | bytes 393224 | tf_op jit(solution)/shard_map/ppermute | solution.py:32
  7.5 17.8 %copy-start.4 = (s32[32,32]{1,0:T(8,128)S(1)}, s32[32,32]{1,0:T(8,128)}, u32[]{:S(2)}) copy-start(s32[32,32]{1,0:T(8,128)} %mask.1) | copy-start | bytes 12292
  7.5 17.8 %copy-start.5 = (s32[4096]{0:T(1024)S(1)}, s32[4096]{0:T(1024)}, u32[]{:S(2)}) copy-start(s32[4096]{0:T(1024)} %param.21) | copy-start | bytes 49156
  7.5 17.8 %copy-start.6 = (f32[5,256]{1,0:T(8,128)S(1)}, f32[5,256]{1,0:T(8,128)}, u32[]{:S(2)}) copy-start(f32[5,256]{1,0:T(8,128)} %lse.1) | copy-start | bytes 15364
  7.5 8.1 %collective-permute-start.1 = (bf16[256,256]{1,0:T(8,128)(2,1)S(1)}, bf16[256,256]{1,0:T(8,128)(2,1)S(1)}, u32[]{:S(2)}, u32[]{:S(2)}) collective-permute-start(bf16[256,256]{1,0:T(8,128)(2,1)S(1)} %copy-done.7), channel_id=1, source_target_pairs={{0,32},{32,64},{64,96},{96,0},{1,33},{33,65},{65,97},{97,1},{2,34}... | collective-permute-start | bytes 393224 | tf_op jit(solution)/shard_map/ppermute | solution.py:32
  9.2 9.8 %collective-permute-start.3 = (bf16[256,256]{1,0:T(8,128)(2,1)S(1)}, bf16[256,256]{1,0:T(8,128)(2,1)S(1)}, u32[]{:S(2)}, u32[]{:S(2)}) collective-permute-start(bf16[256,256]{1,0:T(8,128)(2,1)S(1)} %copy-done.7), channel_id=1, source_target_pairs={{0,96},{32,0},{64,32},{96,64},{1,97},{33,1},{65,33},{97,65},{2,98}... | collective-permute-start | bytes 393224 | tf_op jit(solution)/shard_map/ppermute | solution.py:32
  10.8 8.1 %collective-permute-start.2 = (bf16[256,256]{1,0:T(8,128)(2,1)S(1)}, bf16[256,256]{1,0:T(8,128)(2,1)S(1)}, u32[]{:S(2)}, u32[]{:S(2)}) collective-permute-start(bf16[256,256]{1,0:T(8,128)(2,1)S(1)} %copy-done.7), channel_id=1, source_target_pairs={{0,64},{32,96},{64,0},{96,32},{1,65},{33,97},{65,1},{97,33},{2,66}... | collective-permute-start | bytes 393224 | tf_op jit(solution)/shard_map/ppermute | solution.py:32
  12.8 10.6 %collective-permute-start.7 = (bf16[256,256]{1,0:T(8,128)(2,1)S(1)}, bf16[256,256]{1,0:T(8,128)(2,1)S(1)}, u32[]{:S(2)}, u32[]{:S(2)}) collective-permute-start(bf16[256,256]{1,0:T(8,128)(2,1)S(1)} %collective-permute-done), channel_id=1, source_target_pairs={{0,96},{32,0},{64,32},{96,64},{1,97},{33,1},{65,33},{97,65},{2,98}... | collective-permute-start | bytes 393224 | tf_op jit(solution)/shard_map/ppermute | solution.py:32
  14.0 9.5 %collective-permute-start.6 = (bf16[256,256]{1,0:T(8,128)(2,1)S(1)}, bf16[256,256]{1,0:T(8,128)(2,1)S(1)}, u32[]{:S(2)}, u32[]{:S(2)}) collective-permute-start(bf16[256,256]{1,0:T(8,128)(2,1)S(1)} %collective-permute-done), channel_id=1, source_target_pairs={{0,64},{32,96},{64,0},{96,32},{1,65},{33,97},{65,1},{97,33},{2,66}... | collective-permute-start | bytes 393224 | tf_op jit(solution)/shard_map/ppermute | solution.py:32
  15.7 7.8 %collective-permute-start.5 = (bf16[256,256]{1,0:T(8,128)(2,1)S(1)}, bf16[256,256]{1,0:T(8,128)(2,1)S(1)}, u32[]{:S(2)}, u32[]{:S(2)}) collective-permute-start(bf16[256,256]{1,0:T(8,128)(2,1)S(1)} %collective-permute-done), channel_id=1, source_target_pairs={{0,32},{32,64},{64,96},{96,0},{1,33},{33,65},{65,97},{97,1},{2,34}... | collective-permute-start | bytes 393224 | tf_op jit(solution)/shard_map/ppermute | solution.py:32
  19.0 6.3 %collective-permute-start.4 = (bf16[1280,256]{1,0:T(8,128)(2,1)S(1)}, bf16[1280,256]{1,0:T(8,128)(2,1)S(1)}, u32[]{:S(2)}, u32[]{:S(2)}) collective-permute-start(bf16[1280,256]{1,0:T(8,128)(2,1)S(1)} %constant_dynamic-update-slice_fusion.early_mine), channel_id=1, source_target_pairs={{0,8},{8,0},{1,9},{9,1},{2,10},{10,2},{3,11},{11,3},{4,12},{12,4},... | collective-permute-start | bytes 1966088 | tf_op jit(solution)/shard_map/ppermute | solution.py:32
  23.5 1.8 %collective-permute-start.8 = (bf16[768,256]{1,0:T(8,128)(2,1)S(1)}, bf16[768,256]{1,0:T(8,128)(2,1)S(1)}, u32[]{:S(2)}, u32[]{:S(2)}) collective-permute-start(bf16[768,256]{1,0:T(8,128)(2,1)S(1)} %constant_dynamic-update-slice_fusion.5.late_mine), channel_id=1, source_target_pairs={{0,8},{8,0},{1,9},{9,1},{2,10},{10,2},{3,11},{11,3},{4,12},{12,4},... | collective-permute-start | bytes 1179656 | tf_op jit(solution)/shard_map/ppermute | solution.py:32
  25.3 27.3 %slice-start = ((s8[6553600]{0:T(1024)(128)(4,1)}), s8[4194304]{0:T(1024)(128)(4,1)S(1)}, s32[]{:S(2)}) async-start(s8[6553600]{0:T(1024)(128)(4,1)} %bitcast.5), calls=%async_computation.1 | async-start | bytes 8388608
  29.1 2.6 %collective-permute-start.10 = (bf16[768,256]{1,0:T(8,128)(2,1)S(1)}, bf16[768,256]{1,0:T(8,128)(2,1)S(1)}, u32[]{:S(2)}, u32[]{:S(2)}) collective-permute-start(bf16[768,256]{1,0:T(8,128)(2,1)S(1)} %get-tuple-element.45), channel_id=1, source_target_pairs={{0,8},{8,0},{1,9},{9,1},{2,10},{10,2},{3,11},{11,3},{4,12},{12,4},... | collective-permute-start | bytes 1179656 | tf_op jit(solution)/shard_map/ppermute | solution.py:32
  30.4 2.3 %collective-permute-start.9 = (bf16[1280,256]{1,0:T(8,128)(2,1)S(1)}, bf16[1280,256]{1,0:T(8,128)(2,1)S(1)}, u32[]{:S(2)}, u32[]{:S(2)}) collective-permute-start(bf16[1280,256]{1,0:T(8,128)(2,1)S(1)} %get-tuple-element.43), channel_id=1, source_target_pairs={{0,8},{8,0},{1,9},{9,1},{2,10},{10,2},{3,11},{11,3},{4,12},{12,4},... | collective-permute-start | bytes 1966088 | tf_op jit(solution)/shard_map/ppermute | solution.py:32
  31.7 20.9 %slice-start.1 = ((s8[6553600]{0:T(1024)(128)(4,1)}), s8[2359296]{0:T(1024)(128)(4,1)S(1)}, s32[]{:S(2)}) async-start(s8[6553600]{0:T(1024)(128)(4,1)} %bitcast.5), calls=%async_computation.2 | async-start | bytes 4718592
  32.9 19.8 %copy-start = (bf16[5120,128]{1,0:T(8,128)(2,1)S(1)}, bf16[5120,128]{1,0:T(8,128)(2,1)}, u32[]{:S(2)}) copy-start(bf16[5120,128]{1,0:T(8,128)(2,1)} %wk.1) | copy-start | bytes 3932164
  32.9 19.8 %copy-start.1 = (bf16[5120,128]{1,0:T(8,128)(2,1)S(1)}, bf16[5120,128]{1,0:T(8,128)(2,1)}, u32[]{:S(2)}) copy-start(bf16[5120,128]{1,0:T(8,128)(2,1)} %wv.1) | copy-start | bytes 3932164
  33.0 8.2 %collective-permute-start.11 = (bf16[256,256]{1,0:T(8,128)(2,1)S(1)}, bf16[256,256]{1,0:T(8,128)(2,1)S(1)}, u32[]{:S(2)}, u32[]{:S(2)}) collective-permute-start(bf16[256,256]{1,0:T(8,128)(2,1)S(1)} %get-tuple-element.48), channel_id=1, source_target_pairs={{0,96},{32,0},{64,32},{96,64},{1,97},{33,1},{65,33},{97,65},{2,98}... | collective-permute-start | bytes 393224 | tf_op jit(solution)/shard_map/ppermute | solution.py:32
  35.0 7.9 %collective-permute-start.12 = (bf16[256,256]{1,0:T(8,128)(2,1)S(1)}, bf16[256,256]{1,0:T(8,128)(2,1)S(1)}, u32[]{:S(2)}, u32[]{:S(2)}) collective-permute-start(bf16[256,256]{1,0:T(8,128)(2,1)S(1)} %get-tuple-element.49), channel_id=1, source_target_pairs={{0,64},{32,96},{64,0},{96,32},{1,65},{33,97},{65,1},{97,33},{2,66}... | collective-permute-start | bytes 393224 | tf_op jit(solution)/shard_map/ppermute | solution.py:32
  36.2 9.6 %collective-permute-start.13 = (bf16[256,256]{1,0:T(8,128)(2,1)S(1)}, bf16[256,256]{1,0:T(8,128)(2,1)S(1)}, u32[]{:S(2)}, u32[]{:S(2)}) collective-permute-start(bf16[256,256]{1,0:T(8,128)(2,1)S(1)} %get-tuple-element.50), channel_id=1, source_target_pairs={{0,32},{32,64},{64,96},{96,0},{1,33},{33,65},{65,97},{97,1},{2,34}... | collective-permute-start | bytes 393224 | tf_op jit(solution)/shard_map/ppermute | solution.py:32
  36.2 12.1 %collective-permute-start.15 = (bf16[256,256]{1,0:T(8,128)(2,1)S(1)}, bf16[256,256]{1,0:T(8,128)(2,1)S(1)}, u32[]{:S(2)}, u32[]{:S(2)}) collective-permute-start(bf16[256,256]{1,0:T(8,128)(2,1)S(1)} %get-tuple-element.51), channel_id=1, source_target_pairs={{0,96},{32,0},{64,32},{96,64},{1,97},{33,1},{65,33},{97,65},{2,98}... | collective-permute-start | bytes 393224 | tf_op jit(solution)/shard_map/ppermute | solution.py:32
  39.5 9.1 %collective-permute-start.16 = (bf16[256,256]{1,0:T(8,128)(2,1)S(1)}, bf16[256,256]{1,0:T(8,128)(2,1)S(1)}, u32[]{:S(2)}, u32[]{:S(2)}) collective-permute-start(bf16[256,256]{1,0:T(8,128)(2,1)S(1)} %get-tuple-element.52), channel_id=1, source_target_pairs={{0,64},{32,96},{64,0},{96,32},{1,65},{33,97},{65,1},{97,33},{2,66}... | collective-permute-start | bytes 393224 | tf_op jit(solution)/shard_map/ppermute | solution.py:32
  41.2 9.2 %collective-permute-start.17 = (bf16[256,256]{1,0:T(8,128)(2,1)S(1)}, bf16[256,256]{1,0:T(8,128)(2,1)S(1)}, u32[]{:S(2)}, u32[]{:S(2)}) collective-permute-start(bf16[256,256]{1,0:T(8,128)(2,1)S(1)} %get-tuple-element.53), channel_id=1, source_target_pairs={{0,32},{32,64},{64,96},{96,0},{1,33},{33,65},{65,97},{97,1},{2,34}... | collective-permute-start | bytes 393224 | tf_op jit(solution)/shard_map/ppermute | solution.py:32
  45.8 6.8 %collective-permute-start.14 = (bf16[256,256]{1,0:T(8,128)(2,1)S(1)}, bf16[256,256]{1,0:T(8,128)(2,1)S(1)}, u32[]{:S(2)}, u32[]{:S(2)}) collective-permute-start(bf16[256,256]{1,0:T(8,128)(2,1)S(1)} %add_convert_fusion.1), channel_id=1, source_target_pairs={{0,16},{16,0},{1,17},{17,1},{2,18},{18,2},{3,19},{19,3},{4,20},{20... | collective-permute-start | bytes 393224 | tf_op jit(solution)/shard_map/ppermute | solution.py:32

commit v7 on v6

--- a/solution.py
+++ b/solution.py
@@ -293,12 +293,43 @@
     )(key, value, positions.reshape(2, 1, TILE), inverse)
 
 
-WIDTH = 5120
 STEP_ROWS = 640
 
 
-def project_kernel(
-    own, across, near1, near2, near3, cos, sin, qg, wq, wk, wv, out, grads
+ORDERS = (
+    ((0, 1), (1, 1), (2, 1), (3, 1), (0, 0), (1, 0), (2, 0), (3, 0)),
+    ((1, 0), (1, 1), (3, 0), (3, 1), (0, 0), (0, 1), (2, 0), (2, 1)),
+)
+
+
+def by_core(offsets):
+    pairs = []
+    for core, offset in enumerate(offsets):
+        if offset is not None:
+            for x in range(4):
+                for zl in range(2):
+                    to = (core * 4 + (x + offset[0]) % 4) * 2 + (zl + offset[1]) % 2
+                    pairs.append(((core * 4 + x) * 2 + zl, to))
+    return pairs
+
+
+def send(x, *offsets):
+    return lax.ppermute(x, ("core", "x", "zl"), by_core(offsets))
+
+
+def make_blocks(tp, core, first, count, grads, wq, wk, wv, put):
+    x, zl = lax.shift_right_logical(tp[0], 1), tp[0] & 1
+    for i in range(count):
+        (x0, z0), (x1, z1) = ORDERS[0][first + i], ORDERS[1][first + i]
+        to_x = (x + jnp.where(core[0] == 0, x0, x1)) & 3
+        to_z = zl ^ jnp.where(core[0] == 0, z0, z1)
+        rows = pl.ds(pl.multiple_of((2 * to_x + to_z) * STEP_ROWS, STEP_ROWS), STEP_ROWS)
+        weights = jnp.concatenate([wq[rows, :], wk[rows, :], wv[rows, :]], 1)
+        put(i, jnp.dot(weights, grads[...], preferred_element_type=f32))
+
+
+def first_kernel(
+    tp, core, own, across, near1, near2, near3, cos, sin, qg, wq, wk, wv, out1, out2, out3, grads
 ):
     total = own[...].astype(f32) + across[...].astype(f32)
     for near in (near1, near2, near3):
@@ -310,53 +341,110 @@
     grads[ROWS : ROWS + HEAD, :] = key_grad.T.astype(bf16)
     grads[ROWS + HEAD :, :] = total[:, HEAD:].T.astype(bf16)
 
-    def step(i, carry):
-        rows = pl.ds(pl.multiple_of(i * STEP_ROWS, STEP_ROWS), STEP_ROWS)
-        weights = jnp.concatenate([wq[rows, :], wk[rows, :], wv[rows, :]], 1)
-        result = jnp.dot(weights, grads[...], preferred_element_type=f32)
-        out[rows, :] = result.astype(bf16)
-        return carry
-
-    lax.fori_loop(0, WIDTH // STEP_ROWS, step, 0)
-
-
-def project(own, across, near, cos, sin, qg, wq, wk, wv):
+    def put_in(out):
+        def put(i, block):
+            out[i] = block.astype(bf16)
+
+        return put
+
+    make_blocks(tp, core, 0, 2, grads, wq, wk, wv, put_in(out1))
+    make_blocks(tp, core, 2, 2, grads, wq, wk, wv, put_in(out2))
+
+    @pl.when(core[0] != 0)
+    def _():
+        make_blocks(tp, core, 6, 2, grads, wq, wk, wv, put_in(out3))
+
+
+def kept_kernel(tp, core, grads, wq, wk, wv, kept):
+    def put(i, block):
+        kept[i] = block
+
+    def put_more(i, block):
+        kept[2 + i] = block
+
+    make_blocks(tp, core, 4, 2, grads, wq, wk, wv, put)
+
+    @pl.when(core[0] == 0)
+    def _():
+        make_blocks(tp, core, 6, 2, grads, wq, wk, wv, put_more)
+
+
+def middle_kernel(core, kept, got1, got2, got3, base, out1, out2, out3):
+    @pl.when(core[0] == 0)
+    def _():
+        base[...] = kept[0] + got1[0].astype(f32)
+        out1[...] = (kept[1] + got1[1].astype(f32)).astype(bf16)
+        out2[...] = (kept[2] + got2[0].astype(f32)).astype(bf16)
+        out3[...] = (kept[3] + got2[1].astype(f32)).astype(bf16)
+
+    @pl.when(core[0] != 0)
+    def _():
+        total = [
+            kept[i] + got1[i].astype(f32) + got2[i].astype(f32) + got3[i].astype(f32)
+            for i in range(2)
+        ]
+        base[...] = total[0]
+        out1[...] = total[1].astype(bf16)
+        out2[...] = jnp.zeros_like(out2)
+        out3[...] = jnp.zeros_like(out3)
+
+
+def last_kernel(core, base, got1, got2, got3, out):
+    @pl.when(core[0] == 0)
+    def _():
+        total = base[...] + got1[...].astype(f32) + got2[...].astype(f32)
+        out[...] = (total + got3[...].astype(f32)).astype(bf16)
+
+    @pl.when(core[0] != 0)
+    def _():
+        out[...] = (base[...] + got1[...].astype(f32)).astype(bf16)
+
+
+def whole_call(kernel, name, flops, outs, scalars, *operands):
+    outs = tuple(jax.ShapeDtypeStruct(shape, dtype) for shape, dtype in outs)
     return pl.pallas_call(
-        project_kernel,
-        out_shape=jax.ShapeDtypeStruct((WIDTH, TOK), bf16),
-        in_specs=vmem(11),
-        out_specs=vmem(1)[0],
-        scratch_shapes=[pltpu.VMEM((ROWS + 2 * HEAD, TOK), bf16)],
+        kernel,
+        out_shape=outs,
+        in_specs=[pl.BlockSpec(memory_space=pltpu.SMEM)] * len(scalars) + vmem(len(operands)),
+        out_specs=tuple(vmem(len(outs))),
         compiler_params=pltpu.CompilerParams(vmem_limit_bytes=16 << 20),
-        cost_estimate=pl.CostEstimate(
-            flops=2350000000, bytes_accessed=12000000, transcendentals=0
-        ),
-        name="project",
-    )(own, across, *near, cos, sin, qg, wq, wk, wv)
-
-
-def last_kernel(parts, out):
-    def step(i, carry):
-        rows = pl.ds(pl.multiple_of(i * TILE, TILE), TILE)
-        total = parts[0, rows, :].astype(f32)
-        for k in range(1, 8):
-            total += parts[k, rows, :].astype(f32)
-        out[rows, :] = total.astype(bf16)
-        return carry
-
-    lax.fori_loop(0, 5, step, 0)
-
-
-def last_sum(parts):
-    return pl.pallas_call(
-        last_kernel,
-        out_shape=jax.ShapeDtypeStruct((640, TOK), bf16),
-        in_specs=vmem(1),
-        out_specs=vmem(1)[0],
-        compiler_params=pltpu.CompilerParams(vmem_limit_bytes=16 << 20),
-        cost_estimate=pl.CostEstimate(flops=1300000, bytes_accessed=3000000, transcendentals=0),
-        name="last_sum",
-    )(parts)
+        cost_estimate=pl.CostEstimate(flops=flops, bytes_accessed=10000, transcendentals=0),
+        name=name,
+    )(*scalars, *operands)
+
+
+def project_and_sum(own, across, near, cos, sin, qg, wq, wk, wv):
+    tp = lax.axis_index(TP).reshape(1)
+    core = lax.axis_index("core").reshape(1)
+    one, two, four = ((n, STEP_ROWS, TOK) for n in (1, 2, 4))
+    one = one[1:]
+    first, second, third, grads = whole_call(
+        first_kernel,
+        "first",
+        1000000,
+        [(two, bf16), (two, bf16), (two, bf16), ((ROWS + 2 * HEAD, TOK), bf16)],
+        (tp, core),
+        own, across, *near, cos, sin, qg, wq, wk, wv,
+    )
+    got1 = send(first, (0, 1), (1, 0))
+    got2 = send(second, (0, 1), (3, 0))
+    got3 = send(third, None, (2, 0))
+    got1, grads = lax.optimization_barrier((got1, grads))
+    (kept,) = whole_call(
+        kept_kernel, "kept", 1000000, [(four, f32)], (tp, core), grads, wq, wk, wv
+    )
+    base, out1, out2, out3 = whole_call(
+        middle_kernel,
+        "middle",
+        1000000,
+        [(one, f32), (one, bf16), (one, bf16), (one, bf16)],
+        (core,),
+        kept, got1, got2, got3,
+    )
+    got1 = send(out1, (1, 0), (0, 1))
+    got2 = send(out2, (2, 0), None)
+    got3 = send(out3, (3, 0), None)
+    return whole_call(last_kernel, "last", 1000000, [(one, bf16)], (core,), base, got1, got2, got3)[0]
 
 
 def local(
@@ -391,8 +479,9 @@
     near = [shift_y(parts[k - 1], -k) for k in (1, 2, 3)]
     across = across + sum(p.astype(f32) for p in far)
     across = swap_zh(lax.optimization_barrier(across.astype(bf16)))
-    send = project(own, across, near, cos, sin, query_grad, w_query, key_weight, value_weight)
-    return last_sum(lax.all_to_all(send.reshape(8, 640, TOK), TP, 0, 0))
+    return project_and_sum(
+        own, across, near, cos, sin, query_grad, w_query, key_weight, value_weight
+    )
 
 
 def solution(mesh):

time: 94.1 us -> 99.1 us (1.053)
  blocking collectives: 35.9 us -> 0 us
  waiting for transfers between devices: 19.8 us -> 39 us
  starting transfers between devices: 24 us -> 36.2 us
  local copies, waits for them, and re-layouts: 0.23 us -> 8.39 us
    all_to_all x1 -> x0, blocking collectives: 35.9 us -> none  [local(): return last_sum(lax.all_to_all(send.reshape(8, 640, TOK), TP, 0, 0))]
    ppermute x0 -> x6, waiting for transfers between devices: none -> 18.8 us  [send(): return lax.ppermute(x, ('core', 'x', 'zl'), by_core(offsets))]
    ppermute x0 -> x6, starting transfers between devices: none -> 12.3 us  [send(): return lax.ppermute(x, ('core', 'x', 'zl'), by_core(offsets))]
    unnamed x26 -> x36, local copies, waits for them, and re-layouts: 0.11 us -> 7.53 us
    pallas_call x2 -> x4, Pallas kernels: 5.32 us -> 5.61 us  [whole_call(): pl.pallas_call(kernel, out_shape=outs, in_specs=[pl.BlockSpec(memory_spac...]
  transfers between devices with their start and end apart: 18 -> 24, of which waited for: 11 -> 14; matrix products, arithmetic and copies ran while one was open for 2% -> 2% of each run, Pallas kernels for 1% -> 3%
where the time goes in v7:
time: 99.1 us; the launch traced here: 98.5 us
  waiting for transfers between devices  39 us (39%)
  starting transfers between devices  36.2 us (37%)
  Pallas kernels  12.3 us (12%)
  local copies, waits for them, and re-layouts  8.39 us (8%)
  other arithmetic  2.27 us (2%)
    ppermute x18, starting transfers between devices, shift(): return lax.ppermute(x, axes, perm)  23.8 us
    ppermute x18, waiting for transfers between devices, shift(): return lax.ppermute(x, axes, perm)  20.2 us
    ppermute x6, waiting for transfers between devices, send(): return lax.ppermute(x, ('core', 'x', 'zl'), by_core(offsets))  18.8 us
    ppermute x6, starting transfers between devices, send(): return lax.ppermute(x, ('core', 'x', 'zl'), by_core(offsets))  12.3 us
    unnamed x36, local copies, waits for them, and re-layouts  7.53 us
    pallas_call x4, Pallas kernels, whole_call(): pl.pallas_call(kernel, out_shape=outs, in_specs=[pl.BlockSpec(memory_spac...  5.61 us
    pallas_call x1, Pallas kernels, attention(): pl.pallas_call(attention_kernel, out_shape=(early, early, late, late, s((...  3.7 us
    pallas_call x1, Pallas kernels, make_block(): pl.pallas_call(block_kernel, out_shape=(s((TOK, HEAD), f32), s((TOK, HEAD...  2.18 us
  transfers between devices with their start and end apart: 24, of which 14 were waited for; matrix products, arithmetic and copies ran while one was open for 2% of the time, Pallas kernels for 3%

profile of v7, /device:TPU:0, one launch (start us, length us, event | category | flops | bytes accessed | tf_op | source)
XLA Modules:
  0.0 98.5 jit_solution(8931882882417207636)
XLA Ops:
  0.0 2.2 %block.1 = (f32[256,128]{1,0:T(8,128)}, f32[256,128]{1,0:T(8,128)}, bf16[256,256]{1,0:T(8,128)(2,1)}) custom-call(bf16[256,128]{1,0:T(8,128)(2,1)} %key.1, bf16[256,128]{1,0:T(8,128)(2,1)} %value.1, s32[2,1,128]{2,1,0:T(1,128)} %bitcast.8, f32[1,128]{1,0:T(1,128)} %constant.25.clone.inverse), custom_call_target="tpu_custom_call" | custom-call | flops 5000000 | bytes 700000 | tf_op jit(solution)/shard_map/block/pallas_call | solution.py:286
  2.2 4.0 %collective-permute-start = (bf16[256,256]{1,0:T(8,128)(2,1)}, bf16[256,256]{1,0:T(8,128)(2,1)S(1)}, u32[]{:S(2)}, u32[]{:S(2)}) collective-permute-start(bf16[256,256]{1,0:T(8,128)(2,1)} %get-tuple-element.50), channel_id=1, source_target_pairs={{0,16},{16,0},{1,17},{17,1},{2,18},{18,2},{3,19},{19,3},{4,20},{20... | collective-permute-start | bytes 393224 | tf_op jit(solution)/shard_map/ppermute | solution.py:32
  6.2 1.2 %pad_maximum_fusion.joined = bf16[256,1920]{1,0:T(8,128)(2,1)S(1)} fusion(bf16[256,640]{1,0:T(8,128)(2,1)} %param.16, bf16[256,640]{1,0:T(8,128)(2,1)} %param.17, bf16[256,640]{1,0:T(8,128)(2,1)} %param.13), kind=kLoop, calls=%fused_computation.1 | loop fusion | flops 2949120 | bytes 1966080 | tf_op jit(solution)/shard_map/concatenate | solution.py:458
  7.5 1.6 %collective-permute-start.1 = (bf16[256,256]{1,0:T(8,128)(2,1)S(1)}, bf16[256,256]{1,0:T(8,128)(2,1)S(1)}, u32[]{:S(2)}, u32[]{:S(2)}) collective-permute-start(bf16[256,256]{1,0:T(8,128)(2,1)S(1)} %copy-done.12), channel_id=1, source_target_pairs={{0,32},{32,64},{64,96},{96,0},{1,33},{33,65},{65,97},{97,1},{2,34}... | collective-permute-start | bytes 393224 | tf_op jit(solution)/shard_map/ppermute | solution.py:32
  9.2 1.7 %collective-permute-start.3 = (bf16[256,256]{1,0:T(8,128)(2,1)S(1)}, bf16[256,256]{1,0:T(8,128)(2,1)S(1)}, u32[]{:S(2)}, u32[]{:S(2)}) collective-permute-start(bf16[256,256]{1,0:T(8,128)(2,1)S(1)} %copy-done.12), channel_id=1, source_target_pairs={{0,96},{32,0},{64,32},{96,64},{1,97},{33,1},{65,33},{97,65},{2,98}... | collective-permute-start | bytes 393224 | tf_op jit(solution)/shard_map/ppermute | solution.py:32
  10.8 2.0 %collective-permute-start.2 = (bf16[256,256]{1,0:T(8,128)(2,1)S(1)}, bf16[256,256]{1,0:T(8,128)(2,1)S(1)}, u32[]{:S(2)}, u32[]{:S(2)}) collective-permute-start(bf16[256,256]{1,0:T(8,128)(2,1)S(1)} %copy-done.12), channel_id=1, source_target_pairs={{0,64},{32,96},{64,0},{96,32},{1,65},{33,97},{65,1},{97,33},{2,66}... | collective-permute-start | bytes 393224 | tf_op jit(solution)/shard_map/ppermute | solution.py:32
  12.8 1.1 %collective-permute-start.7 = (bf16[256,256]{1,0:T(8,128)(2,1)S(1)}, bf16[256,256]{1,0:T(8,128)(2,1)S(1)}, u32[]{:S(2)}, u32[]{:S(2)}) collective-permute-start(bf16[256,256]{1,0:T(8,128)(2,1)S(1)} %collective-permute-done), channel_id=1, source_target_pairs={{0,96},{32,0},{64,32},{96,64},{1,97},{33,1},{65,33},{97,65},{2,98}... | collective-permute-start | bytes 393224 | tf_op jit(solution)/shard_map/ppermute | solution.py:32
  14.0 1.7 %collective-permute-start.6 = (bf16[256,256]{1,0:T(8,128)(2,1)S(1)}, bf16[256,256]{1,0:T(8,128)(2,1)S(1)}, u32[]{:S(2)}, u32[]{:S(2)}) collective-permute-start(bf16[256,256]{1,0:T(8,128)(2,1)S(1)} %collective-permute-done), channel_id=1, source_target_pairs={{0,64},{32,96},{64,0},{96,32},{1,65},{33,97},{65,1},{97,33},{2,66}... | collective-permute-start | bytes 393224 | tf_op jit(solution)/shard_map/ppermute | solution.py:32
  15.7 0.2 collective-permute-start.5
  15.9 3.1 %collective-permute-done.2 = bf16[256,256]{1,0:T(8,128)(2,1)S(1)} collective-permute-done((bf16[256,256]{1,0:T(8,128)(2,1)S(1)}, bf16[256,256]{1,0:T(8,128)(2,1)S(1)}, u32[]{:S(2)}, u32[]{:S(2)}) %collective-permute-start.2) | collective-permute-done | bytes 131104 | tf_op jit(solution)/shard_map/ppermute | solution.py:32
  19.1 4.3 %collective-permute-done.5 = bf16[256,256]{1,0:T(8,128)(2,1)S(1)} collective-permute-done((bf16[256,256]{1,0:T(8,128)(2,1)S(1)}, bf16[256,256]{1,0:T(8,128)(2,1)S(1)}, u32[]{:S(2)}, u32[]{:S(2)}) %collective-permute-start.5) | collective-permute-done | bytes 131104 | tf_op jit(solution)/shard_map/ppermute | solution.py:32
  23.6 0.8 prep.1
  24.5 0.9 collective-permute-done.8.late_other
  25.3 0.8 copy-done.7
  26.2 1.1 %copy-done.8 = bf16[1280,256]{1,0:T(8,128)(2,1)S(1)} copy-done((bf16[1280,256]{1,0:T(8,128)(2,1)S(1)}, bf16[1280,256]{1,0:T(8,128)(2,1)}, u32[]{:S(2)}) %copy-start.8) | copy-done | bytes 655384
  27.3 3.7 %attention.1 = (bf16[1280,256]{1,0:T(8,128)(2,1)S(1)}, bf16[1280,256]{1,0:T(8,128)(2,1)S(1)}, bf16[768,256]{1,0:T(8,128)(2,1)S(1)}, bf16[768,256]{1,0:T(8,128)(2,1)S(1)}, bf16[640,256]{1,0:T(8,128)(2,1)S(1)}) custom-call(s32[32,32]{1,0:T(8,128)S(1)} %copy-done.9, s32[1]{0:T(128)} %bitcast.2.info, s32[32,1,128]{2,1,0:T(1,128)S(1)} %bitcast.7, ...), custom_call_target="tpu_custom_call" | custom-call | flops 2000000000 | bytes 8000000 | tf_op jit(solution)/shard_map/attention/pallas_call | solution.py:261
  31.0 1.3 %collective-permute-start.10 = (bf16[768,256]{1,0:T(8,128)(2,1)S(1)}, bf16[768,256]{1,0:T(8,128)(2,1)S(1)}, u32[]{:S(2)}, u32[]{:S(2)}) collective-permute-start(bf16[768,256]{1,0:T(8,128)(2,1)S(1)} %get-tuple-element.55), channel_id=1, source_target_pairs={{0,8},{8,0},{1,9},{9,1},{2,10},{10,2},{3,11},{11,3},{4,12},{12,4},... | collective-permute-start | bytes 1179656 | tf_op jit(solution)/shard_map/ppermute | solution.py:32
  32.4 1.3 %collective-permute-done.10 = bf16[768,256]{1,0:T(8,128)(2,1)S(1)} collective-permute-done((bf16[768,256]{1,0:T(8,128)(2,1)S(1)}, bf16[768,256]{1,0:T(8,128)(2,1)S(1)}, u32[]{:S(2)}, u32[]{:S(2)}) %collective-permute-start.10) | collective-permute-done | bytes 393248 | tf_op jit(solution)/shard_map/ppermute | solution.py:32
  33.8 0.8 collective-permute-done.9
  34.8 0.8 fusion.2
  35.6 2.0 %collective-permute-start.11 = (bf16[256,256]{1,0:T(8,128)(2,1)S(1)}, bf16[256,256]{1,0:T(8,128)(2,1)S(1)}, u32[]{:S(2)}, u32[]{:S(2)}) collective-permute-start(bf16[256,256]{1,0:T(8,128)(2,1)S(1)} %get-tuple-element.58), channel_id=1, source_target_pairs={{0,96},{32,0},{64,32},{96,64},{1,97},{33,1},{65,33},{97,65},{2,98}... | collective-permute-start | bytes 393224 | tf_op jit(solution)/shard_map/ppermute | solution.py:32
  37.6 1.2 %collective-permute-start.12 = (bf16[256,256]{1,0:T(8,128)(2,1)S(1)}, bf16[256,256]{1,0:T(8,128)(2,1)S(1)}, u32[]{:S(2)}, u32[]{:S(2)}) collective-permute-start(bf16[256,256]{1,0:T(8,128)(2,1)S(1)} %get-tuple-element.59), channel_id=1, source_target_pairs={{0,64},{32,96},{64,0},{96,32},{1,65},{33,97},{65,1},{97,33},{2,66}... | collective-permute-start | bytes 393224 | tf_op jit(solution)/shard_map/ppermute | solution.py:32
  38.8 3.2 %collective-permute-start.15 = (bf16[256,256]{1,0:T(8,128)(2,1)}, bf16[256,256]{1,0:T(8,128)(2,1)S(1)}, u32[]{:S(2)}, u32[]{:S(2)}) collective-permute-start(bf16[256,256]{1,0:T(8,128)(2,1)} %get-tuple-element.61), channel_id=1, source_target_pairs={{0,96},{32,0},{64,32},{96,64},{1,97},{33,1},{65,33},{97,65},{2,98}... | collective-permute-start | bytes 393224 | tf_op jit(solution)/shard_map/ppermute | solution.py:32
  42.1 1.1 %collective-permute-start.16 = (bf16[256,256]{1,0:T(8,128)(2,1)}, bf16[256,256]{1,0:T(8,128)(2,1)S(1)}, u32[]{:S(2)}, u32[]{:S(2)}) collective-permute-start(bf16[256,256]{1,0:T(8,128)(2,1)} %get-tuple-element.62), channel_id=1, source_target_pairs={{0,64},{32,96},{64,0},{96,32},{1,65},{33,97},{65,1},{97,33},{2,66}... | collective-permute-start | bytes 393224 | tf_op jit(solution)/shard_map/ppermute | solution.py:32
  43.2 0.6 collective-permute-done.11
  43.7 1.7 %collective-permute-done.12 = bf16[256,256]{1,0:T(8,128)(2,1)S(1)} collective-permute-done((bf16[256,256]{1,0:T(8,128)(2,1)S(1)}, bf16[256,256]{1,0:T(8,128)(2,1)S(1)}, u32[]{:S(2)}, u32[]{:S(2)}) %collective-permute-start.12) | collective-permute-done | bytes 131104 | tf_op jit(solution)/shard_map/ppermute | solution.py:32
  45.5 2.9 %collective-permute-done.13 = bf16[256,256]{1,0:T(8,128)(2,1)S(1)} collective-permute-done((bf16[256,256]{1,0:T(8,128)(2,1)S(1)}, bf16[256,256]{1,0:T(8,128)(2,1)S(1)}, u32[]{:S(2)}, u32[]{:S(2)}) %collective-permute-start.13) | collective-permute-done | bytes 131104 | tf_op jit(solution)/shard_map/ppermute | solution.py:32
  48.4 0.7 add_convert_fusion.1
  49.1 2.3 %collective-permute-start.14 = (bf16[256,256]{1,0:T(8,128)(2,1)}, bf16[256,256]{1,0:T(8,128)(2,1)}, u32[]{:S(2)}, u32[]{:S(2)}) collective-permute-start(bf16[256,256]{1,0:T(8,128)(2,1)} %add_convert_fusion.1), channel_id=1, source_target_pairs={{0,16},{16,0},{1,17},{17,1},{2,18},{18,2},{3,19},{19,3},{4,20},{20... | collective-permute-start | bytes 393224 | tf_op jit(solution)/shard_map/ppermute | solution.py:32
  51.4 1.7 %collective-permute-done.17.near3 = bf16[256,256]{1,0:T(8,128)(2,1)} collective-permute-done((bf16[256,256]{1,0:T(8,128)(2,1)}, bf16[256,256]{1,0:T(8,128)(2,1)}, u32[]{:S(2)}, u32[]{:S(2)}) %collective-permute-start.17) | collective-permute-done | bytes 131104 | tf_op jit(solution)/shard_map/ppermute | solution.py:32
  53.1 3.0 %collective-permute-done.14.across = bf16[256,256]{1,0:T(8,128)(2,1)} collective-permute-done((bf16[256,256]{1,0:T(8,128)(2,1)}, bf16[256,256]{1,0:T(8,128)(2,1)}, u32[]{:S(2)}, u32[]{:S(2)}) %collective-permute-start.14) | collective-permute-done | bytes 131104 | tf_op jit(solution)/shard_map/ppermute | solution.py:32
  56.1 2.9 %copy-done = bf16[5120,640]{1,0:T(8,128)(2,1)S(1)} copy-done((bf16[5120,640]{1,0:T(8,128)(2,1)S(1)}, bf16[5120,640]{1,0:T(8,128)(2,1)}, u32[]{:S(2)}) %copy-start) | copy-done | bytes 6553624
  59.0 1.3 %copy-done.1 = bf16[5120,128]{1,0:T(8,128)(2,1)S(1)} copy-done((bf16[5120,128]{1,0:T(8,128)(2,1)S(1)}, bf16[5120,128]{1,0:T(8,128)(2,1)}, u32[]{:S(2)}) %copy-start.1) | copy-done | bytes 1310744
  60.3 1.3 %copy-done.3 = bf16[5120,128]{1,0:T(8,128)(2,1)S(1)} copy-done((bf16[5120,128]{1,0:T(8,128)(2,1)S(1)}, bf16[5120,128]{1,0:T(8,128)(2,1)}, u32[]{:S(2)}) %copy-start.3) | copy-done | bytes 1310744
  61.6 2.8 %first.1 = (bf16[2,640,256]{2,1,0:T(8,128)(2,1)S(1)}, bf16[2,640,256]{2,1,0:T(8,128)(2,1)S(1)}, bf16[2,640,256]{2,1,0:T(8,128)(2,1)S(1)}, bf16[896,256]{1,0:T(8,128)(2,1)S(1)}) custom-call(s32[1]{0:T(128)} %bitcast.1.tp, s32[1]{0:T(128)} %bitcast.core, f32[256,256]{1,0:T(8,128)S(1)} %get-tuple-element.56.own, ...), custom_call_target="tpu_custom_call" | custom-call | flops 1000000 | bytes 10000 | tf_op jit(solution)/shard_map/first/pallas_call | solution.py:405
  64.5 1.1 %collective-permute-start.18 = (bf16[2,640,256]{2,1,0:T(8,128)(2,1)S(1)}, bf16[2,640,256]{2,1,0:T(8,128)(2,1)S(1)}, u32[]{:S(2)}, u32[]{:S(2)}) collective-permute-start(bf16[2,640,256]{2,1,0:T(8,128)(2,1)S(1)} %get-tuple-element.65), channel_id=1, source_target_pairs={{0,1},{1,0},{2,3},{3,2},{4,5},{5,4},{6,7},{7,6},{8,10},{9,11},{10,... | collective-permute-start | bytes 1966088 | tf_op jit(solution)/shard_map/ppermute | solution.py:317
  65.6 1.0 %collective-permute-start.19 = (bf16[2,640,256]{2,1,0:T(8,128)(2,1)S(1)}, bf16[2,640,256]{2,1,0:T(8,128)(2,1)S(1)}, u32[]{:S(2)}, u32[]{:S(2)}) collective-permute-start(bf16[2,640,256]{2,1,0:T(8,128)(2,1)S(1)} %get-tuple-element.69), channel_id=1, source_target_pairs={{0,1},{1,0},{2,3},{3,2},{4,5},{5,4},{6,7},{7,6},{8,14},{9,15},{10,... | collective-permute-start | bytes 1966088 | tf_op jit(solution)/shard_map/ppermute | solution.py:317
  66.6 0.7 collective-permute-start.20
  67.3 7.9 %collective-permute-done.18.got1 = bf16[2,640,256]{2,1,0:T(8,128)(2,1)S(1)} collective-permute-done((bf16[2,640,256]{2,1,0:T(8,128)(2,1)S(1)}, bf16[2,640,256]{2,1,0:T(8,128)(2,1)S(1)}, u32[]{:S(2)}, u32[]{:S(2)}) %collective-permute-start.18) | collective-permute-done | bytes 655392 | tf_op jit(solution)/shard_map/ppermute | solution.py:317
  75.2 1.7 %kept.1 = f32[4,640,256]{2,1,0:T(8,128)S(1)} custom-call(s32[1]{0:T(128)} %bitcast.1.tp, s32[1]{0:T(128)} %bitcast.core, bf16[896,256]{1,0:T(8,128)(2,1)S(1)} %get-tuple-element.67.grads, bf16[5120,640]{1,0:T(8,128)(2,1)S(1)} %bitcast.6, bf16[5120,128]{1,0:T(8,128)(2,1)S(1)} %copy-done.2, bf16[5120,128]{1,0:T(8,128)(2,1)S(1)} %copy-done.4), custom_call_target="tpu_custom_call" | custom-call | flops 1000000 | bytes 10000 | tf_op jit(solution)/shard_map/kept/pallas_call | solution.py:405
  76.8 5.3 %collective-permute-done.19.got2 = bf16[2,640,256]{2,1,0:T(8,128)(2,1)S(1)} collective-permute-done((bf16[2,640,256]{2,1,0:T(8,128)(2,1)S(1)}, bf16[2,640,256]{2,1,0:T(8,128)(2,1)S(1)}, u32[]{:S(2)}, u32[]{:S(2)}) %collective-permute-start.19) | collective-permute-done | bytes 655392 | tf_op jit(solution)/shard_map/ppermute | solution.py:317
  82.2 0.2 middle.1
  82.4 1.6 %collective-permute-start.21 = (bf16[640,256]{1,0:T(8,128)(2,1)S(1)}, bf16[640,256]{1,0:T(8,128)(2,1)S(1)}, u32[]{:S(2)}, u32[]{:S(2)}) collective-permute-start(bf16[640,256]{1,0:T(8,128)(2,1)S(1)} %get-tuple-element.72), channel_id=1, source_target_pairs={{0,2},{1,3},{2,4},{3,5},{4,6},{5,7},{6,0},{7,1},{8,9},{9,8},{10,11... | collective-permute-start | bytes 983048 | tf_op jit(solution)/shard_map/ppermute | solution.py:317
  84.0 4.6 %collective-permute-start.22 = (bf16[640,256]{1,0:T(8,128)(2,1)S(1)}, bf16[640,256]{1,0:T(8,128)(2,1)S(1)}, u32[]{:S(2)}, u32[]{:S(2)}) collective-permute-start(bf16[640,256]{1,0:T(8,128)(2,1)S(1)} %get-tuple-element.73), channel_id=1, source_target_pairs={{0,4},{1,5},{2,6},{3,7},{4,0},{5,1},{6,2},{7,3},{16,20},{17,21},{1... | collective-permute-start | bytes 983048 | tf_op jit(solution)/shard_map/ppermute | solution.py:317
  88.6 3.3 %collective-permute-start.23 = (bf16[640,256]{1,0:T(8,128)(2,1)S(1)}, bf16[640,256]{1,0:T(8,128)(2,1)S(1)}, u32[]{:S(2)}, u32[]{:S(2)}) collective-permute-start(bf16[640,256]{1,0:T(8,128)(2,1)S(1)} %get-tuple-element.74), channel_id=1, source_target_pairs={{0,6},{1,7},{2,0},{3,1},{4,2},{5,3},{6,4},{7,5},{16,22},{17,23},{1... | collective-permute-start | bytes 983048 | tf_op jit(solution)/shard_map/ppermute | solution.py:317
  92.0 3.3 %collective-permute-done.22.got2 = bf16[640,256]{1,0:T(8,128)(2,1)S(1)} collective-permute-done((bf16[640,256]{1,0:T(8,128)(2,1)S(1)}, bf16[640,256]{1,0:T(8,128)(2,1)S(1)}, u32[]{:S(2)}, u32[]{:S(2)}) %collective-permute-start.22) | collective-permute-done | bytes 327712 | tf_op jit(solution)/shard_map/ppermute | solution.py:317
  95.3 2.3 %collective-permute-done.23.got3 = bf16[640,256]{1,0:T(8,128)(2,1)S(1)} collective-permute-done((bf16[640,256]{1,0:T(8,128)(2,1)S(1)}, bf16[640,256]{1,0:T(8,128)(2,1)S(1)}, u32[]{:S(2)}, u32[]{:S(2)}) %collective-permute-start.23) | collective-permute-done | bytes 327712 | tf_op jit(solution)/shard_map/ppermute | solution.py:317
  97.6 0.9 last.1
  (53 shorter events, 0.8 us)
Async XLA Ops:
  2.2 5.3 %copy-start.12 = (bf16[256,256]{1,0:T(8,128)(2,1)S(1)}, bf16[256,256]{1,0:T(8,128)(2,1)}, u32[]{:S(2)}) copy-start(bf16[256,256]{1,0:T(8,128)(2,1)} %get-tuple-element.50) | copy-start | bytes 393220
  2.2 21.4 %copy-start.5 = (f32[256,128]{1,0:T(8,128)S(1)}, f32[256,128]{1,0:T(8,128)}, u32[]{:S(2)}) copy-start(f32[256,128]{1,0:T(8,128)} %get-tuple-element.43.cos) | copy-start | bytes 393220
  2.2 21.4 %copy-start.6 = (f32[256,128]{1,0:T(8,128)S(1)}, f32[256,128]{1,0:T(8,128)}, u32[]{:S(2)}) copy-start(f32[256,128]{1,0:T(8,128)} %get-tuple-element.44.sin) | copy-start | bytes 393220
  2.2 10.6 %collective-permute-start = (bf16[256,256]{1,0:T(8,128)(2,1)}, bf16[256,256]{1,0:T(8,128)(2,1)S(1)}, u32[]{:S(2)}, u32[]{:S(2)}) collective-permute-start(bf16[256,256]{1,0:T(8,128)(2,1)} %get-tuple-element.50), channel_id=1, source_target_pairs={{0,16},{16,0},{1,17},{17,1},{2,18},{18,2},{3,19},{19,3},{4,20},{20... | collective-permute-start | bytes 393224 | tf_op jit(solution)/shard_map/ppermute | solution.py:32
  7.5 18.7 %copy-start.9 = (s32[32,32]{1,0:T(8,128)S(1)}, s32[32,32]{1,0:T(8,128)}, u32[]{:S(2)}) copy-start(s32[32,32]{1,0:T(8,128)} %mask.1) | copy-start | bytes 12292
  7.5 18.7 %copy-start.10 = (s32[4096]{0:T(1024)S(1)}, s32[4096]{0:T(1024)}, u32[]{:S(2)}) copy-start(s32[4096]{0:T(1024)} %param.21) | copy-start | bytes 49156
  7.5 18.7 %copy-start.11 = (f32[5,256]{1,0:T(8,128)S(1)}, f32[5,256]{1,0:T(8,128)}, u32[]{:S(2)}) copy-start(f32[5,256]{1,0:T(8,128)} %lse.1) | copy-start | bytes 15364
  7.5 8.1 %collective-permute-start.1 = (bf16[256,256]{1,0:T(8,128)(2,1)S(1)}, bf16[256,256]{1,0:T(8,128)(2,1)S(1)}, u32[]{:S(2)}, u32[]{:S(2)}) collective-permute-start(bf16[256,256]{1,0:T(8,128)(2,1)S(1)} %copy-done.12), channel_id=1, source_target_pairs={{0,32},{32,64},{64,96},{96,0},{1,33},{33,65},{65,97},{97,1},{2,34}... | collective-permute-start | bytes 393224 | tf_op jit(solution)/shard_map/ppermute | solution.py:32
  9.2 9.8 %collective-permute-start.3 = (bf16[256,256]{1,0:T(8,128)(2,1)S(1)}, bf16[256,256]{1,0:T(8,128)(2,1)S(1)}, u32[]{:S(2)}, u32[]{:S(2)}) collective-permute-start(bf16[256,256]{1,0:T(8,128)(2,1)S(1)} %copy-done.12), channel_id=1, source_target_pairs={{0,96},{32,0},{64,32},{96,64},{1,97},{33,1},{65,33},{97,65},{2,98}... | collective-permute-start | bytes 393224 | tf_op jit(solution)/shard_map/ppermute | solution.py:32
  10.8 8.1 %collective-permute-start.2 = (bf16[256,256]{1,0:T(8,128)(2,1)S(1)}, bf16[256,256]{1,0:T(8,128)(2,1)S(1)}, u32[]{:S(2)}, u32[]{:S(2)}) collective-permute-start(bf16[256,256]{1,0:T(8,128)(2,1)S(1)} %copy-done.12), channel_id=1, source_target_pairs={{0,64},{32,96},{64,0},{96,32},{1,65},{33,97},{65,1},{97,33},{2,66}... | collective-permute-start | bytes 393224 | tf_op jit(solution)/shard_map/ppermute | solution.py:32
  12.8 10.6 %collective-permute-start.7 = (bf16[256,256]{1,0:T(8,128)(2,1)S(1)}, bf16[256,256]{1,0:T(8,128)(2,1)S(1)}, u32[]{:S(2)}, u32[]{:S(2)}) collective-permute-start(bf16[256,256]{1,0:T(8,128)(2,1)S(1)} %collective-permute-done), channel_id=1, source_target_pairs={{0,96},{32,0},{64,32},{96,64},{1,97},{33,1},{65,33},{97,65},{2,98}... | collective-permute-start | bytes 393224 | tf_op jit(solution)/shard_map/ppermute | solution.py:32
  14.0 9.5 %collective-permute-start.6 = (bf16[256,256]{1,0:T(8,128)(2,1)S(1)}, bf16[256,256]{1,0:T(8,128)(2,1)S(1)}, u32[]{:S(2)}, u32[]{:S(2)}) collective-permute-start(bf16[256,256]{1,0:T(8,128)(2,1)S(1)} %collective-permute-done), channel_id=1, source_target_pairs={{0,64},{32,96},{64,0},{96,32},{1,65},{33,97},{65,1},{97,33},{2,66}... | collective-permute-start | bytes 393224 | tf_op jit(solution)/shard_map/ppermute | solution.py:32
  15.7 7.8 %collective-permute-start.5 = (bf16[256,256]{1,0:T(8,128)(2,1)S(1)}, bf16[256,256]{1,0:T(8,128)(2,1)S(1)}, u32[]{:S(2)}, u32[]{:S(2)}) collective-permute-start(bf16[256,256]{1,0:T(8,128)(2,1)S(1)} %collective-permute-done), channel_id=1, source_target_pairs={{0,32},{32,64},{64,96},{96,0},{1,33},{33,65},{65,97},{97,1},{2,34}... | collective-permute-start | bytes 393224 | tf_op jit(solution)/shard_map/ppermute | solution.py:32
  19.0 6.3 %collective-permute-start.4 = (bf16[1280,256]{1,0:T(8,128)(2,1)S(1)}, bf16[1280,256]{1,0:T(8,128)(2,1)S(1)}, u32[]{:S(2)}, u32[]{:S(2)}) collective-permute-start(bf16[1280,256]{1,0:T(8,128)(2,1)S(1)} %constant_dynamic-update-slice_fusion.early_mine), channel_id=1, source_target_pairs={{0,8},{8,0},{1,9},{9,1},{2,10},{10,2},{3,11},{11,3},{4,12},{12,4},... | collective-permute-start | bytes 1966088 | tf_op jit(solution)/shard_map/ppermute | solution.py:32
  23.5 1.8 %collective-permute-start.8 = (bf16[768,256]{1,0:T(8,128)(2,1)S(1)}, bf16[768,256]{1,0:T(8,128)(2,1)S(1)}, u32[]{:S(2)}, u32[]{:S(2)}) collective-permute-start(bf16[768,256]{1,0:T(8,128)(2,1)S(1)} %constant_dynamic-update-slice_fusion.5.late_mine), channel_id=1, source_target_pairs={{0,8},{8,0},{1,9},{9,1},{2,10},{10,2},{3,11},{11,3},{4,12},{12,4},... | collective-permute-start | bytes 1179656 | tf_op jit(solution)/shard_map/ppermute | solution.py:32
  25.3 0.8 copy-start.7
  26.2 1.1 %copy-start.8 = (bf16[1280,256]{1,0:T(8,128)(2,1)S(1)}, bf16[1280,256]{1,0:T(8,128)(2,1)}, u32[]{:S(2)}) copy-start(bf16[1280,256]{1,0:T(8,128)(2,1)} %copy-done.7) | copy-start | bytes 1966084
  31.0 2.6 %collective-permute-start.10 = (bf16[768,256]{1,0:T(8,128)(2,1)S(1)}, bf16[768,256]{1,0:T(8,128)(2,1)S(1)}, u32[]{:S(2)}, u32[]{:S(2)}) collective-permute-start(bf16[768,256]{1,0:T(8,128)(2,1)S(1)} %get-tuple-element.55), channel_id=1, source_target_pairs={{0,8},{8,0},{1,9},{9,1},{2,10},{10,2},{3,11},{11,3},{4,12},{12,4},... | collective-permute-start | bytes 1179656 | tf_op jit(solution)/shard_map/ppermute | solution.py:32
  32.3 2.3 %collective-permute-start.9 = (bf16[1280,256]{1,0:T(8,128)(2,1)S(1)}, bf16[1280,256]{1,0:T(8,128)(2,1)S(1)}, u32[]{:S(2)}, u32[]{:S(2)}) collective-permute-start(bf16[1280,256]{1,0:T(8,128)(2,1)S(1)} %get-tuple-element.53), channel_id=1, source_target_pairs={{0,8},{8,0},{1,9},{9,1},{2,10},{10,2},{3,11},{11,3},{4,12},{12,4},... | collective-permute-start | bytes 1966088 | tf_op jit(solution)/shard_map/ppermute | solution.py:32
  34.6 40.6 %slice-start = ((s8[6553600]{0:T(1024)(128)(4,1)}), s8[2359296]{0:T(1024)(128)(4,1)S(1)}, s32[]{:S(2)}) async-start(s8[6553600]{0:T(1024)(128)(4,1)} %bitcast.5), calls=%async_computation | async-start | bytes 4718592
  35.6 8.2 %collective-permute-start.11 = (bf16[256,256]{1,0:T(8,128)(2,1)S(1)}, bf16[256,256]{1,0:T(8,128)(2,1)S(1)}, u32[]{:S(2)}, u32[]{:S(2)}) collective-permute-start(bf16[256,256]{1,0:T(8,128)(2,1)S(1)} %get-tuple-element.58), channel_id=1, source_target_pairs={{0,96},{32,0},{64,32},{96,64},{1,97},{33,1},{65,33},{97,65},{2,98}... | collective-permute-start | bytes 393224 | tf_op jit(solution)/shard_map/ppermute | solution.py:32
  37.6 7.9 %collective-permute-start.12 = (bf16[256,256]{1,0:T(8,128)(2,1)S(1)}, bf16[256,256]{1,0:T(8,128)(2,1)S(1)}, u32[]{:S(2)}, u32[]{:S(2)}) collective-permute-start(bf16[256,256]{1,0:T(8,128)(2,1)S(1)} %get-tuple-element.59), channel_id=1, source_target_pairs={{0,64},{32,96},{64,0},{96,32},{1,65},{33,97},{65,1},{97,33},{2,66}... | collective-permute-start | bytes 393224 | tf_op jit(solution)/shard_map/ppermute | solution.py:32
  38.8 9.5 %collective-permute-start.13 = (bf16[256,256]{1,0:T(8,128)(2,1)S(1)}, bf16[256,256]{1,0:T(8,128)(2,1)S(1)}, u32[]{:S(2)}, u32[]{:S(2)}) collective-permute-start(bf16[256,256]{1,0:T(8,128)(2,1)S(1)} %get-tuple-element.60), channel_id=1, source_target_pairs={{0,32},{32,64},{64,96},{96,0},{1,33},{33,65},{65,97},{97,1},{2,34}... | collective-permute-start | bytes 393224 | tf_op jit(solution)/shard_map/ppermute | solution.py:32
  38.8 12.6 %collective-permute-start.15 = (bf16[256,256]{1,0:T(8,128)(2,1)}, bf16[256,256]{1,0:T(8,128)(2,1)S(1)}, u32[]{:S(2)}, u32[]{:S(2)}) collective-permute-start(bf16[256,256]{1,0:T(8,128)(2,1)} %get-tuple-element.61), channel_id=1, source_target_pairs={{0,96},{32,0},{64,32},{96,64},{1,97},{33,1},{65,33},{97,65},{2,98}... | collective-permute-start | bytes 393224 | tf_op jit(solution)/shard_map/ppermute | solution.py:32
  42.1 9.4 %collective-permute-start.16 = (bf16[256,256]{1,0:T(8,128)(2,1)}, bf16[256,256]{1,0:T(8,128)(2,1)S(1)}, u32[]{:S(2)}, u32[]{:S(2)}) collective-permute-start(bf16[256,256]{1,0:T(8,128)(2,1)} %get-tuple-element.62), channel_id=1, source_target_pairs={{0,64},{32,96},{64,0},{96,32},{1,65},{33,97},{65,1},{97,33},{2,66}... | collective-permute-start | bytes 393224 | tf_op jit(solution)/shard_map/ppermute | solution.py:32
  43.7 9.4 %collective-permute-start.17 = (bf16[256,256]{1,0:T(8,128)(2,1)}, bf16[256,256]{1,0:T(8,128)(2,1)}, u32[]{:S(2)}, u32[]{:S(2)}) collective-permute-start(bf16[256,256]{1,0:T(8,128)(2,1)} %get-tuple-element.63), channel_id=1, source_target_pairs={{0,32},{32,64},{64,96},{96,0},{1,33},{33,65},{65,97},{97,1},{2,34}... | collective-permute-start | bytes 393224 | tf_op jit(solution)/shard_map/ppermute | solution.py:32
  49.1 7.0 %collective-permute-start.14 = (bf16[256,256]{1,0:T(8,128)(2,1)}, bf16[256,256]{1,0:T(8,128)(2,1)}, u32[]{:S(2)}, u32[]{:S(2)}) collective-permute-start(bf16[256,256]{1,0:T(8,128)(2,1)} %add_convert_fusion.1), channel_id=1, source_target_pairs={{0,16},{16,0},{1,17},{17,1},{2,18},{18,2},{3,19},{19,3},{4,20},{20... | collective-permute-start | bytes 393224 | tf_op jit(solution)/shard_map/ppermute | solution.py:32
  56.1 2.9 %copy-start = (bf16[5120,640]{1,0:T(8,128)(2,1)S(1)}, bf16[5120,640]{1,0:T(8,128)(2,1)}, u32[]{:S(2)}) copy-start(bf16[5120,640]{1,0:T(8,128)(2,1)} %wq.3) | copy-start | bytes 19660804
  59.0 1.3 %copy-start.1 = (bf16[5120,128]{1,0:T(8,128)(2,1)S(1)}, bf16[5120,128]{1,0:T(8,128)(2,1)}, u32[]{:S(2)}) copy-start(bf16[5120,128]{1,0:T(8,128)(2,1)} %wk.3) | copy-start | bytes 3932164
  60.3 1.3 %copy-start.3 = (bf16[5120,128]{1,0:T(8,128)(2,1)S(1)}, bf16[5120,128]{1,0:T(8,128)(2,1)}, u32[]{:S(2)}) copy-start(bf16[5120,128]{1,0:T(8,128)(2,1)} %wv.3) | copy-start | bytes 3932164
  61.6 13.5 %slice-start.1 = ((s8[6553600]{0:T(1024)(128)(4,1)}), s8[4194304]{0:T(1024)(128)(4,1)S(1)}, s32[]{:S(2)}) async-start(s8[6553600]{0:T(1024)(128)(4,1)} %bitcast.5), calls=%async_computation.1 | async-start | bytes 8388608
  61.6 13.5 %copy-start.2 = (bf16[5120,128]{1,0:T(8,128)(2,1)S(1)}, bf16[5120,128]{1,0:T(8,128)(2,1)}, u32[]{:S(2)}) copy-start(bf16[5120,128]{1,0:T(8,128)(2,1)} %wk.3) | copy-start | bytes 3932164
  61.6 13.5 %copy-start.4 = (bf16[5120,128]{1,0:T(8,128)(2,1)S(1)}, bf16[5120,128]{1,0:T(8,128)(2,1)}, u32[]{:S(2)}) copy-start(bf16[5120,128]{1,0:T(8,128)(2,1)} %wv.3) | copy-start | bytes 3932164
  64.5 10.7 %collective-permute-start.18 = (bf16[2,640,256]{2,1,0:T(8,128)(2,1)S(1)}, bf16[2,640,256]{2,1,0:T(8,128)(2,1)S(1)}, u32[]{:S(2)}, u32[]{:S(2)}) collective-permute-start(bf16[2,640,256]{2,1,0:T(8,128)(2,1)S(1)} %get-tuple-element.65), channel_id=1, source_target_pairs={{0,1},{1,0},{2,3},{3,2},{4,5},{5,4},{6,7},{7,6},{8,10},{9,11},{10,... | collective-permute-start | bytes 1966088 | tf_op jit(solution)/shard_map/ppermute | solution.py:317
  65.6 16.6 %collective-permute-start.19 = (bf16[2,640,256]{2,1,0:T(8,128)(2,1)S(1)}, bf16[2,640,256]{2,1,0:T(8,128)(2,1)S(1)}, u32[]{:S(2)}, u32[]{:S(2)}) collective-permute-start(bf16[2,640,256]{2,1,0:T(8,128)(2,1)S(1)} %get-tuple-element.69), channel_id=1, source_target_pairs={{0,1},{1,0},{2,3},{3,2},{4,5},{5,4},{6,7},{7,6},{8,14},{9,15},{10,... | collective-permute-start | bytes 1966088 | tf_op jit(solution)/shard_map/ppermute | solution.py:317
  66.6 15.6 %collective-permute-start.20 = (bf16[2,640,256]{2,1,0:T(8,128)(2,1)S(1)}, bf16[2,640,256]{2,1,0:T(8,128)(2,1)S(1)}, u32[]{:S(2)}, u32[]{:S(2)}) collective-permute-start(bf16[2,640,256]{2,1,0:T(8,128)(2,1)S(1)} %get-tuple-element.70), channel_id=1, source_target_pairs={{8,12},{9,13},{10,14},{11,15},{12,8},{13,9},{14,10},{15,11},{24,28... | collective-permute-start | bytes 1966088 | tf_op jit(solution)/shard_map/ppermute | solution.py:317
  82.4 9.5 %collective-permute-start.21 = (bf16[640,256]{1,0:T(8,128)(2,1)S(1)}, bf16[640,256]{1,0:T(8,128)(2,1)S(1)}, u32[]{:S(2)}, u32[]{:S(2)}) collective-permute-start(bf16[640,256]{1,0:T(8,128)(2,1)S(1)} %get-tuple-element.72), channel_id=1, source_target_pairs={{0,2},{1,3},{2,4},{3,5},{4,6},{5,7},{6,0},{7,1},{8,9},{9,8},{10,11... | collective-permute-start | bytes 983048 | tf_op jit(solution)/shard_map/ppermute | solution.py:317
  84.0 11.3 %collective-permute-start.22 = (bf16[640,256]{1,0:T(8,128)(2,1)S(1)}, bf16[640,256]{1,0:T(8,128)(2,1)S(1)}, u32[]{:S(2)}, u32[]{:S(2)}) collective-permute-start(bf16[640,256]{1,0:T(8,128)(2,1)S(1)} %get-tuple-element.73), channel_id=1, source_target_pairs={{0,4},{1,5},{2,6},{3,7},{4,0},{5,1},{6,2},{7,3},{16,20},{17,21},{1... | collective-permute-start | bytes 983048 | tf_op jit(solution)/shard_map/ppermute | solution.py:317
  88.6 9.0 %collective-permute-start.23 = (bf16[640,256]{1,0:T(8,128)(2,1)S(1)}, bf16[640,256]{1,0:T(8,128)(2,1)S(1)}, u32[]{:S(2)}, u32[]{:S(2)}) collective-permute-start(bf16[640,256]{1,0:T(8,128)(2,1)S(1)} %get-tuple-element.74), channel_id=1, source_target_pairs={{0,6},{1,7},{2,0},{3,1},{4,2},{5,3},{6,4},{7,5},{16,22},{17,23},{1... | collective-permute-start | bytes 983048 | tf_op jit(solution)/shard_map/ppermute | solution.py:317

commit v8 on v7

--- a/solution.py
+++ b/solution.py
@@ -249,7 +249,7 @@
         ),
         in_specs=vmem(3),
         out_specs=tuple(vmem(5)),
-        compiler_params=pltpu.CompilerParams(vmem_limit_bytes=12 << 20),
+        compiler_params=pltpu.CompilerParams(vmem_limit_bytes=6 << 20),
         cost_estimate=pl.CostEstimate(flops=1000000, bytes_accessed=10000, transcendentals=0),
         name="prep",
     )(joined, cos, sin)
@@ -317,20 +317,31 @@
     return lax.ppermute(x, ("core", "x", "zl"), by_core(offsets))
 
 
-def make_blocks(tp, core, first, count, grads, wq, wk, wv, put):
+def first_kernel(
+    tp, core, own, across, near1, near2, near3, cos, sin, qg, wq, wk, wv,
+    out1, out2, out3, kept, grads, weights, sem,
+):
     x, zl = lax.shift_right_logical(tp[0], 1), tp[0] & 1
-    for i in range(count):
-        (x0, z0), (x1, z1) = ORDERS[0][first + i], ORDERS[1][first + i]
+
+    def fetch(i):
+        (x0, z0), (x1, z1) = ORDERS[0][i], ORDERS[1][i]
         to_x = (x + jnp.where(core[0] == 0, x0, x1)) & 3
         to_z = zl ^ jnp.where(core[0] == 0, z0, z1)
         rows = pl.ds(pl.multiple_of((2 * to_x + to_z) * STEP_ROWS, STEP_ROWS), STEP_ROWS)
-        weights = jnp.concatenate([wq[rows, :], wk[rows, :], wv[rows, :]], 1)
-        put(i, jnp.dot(weights, grads[...], preferred_element_type=f32))
-
-
-def first_kernel(
-    tp, core, own, across, near1, near2, near3, cos, sin, qg, wq, wk, wv, out1, out2, out3, grads
-):
+        slot = i % 3
+        return [
+            pltpu.make_async_copy(
+                source.at[rows, :],
+                weights.at[slot, :, pl.ds(start, source.shape[1])],
+                sem.at[slot, k],
+            )
+            for k, (source, start) in enumerate(((wq, 0), (wk, ROWS), (wv, ROWS + HEAD)))
+        ]
+
+    flights = [fetch(i) for i in range(8)]
+    for flight in flights[:3]:
+        for copy in flight:
+            copy.start()
     total = own[...].astype(f32) + across[...].astype(f32)
     for near in (near1, near2, near3):
         total += near[...].astype(f32)
@@ -340,33 +351,19 @@
     grads[:ROWS, :] = qg[...]
     grads[ROWS : ROWS + HEAD, :] = key_grad.T.astype(bf16)
     grads[ROWS + HEAD :, :] = total[:, HEAD:].T.astype(bf16)
-
-    def put_in(out):
-        def put(i, block):
-            out[i] = block.astype(bf16)
-
-        return put
-
-    make_blocks(tp, core, 0, 2, grads, wq, wk, wv, put_in(out1))
-    make_blocks(tp, core, 2, 2, grads, wq, wk, wv, put_in(out2))
-
-    @pl.when(core[0] != 0)
-    def _():
-        make_blocks(tp, core, 6, 2, grads, wq, wk, wv, put_in(out3))
-
-
-def kept_kernel(tp, core, grads, wq, wk, wv, kept):
-    def put(i, block):
-        kept[i] = block
-
-    def put_more(i, block):
-        kept[2 + i] = block
-
-    make_blocks(tp, core, 4, 2, grads, wq, wk, wv, put)
-
-    @pl.when(core[0] == 0)
-    def _():
-        make_blocks(tp, core, 6, 2, grads, wq, wk, wv, put_more)
+    for i in range(8):
+        for copy in flights[i]:
+            copy.wait()
+        block = jnp.dot(weights[i % 3], grads[...], preferred_element_type=f32)
+        if i < 4:
+            (out1, out2)[i // 2][i % 2] = block.astype(bf16)
+        else:
+            kept[i - 4] = block
+        if i >= 6:
+            out3[i - 6] = block.astype(bf16)
+        if i + 3 < 8:
+            for copy in flights[i + 3]:
+                copy.start()
 
 
 def middle_kernel(core, kept, got1, got2, got3, base, out1, out2, out3):
@@ -400,17 +397,20 @@
         out[...] = (base[...] + got1[...].astype(f32)).astype(bf16)
 
 
-def whole_call(kernel, name, flops, outs, scalars, *operands):
+def whole_call(kernel, name, outs, scalars, *operands, large=(), scratch=()):
     outs = tuple(jax.ShapeDtypeStruct(shape, dtype) for shape, dtype in outs)
     return pl.pallas_call(
         kernel,
         out_shape=outs,
-        in_specs=[pl.BlockSpec(memory_space=pltpu.SMEM)] * len(scalars) + vmem(len(operands)),
+        in_specs=[pl.BlockSpec(memory_space=pltpu.SMEM)] * len(scalars)
+        + vmem(len(operands))
+        + [pl.BlockSpec(memory_space=pl.ANY)] * len(large),
         out_specs=tuple(vmem(len(outs))),
-        compiler_params=pltpu.CompilerParams(vmem_limit_bytes=16 << 20),
-        cost_estimate=pl.CostEstimate(flops=flops, bytes_accessed=10000, transcendentals=0),
+        scratch_shapes=scratch,
+        compiler_params=pltpu.CompilerParams(vmem_limit_bytes=(48 if large else 10) << 20),
+        cost_estimate=pl.CostEstimate(flops=1000000, bytes_accessed=10000, transcendentals=0),
         name=name,
-    )(*scalars, *operands)
+    )(*scalars, *operands, *large)
 
 
 def project_and_sum(own, across, near, cos, sin, qg, wq, wk, wv):
@@ -418,25 +418,25 @@
     core = lax.axis_index("core").reshape(1)
     one, two, four = ((n, STEP_ROWS, TOK) for n in (1, 2, 4))
     one = one[1:]
-    first, second, third, grads = whole_call(
+    first, second, third, kept = whole_call(
         first_kernel,
         "first",
-        1000000,
-        [(two, bf16), (two, bf16), (two, bf16), ((ROWS + 2 * HEAD, TOK), bf16)],
+        [(two, bf16), (two, bf16), (two, bf16), (four, f32)],
         (tp, core),
-        own, across, *near, cos, sin, qg, wq, wk, wv,
+        own, across, *near, cos, sin, qg,
+        large=(wq, wk, wv),
+        scratch=[
+            pltpu.VMEM((ROWS + 2 * HEAD, TOK), bf16),
+            pltpu.VMEM((3, STEP_ROWS, ROWS + 2 * HEAD), bf16),
+            pltpu.SemaphoreType.DMA((3, 3)),
+        ],
     )
     got1 = send(first, (0, 1), (1, 0))
     got2 = send(second, (0, 1), (3, 0))
     got3 = send(third, None, (2, 0))
-    got1, grads = lax.optimization_barrier((got1, grads))
-    (kept,) = whole_call(
-        kept_kernel, "kept", 1000000, [(four, f32)], (tp, core), grads, wq, wk, wv
-    )
     base, out1, out2, out3 = whole_call(
         middle_kernel,
         "middle",
-        1000000,
         [(one, f32), (one, bf16), (one, bf16), (one, bf16)],
         (core,),
         kept, got1, got2, got3,
@@ -444,7 +444,7 @@
     got1 = send(out1, (1, 0), (0, 1))
     got2 = send(out2, (2, 0), None)
     got3 = send(out3, (3, 0), None)
-    return whole_call(last_kernel, "last", 1000000, [(one, bf16)], (core,), base, got1, got2, got3)[0]
+    return whole_call(last_kernel, "last", [(one, bf16)], (core,), base, got1, got2, got3)[0]
 
 
 def local(

time: 99.1 us -> 103 us (1.039)
  Pallas kernels: 12.3 us -> 18.3 us
  local copies, waits for them, and re-layouts: 8.39 us -> 4.4 us
  waiting for transfers between devices: 39 us -> 40.7 us
    pallas_call x4 -> x3, Pallas kernels: 5.61 us -> 11.6 us  [whole_call(): pl.pallas_call(kernel, out_shape=outs, in_specs=[pl.BlockSpec(memory_spac...]
    unnamed x36 -> x28, local copies, waits for them, and re-layouts: 7.53 us -> 3.57 us
    ppermute x6, waiting for transfers between devices: 18.8 us -> 20.5 us  [send(): return lax.ppermute(x, ('core', 'x', 'zl'), by_core(offsets))]
  transfers between devices with their start and end apart: 24 -> 24, of which waited for: 14 -> 14; matrix products, arithmetic and copies ran while one was open for 2% -> 2% of each run, Pallas kernels for 3% -> 1%
where the time goes in v8:
time: 103 us; the launch traced here: 102 us
  waiting for transfers between devices  40.7 us (40%)
  starting transfers between devices  36.2 us (35%)
  Pallas kernels  18.3 us (18%)
  local copies, waits for them, and re-layouts  4.4 us (4%)
  other arithmetic  2.28 us (2%)
    ppermute x18, starting transfers between devices, shift(): return lax.ppermute(x, axes, perm)  23.8 us
    ppermute x6, waiting for transfers between devices, send(): return lax.ppermute(x, ('core', 'x', 'zl'), by_core(offsets))  20.5 us
    ppermute x18, waiting for transfers between devices, shift(): return lax.ppermute(x, axes, perm)  20.2 us
    ppermute x6, starting transfers between devices, send(): return lax.ppermute(x, ('core', 'x', 'zl'), by_core(offsets))  12.3 us
    pallas_call x3, Pallas kernels, whole_call(): pl.pallas_call(kernel, out_shape=outs, in_specs=[pl.BlockSpec(memory_spac...  11.6 us
    pallas_call x1, Pallas kernels, attention(): pl.pallas_call(attention_kernel, out_shape=(early, early, late, late, s((...  3.7 us
    unnamed x28, local copies, waits for them, and re-layouts  3.57 us
    pallas_call x1, Pallas kernels, make_block(): pl.pallas_call(block_kernel, out_shape=(s((TOK, HEAD), f32), s((TOK, HEAD...  2.17 us
  transfers between devices with their start and end apart: 24, of which 14 were waited for; matrix products, arithmetic and copies ran while one was open for 2% of the time, Pallas kernels for 1%

profile of v8, /device:TPU:0, one launch (start us, length us, event | category | flops | bytes accessed | tf_op | source)
XLA Modules:
  0.0 102.2 jit_solution(11449486949054090322)
XLA Ops:
  0.0 2.2 %block.1 = (f32[256,128]{1,0:T(8,128)}, f32[256,128]{1,0:T(8,128)}, bf16[256,256]{1,0:T(8,128)(2,1)}) custom-call(bf16[256,128]{1,0:T(8,128)(2,1)} %key.1, bf16[256,128]{1,0:T(8,128)(2,1)} %value.1, s32[2,1,128]{2,1,0:T(1,128)} %bitcast.6, f32[1,128]{1,0:T(1,128)} %constant.25.clone.inverse), custom_call_target="tpu_custom_call" | custom-call | flops 5000000 | bytes 700000 | tf_op jit(solution)/shard_map/block/pallas_call | solution.py:286
  2.2 4.0 %collective-permute-start = (bf16[256,256]{1,0:T(8,128)(2,1)}, bf16[256,256]{1,0:T(8,128)(2,1)S(1)}, u32[]{:S(2)}, u32[]{:S(2)}) collective-permute-start(bf16[256,256]{1,0:T(8,128)(2,1)} %get-tuple-element.48), channel_id=1, source_target_pairs={{0,16},{16,0},{1,17},{17,1},{2,18},{18,2},{3,19},{19,3},{4,20},{20... | collective-permute-start | bytes 393224 | tf_op jit(solution)/shard_map/ppermute | solution.py:32
  6.2 1.2 %pad_maximum_fusion.joined = bf16[256,1920]{1,0:T(8,128)(2,1)S(1)} fusion(bf16[256,640]{1,0:T(8,128)(2,1)} %param.16, bf16[256,640]{1,0:T(8,128)(2,1)} %param.17, bf16[256,640]{1,0:T(8,128)(2,1)} %param.13), kind=kLoop, calls=%fused_computation.1 | loop fusion | flops 2949120 | bytes 1966080 | tf_op jit(solution)/shard_map/concatenate | solution.py:458
  7.5 1.6 %collective-permute-start.1 = (bf16[256,256]{1,0:T(8,128)(2,1)S(1)}, bf16[256,256]{1,0:T(8,128)(2,1)S(1)}, u32[]{:S(2)}, u32[]{:S(2)}) collective-permute-start(bf16[256,256]{1,0:T(8,128)(2,1)S(1)} %copy-done.10), channel_id=1, source_target_pairs={{0,32},{32,64},{64,96},{96,0},{1,33},{33,65},{65,97},{97,1},{2,34}... | collective-permute-start | bytes 393224 | tf_op jit(solution)/shard_map/ppermute | solution.py:32
  9.2 1.7 %collective-permute-start.3 = (bf16[256,256]{1,0:T(8,128)(2,1)S(1)}, bf16[256,256]{1,0:T(8,128)(2,1)S(1)}, u32[]{:S(2)}, u32[]{:S(2)}) collective-permute-start(bf16[256,256]{1,0:T(8,128)(2,1)S(1)} %copy-done.10), channel_id=1, source_target_pairs={{0,96},{32,0},{64,32},{96,64},{1,97},{33,1},{65,33},{97,65},{2,98}... | collective-permute-start | bytes 393224 | tf_op jit(solution)/shard_map/ppermute | solution.py:32
  10.8 2.0 %collective-permute-start.2 = (bf16[256,256]{1,0:T(8,128)(2,1)S(1)}, bf16[256,256]{1,0:T(8,128)(2,1)S(1)}, u32[]{:S(2)}, u32[]{:S(2)}) collective-permute-start(bf16[256,256]{1,0:T(8,128)(2,1)S(1)} %copy-done.10), channel_id=1, source_target_pairs={{0,64},{32,96},{64,0},{96,32},{1,65},{33,97},{65,1},{97,33},{2,66}... | collective-permute-start | bytes 393224 | tf_op jit(solution)/shard_map/ppermute | solution.py:32
  12.8 1.1 %collective-permute-start.7 = (bf16[256,256]{1,0:T(8,128)(2,1)S(1)}, bf16[256,256]{1,0:T(8,128)(2,1)S(1)}, u32[]{:S(2)}, u32[]{:S(2)}) collective-permute-start(bf16[256,256]{1,0:T(8,128)(2,1)S(1)} %collective-permute-done), channel_id=1, source_target_pairs={{0,96},{32,0},{64,32},{96,64},{1,97},{33,1},{65,33},{97,65},{2,98}... | collective-permute-start | bytes 393224 | tf_op jit(solution)/shard_map/ppermute | solution.py:32
  14.0 1.7 %collective-permute-start.6 = (bf16[256,256]{1,0:T(8,128)(2,1)S(1)}, bf16[256,256]{1,0:T(8,128)(2,1)S(1)}, u32[]{:S(2)}, u32[]{:S(2)}) collective-permute-start(bf16[256,256]{1,0:T(8,128)(2,1)S(1)} %collective-permute-done), channel_id=1, source_target_pairs={{0,64},{32,96},{64,0},{96,32},{1,65},{33,97},{65,1},{97,33},{2,66}... | collective-permute-start | bytes 393224 | tf_op jit(solution)/shard_map/ppermute | solution.py:32
  15.7 0.2 collective-permute-start.5
  15.9 3.1 %collective-permute-done.2 = bf16[256,256]{1,0:T(8,128)(2,1)S(1)} collective-permute-done((bf16[256,256]{1,0:T(8,128)(2,1)S(1)}, bf16[256,256]{1,0:T(8,128)(2,1)S(1)}, u32[]{:S(2)}, u32[]{:S(2)}) %collective-permute-start.2) | collective-permute-done | bytes 131104 | tf_op jit(solution)/shard_map/ppermute | solution.py:32
  19.1 4.3 %collective-permute-done.5 = bf16[256,256]{1,0:T(8,128)(2,1)S(1)} collective-permute-done((bf16[256,256]{1,0:T(8,128)(2,1)S(1)}, bf16[256,256]{1,0:T(8,128)(2,1)S(1)}, u32[]{:S(2)}, u32[]{:S(2)}) %collective-permute-start.5) | collective-permute-done | bytes 131104 | tf_op jit(solution)/shard_map/ppermute | solution.py:32
  23.6 0.8 prep.1
  24.4 0.9 collective-permute-done.8.late_other
  25.3 0.7 copy-done.5
  26.1 1.0 copy-done.6
  27.1 3.7 %attention.1 = (bf16[1280,256]{1,0:T(8,128)(2,1)S(1)}, bf16[1280,256]{1,0:T(8,128)(2,1)S(1)}, bf16[768,256]{1,0:T(8,128)(2,1)S(1)}, bf16[768,256]{1,0:T(8,128)(2,1)S(1)}, bf16[640,256]{1,0:T(8,128)(2,1)S(1)}) custom-call(s32[32,32]{1,0:T(8,128)S(1)} %copy-done.7, s32[1]{0:T(128)} %bitcast.2.info, s32[32,1,128]{2,1,0:T(1,128)S(1)} %bitcast.5, ...), custom_call_target="tpu_custom_call" | custom-call | flops 2000000000 | bytes 8000000 | tf_op jit(solution)/shard_map/attention/pallas_call | solution.py:261
  30.8 1.3 %collective-permute-start.10 = (bf16[768,256]{1,0:T(8,128)(2,1)S(1)}, bf16[768,256]{1,0:T(8,128)(2,1)S(1)}, u32[]{:S(2)}, u32[]{:S(2)}) collective-permute-start(bf16[768,256]{1,0:T(8,128)(2,1)S(1)} %get-tuple-element.53), channel_id=1, source_target_pairs={{0,8},{8,0},{1,9},{9,1},{2,10},{10,2},{3,11},{11,3},{4,12},{12,4},... | collective-permute-start | bytes 1179656 | tf_op jit(solution)/shard_map/ppermute | solution.py:32
  32.1 0.1 collective-permute-start.9
  32.2 1.3 %collective-permute-done.10 = bf16[768,256]{1,0:T(8,128)(2,1)S(1)} collective-permute-done((bf16[768,256]{1,0:T(8,128)(2,1)S(1)}, bf16[768,256]{1,0:T(8,128)(2,1)S(1)}, u32[]{:S(2)}, u32[]{:S(2)}) %collective-permute-start.10) | collective-permute-done | bytes 393248 | tf_op jit(solution)/shard_map/ppermute | solution.py:32
  33.4 0.1 add_convert_fusion
  33.6 0.8 collective-permute-done.9
  34.4 0.2 fusion
  34.6 0.7 fusion.2
  35.4 2.1 %collective-permute-start.11 = (bf16[256,256]{1,0:T(8,128)(2,1)S(1)}, bf16[256,256]{1,0:T(8,128)(2,1)S(1)}, u32[]{:S(2)}, u32[]{:S(2)}) collective-permute-start(bf16[256,256]{1,0:T(8,128)(2,1)S(1)} %get-tuple-element.56), channel_id=1, source_target_pairs={{0,96},{32,0},{64,32},{96,64},{1,97},{33,1},{65,33},{97,65},{2,98}... | collective-permute-start | bytes 393224 | tf_op jit(solution)/shard_map/ppermute | solution.py:32
  37.4 1.2 %collective-permute-start.12 = (bf16[256,256]{1,0:T(8,128)(2,1)S(1)}, bf16[256,256]{1,0:T(8,128)(2,1)S(1)}, u32[]{:S(2)}, u32[]{:S(2)}) collective-permute-start(bf16[256,256]{1,0:T(8,128)(2,1)S(1)} %get-tuple-element.57), channel_id=1, source_target_pairs={{0,64},{32,96},{64,0},{96,32},{1,65},{33,97},{65,1},{97,33},{2,66}... | collective-permute-start | bytes 393224 | tf_op jit(solution)/shard_map/ppermute | solution.py:32
  38.7 3.2 %collective-permute-start.15 = (bf16[256,256]{1,0:T(8,128)(2,1)}, bf16[256,256]{1,0:T(8,128)(2,1)}, u32[]{:S(2)}, u32[]{:S(2)}) collective-permute-start(bf16[256,256]{1,0:T(8,128)(2,1)} %get-tuple-element.59), channel_id=1, source_target_pairs={{0,96},{32,0},{64,32},{96,64},{1,97},{33,1},{65,33},{97,65},{2,98}... | collective-permute-start | bytes 393224 | tf_op jit(solution)/shard_map/ppermute | solution.py:32
  41.9 1.1 %collective-permute-start.16 = (bf16[256,256]{1,0:T(8,128)(2,1)}, bf16[256,256]{1,0:T(8,128)(2,1)}, u32[]{:S(2)}, u32[]{:S(2)}) collective-permute-start(bf16[256,256]{1,0:T(8,128)(2,1)} %get-tuple-element.60), channel_id=1, source_target_pairs={{0,64},{32,96},{64,0},{96,32},{1,65},{33,97},{65,1},{97,33},{2,66}... | collective-permute-start | bytes 393224 | tf_op jit(solution)/shard_map/ppermute | solution.py:32
  43.0 0.6 collective-permute-done.11
  43.6 1.7 %collective-permute-done.12 = bf16[256,256]{1,0:T(8,128)(2,1)S(1)} collective-permute-done((bf16[256,256]{1,0:T(8,128)(2,1)S(1)}, bf16[256,256]{1,0:T(8,128)(2,1)S(1)}, u32[]{:S(2)}, u32[]{:S(2)}) %collective-permute-start.12) | collective-permute-done | bytes 131104 | tf_op jit(solution)/shard_map/ppermute | solution.py:32
  45.3 2.9 %collective-permute-done.13 = bf16[256,256]{1,0:T(8,128)(2,1)S(1)} collective-permute-done((bf16[256,256]{1,0:T(8,128)(2,1)S(1)}, bf16[256,256]{1,0:T(8,128)(2,1)S(1)}, u32[]{:S(2)}, u32[]{:S(2)}) %collective-permute-start.13) | collective-permute-done | bytes 131104 | tf_op jit(solution)/shard_map/ppermute | solution.py:32
  48.2 0.7 add_convert_fusion.1
  48.9 2.3 %collective-permute-start.14 = (bf16[256,256]{1,0:T(8,128)(2,1)}, bf16[256,256]{1,0:T(8,128)(2,1)}, u32[]{:S(2)}, u32[]{:S(2)}) collective-permute-start(bf16[256,256]{1,0:T(8,128)(2,1)} %add_convert_fusion.1), channel_id=1, source_target_pairs={{0,16},{16,0},{1,17},{17,1},{2,18},{18,2},{3,19},{19,3},{4,20},{20... | collective-permute-start | bytes 393224 | tf_op jit(solution)/shard_map/ppermute | solution.py:32
  51.2 1.7 %collective-permute-done.17.near3 = bf16[256,256]{1,0:T(8,128)(2,1)} collective-permute-done((bf16[256,256]{1,0:T(8,128)(2,1)}, bf16[256,256]{1,0:T(8,128)(2,1)}, u32[]{:S(2)}, u32[]{:S(2)}) %collective-permute-start.17) | collective-permute-done | bytes 131104 | tf_op jit(solution)/shard_map/ppermute | solution.py:32
  52.9 3.0 %collective-permute-done.14.across = bf16[256,256]{1,0:T(8,128)(2,1)} collective-permute-done((bf16[256,256]{1,0:T(8,128)(2,1)}, bf16[256,256]{1,0:T(8,128)(2,1)}, u32[]{:S(2)}, u32[]{:S(2)}) %collective-permute-start.14) | collective-permute-done | bytes 131104 | tf_op jit(solution)/shard_map/ppermute | solution.py:32
  55.9 10.6 %first.1 = (bf16[2,640,256]{2,1,0:T(8,128)(2,1)S(1)}, bf16[2,640,256]{2,1,0:T(8,128)(2,1)S(1)}, bf16[2,640,256]{2,1,0:T(8,128)(2,1)S(1)}, f32[4,640,256]{2,1,0:T(8,128)}) custom-call(s32[1]{0:T(128)} %bitcast.1.tp, s32[1]{0:T(128)} %bitcast.core, f32[256,256]{1,0:T(8,128)S(1)} %get-tuple-element.54.own, bf16[256,256]{1,0:T(8,128)(2,1)} %collective-permute-done.14.across, ...), custom_call_target="tpu_custom_call" | custom-call | flops 1000000 | bytes 10000 | tf_op jit(solution)/shard_map/first/pallas_call | solution.py:402
  66.5 1.1 %collective-permute-start.18 = (bf16[2,640,256]{2,1,0:T(8,128)(2,1)S(1)}, bf16[2,640,256]{2,1,0:T(8,128)(2,1)S(1)}, u32[]{:S(2)}, u32[]{:S(2)}) collective-permute-start(bf16[2,640,256]{2,1,0:T(8,128)(2,1)S(1)} %get-tuple-element.64), channel_id=1, source_target_pairs={{0,1},{1,0},{2,3},{3,2},{4,5},{5,4},{6,7},{7,6},{8,10},{9,11},{10,... | collective-permute-start | bytes 1966088 | tf_op jit(solution)/shard_map/ppermute | solution.py:317
  67.6 1.0 collective-permute-start.19
  68.6 0.7 collective-permute-start.20
  69.3 7.9 %collective-permute-done.18.got1 = bf16[2,640,256]{2,1,0:T(8,128)(2,1)S(1)} collective-permute-done((bf16[2,640,256]{2,1,0:T(8,128)(2,1)S(1)}, bf16[2,640,256]{2,1,0:T(8,128)(2,1)S(1)}, u32[]{:S(2)}, u32[]{:S(2)}) %collective-permute-start.18) | collective-permute-done | bytes 655392 | tf_op jit(solution)/shard_map/ppermute | solution.py:317
  77.2 7.0 %collective-permute-done.19.got2 = bf16[2,640,256]{2,1,0:T(8,128)(2,1)S(1)} collective-permute-done((bf16[2,640,256]{2,1,0:T(8,128)(2,1)S(1)}, bf16[2,640,256]{2,1,0:T(8,128)(2,1)S(1)}, u32[]{:S(2)}, u32[]{:S(2)}) %collective-permute-start.19) | collective-permute-done | bytes 655392 | tf_op jit(solution)/shard_map/ppermute | solution.py:317
  84.2 1.7 %copy-done = f32[4,640,256]{2,1,0:T(8,128)S(1)} copy-done((f32[4,640,256]{2,1,0:T(8,128)S(1)}, f32[4,640,256]{2,1,0:T(8,128)}, u32[]{:S(2)}) %copy-start) | copy-done | bytes 2621464
  85.9 0.2 middle.1
  86.2 1.6 %collective-permute-start.21 = (bf16[640,256]{1,0:T(8,128)(2,1)S(1)}, bf16[640,256]{1,0:T(8,128)(2,1)S(1)}, u32[]{:S(2)}, u32[]{:S(2)}) collective-permute-start(bf16[640,256]{1,0:T(8,128)(2,1)S(1)} %get-tuple-element.68), channel_id=1, source_target_pairs={{0,2},{1,3},{2,4},{3,5},{4,6},{5,7},{6,0},{7,1},{8,9},{9,8},{10,11... | collective-permute-start | bytes 983048 | tf_op jit(solution)/shard_map/ppermute | solution.py:317
  87.7 4.6 %collective-permute-start.22 = (bf16[640,256]{1,0:T(8,128)(2,1)S(1)}, bf16[640,256]{1,0:T(8,128)(2,1)S(1)}, u32[]{:S(2)}, u32[]{:S(2)}) collective-permute-start(bf16[640,256]{1,0:T(8,128)(2,1)S(1)} %get-tuple-element.69), channel_id=1, source_target_pairs={{0,4},{1,5},{2,6},{3,7},{4,0},{5,1},{6,2},{7,3},{16,20},{17,21},{1... | collective-permute-start | bytes 983048 | tf_op jit(solution)/shard_map/ppermute | solution.py:317
  92.4 3.3 %collective-permute-start.23 = (bf16[640,256]{1,0:T(8,128)(2,1)S(1)}, bf16[640,256]{1,0:T(8,128)(2,1)S(1)}, u32[]{:S(2)}, u32[]{:S(2)}) collective-permute-start(bf16[640,256]{1,0:T(8,128)(2,1)S(1)} %get-tuple-element.70), channel_id=1, source_target_pairs={{0,6},{1,7},{2,0},{3,1},{4,2},{5,3},{6,4},{7,5},{16,22},{17,23},{1... | collective-permute-start | bytes 983048 | tf_op jit(solution)/shard_map/ppermute | solution.py:317
  95.7 3.3 %collective-permute-done.22.got2 = bf16[640,256]{1,0:T(8,128)(2,1)S(1)} collective-permute-done((bf16[640,256]{1,0:T(8,128)(2,1)S(1)}, bf16[640,256]{1,0:T(8,128)(2,1)S(1)}, u32[]{:S(2)}, u32[]{:S(2)}) %collective-permute-start.22) | collective-permute-done | bytes 327712 | tf_op jit(solution)/shard_map/ppermute | solution.py:317
  99.0 2.3 %collective-permute-done.23.got3 = bf16[640,256]{1,0:T(8,128)(2,1)S(1)} collective-permute-done((bf16[640,256]{1,0:T(8,128)(2,1)S(1)}, bf16[640,256]{1,0:T(8,128)(2,1)S(1)}, u32[]{:S(2)}, u32[]{:S(2)}) %collective-permute-start.23) | collective-permute-done | bytes 327712 | tf_op jit(solution)/shard_map/ppermute | solution.py:317
  101.3 0.9 last.1
  (43 shorter events, 0.4 us)
Async XLA Ops:
  2.2 5.3 %copy-start.10 = (bf16[256,256]{1,0:T(8,128)(2,1)S(1)}, bf16[256,256]{1,0:T(8,128)(2,1)}, u32[]{:S(2)}) copy-start(bf16[256,256]{1,0:T(8,128)(2,1)} %get-tuple-element.48) | copy-start | bytes 393220
  2.2 21.4 %copy-start.3 = (f32[256,128]{1,0:T(8,128)S(1)}, f32[256,128]{1,0:T(8,128)}, u32[]{:S(2)}) copy-start(f32[256,128]{1,0:T(8,128)} %get-tuple-element.41.cos) | copy-start | bytes 393220
  2.2 21.4 %copy-start.4 = (f32[256,128]{1,0:T(8,128)S(1)}, f32[256,128]{1,0:T(8,128)}, u32[]{:S(2)}) copy-start(f32[256,128]{1,0:T(8,128)} %get-tuple-element.42.sin) | copy-start | bytes 393220
  2.2 10.6 %collective-permute-start = (bf16[256,256]{1,0:T(8,128)(2,1)}, bf16[256,256]{1,0:T(8,128)(2,1)S(1)}, u32[]{:S(2)}, u32[]{:S(2)}) collective-permute-start(bf16[256,256]{1,0:T(8,128)(2,1)} %get-tuple-element.48), channel_id=1, source_target_pairs={{0,16},{16,0},{1,17},{17,1},{2,18},{18,2},{3,19},{19,3},{4,20},{20... | collective-permute-start | bytes 393224 | tf_op jit(solution)/shard_map/ppermute | solution.py:32
  7.5 18.6 %copy-start.7 = (s32[32,32]{1,0:T(8,128)S(1)}, s32[32,32]{1,0:T(8,128)}, u32[]{:S(2)}) copy-start(s32[32,32]{1,0:T(8,128)} %mask.1) | copy-start | bytes 12292
  7.5 18.6 %copy-start.8 = (s32[4096]{0:T(1024)S(1)}, s32[4096]{0:T(1024)}, u32[]{:S(2)}) copy-start(s32[4096]{0:T(1024)} %param.21) | copy-start | bytes 49156
  7.5 18.6 %copy-start.9 = (f32[5,256]{1,0:T(8,128)S(1)}, f32[5,256]{1,0:T(8,128)}, u32[]{:S(2)}) copy-start(f32[5,256]{1,0:T(8,128)} %lse.1) | copy-start | bytes 15364
  7.5 8.1 %collective-permute-start.1 = (bf16[256,256]{1,0:T(8,128)(2,1)S(1)}, bf16[256,256]{1,0:T(8,128)(2,1)S(1)}, u32[]{:S(2)}, u32[]{:S(2)}) collective-permute-start(bf16[256,256]{1,0:T(8,128)(2,1)S(1)} %copy-done.10), channel_id=1, source_target_pairs={{0,32},{32,64},{64,96},{96,0},{1,33},{33,65},{65,97},{97,1},{2,34}... | collective-permute-start | bytes 393224 | tf_op jit(solution)/shard_map/ppermute | solution.py:32
  9.2 9.8 %collective-permute-start.3 = (bf16[256,256]{1,0:T(8,128)(2,1)S(1)}, bf16[256,256]{1,0:T(8,128)(2,1)S(1)}, u32[]{:S(2)}, u32[]{:S(2)}) collective-permute-start(bf16[256,256]{1,0:T(8,128)(2,1)S(1)} %copy-done.10), channel_id=1, source_target_pairs={{0,96},{32,0},{64,32},{96,64},{1,97},{33,1},{65,33},{97,65},{2,98}... | collective-permute-start | bytes 393224 | tf_op jit(solution)/shard_map/ppermute | solution.py:32
  10.8 8.1 %collective-permute-start.2 = (bf16[256,256]{1,0:T(8,128)(2,1)S(1)}, bf16[256,256]{1,0:T(8,128)(2,1)S(1)}, u32[]{:S(2)}, u32[]{:S(2)}) collective-permute-start(bf16[256,256]{1,0:T(8,128)(2,1)S(1)} %copy-done.10), channel_id=1, source_target_pairs={{0,64},{32,96},{64,0},{96,32},{1,65},{33,97},{65,1},{97,33},{2,66}... | collective-permute-start | bytes 393224 | tf_op jit(solution)/shard_map/ppermute | solution.py:32
  12.8 10.6 %collective-permute-start.7 = (bf16[256,256]{1,0:T(8,128)(2,1)S(1)}, bf16[256,256]{1,0:T(8,128)(2,1)S(1)}, u32[]{:S(2)}, u32[]{:S(2)}) collective-permute-start(bf16[256,256]{1,0:T(8,128)(2,1)S(1)} %collective-permute-done), channel_id=1, source_target_pairs={{0,96},{32,0},{64,32},{96,64},{1,97},{33,1},{65,33},{97,65},{2,98}... | collective-permute-start | bytes 393224 | tf_op jit(solution)/shard_map/ppermute | solution.py:32
  14.0 9.5 %collective-permute-start.6 = (bf16[256,256]{1,0:T(8,128)(2,1)S(1)}, bf16[256,256]{1,0:T(8,128)(2,1)S(1)}, u32[]{:S(2)}, u32[]{:S(2)}) collective-permute-start(bf16[256,256]{1,0:T(8,128)(2,1)S(1)} %collective-permute-done), channel_id=1, source_target_pairs={{0,64},{32,96},{64,0},{96,32},{1,65},{33,97},{65,1},{97,33},{2,66}... | collective-permute-start | bytes 393224 | tf_op jit(solution)/shard_map/ppermute | solution.py:32
  15.7 7.8 %collective-permute-start.5 = (bf16[256,256]{1,0:T(8,128)(2,1)S(1)}, bf16[256,256]{1,0:T(8,128)(2,1)S(1)}, u32[]{:S(2)}, u32[]{:S(2)}) collective-permute-start(bf16[256,256]{1,0:T(8,128)(2,1)S(1)} %collective-permute-done), channel_id=1, source_target_pairs={{0,32},{32,64},{64,96},{96,0},{1,33},{33,65},{65,97},{97,1},{2,34}... | collective-permute-start | bytes 393224 | tf_op jit(solution)/shard_map/ppermute | solution.py:32
  19.0 7.0 %collective-permute-start.4 = (bf16[1280,256]{1,0:T(8,128)(2,1)S(1)}, bf16[1280,256]{1,0:T(8,128)(2,1)S(1)}, u32[]{:S(2)}, u32[]{:S(2)}) collective-permute-start(bf16[1280,256]{1,0:T(8,128)(2,1)S(1)} %constant_dynamic-update-slice_fusion.early_mine), channel_id=1, source_target_pairs={{0,8},{8,0},{1,9},{9,1},{2,10},{10,2},{3,11},{11,3},{4,12},{12,4},... | collective-permute-start | bytes 1966088 | tf_op jit(solution)/shard_map/ppermute | solution.py:32
  23.5 1.8 %collective-permute-start.8 = (bf16[768,256]{1,0:T(8,128)(2,1)S(1)}, bf16[768,256]{1,0:T(8,128)(2,1)S(1)}, u32[]{:S(2)}, u32[]{:S(2)}) collective-permute-start(bf16[768,256]{1,0:T(8,128)(2,1)S(1)} %constant_dynamic-update-slice_fusion.5.late_mine), channel_id=1, source_target_pairs={{0,8},{8,0},{1,9},{9,1},{2,10},{10,2},{3,11},{11,3},{4,12},{12,4},... | collective-permute-start | bytes 1179656 | tf_op jit(solution)/shard_map/ppermute | solution.py:32
  25.3 0.7 copy-start.5
  26.1 1.0 copy-start.6
  30.8 2.6 %collective-permute-start.10 = (bf16[768,256]{1,0:T(8,128)(2,1)S(1)}, bf16[768,256]{1,0:T(8,128)(2,1)S(1)}, u32[]{:S(2)}, u32[]{:S(2)}) collective-permute-start(bf16[768,256]{1,0:T(8,128)(2,1)S(1)} %get-tuple-element.53), channel_id=1, source_target_pairs={{0,8},{8,0},{1,9},{9,1},{2,10},{10,2},{3,11},{11,3},{4,12},{12,4},... | collective-permute-start | bytes 1179656 | tf_op jit(solution)/shard_map/ppermute | solution.py:32
  32.1 2.3 %collective-permute-start.9 = (bf16[1280,256]{1,0:T(8,128)(2,1)S(1)}, bf16[1280,256]{1,0:T(8,128)(2,1)S(1)}, u32[]{:S(2)}, u32[]{:S(2)}) collective-permute-start(bf16[1280,256]{1,0:T(8,128)(2,1)S(1)} %get-tuple-element.51), channel_id=1, source_target_pairs={{0,8},{8,0},{1,9},{9,1},{2,10},{10,2},{3,11},{11,3},{4,12},{12,4},... | collective-permute-start | bytes 1966088 | tf_op jit(solution)/shard_map/ppermute | solution.py:32
  34.6 21.4 %copy-start.1 = (bf16[5120,128]{1,0:T(8,128)(2,1)S(1)}, bf16[5120,128]{1,0:T(8,128)(2,1)}, u32[]{:S(2)}) copy-start(bf16[5120,128]{1,0:T(8,128)(2,1)} %wk.1) | copy-start | bytes 3932164
  34.6 21.4 %copy-start.2 = (bf16[5120,128]{1,0:T(8,128)(2,1)S(1)}, bf16[5120,128]{1,0:T(8,128)(2,1)}, u32[]{:S(2)}) copy-start(bf16[5120,128]{1,0:T(8,128)(2,1)} %wv.1) | copy-start | bytes 3932164
  35.4 8.2 %collective-permute-start.11 = (bf16[256,256]{1,0:T(8,128)(2,1)S(1)}, bf16[256,256]{1,0:T(8,128)(2,1)S(1)}, u32[]{:S(2)}, u32[]{:S(2)}) collective-permute-start(bf16[256,256]{1,0:T(8,128)(2,1)S(1)} %get-tuple-element.56), channel_id=1, source_target_pairs={{0,96},{32,0},{64,32},{96,64},{1,97},{33,1},{65,33},{97,65},{2,98}... | collective-permute-start | bytes 393224 | tf_op jit(solution)/shard_map/ppermute | solution.py:32
  37.4 7.9 %collective-permute-start.12 = (bf16[256,256]{1,0:T(8,128)(2,1)S(1)}, bf16[256,256]{1,0:T(8,128)(2,1)S(1)}, u32[]{:S(2)}, u32[]{:S(2)}) collective-permute-start(bf16[256,256]{1,0:T(8,128)(2,1)S(1)} %get-tuple-element.57), channel_id=1, source_target_pairs={{0,64},{32,96},{64,0},{96,32},{1,65},{33,97},{65,1},{97,33},{2,66}... | collective-permute-start | bytes 393224 | tf_op jit(solution)/shard_map/ppermute | solution.py:32
  38.7 9.5 %collective-permute-start.13 = (bf16[256,256]{1,0:T(8,128)(2,1)S(1)}, bf16[256,256]{1,0:T(8,128)(2,1)S(1)}, u32[]{:S(2)}, u32[]{:S(2)}) collective-permute-start(bf16[256,256]{1,0:T(8,128)(2,1)S(1)} %get-tuple-element.58), channel_id=1, source_target_pairs={{0,32},{32,64},{64,96},{96,0},{1,33},{33,65},{65,97},{97,1},{2,34}... | collective-permute-start | bytes 393224 | tf_op jit(solution)/shard_map/ppermute | solution.py:32
  38.7 12.6 %collective-permute-start.15 = (bf16[256,256]{1,0:T(8,128)(2,1)}, bf16[256,256]{1,0:T(8,128)(2,1)}, u32[]{:S(2)}, u32[]{:S(2)}) collective-permute-start(bf16[256,256]{1,0:T(8,128)(2,1)} %get-tuple-element.59), channel_id=1, source_target_pairs={{0,96},{32,0},{64,32},{96,64},{1,97},{33,1},{65,33},{97,65},{2,98}... | collective-permute-start | bytes 393224 | tf_op jit(solution)/shard_map/ppermute | solution.py:32
  41.9 9.3 %collective-permute-start.16 = (bf16[256,256]{1,0:T(8,128)(2,1)}, bf16[256,256]{1,0:T(8,128)(2,1)}, u32[]{:S(2)}, u32[]{:S(2)}) collective-permute-start(bf16[256,256]{1,0:T(8,128)(2,1)} %get-tuple-element.60), channel_id=1, source_target_pairs={{0,64},{32,96},{64,0},{96,32},{1,65},{33,97},{65,1},{97,33},{2,66}... | collective-permute-start | bytes 393224 | tf_op jit(solution)/shard_map/ppermute | solution.py:32
  43.6 9.3 %collective-permute-start.17 = (bf16[256,256]{1,0:T(8,128)(2,1)}, bf16[256,256]{1,0:T(8,128)(2,1)}, u32[]{:S(2)}, u32[]{:S(2)}) collective-permute-start(bf16[256,256]{1,0:T(8,128)(2,1)} %get-tuple-element.61), channel_id=1, source_target_pairs={{0,32},{32,64},{64,96},{96,0},{1,33},{33,65},{65,97},{97,1},{2,34}... | collective-permute-start | bytes 393224 | tf_op jit(solution)/shard_map/ppermute | solution.py:32
  48.9 7.0 %collective-permute-start.14 = (bf16[256,256]{1,0:T(8,128)(2,1)}, bf16[256,256]{1,0:T(8,128)(2,1)}, u32[]{:S(2)}, u32[]{:S(2)}) collective-permute-start(bf16[256,256]{1,0:T(8,128)(2,1)} %add_convert_fusion.1), channel_id=1, source_target_pairs={{0,16},{16,0},{1,17},{17,1},{2,18},{18,2},{3,19},{19,3},{4,20},{20... | collective-permute-start | bytes 393224 | tf_op jit(solution)/shard_map/ppermute | solution.py:32
  66.5 10.7 %collective-permute-start.18 = (bf16[2,640,256]{2,1,0:T(8,128)(2,1)S(1)}, bf16[2,640,256]{2,1,0:T(8,128)(2,1)S(1)}, u32[]{:S(2)}, u32[]{:S(2)}) collective-permute-start(bf16[2,640,256]{2,1,0:T(8,128)(2,1)S(1)} %get-tuple-element.64), channel_id=1, source_target_pairs={{0,1},{1,0},{2,3},{3,2},{4,5},{5,4},{6,7},{7,6},{8,10},{9,11},{10,... | collective-permute-start | bytes 1966088 | tf_op jit(solution)/shard_map/ppermute | solution.py:317
  67.6 16.6 %collective-permute-start.19 = (bf16[2,640,256]{2,1,0:T(8,128)(2,1)S(1)}, bf16[2,640,256]{2,1,0:T(8,128)(2,1)S(1)}, u32[]{:S(2)}, u32[]{:S(2)}) collective-permute-start(bf16[2,640,256]{2,1,0:T(8,128)(2,1)S(1)} %get-tuple-element.65), channel_id=1, source_target_pairs={{0,1},{1,0},{2,3},{3,2},{4,5},{5,4},{6,7},{7,6},{8,14},{9,15},{10,... | collective-permute-start | bytes 1966088 | tf_op jit(solution)/shard_map/ppermute | solution.py:317
  68.6 15.6 %collective-permute-start.20 = (bf16[2,640,256]{2,1,0:T(8,128)(2,1)S(1)}, bf16[2,640,256]{2,1,0:T(8,128)(2,1)S(1)}, u32[]{:S(2)}, u32[]{:S(2)}) collective-permute-start(bf16[2,640,256]{2,1,0:T(8,128)(2,1)S(1)} %get-tuple-element.66), channel_id=1, source_target_pairs={{8,12},{9,13},{10,14},{11,15},{12,8},{13,9},{14,10},{15,11},{24,28... | collective-permute-start | bytes 1966088 | tf_op jit(solution)/shard_map/ppermute | solution.py:317
  84.2 1.7 %copy-start = (f32[4,640,256]{2,1,0:T(8,128)S(1)}, f32[4,640,256]{2,1,0:T(8,128)}, u32[]{:S(2)}) copy-start(f32[4,640,256]{2,1,0:T(8,128)} %get-tuple-element.63.kept) | copy-start | bytes 7864324
  86.2 9.6 %collective-permute-start.21 = (bf16[640,256]{1,0:T(8,128)(2,1)S(1)}, bf16[640,256]{1,0:T(8,128)(2,1)S(1)}, u32[]{:S(2)}, u32[]{:S(2)}) collective-permute-start(bf16[640,256]{1,0:T(8,128)(2,1)S(1)} %get-tuple-element.68), channel_id=1, source_target_pairs={{0,2},{1,3},{2,4},{3,5},{4,6},{5,7},{6,0},{7,1},{8,9},{9,8},{10,11... | collective-permute-start | bytes 983048 | tf_op jit(solution)/shard_map/ppermute | solution.py:317
  87.7 11.3 %collective-permute-start.22 = (bf16[640,256]{1,0:T(8,128)(2,1)S(1)}, bf16[640,256]{1,0:T(8,128)(2,1)S(1)}, u32[]{:S(2)}, u32[]{:S(2)}) collective-permute-start(bf16[640,256]{1,0:T(8,128)(2,1)S(1)} %get-tuple-element.69), channel_id=1, source_target_pairs={{0,4},{1,5},{2,6},{3,7},{4,0},{5,1},{6,2},{7,3},{16,20},{17,21},{1... | collective-permute-start | bytes 983048 | tf_op jit(solution)/shard_map/ppermute | solution.py:317
  92.4 9.0 %collective-permute-start.23 = (bf16[640,256]{1,0:T(8,128)(2,1)S(1)}, bf16[640,256]{1,0:T(8,128)(2,1)S(1)}, u32[]{:S(2)}, u32[]{:S(2)}) collective-permute-start(bf16[640,256]{1,0:T(8,128)(2,1)S(1)} %get-tuple-element.70), channel_id=1, source_target_pairs={{0,6},{1,7},{2,0},{3,1},{4,2},{5,3},{6,4},{7,5},{16,22},{17,23},{1... | collective-permute-start | bytes 983048 | tf_op jit(solution)/shard_map/ppermute | solution.py:317

commit v9 on v8

--- a/solution.py
+++ b/solution.py
@@ -249,7 +249,7 @@
         ),
         in_specs=vmem(3),
         out_specs=tuple(vmem(5)),
-        compiler_params=pltpu.CompilerParams(vmem_limit_bytes=6 << 20),
+        compiler_params=pltpu.CompilerParams(vmem_limit_bytes=12 << 20),
         cost_estimate=pl.CostEstimate(flops=1000000, bytes_accessed=10000, transcendentals=0),
         name="prep",
     )(joined, cos, sin)
@@ -318,30 +318,22 @@
 
 
 def first_kernel(
-    tp, core, own, across, near1, near2, near3, cos, sin, qg, wq, wk, wv,
-    out1, out2, out3, kept, grads, weights, sem,
+    tp, core, own, across, near1, near2, near3, cos, sin, qg, wk, wv, wq,
+    out1, out2, kept, out3, grads, weights, sem,
 ):
     x, zl = lax.shift_right_logical(tp[0], 1), tp[0] & 1
-
-    def fetch(i):
-        (x0, z0), (x1, z1) = ORDERS[0][i], ORDERS[1][i]
+    places = []
+    for (x0, z0), (x1, z1) in zip(*ORDERS):
         to_x = (x + jnp.where(core[0] == 0, x0, x1)) & 3
         to_z = zl ^ jnp.where(core[0] == 0, z0, z1)
-        rows = pl.ds(pl.multiple_of((2 * to_x + to_z) * STEP_ROWS, STEP_ROWS), STEP_ROWS)
-        slot = i % 3
-        return [
-            pltpu.make_async_copy(
-                source.at[rows, :],
-                weights.at[slot, :, pl.ds(start, source.shape[1])],
-                sem.at[slot, k],
-            )
-            for k, (source, start) in enumerate(((wq, 0), (wk, ROWS), (wv, ROWS + HEAD)))
-        ]
-
-    flights = [fetch(i) for i in range(8)]
-    for flight in flights[:3]:
-        for copy in flight:
-            copy.start()
+        start = pl.multiple_of((2 * to_x + to_z) * STEP_ROWS, STEP_ROWS)
+        places.append(pl.ds(start, STEP_ROWS))
+    copies = [
+        pltpu.make_async_copy(wq.at[places[i], :], weights.at[i % 3], sem.at[i % 3])
+        for i in range(8)
+    ]
+    for copy in copies[:3]:
+        copy.start()
     total = own[...].astype(f32) + across[...].astype(f32)
     for near in (near1, near2, near3):
         total += near[...].astype(f32)
@@ -352,34 +344,28 @@
     grads[ROWS : ROWS + HEAD, :] = key_grad.T.astype(bf16)
     grads[ROWS + HEAD :, :] = total[:, HEAD:].T.astype(bf16)
     for i in range(8):
-        for copy in flights[i]:
-            copy.wait()
-        block = jnp.dot(weights[i % 3], grads[...], preferred_element_type=f32)
-        if i < 4:
-            (out1, out2)[i // 2][i % 2] = block.astype(bf16)
-        else:
-            kept[i - 4] = block
-        if i >= 6:
-            out3[i - 6] = block.astype(bf16)
+        copies[i].wait()
+        joined = jnp.concatenate([weights[i % 3], wk[places[i], :], wv[places[i], :]], 1)
+        block = jnp.dot(joined, grads[...], preferred_element_type=f32)
+        (out1, out2, kept, out3)[i // 2][i % 2] = block.astype(bf16)
         if i + 3 < 8:
-            for copy in flights[i + 3]:
-                copy.start()
-
-
-def middle_kernel(core, kept, got1, got2, got3, base, out1, out2, out3):
+            copies[i + 3].start()
+
+
+def middle_kernel(core, kept, more, got1, got2, got3, base, out1, out2, out3):
     @pl.when(core[0] == 0)
     def _():
-        base[...] = kept[0] + got1[0].astype(f32)
-        out1[...] = (kept[1] + got1[1].astype(f32)).astype(bf16)
-        out2[...] = (kept[2] + got2[0].astype(f32)).astype(bf16)
-        out3[...] = (kept[3] + got2[1].astype(f32)).astype(bf16)
+        base[...] = kept[0].astype(f32) + got1[0].astype(f32)
+        out1[...] = (kept[1].astype(f32) + got1[1].astype(f32)).astype(bf16)
+        out2[...] = (more[0].astype(f32) + got2[0].astype(f32)).astype(bf16)
+        out3[...] = (more[1].astype(f32) + got2[1].astype(f32)).astype(bf16)
 
     @pl.when(core[0] != 0)
     def _():
-        total = [
-            kept[i] + got1[i].astype(f32) + got2[i].astype(f32) + got3[i].astype(f32)
-            for i in range(2)
-        ]
+        total = []
+        for i in range(2):
+            arrived = got1[i].astype(f32) + got2[i].astype(f32) + got3[i].astype(f32)
+            total.append(kept[i].astype(f32) + arrived)
         base[...] = total[0]
         out1[...] = total[1].astype(bf16)
         out2[...] = jnp.zeros_like(out2)
@@ -397,7 +383,7 @@
         out[...] = (base[...] + got1[...].astype(f32)).astype(bf16)
 
 
-def whole_call(kernel, name, outs, scalars, *operands, large=(), scratch=()):
+def whole_call(kernel, name, outs, scalars, *operands, large=(), scratch=(), cost=(1300000, 3000000)):
     outs = tuple(jax.ShapeDtypeStruct(shape, dtype) for shape, dtype in outs)
     return pl.pallas_call(
         kernel,
@@ -407,8 +393,10 @@
         + [pl.BlockSpec(memory_space=pl.ANY)] * len(large),
         out_specs=tuple(vmem(len(outs))),
         scratch_shapes=scratch,
-        compiler_params=pltpu.CompilerParams(vmem_limit_bytes=(48 if large else 10) << 20),
-        cost_estimate=pl.CostEstimate(flops=1000000, bytes_accessed=10000, transcendentals=0),
+        compiler_params=pltpu.CompilerParams(vmem_limit_bytes=(44 if large else 16) << 20),
+        cost_estimate=pl.CostEstimate(
+            flops=cost[0], bytes_accessed=cost[1], transcendentals=0
+        ),
         name=name,
     )(*scalars, *operands, *large)
 
@@ -416,20 +404,20 @@
 def project_and_sum(own, across, near, cos, sin, qg, wq, wk, wv):
     tp = lax.axis_index(TP).reshape(1)
     core = lax.axis_index("core").reshape(1)
-    one, two, four = ((n, STEP_ROWS, TOK) for n in (1, 2, 4))
-    one = one[1:]
-    first, second, third, kept = whole_call(
+    one, two = (STEP_ROWS, TOK), (2, STEP_ROWS, TOK)
+    first, second, kept, third = whole_call(
         first_kernel,
         "first",
-        [(two, bf16), (two, bf16), (two, bf16), (four, f32)],
+        [(two, bf16)] * 4,
         (tp, core),
-        own, across, *near, cos, sin, qg,
-        large=(wq, wk, wv),
+        own, across, *near, cos, sin, qg, wk, wv,
+        large=(wq,),
         scratch=[
             pltpu.VMEM((ROWS + 2 * HEAD, TOK), bf16),
-            pltpu.VMEM((3, STEP_ROWS, ROWS + 2 * HEAD), bf16),
-            pltpu.SemaphoreType.DMA((3, 3)),
+            pltpu.VMEM((3, STEP_ROWS, ROWS), bf16),
+            pltpu.SemaphoreType.DMA((3,)),
         ],
+        cost=(2350000000, 12000000),
     )
     got1 = send(first, (0, 1), (1, 0))
     got2 = send(second, (0, 1), (3, 0))
@@ -439,7 +427,7 @@
         "middle",
         [(one, f32), (one, bf16), (one, bf16), (one, bf16)],
         (core,),
-        kept, got1, got2, got3,
+        kept, third, got1, got2, got3,
     )
     got1 = send(out1, (1, 0), (0, 1))
     got2 = send(out2, (2, 0), None)

time: 103 us -> 99.5 us (0.966)
  local copies, waits for them, and re-layouts: 4.4 us -> 2.68 us
  Pallas kernels: 18.3 us -> 16.8 us
    unnamed x28 -> x26, local copies, waits for them, and re-layouts: 3.57 us -> 1.84 us
    pallas_call x3, Pallas kernels: 11.6 us -> 10.2 us  [whole_call(): pl.pallas_call(kernel, out_shape=outs, in_specs=[pl.BlockSpec(memory_spac...]
where the time goes in v9:
time: 99.5 us; the launch traced here: 98.9 us
  waiting for transfers between devices  40.7 us (41%)
  starting transfers between devices  36 us (36%)
  Pallas kernels  16.8 us (17%)
  local copies, waits for them, and re-layouts  2.68 us (3%)
  other arithmetic  2.28 us (2%)
    ppermute x18, starting transfers between devices, shift(): return lax.ppermute(x, axes, perm)  23.7 us
    ppermute x6, waiting for transfers between devices, send(): return lax.ppermute(x, ('core', 'x', 'zl'), by_core(offsets))  20.5 us
    ppermute x18, waiting for transfers between devices, shift(): return lax.ppermute(x, axes, perm)  20.3 us
    ppermute x6, starting transfers between devices, send(): return lax.ppermute(x, ('core', 'x', 'zl'), by_core(offsets))  12.3 us
    pallas_call x3, Pallas kernels, whole_call(): pl.pallas_call(kernel, out_shape=outs, in_specs=[pl.BlockSpec(memory_spac...  10.2 us
    pallas_call x1, Pallas kernels, attention(): pl.pallas_call(attention_kernel, out_shape=(early, early, late, late, s((...  3.7 us
    pallas_call x1, Pallas kernels, make_block(): pl.pallas_call(block_kernel, out_shape=(s((TOK, HEAD), f32), s((TOK, HEAD...  2.18 us
  transfers between devices with their start and end apart: 24, of which 14 were waited for; matrix products, arithmetic and copies ran while one was open for 2% of the time, Pallas kernels for 1%

profile of v9, /device:TPU:0, one launch (start us, length us, event | category | flops | bytes accessed | tf_op | source)
XLA Modules:
  0.0 98.9 jit_solution(17956374482260121543)
XLA Ops:
  0.0 2.2 %block.1 = (f32[256,128]{1,0:T(8,128)}, f32[256,128]{1,0:T(8,128)}, bf16[256,256]{1,0:T(8,128)(2,1)}) custom-call(bf16[256,128]{1,0:T(8,128)(2,1)} %key.1, bf16[256,128]{1,0:T(8,128)(2,1)} %value.1, s32[2,1,128]{2,1,0:T(1,128)} %bitcast.6, f32[1,128]{1,0:T(1,128)} %constant.25.clone.inverse), custom_call_target="tpu_custom_call" | custom-call | flops 5000000 | bytes 700000 | tf_op jit(solution)/shard_map/block/pallas_call | solution.py:286
  2.2 4.0 %collective-permute-start = (bf16[256,256]{1,0:T(8,128)(2,1)}, bf16[256,256]{1,0:T(8,128)(2,1)S(1)}, u32[]{:S(2)}, u32[]{:S(2)}) collective-permute-start(bf16[256,256]{1,0:T(8,128)(2,1)} %get-tuple-element.48), channel_id=1, source_target_pairs={{0,16},{16,0},{1,17},{17,1},{2,18},{18,2},{3,19},{19,3},{4,20},{20... | collective-permute-start | bytes 393224 | tf_op jit(solution)/shard_map/ppermute | solution.py:32
  6.1 1.2 %pad_maximum_fusion.joined = bf16[256,1920]{1,0:T(8,128)(2,1)S(1)} fusion(bf16[256,640]{1,0:T(8,128)(2,1)} %param.16, bf16[256,640]{1,0:T(8,128)(2,1)} %param.17, bf16[256,640]{1,0:T(8,128)(2,1)} %param.13), kind=kLoop, calls=%fused_computation.1 | loop fusion | flops 2949120 | bytes 1966080 | tf_op jit(solution)/shard_map/concatenate | solution.py:446
  7.4 1.6 %collective-permute-start.1 = (bf16[256,256]{1,0:T(8,128)(2,1)S(1)}, bf16[256,256]{1,0:T(8,128)(2,1)S(1)}, u32[]{:S(2)}, u32[]{:S(2)}) collective-permute-start(bf16[256,256]{1,0:T(8,128)(2,1)S(1)} %copy-done.9), channel_id=1, source_target_pairs={{0,32},{32,64},{64,96},{96,0},{1,33},{33,65},{65,97},{97,1},{2,34}... | collective-permute-start | bytes 393224 | tf_op jit(solution)/shard_map/ppermute | solution.py:32
  9.1 1.7 %collective-permute-start.3 = (bf16[256,256]{1,0:T(8,128)(2,1)S(1)}, bf16[256,256]{1,0:T(8,128)(2,1)S(1)}, u32[]{:S(2)}, u32[]{:S(2)}) collective-permute-start(bf16[256,256]{1,0:T(8,128)(2,1)S(1)} %copy-done.9), channel_id=1, source_target_pairs={{0,96},{32,0},{64,32},{96,64},{1,97},{33,1},{65,33},{97,65},{2,98}... | collective-permute-start | bytes 393224 | tf_op jit(solution)/shard_map/ppermute | solution.py:32
  10.7 2.0 %collective-permute-start.2 = (bf16[256,256]{1,0:T(8,128)(2,1)S(1)}, bf16[256,256]{1,0:T(8,128)(2,1)S(1)}, u32[]{:S(2)}, u32[]{:S(2)}) collective-permute-start(bf16[256,256]{1,0:T(8,128)(2,1)S(1)} %copy-done.9), channel_id=1, source_target_pairs={{0,64},{32,96},{64,0},{96,32},{1,65},{33,97},{65,1},{97,33},{2,66}... | collective-permute-start | bytes 393224 | tf_op jit(solution)/shard_map/ppermute | solution.py:32
  12.7 1.1 %collective-permute-start.7 = (bf16[256,256]{1,0:T(8,128)(2,1)S(1)}, bf16[256,256]{1,0:T(8,128)(2,1)S(1)}, u32[]{:S(2)}, u32[]{:S(2)}) collective-permute-start(bf16[256,256]{1,0:T(8,128)(2,1)S(1)} %collective-permute-done), channel_id=1, source_target_pairs={{0,96},{32,0},{64,32},{96,64},{1,97},{33,1},{65,33},{97,65},{2,98}... | collective-permute-start | bytes 393224 | tf_op jit(solution)/shard_map/ppermute | solution.py:32
  13.9 1.7 %collective-permute-start.6 = (bf16[256,256]{1,0:T(8,128)(2,1)S(1)}, bf16[256,256]{1,0:T(8,128)(2,1)S(1)}, u32[]{:S(2)}, u32[]{:S(2)}) collective-permute-start(bf16[256,256]{1,0:T(8,128)(2,1)S(1)} %collective-permute-done), channel_id=1, source_target_pairs={{0,64},{32,96},{64,0},{96,32},{1,65},{33,97},{65,1},{97,33},{2,66}... | collective-permute-start | bytes 393224 | tf_op jit(solution)/shard_map/ppermute | solution.py:32
  15.6 0.2 collective-permute-start.5
  15.8 3.1 %collective-permute-done.2 = bf16[256,256]{1,0:T(8,128)(2,1)S(1)} collective-permute-done((bf16[256,256]{1,0:T(8,128)(2,1)S(1)}, bf16[256,256]{1,0:T(8,128)(2,1)S(1)}, u32[]{:S(2)}, u32[]{:S(2)}) %collective-permute-start.2) | collective-permute-done | bytes 131104 | tf_op jit(solution)/shard_map/ppermute | solution.py:32
  19.0 4.3 %collective-permute-done.5 = bf16[256,256]{1,0:T(8,128)(2,1)S(1)} collective-permute-done((bf16[256,256]{1,0:T(8,128)(2,1)S(1)}, bf16[256,256]{1,0:T(8,128)(2,1)S(1)}, u32[]{:S(2)}, u32[]{:S(2)}) %collective-permute-start.5) | collective-permute-done | bytes 131104 | tf_op jit(solution)/shard_map/ppermute | solution.py:32
  23.4 0.1 collective-permute-start.8
  23.5 0.8 prep.1
  24.4 0.9 collective-permute-done.8.late_other
  25.2 0.7 copy-done.4
  26.0 1.0 copy-done.5
  27.0 3.7 %attention.1 = (bf16[1280,256]{1,0:T(8,128)(2,1)S(1)}, bf16[1280,256]{1,0:T(8,128)(2,1)S(1)}, bf16[768,256]{1,0:T(8,128)(2,1)S(1)}, bf16[768,256]{1,0:T(8,128)(2,1)S(1)}, bf16[640,256]{1,0:T(8,128)(2,1)S(1)}) custom-call(s32[32,32]{1,0:T(8,128)S(1)} %copy-done.6, s32[1]{0:T(128)} %bitcast.2.info, s32[32,1,128]{2,1,0:T(1,128)S(1)} %bitcast.5, ...), custom_call_target="tpu_custom_call" | custom-call | flops 2000000000 | bytes 8000000 | tf_op jit(solution)/shard_map/attention/pallas_call | solution.py:261
  30.7 1.3 %collective-permute-start.10 = (bf16[768,256]{1,0:T(8,128)(2,1)S(1)}, bf16[768,256]{1,0:T(8,128)(2,1)S(1)}, u32[]{:S(2)}, u32[]{:S(2)}) collective-permute-start(bf16[768,256]{1,0:T(8,128)(2,1)S(1)} %get-tuple-element.53), channel_id=1, source_target_pairs={{0,8},{8,0},{1,9},{9,1},{2,10},{10,2},{3,11},{11,3},{4,12},{12,4},... | collective-permute-start | bytes 1179656 | tf_op jit(solution)/shard_map/ppermute | solution.py:32
  32.0 0.1 collective-permute-start.9
  32.1 1.3 %collective-permute-done.10 = bf16[768,256]{1,0:T(8,128)(2,1)S(1)} collective-permute-done((bf16[768,256]{1,0:T(8,128)(2,1)S(1)}, bf16[768,256]{1,0:T(8,128)(2,1)S(1)}, u32[]{:S(2)}, u32[]{:S(2)}) %collective-permute-start.10) | collective-permute-done | bytes 393248 | tf_op jit(solution)/shard_map/ppermute | solution.py:32
  33.3 0.1 add_convert_fusion
  33.5 0.8 collective-permute-done.9
  34.3 0.2 fusion
  34.5 0.8 fusion.2
  35.3 2.1 %collective-permute-start.11 = (bf16[256,256]{1,0:T(8,128)(2,1)S(1)}, bf16[256,256]{1,0:T(8,128)(2,1)S(1)}, u32[]{:S(2)}, u32[]{:S(2)}) collective-permute-start(bf16[256,256]{1,0:T(8,128)(2,1)S(1)} %get-tuple-element.56), channel_id=1, source_target_pairs={{0,96},{32,0},{64,32},{96,64},{1,97},{33,1},{65,33},{97,65},{2,98}... | collective-permute-start | bytes 393224 | tf_op jit(solution)/shard_map/ppermute | solution.py:32
  37.4 1.2 %collective-permute-start.12 = (bf16[256,256]{1,0:T(8,128)(2,1)S(1)}, bf16[256,256]{1,0:T(8,128)(2,1)S(1)}, u32[]{:S(2)}, u32[]{:S(2)}) collective-permute-start(bf16[256,256]{1,0:T(8,128)(2,1)S(1)} %get-tuple-element.57), channel_id=1, source_target_pairs={{0,64},{32,96},{64,0},{96,32},{1,65},{33,97},{65,1},{97,33},{2,66}... | collective-permute-start | bytes 393224 | tf_op jit(solution)/shard_map/ppermute | solution.py:32
  38.6 3.2 %collective-permute-start.15 = (bf16[256,256]{1,0:T(8,128)(2,1)}, bf16[256,256]{1,0:T(8,128)(2,1)}, u32[]{:S(2)}, u32[]{:S(2)}) collective-permute-start(bf16[256,256]{1,0:T(8,128)(2,1)} %get-tuple-element.59), channel_id=1, source_target_pairs={{0,96},{32,0},{64,32},{96,64},{1,97},{33,1},{65,33},{97,65},{2,98}... | collective-permute-start | bytes 393224 | tf_op jit(solution)/shard_map/ppermute | solution.py:32
  41.8 1.1 %collective-permute-start.16 = (bf16[256,256]{1,0:T(8,128)(2,1)}, bf16[256,256]{1,0:T(8,128)(2,1)}, u32[]{:S(2)}, u32[]{:S(2)}) collective-permute-start(bf16[256,256]{1,0:T(8,128)(2,1)} %get-tuple-element.60), channel_id=1, source_target_pairs={{0,64},{32,96},{64,0},{96,32},{1,65},{33,97},{65,1},{97,33},{2,66}... | collective-permute-start | bytes 393224 | tf_op jit(solution)/shard_map/ppermute | solution.py:32
  42.9 0.7 collective-permute-done.11
  43.6 1.6 %collective-permute-done.12 = bf16[256,256]{1,0:T(8,128)(2,1)S(1)} collective-permute-done((bf16[256,256]{1,0:T(8,128)(2,1)S(1)}, bf16[256,256]{1,0:T(8,128)(2,1)S(1)}, u32[]{:S(2)}, u32[]{:S(2)}) %collective-permute-start.12) | collective-permute-done | bytes 131104 | tf_op jit(solution)/shard_map/ppermute | solution.py:32
  45.2 2.9 %collective-permute-done.13 = bf16[256,256]{1,0:T(8,128)(2,1)S(1)} collective-permute-done((bf16[256,256]{1,0:T(8,128)(2,1)S(1)}, bf16[256,256]{1,0:T(8,128)(2,1)S(1)}, u32[]{:S(2)}, u32[]{:S(2)}) %collective-permute-start.13) | collective-permute-done | bytes 131104 | tf_op jit(solution)/shard_map/ppermute | solution.py:32
  48.1 0.7 add_convert_fusion.1
  48.8 2.3 %collective-permute-start.14 = (bf16[256,256]{1,0:T(8,128)(2,1)}, bf16[256,256]{1,0:T(8,128)(2,1)}, u32[]{:S(2)}, u32[]{:S(2)}) collective-permute-start(bf16[256,256]{1,0:T(8,128)(2,1)} %add_convert_fusion.1), channel_id=1, source_target_pairs={{0,16},{16,0},{1,17},{17,1},{2,18},{18,2},{3,19},{19,3},{4,20},{20... | collective-permute-start | bytes 393224 | tf_op jit(solution)/shard_map/ppermute | solution.py:32
  51.1 1.8 %collective-permute-done.17.near3 = bf16[256,256]{1,0:T(8,128)(2,1)} collective-permute-done((bf16[256,256]{1,0:T(8,128)(2,1)}, bf16[256,256]{1,0:T(8,128)(2,1)}, u32[]{:S(2)}, u32[]{:S(2)}) %collective-permute-start.17) | collective-permute-done | bytes 131104 | tf_op jit(solution)/shard_map/ppermute | solution.py:32
  52.9 3.0 %collective-permute-done.14.across = bf16[256,256]{1,0:T(8,128)(2,1)} collective-permute-done((bf16[256,256]{1,0:T(8,128)(2,1)}, bf16[256,256]{1,0:T(8,128)(2,1)}, u32[]{:S(2)}, u32[]{:S(2)}) %collective-permute-start.14) | collective-permute-done | bytes 131104 | tf_op jit(solution)/shard_map/ppermute | solution.py:32
  55.9 9.0 %first.1 = (bf16[2,640,256]{2,1,0:T(8,128)(2,1)S(1)}, bf16[2,640,256]{2,1,0:T(8,128)(2,1)S(1)}, bf16[2,640,256]{2,1,0:T(8,128)(2,1)S(1)}, bf16[2,640,256]{2,1,0:T(8,128)(2,1)S(1)}) custom-call(s32[1]{0:T(128)} %bitcast.1.tp, s32[1]{0:T(128)} %bitcast.core, f32[256,256]{1,0:T(8,128)S(1)} %get-tuple-element.54.own, ...), custom_call_target="tpu_custom_call" | custom-call | flops 2350000128 | bytes 12000000 | tf_op jit(solution)/shard_map/first/pallas_call | solution.py:388
  64.9 1.1 %collective-permute-start.18 = (bf16[2,640,256]{2,1,0:T(8,128)(2,1)S(1)}, bf16[2,640,256]{2,1,0:T(8,128)(2,1)S(1)}, u32[]{:S(2)}, u32[]{:S(2)}) collective-permute-start(bf16[2,640,256]{2,1,0:T(8,128)(2,1)S(1)} %get-tuple-element.65), channel_id=1, source_target_pairs={{0,1},{1,0},{2,3},{3,2},{4,5},{5,4},{6,7},{7,6},{8,10},{9,11},{10,... | collective-permute-start | bytes 1966088 | tf_op jit(solution)/shard_map/ppermute | solution.py:317
  66.0 1.0 %collective-permute-start.19 = (bf16[2,640,256]{2,1,0:T(8,128)(2,1)S(1)}, bf16[2,640,256]{2,1,0:T(8,128)(2,1)S(1)}, u32[]{:S(2)}, u32[]{:S(2)}) collective-permute-start(bf16[2,640,256]{2,1,0:T(8,128)(2,1)S(1)} %get-tuple-element.66), channel_id=1, source_target_pairs={{0,1},{1,0},{2,3},{3,2},{4,5},{5,4},{6,7},{7,6},{8,14},{9,15},{10,... | collective-permute-start | bytes 1966088 | tf_op jit(solution)/shard_map/ppermute | solution.py:317
  67.0 0.7 collective-permute-start.20
  67.7 7.9 %collective-permute-done.18.got1 = bf16[2,640,256]{2,1,0:T(8,128)(2,1)S(1)} collective-permute-done((bf16[2,640,256]{2,1,0:T(8,128)(2,1)S(1)}, bf16[2,640,256]{2,1,0:T(8,128)(2,1)S(1)}, u32[]{:S(2)}, u32[]{:S(2)}) %collective-permute-start.18) | collective-permute-done | bytes 655392 | tf_op jit(solution)/shard_map/ppermute | solution.py:317
  75.5 7.0 %collective-permute-done.19.got2 = bf16[2,640,256]{2,1,0:T(8,128)(2,1)S(1)} collective-permute-done((bf16[2,640,256]{2,1,0:T(8,128)(2,1)S(1)}, bf16[2,640,256]{2,1,0:T(8,128)(2,1)S(1)}, u32[]{:S(2)}, u32[]{:S(2)}) %collective-permute-start.19) | collective-permute-done | bytes 655392 | tf_op jit(solution)/shard_map/ppermute | solution.py:317
  82.6 0.3 middle.1
  82.9 1.6 %collective-permute-start.21 = (bf16[640,256]{1,0:T(8,128)(2,1)S(1)}, bf16[640,256]{1,0:T(8,128)(2,1)S(1)}, u32[]{:S(2)}, u32[]{:S(2)}) collective-permute-start(bf16[640,256]{1,0:T(8,128)(2,1)S(1)} %get-tuple-element.68), channel_id=1, source_target_pairs={{0,2},{1,3},{2,4},{3,5},{4,6},{5,7},{6,0},{7,1},{8,9},{9,8},{10,11... | collective-permute-start | bytes 983048 | tf_op jit(solution)/shard_map/ppermute | solution.py:317
  84.4 4.6 %collective-permute-start.22 = (bf16[640,256]{1,0:T(8,128)(2,1)S(1)}, bf16[640,256]{1,0:T(8,128)(2,1)S(1)}, u32[]{:S(2)}, u32[]{:S(2)}) collective-permute-start(bf16[640,256]{1,0:T(8,128)(2,1)S(1)} %get-tuple-element.69), channel_id=1, source_target_pairs={{0,4},{1,5},{2,6},{3,7},{4,0},{5,1},{6,2},{7,3},{16,20},{17,21},{1... | collective-permute-start | bytes 983048 | tf_op jit(solution)/shard_map/ppermute | solution.py:317
  89.1 3.3 %collective-permute-start.23 = (bf16[640,256]{1,0:T(8,128)(2,1)S(1)}, bf16[640,256]{1,0:T(8,128)(2,1)S(1)}, u32[]{:S(2)}, u32[]{:S(2)}) collective-permute-start(bf16[640,256]{1,0:T(8,128)(2,1)S(1)} %get-tuple-element.70), channel_id=1, source_target_pairs={{0,6},{1,7},{2,0},{3,1},{4,2},{5,3},{6,4},{7,5},{16,22},{17,23},{1... | collective-permute-start | bytes 983048 | tf_op jit(solution)/shard_map/ppermute | solution.py:317
  92.4 3.3 %collective-permute-done.22.got2 = bf16[640,256]{1,0:T(8,128)(2,1)S(1)} collective-permute-done((bf16[640,256]{1,0:T(8,128)(2,1)S(1)}, bf16[640,256]{1,0:T(8,128)(2,1)S(1)}, u32[]{:S(2)}, u32[]{:S(2)}) %collective-permute-start.22) | collective-permute-done | bytes 327712 | tf_op jit(solution)/shard_map/ppermute | solution.py:317
  95.7 2.3 %collective-permute-done.23.got3 = bf16[640,256]{1,0:T(8,128)(2,1)S(1)} collective-permute-done((bf16[640,256]{1,0:T(8,128)(2,1)S(1)}, bf16[640,256]{1,0:T(8,128)(2,1)S(1)}, u32[]{:S(2)}, u32[]{:S(2)}) %collective-permute-start.23) | collective-permute-done | bytes 327712 | tf_op jit(solution)/shard_map/ppermute | solution.py:317
  98.0 0.9 last.1
  (41 shorter events, 0.3 us)
Async XLA Ops:
  2.2 5.2 %copy-start.9 = (bf16[256,256]{1,0:T(8,128)(2,1)S(1)}, bf16[256,256]{1,0:T(8,128)(2,1)}, u32[]{:S(2)}) copy-start(bf16[256,256]{1,0:T(8,128)(2,1)} %get-tuple-element.48) | copy-start | bytes 393220
  2.2 10.5 %collective-permute-start = (bf16[256,256]{1,0:T(8,128)(2,1)}, bf16[256,256]{1,0:T(8,128)(2,1)S(1)}, u32[]{:S(2)}, u32[]{:S(2)}) collective-permute-start(bf16[256,256]{1,0:T(8,128)(2,1)} %get-tuple-element.48), channel_id=1, source_target_pairs={{0,16},{16,0},{1,17},{17,1},{2,18},{18,2},{3,19},{19,3},{4,20},{20... | collective-permute-start | bytes 393224 | tf_op jit(solution)/shard_map/ppermute | solution.py:32
  7.4 16.1 %copy-start.2 = (f32[256,128]{1,0:T(8,128)S(1)}, f32[256,128]{1,0:T(8,128)}, u32[]{:S(2)}) copy-start(f32[256,128]{1,0:T(8,128)} %get-tuple-element.41.cos) | copy-start | bytes 393220
  7.4 16.1 %copy-start.3 = (f32[256,128]{1,0:T(8,128)S(1)}, f32[256,128]{1,0:T(8,128)}, u32[]{:S(2)}) copy-start(f32[256,128]{1,0:T(8,128)} %get-tuple-element.42.sin) | copy-start | bytes 393220
  7.4 8.1 %collective-permute-start.1 = (bf16[256,256]{1,0:T(8,128)(2,1)S(1)}, bf16[256,256]{1,0:T(8,128)(2,1)S(1)}, u32[]{:S(2)}, u32[]{:S(2)}) collective-permute-start(bf16[256,256]{1,0:T(8,128)(2,1)S(1)} %copy-done.9), channel_id=1, source_target_pairs={{0,32},{32,64},{64,96},{96,0},{1,33},{33,65},{65,97},{97,1},{2,34}... | collective-permute-start | bytes 393224 | tf_op jit(solution)/shard_map/ppermute | solution.py:32
  9.1 9.8 %collective-permute-start.3 = (bf16[256,256]{1,0:T(8,128)(2,1)S(1)}, bf16[256,256]{1,0:T(8,128)(2,1)S(1)}, u32[]{:S(2)}, u32[]{:S(2)}) collective-permute-start(bf16[256,256]{1,0:T(8,128)(2,1)S(1)} %copy-done.9), channel_id=1, source_target_pairs={{0,96},{32,0},{64,32},{96,64},{1,97},{33,1},{65,33},{97,65},{2,98}... | collective-permute-start | bytes 393224 | tf_op jit(solution)/shard_map/ppermute | solution.py:32
  10.7 8.1 %collective-permute-start.2 = (bf16[256,256]{1,0:T(8,128)(2,1)S(1)}, bf16[256,256]{1,0:T(8,128)(2,1)S(1)}, u32[]{:S(2)}, u32[]{:S(2)}) collective-permute-start(bf16[256,256]{1,0:T(8,128)(2,1)S(1)} %copy-done.9), channel_id=1, source_target_pairs={{0,64},{32,96},{64,0},{96,32},{1,65},{33,97},{65,1},{97,33},{2,66}... | collective-permute-start | bytes 393224 | tf_op jit(solution)/shard_map/ppermute | solution.py:32
  12.7 10.6 %collective-permute-start.7 = (bf16[256,256]{1,0:T(8,128)(2,1)S(1)}, bf16[256,256]{1,0:T(8,128)(2,1)S(1)}, u32[]{:S(2)}, u32[]{:S(2)}) collective-permute-start(bf16[256,256]{1,0:T(8,128)(2,1)S(1)} %collective-permute-done), channel_id=1, source_target_pairs={{0,96},{32,0},{64,32},{96,64},{1,97},{33,1},{65,33},{97,65},{2,98}... | collective-permute-start | bytes 393224 | tf_op jit(solution)/shard_map/ppermute | solution.py:32
  13.9 9.5 %collective-permute-start.6 = (bf16[256,256]{1,0:T(8,128)(2,1)S(1)}, bf16[256,256]{1,0:T(8,128)(2,1)S(1)}, u32[]{:S(2)}, u32[]{:S(2)}) collective-permute-start(bf16[256,256]{1,0:T(8,128)(2,1)S(1)} %collective-permute-done), channel_id=1, source_target_pairs={{0,64},{32,96},{64,0},{96,32},{1,65},{33,97},{65,1},{97,33},{2,66}... | collective-permute-start | bytes 393224 | tf_op jit(solution)/shard_map/ppermute | solution.py:32
  15.6 7.8 %collective-permute-start.5 = (bf16[256,256]{1,0:T(8,128)(2,1)S(1)}, bf16[256,256]{1,0:T(8,128)(2,1)S(1)}, u32[]{:S(2)}, u32[]{:S(2)}) collective-permute-start(bf16[256,256]{1,0:T(8,128)(2,1)S(1)} %collective-permute-done), channel_id=1, source_target_pairs={{0,32},{32,64},{64,96},{96,0},{1,33},{33,65},{65,97},{97,1},{2,34}... | collective-permute-start | bytes 393224 | tf_op jit(solution)/shard_map/ppermute | solution.py:32
  18.9 7.1 %copy-start.6 = (s32[32,32]{1,0:T(8,128)S(1)}, s32[32,32]{1,0:T(8,128)}, u32[]{:S(2)}) copy-start(s32[32,32]{1,0:T(8,128)} %mask.1) | copy-start | bytes 12292
  18.9 7.1 %copy-start.7 = (s32[4096]{0:T(1024)S(1)}, s32[4096]{0:T(1024)}, u32[]{:S(2)}) copy-start(s32[4096]{0:T(1024)} %param.21) | copy-start | bytes 49156
  18.9 7.1 %copy-start.8 = (f32[5,256]{1,0:T(8,128)S(1)}, f32[5,256]{1,0:T(8,128)}, u32[]{:S(2)}) copy-start(f32[5,256]{1,0:T(8,128)} %lse.1) | copy-start | bytes 15364
  18.9 7.0 %collective-permute-start.4 = (bf16[1280,256]{1,0:T(8,128)(2,1)S(1)}, bf16[1280,256]{1,0:T(8,128)(2,1)S(1)}, u32[]{:S(2)}, u32[]{:S(2)}) collective-permute-start(bf16[1280,256]{1,0:T(8,128)(2,1)S(1)} %constant_dynamic-update-slice_fusion.early_mine), channel_id=1, source_target_pairs={{0,8},{8,0},{1,9},{9,1},{2,10},{10,2},{3,11},{11,3},{4,12},{12,4},... | collective-permute-start | bytes 1966088 | tf_op jit(solution)/shard_map/ppermute | solution.py:32
  23.4 1.8 %collective-permute-start.8 = (bf16[768,256]{1,0:T(8,128)(2,1)S(1)}, bf16[768,256]{1,0:T(8,128)(2,1)S(1)}, u32[]{:S(2)}, u32[]{:S(2)}) collective-permute-start(bf16[768,256]{1,0:T(8,128)(2,1)S(1)} %constant_dynamic-update-slice_fusion.5.late_mine), channel_id=1, source_target_pairs={{0,8},{8,0},{1,9},{9,1},{2,10},{10,2},{3,11},{11,3},{4,12},{12,4},... | collective-permute-start | bytes 1179656 | tf_op jit(solution)/shard_map/ppermute | solution.py:32
  25.2 0.7 copy-start.4
  26.0 1.0 %copy-start.5 = (bf16[768,256]{1,0:T(8,128)(2,1)S(1)}, bf16[768,256]{1,0:T(8,128)(2,1)}, u32[]{:S(2)}) copy-start(bf16[768,256]{1,0:T(8,128)(2,1)} %copy-done.4) | copy-start | bytes 1179652
  30.7 2.6 %collective-permute-start.10 = (bf16[768,256]{1,0:T(8,128)(2,1)S(1)}, bf16[768,256]{1,0:T(8,128)(2,1)S(1)}, u32[]{:S(2)}, u32[]{:S(2)}) collective-permute-start(bf16[768,256]{1,0:T(8,128)(2,1)S(1)} %get-tuple-element.53), channel_id=1, source_target_pairs={{0,8},{8,0},{1,9},{9,1},{2,10},{10,2},{3,11},{11,3},{4,12},{12,4},... | collective-permute-start | bytes 1179656 | tf_op jit(solution)/shard_map/ppermute | solution.py:32
  32.0 2.3 %collective-permute-start.9 = (bf16[1280,256]{1,0:T(8,128)(2,1)S(1)}, bf16[1280,256]{1,0:T(8,128)(2,1)S(1)}, u32[]{:S(2)}, u32[]{:S(2)}) collective-permute-start(bf16[1280,256]{1,0:T(8,128)(2,1)S(1)} %get-tuple-element.51), channel_id=1, source_target_pairs={{0,8},{8,0},{1,9},{9,1},{2,10},{10,2},{3,11},{11,3},{4,12},{12,4},... | collective-permute-start | bytes 1966088 | tf_op jit(solution)/shard_map/ppermute | solution.py:32
  34.5 21.4 %copy-start = (bf16[5120,128]{1,0:T(8,128)(2,1)S(1)}, bf16[5120,128]{1,0:T(8,128)(2,1)}, u32[]{:S(2)}) copy-start(bf16[5120,128]{1,0:T(8,128)(2,1)} %wk.1) | copy-start | bytes 3932164
  34.5 21.4 %copy-start.1 = (bf16[5120,128]{1,0:T(8,128)(2,1)S(1)}, bf16[5120,128]{1,0:T(8,128)(2,1)}, u32[]{:S(2)}) copy-start(bf16[5120,128]{1,0:T(8,128)(2,1)} %wv.1) | copy-start | bytes 3932164
  35.3 8.3 %collective-permute-start.11 = (bf16[256,256]{1,0:T(8,128)(2,1)S(1)}, bf16[256,256]{1,0:T(8,128)(2,1)S(1)}, u32[]{:S(2)}, u32[]{:S(2)}) collective-permute-start(bf16[256,256]{1,0:T(8,128)(2,1)S(1)} %get-tuple-element.56), channel_id=1, source_target_pairs={{0,96},{32,0},{64,32},{96,64},{1,97},{33,1},{65,33},{97,65},{2,98}... | collective-permute-start | bytes 393224 | tf_op jit(solution)/shard_map/ppermute | solution.py:32
  37.4 7.9 %collective-permute-start.12 = (bf16[256,256]{1,0:T(8,128)(2,1)S(1)}, bf16[256,256]{1,0:T(8,128)(2,1)S(1)}, u32[]{:S(2)}, u32[]{:S(2)}) collective-permute-start(bf16[256,256]{1,0:T(8,128)(2,1)S(1)} %get-tuple-element.57), channel_id=1, source_target_pairs={{0,64},{32,96},{64,0},{96,32},{1,65},{33,97},{65,1},{97,33},{2,66}... | collective-permute-start | bytes 393224 | tf_op jit(solution)/shard_map/ppermute | solution.py:32
  38.6 9.6 %collective-permute-start.13 = (bf16[256,256]{1,0:T(8,128)(2,1)S(1)}, bf16[256,256]{1,0:T(8,128)(2,1)S(1)}, u32[]{:S(2)}, u32[]{:S(2)}) collective-permute-start(bf16[256,256]{1,0:T(8,128)(2,1)S(1)} %get-tuple-element.58), channel_id=1, source_target_pairs={{0,32},{32,64},{64,96},{96,0},{1,33},{33,65},{65,97},{97,1},{2,34}... | collective-permute-start | bytes 393224 | tf_op jit(solution)/shard_map/ppermute | solution.py:32
  38.6 12.6 %collective-permute-start.15 = (bf16[256,256]{1,0:T(8,128)(2,1)}, bf16[256,256]{1,0:T(8,128)(2,1)}, u32[]{:S(2)}, u32[]{:S(2)}) collective-permute-start(bf16[256,256]{1,0:T(8,128)(2,1)} %get-tuple-element.59), channel_id=1, source_target_pairs={{0,96},{32,0},{64,32},{96,64},{1,97},{33,1},{65,33},{97,65},{2,98}... | collective-permute-start | bytes 393224 | tf_op jit(solution)/shard_map/ppermute | solution.py:32
  41.8 9.3 %collective-permute-start.16 = (bf16[256,256]{1,0:T(8,128)(2,1)}, bf16[256,256]{1,0:T(8,128)(2,1)}, u32[]{:S(2)}, u32[]{:S(2)}) collective-permute-start(bf16[256,256]{1,0:T(8,128)(2,1)} %get-tuple-element.60), channel_id=1, source_target_pairs={{0,64},{32,96},{64,0},{96,32},{1,65},{33,97},{65,1},{97,33},{2,66}... | collective-permute-start | bytes 393224 | tf_op jit(solution)/shard_map/ppermute | solution.py:32
  43.6 9.3 %collective-permute-start.17 = (bf16[256,256]{1,0:T(8,128)(2,1)}, bf16[256,256]{1,0:T(8,128)(2,1)}, u32[]{:S(2)}, u32[]{:S(2)}) collective-permute-start(bf16[256,256]{1,0:T(8,128)(2,1)} %get-tuple-element.61), channel_id=1, source_target_pairs={{0,32},{32,64},{64,96},{96,0},{1,33},{33,65},{65,97},{97,1},{2,34}... | collective-permute-start | bytes 393224 | tf_op jit(solution)/shard_map/ppermute | solution.py:32
  48.8 7.0 %collective-permute-start.14 = (bf16[256,256]{1,0:T(8,128)(2,1)}, bf16[256,256]{1,0:T(8,128)(2,1)}, u32[]{:S(2)}, u32[]{:S(2)}) collective-permute-start(bf16[256,256]{1,0:T(8,128)(2,1)} %add_convert_fusion.1), channel_id=1, source_target_pairs={{0,16},{16,0},{1,17},{17,1},{2,18},{18,2},{3,19},{19,3},{4,20},{20... | collective-permute-start | bytes 393224 | tf_op jit(solution)/shard_map/ppermute | solution.py:32
  64.9 10.7 %collective-permute-start.18 = (bf16[2,640,256]{2,1,0:T(8,128)(2,1)S(1)}, bf16[2,640,256]{2,1,0:T(8,128)(2,1)S(1)}, u32[]{:S(2)}, u32[]{:S(2)}) collective-permute-start(bf16[2,640,256]{2,1,0:T(8,128)(2,1)S(1)} %get-tuple-element.65), channel_id=1, source_target_pairs={{0,1},{1,0},{2,3},{3,2},{4,5},{5,4},{6,7},{7,6},{8,10},{9,11},{10,... | collective-permute-start | bytes 1966088 | tf_op jit(solution)/shard_map/ppermute | solution.py:317
  66.0 16.6 %collective-permute-start.19 = (bf16[2,640,256]{2,1,0:T(8,128)(2,1)S(1)}, bf16[2,640,256]{2,1,0:T(8,128)(2,1)S(1)}, u32[]{:S(2)}, u32[]{:S(2)}) collective-permute-start(bf16[2,640,256]{2,1,0:T(8,128)(2,1)S(1)} %get-tuple-element.66), channel_id=1, source_target_pairs={{0,1},{1,0},{2,3},{3,2},{4,5},{5,4},{6,7},{7,6},{8,14},{9,15},{10,... | collective-permute-start | bytes 1966088 | tf_op jit(solution)/shard_map/ppermute | solution.py:317
  67.0 15.6 %collective-permute-start.20 = (bf16[2,640,256]{2,1,0:T(8,128)(2,1)S(1)}, bf16[2,640,256]{2,1,0:T(8,128)(2,1)S(1)}, u32[]{:S(2)}, u32[]{:S(2)}) collective-permute-start(bf16[2,640,256]{2,1,0:T(8,128)(2,1)S(1)} %get-tuple-element.64.more), channel_id=1, source_target_pairs={{8,12},{9,13},{10,14},{11,15},{12,8},{13,9},{14,10},{15,11},{24,28... | collective-permute-start | bytes 1966088 | tf_op jit(solution)/shard_map/ppermute | solution.py:317
  82.9 9.6 %collective-permute-start.21 = (bf16[640,256]{1,0:T(8,128)(2,1)S(1)}, bf16[640,256]{1,0:T(8,128)(2,1)S(1)}, u32[]{:S(2)}, u32[]{:S(2)}) collective-permute-start(bf16[640,256]{1,0:T(8,128)(2,1)S(1)} %get-tuple-element.68), channel_id=1, source_target_pairs={{0,2},{1,3},{2,4},{3,5},{4,6},{5,7},{6,0},{7,1},{8,9},{9,8},{10,11... | collective-permute-start | bytes 983048 | tf_op jit(solution)/shard_map/ppermute | solution.py:317
  84.4 11.3 %collective-permute-start.22 = (bf16[640,256]{1,0:T(8,128)(2,1)S(1)}, bf16[640,256]{1,0:T(8,128)(2,1)S(1)}, u32[]{:S(2)}, u32[]{:S(2)}) collective-permute-start(bf16[640,256]{1,0:T(8,128)(2,1)S(1)} %get-tuple-element.69), channel_id=1, source_target_pairs={{0,4},{1,5},{2,6},{3,7},{4,0},{5,1},{6,2},{7,3},{16,20},{17,21},{1... | collective-permute-start | bytes 983048 | tf_op jit(solution)/shard_map/ppermute | solution.py:317
  89.1 9.0 %collective-permute-start.23 = (bf16[640,256]{1,0:T(8,128)(2,1)S(1)}, bf16[640,256]{1,0:T(8,128)(2,1)S(1)}, u32[]{:S(2)}, u32[]{:S(2)}) collective-permute-start(bf16[640,256]{1,0:T(8,128)(2,1)S(1)} %get-tuple-element.70), channel_id=1, source_target_pairs={{0,6},{1,7},{2,0},{3,1},{4,2},{5,3},{6,4},{7,5},{16,22},{17,23},{1... | collective-permute-start | bytes 983048 | tf_op jit(solution)/shard_map/ppermute | solution.py:317

commit v10 on v6

--- a/solution.py
+++ b/solution.py
@@ -297,42 +297,62 @@
 STEP_ROWS = 640
 
 
-def project_kernel(
-    own, across, near1, near2, near3, cos, sin, qg, wq, wk, wv, out, grads
-):
+def query_part_kernel(qg, wq, out):
+    def step(i, carry):
+        rows = pl.ds(pl.multiple_of(i * STEP_ROWS, STEP_ROWS), STEP_ROWS)
+        out[rows, :] = jnp.dot(wq[rows, :], qg[...], preferred_element_type=f32).astype(bf16)
+        return carry
+
+    lax.fori_loop(0, WIDTH // STEP_ROWS, step, 0)
+
+
+def query_part(qg, wq):
+    return pl.pallas_call(
+        query_part_kernel,
+        out_shape=jax.ShapeDtypeStruct((WIDTH, TOK), bf16),
+        in_specs=vmem(2),
+        out_specs=vmem(1)[0],
+        compiler_params=pltpu.CompilerParams(vmem_limit_bytes=16 << 20),
+        cost_estimate=pl.CostEstimate(
+            flops=1700000000, bytes_accessed=9000000, transcendentals=0
+        ),
+        name="query_part",
+    )(qg, wq)
+
+
+def project_kernel(part, own, across, near1, near2, near3, cos, sin, wk, wv, out, grads):
     total = own[...].astype(f32) + across[...].astype(f32)
     for near in (near1, near2, near3):
         total += near[...].astype(f32)
     sign = half_sign((TOK, HEAD), 1)
     g = total[:, :HEAD] * SCALE
     key_grad = g * cos[...] - pltpu.roll(g * sin[...], HEAD // 2, 1) * sign
-    grads[:ROWS, :] = qg[...]
-    grads[ROWS : ROWS + HEAD, :] = key_grad.T.astype(bf16)
-    grads[ROWS + HEAD :, :] = total[:, HEAD:].T.astype(bf16)
+    grads[:HEAD, :] = key_grad.T.astype(bf16)
+    grads[HEAD:, :] = total[:, HEAD:].T.astype(bf16)
 
     def step(i, carry):
         rows = pl.ds(pl.multiple_of(i * STEP_ROWS, STEP_ROWS), STEP_ROWS)
-        weights = jnp.concatenate([wq[rows, :], wk[rows, :], wv[rows, :]], 1)
+        weights = jnp.concatenate([wk[rows, :], wv[rows, :]], 1)
         result = jnp.dot(weights, grads[...], preferred_element_type=f32)
-        out[rows, :] = result.astype(bf16)
+        out[rows, :] = (part[rows, :].astype(f32) + result).astype(bf16)
         return carry
 
     lax.fori_loop(0, WIDTH // STEP_ROWS, step, 0)
 
 
-def project(own, across, near, cos, sin, qg, wq, wk, wv):
+def project(part, own, across, near, cos, sin, wk, wv):
     return pl.pallas_call(
         project_kernel,
         out_shape=jax.ShapeDtypeStruct((WIDTH, TOK), bf16),
-        in_specs=vmem(11),
+        in_specs=vmem(10),
         out_specs=vmem(1)[0],
-        scratch_shapes=[pltpu.VMEM((ROWS + 2 * HEAD, TOK), bf16)],
+        scratch_shapes=[pltpu.VMEM((2 * HEAD, TOK), bf16)],
         compiler_params=pltpu.CompilerParams(vmem_limit_bytes=16 << 20),
         cost_estimate=pl.CostEstimate(
-            flops=2350000000, bytes_accessed=12000000, transcendentals=0
+            flops=700000000, bytes_accessed=6000000, transcendentals=0
         ),
         name="project",
-    )(own, across, *near, cos, sin, qg, wq, wk, wv)
+    )(part, own, across, *near, cos, sin, wk, wv)
 
 
 def last_kernel(parts, out):
@@ -390,8 +410,10 @@
     far = [shift_y(parts[2 + k], -k) for k in (1, 2, 3)]
     near = [shift_y(parts[k - 1], -k) for k in (1, 2, 3)]
     across = across + sum(p.astype(f32) for p in far)
-    across = swap_zh(lax.optimization_barrier(across.astype(bf16)))
-    send = project(own, across, near, cos, sin, query_grad, w_query, key_weight, value_weight)
+    across, query_grad = lax.optimization_barrier((across.astype(bf16), query_grad))
+    across = swap_zh(across)
+    part, near = lax.optimization_barrier((query_part(query_grad, w_query), near))
+    send = project(part, own, across, near, cos, sin, key_weight, value_weight)
     return last_sum(lax.all_to_all(send.reshape(8, 640, TOK), TP, 0, 0))
 
 

time: 94.1 us -> 92 us (0.978)
  waiting for transfers between devices: 19.8 us -> 16.4 us
  Pallas kernels: 12 us -> 13.4 us
    pallas_call x0 -> x1, Pallas kernels: none -> 3.4 us  [query_part(): pl.pallas_call(query_part_kernel, out_shape=jax.ShapeDtypeStruct((WIDTH,...]
    ppermute x18, waiting for transfers between devices: 19.8 us -> 16.4 us  [shift(): return lax.ppermute(x, axes, perm)]
    pallas_call x1, Pallas kernels: 4.24 us -> 2.22 us  [project(): pl.pallas_call(project_kernel, out_shape=jax.ShapeDtypeStruct((WIDTH, TOK...]
  transfers between devices with their start and end apart: 18 -> 18, of which waited for: 11 -> 9; matrix products, arithmetic and copies ran while one was open for 2% -> 2% of each run, Pallas kernels for 1% -> 5%
where the time goes in v10:
time: 92 us; the launch traced here: 91.8 us
  blocking collectives  35.9 us (39%)
  starting transfers between devices  24 us (26%)
  waiting for transfers between devices  16.4 us (18%)
  Pallas kernels  13.4 us (15%)
  other arithmetic  1.58 us (2%)
    all_to_all x1, blocking collectives, local(): return last_sum(lax.all_to_all(send.reshape(8, 640, TOK), TP, 0, 0))  35.9 us
    ppermute x18, starting transfers between devices, shift(): return lax.ppermute(x, axes, perm)  24 us
    ppermute x18, waiting for transfers between devices, shift(): return lax.ppermute(x, axes, perm)  16.4 us
    pallas_call x1, Pallas kernels, attention(): pl.pallas_call(attention_kernel, out_shape=(early, early, late, late, s((...  3.72 us
    pallas_call x1, Pallas kernels, query_part(): pl.pallas_call(query_part_kernel, out_shape=jax.ShapeDtypeStruct((WIDTH,...  3.4 us
    pallas_call x1, Pallas kernels, project(): pl.pallas_call(project_kernel, out_shape=jax.ShapeDtypeStruct((WIDTH, TOK...  2.22 us
    pallas_call x1, Pallas kernels, make_block(): pl.pallas_call(block_kernel, out_shape=(s((TOK, HEAD), f32), s((TOK, HEAD...  2.18 us
  transfers between devices with their start and end apart: 18, of which 9 were waited for; matrix products, arithmetic and copies ran while one was open for 2% of the time, Pallas kernels for 5%

profile of v10, /device:TPU:0, one launch (start us, length us, event | category | flops | bytes accessed | tf_op | source)
XLA Modules:
  0.0 91.8 jit_solution(4603916622631393972)
XLA Ops:
  0.0 2.2 %block.1 = (f32[256,128]{1,0:T(8,128)}, f32[256,128]{1,0:T(8,128)}, bf16[256,256]{1,0:T(8,128)(2,1)}) custom-call(bf16[256,128]{1,0:T(8,128)(2,1)} %key.1, bf16[256,128]{1,0:T(8,128)(2,1)} %value.1, s32[2,1,128]{2,1,0:T(1,128)} %bitcast.8, f32[1,128]{1,0:T(1,128)} %constant.21.clone.inverse), custom_call_target="tpu_custom_call" | custom-call | flops 5000000 | bytes 700000 | tf_op jit(solution)/shard_map/block/pallas_call | solution.py:286
  2.2 4.0 %collective-permute-start = (bf16[256,256]{1,0:T(8,128)(2,1)}, bf16[256,256]{1,0:T(8,128)(2,1)S(1)}, u32[]{:S(2)}, u32[]{:S(2)}) collective-permute-start(bf16[256,256]{1,0:T(8,128)(2,1)} %get-tuple-element.46), channel_id=1, source_target_pairs={{0,16},{16,0},{1,17},{17,1},{2,18},{18,2},{3,19},{19,3},{4,20},{20... | collective-permute-start | bytes 393224 | tf_op jit(solution)/shard_map/ppermute | solution.py:32
  6.2 1.2 %pad_maximum_fusion.joined = bf16[256,1920]{1,0:T(8,128)(2,1)S(1)} fusion(bf16[256,640]{1,0:T(8,128)(2,1)} %param.16, bf16[256,640]{1,0:T(8,128)(2,1)} %param.17, bf16[256,640]{1,0:T(8,128)(2,1)} %param.13), kind=kLoop, calls=%fused_computation.1 | loop fusion | flops 2949120 | bytes 1966080 | tf_op jit(solution)/shard_map/concatenate | solution.py:390
  7.5 0.0 copy-start.4
  7.5 0.0 copy-start.5
  7.5 0.0 copy-start.6
  7.5 1.6 %collective-permute-start.1 = (bf16[256,256]{1,0:T(8,128)(2,1)S(1)}, bf16[256,256]{1,0:T(8,128)(2,1)S(1)}, u32[]{:S(2)}, u32[]{:S(2)}) collective-permute-start(bf16[256,256]{1,0:T(8,128)(2,1)S(1)} %copy-done.7), channel_id=1, source_target_pairs={{0,32},{32,64},{64,96},{96,0},{1,33},{33,65},{65,97},{97,1},{2,34}... | collective-permute-start | bytes 393224 | tf_op jit(solution)/shard_map/ppermute | solution.py:32
  9.2 1.7 %collective-permute-start.3 = (bf16[256,256]{1,0:T(8,128)(2,1)S(1)}, bf16[256,256]{1,0:T(8,128)(2,1)S(1)}, u32[]{:S(2)}, u32[]{:S(2)}) collective-permute-start(bf16[256,256]{1,0:T(8,128)(2,1)S(1)} %copy-done.7), channel_id=1, source_target_pairs={{0,96},{32,0},{64,32},{96,64},{1,97},{33,1},{65,33},{97,65},{2,98}... | collective-permute-start | bytes 393224 | tf_op jit(solution)/shard_map/ppermute | solution.py:32
  10.8 2.0 %collective-permute-start.2 = (bf16[256,256]{1,0:T(8,128)(2,1)S(1)}, bf16[256,256]{1,0:T(8,128)(2,1)S(1)}, u32[]{:S(2)}, u32[]{:S(2)}) collective-permute-start(bf16[256,256]{1,0:T(8,128)(2,1)S(1)} %copy-done.7), channel_id=1, source_target_pairs={{0,64},{32,96},{64,0},{96,32},{1,65},{33,97},{65,1},{97,33},{2,66}... | collective-permute-start | bytes 393224 | tf_op jit(solution)/shard_map/ppermute | solution.py:32
  12.8 0.0 collective-permute-done
  12.8 1.1 %collective-permute-start.7 = (bf16[256,256]{1,0:T(8,128)(2,1)S(1)}, bf16[256,256]{1,0:T(8,128)(2,1)S(1)}, u32[]{:S(2)}, u32[]{:S(2)}) collective-permute-start(bf16[256,256]{1,0:T(8,128)(2,1)S(1)} %collective-permute-done), channel_id=1, source_target_pairs={{0,96},{32,0},{64,32},{96,64},{1,97},{33,1},{65,33},{97,65},{2,98}... | collective-permute-start | bytes 393224 | tf_op jit(solution)/shard_map/ppermute | solution.py:32
  14.0 1.7 %collective-permute-start.6 = (bf16[256,256]{1,0:T(8,128)(2,1)S(1)}, bf16[256,256]{1,0:T(8,128)(2,1)S(1)}, u32[]{:S(2)}, u32[]{:S(2)}) collective-permute-start(bf16[256,256]{1,0:T(8,128)(2,1)S(1)} %collective-permute-done), channel_id=1, source_target_pairs={{0,64},{32,96},{64,0},{96,32},{1,65},{33,97},{65,1},{97,33},{2,66}... | collective-permute-start | bytes 393224 | tf_op jit(solution)/shard_map/ppermute | solution.py:32
  15.7 0.0 collective-permute-done.1
  15.7 0.2 collective-permute-start.5
  15.9 3.1 %collective-permute-done.2 = bf16[256,256]{1,0:T(8,128)(2,1)S(1)} collective-permute-done((bf16[256,256]{1,0:T(8,128)(2,1)S(1)}, bf16[256,256]{1,0:T(8,128)(2,1)S(1)}, u32[]{:S(2)}, u32[]{:S(2)}) %collective-permute-start.2) | collective-permute-done | bytes 131104 | tf_op jit(solution)/shard_map/ppermute | solution.py:32
  19.0 0.0 collective-permute-done.3
  19.0 0.1 collective-permute-start.4
  19.1 4.3 %collective-permute-done.5 = bf16[256,256]{1,0:T(8,128)(2,1)S(1)} collective-permute-done((bf16[256,256]{1,0:T(8,128)(2,1)S(1)}, bf16[256,256]{1,0:T(8,128)(2,1)S(1)}, u32[]{:S(2)}, u32[]{:S(2)}) %collective-permute-start.5) | collective-permute-done | bytes 131104 | tf_op jit(solution)/shard_map/ppermute | solution.py:32
  23.5 0.0 collective-permute-done.6
  23.5 0.1 collective-permute-start.8
  23.6 0.8 prep.1
  24.5 0.9 collective-permute-done.8.late_other
  25.3 0.0 collective-permute-done.4.early_other
  25.3 0.0 slice-start
  25.4 3.7 %attention.1 = (bf16[1280,256]{1,0:T(8,128)(2,1)S(1)}, bf16[1280,256]{1,0:T(8,128)(2,1)S(1)}, bf16[768,256]{1,0:T(8,128)(2,1)S(1)}, bf16[768,256]{1,0:T(8,128)(2,1)S(1)}, bf16[640,256]{1,0:T(8,128)(2,1)S(1)}) custom-call(s32[32,32]{1,0:T(8,128)S(1)} %copy-done.4, s32[1]{0:T(128)} %bitcast.info, s32[32,1,128]{2,1,0:T(1,128)S(1)} %bitcast.7, ...), custom_call_target="tpu_custom_call" | custom-call | flops 2000000000 | bytes 8000000 | tf_op jit(solution)/shard_map/attention/pallas_call | solution.py:261
  29.1 1.3 %collective-permute-start.10 = (bf16[768,256]{1,0:T(8,128)(2,1)S(1)}, bf16[768,256]{1,0:T(8,128)(2,1)S(1)}, u32[]{:S(2)}, u32[]{:S(2)}) collective-permute-start(bf16[768,256]{1,0:T(8,128)(2,1)S(1)} %get-tuple-element.51), channel_id=1, source_target_pairs={{0,8},{8,0},{1,9},{9,1},{2,10},{10,2},{3,11},{11,3},{4,12},{12,4},... | collective-permute-start | bytes 1179656 | tf_op jit(solution)/shard_map/ppermute | solution.py:32
  30.4 0.1 collective-permute-start.9
  30.5 1.3 %collective-permute-done.10 = bf16[768,256]{1,0:T(8,128)(2,1)S(1)} collective-permute-done((bf16[768,256]{1,0:T(8,128)(2,1)S(1)}, bf16[768,256]{1,0:T(8,128)(2,1)S(1)}, u32[]{:S(2)}, u32[]{:S(2)}) %collective-permute-start.10) | collective-permute-done | bytes 393248 | tf_op jit(solution)/shard_map/ppermute | solution.py:32
  31.7 0.1 add_convert_fusion
  31.9 0.8 collective-permute-done.9
  32.7 0.2 fusion
  32.9 2.1 %collective-permute-start.11 = (bf16[256,256]{1,0:T(8,128)(2,1)S(1)}, bf16[256,256]{1,0:T(8,128)(2,1)S(1)}, u32[]{:S(2)}, u32[]{:S(2)}) collective-permute-start(bf16[256,256]{1,0:T(8,128)(2,1)S(1)} %get-tuple-element.53), channel_id=1, source_target_pairs={{0,96},{32,0},{64,32},{96,64},{1,97},{33,1},{65,33},{97,65},{2,98}... | collective-permute-start | bytes 393224 | tf_op jit(solution)/shard_map/ppermute | solution.py:32
  35.0 1.2 %collective-permute-start.12 = (bf16[256,256]{1,0:T(8,128)(2,1)S(1)}, bf16[256,256]{1,0:T(8,128)(2,1)S(1)}, u32[]{:S(2)}, u32[]{:S(2)}) collective-permute-start(bf16[256,256]{1,0:T(8,128)(2,1)S(1)} %get-tuple-element.54), channel_id=1, source_target_pairs={{0,64},{32,96},{64,0},{96,32},{1,65},{33,97},{65,1},{97,33},{2,66}... | collective-permute-start | bytes 393224 | tf_op jit(solution)/shard_map/ppermute | solution.py:32
  36.1 0.0 collective-permute-start.13
  36.2 3.2 %collective-permute-start.14 = (bf16[256,256]{1,0:T(8,128)(2,1)S(1)}, bf16[256,256]{1,0:T(8,128)(2,1)S(1)}, u32[]{:S(2)}, u32[]{:S(2)}) collective-permute-start(bf16[256,256]{1,0:T(8,128)(2,1)S(1)} %get-tuple-element.58), channel_id=1, source_target_pairs={{0,96},{32,0},{64,32},{96,64},{1,97},{33,1},{65,33},{97,65},{2,98}... | collective-permute-start | bytes 393224 | tf_op jit(solution)/shard_map/ppermute | solution.py:32
  39.4 1.1 %collective-permute-start.15 = (bf16[256,256]{1,0:T(8,128)(2,1)S(1)}, bf16[256,256]{1,0:T(8,128)(2,1)S(1)}, u32[]{:S(2)}, u32[]{:S(2)}) collective-permute-start(bf16[256,256]{1,0:T(8,128)(2,1)S(1)} %get-tuple-element.59), channel_id=1, source_target_pairs={{0,64},{32,96},{64,0},{96,32},{1,65},{33,97},{65,1},{97,33},{2,66}... | collective-permute-start | bytes 393224 | tf_op jit(solution)/shard_map/ppermute | solution.py:32
  40.5 0.7 collective-permute-done.11
  41.2 1.6 %collective-permute-done.12 = bf16[256,256]{1,0:T(8,128)(2,1)S(1)} collective-permute-done((bf16[256,256]{1,0:T(8,128)(2,1)S(1)}, bf16[256,256]{1,0:T(8,128)(2,1)S(1)}, u32[]{:S(2)}, u32[]{:S(2)}) %collective-permute-start.12) | collective-permute-done | bytes 131104 | tf_op jit(solution)/shard_map/ppermute | solution.py:32
  42.8 2.9 %collective-permute-done.13 = bf16[256,256]{1,0:T(8,128)(2,1)S(1)} collective-permute-done((bf16[256,256]{1,0:T(8,128)(2,1)S(1)}, bf16[256,256]{1,0:T(8,128)(2,1)S(1)}, u32[]{:S(2)}, u32[]{:S(2)}) %collective-permute-start.13) | collective-permute-done | bytes 131104 | tf_op jit(solution)/shard_map/ppermute | solution.py:32
  45.7 0.1 add_convert_fusion.1
  45.8 0.0 copy-start
  45.8 0.0 copy-start.1
  45.8 2.4 %collective-permute-start.17 = (bf16[256,256]{1,0:T(8,128)(2,1)S(1)}, bf16[256,256]{1,0:T(8,128)(2,1)S(1)}, u32[]{:S(2)}, u32[]{:S(2)}) collective-permute-start(bf16[256,256]{1,0:T(8,128)(2,1)S(1)} %add_convert_fusion.1), channel_id=1, source_target_pairs={{0,16},{16,0},{1,17},{17,1},{2,18},{18,2},{3,19},{19,3},{4,20},{20... | collective-permute-start | bytes 393224 | tf_op jit(solution)/shard_map/ppermute | solution.py:32
  48.3 3.4 %query_part.1.part = bf16[5120,256]{1,0:T(8,128)(2,1)S(1)} custom-call(bf16[640,256]{1,0:T(8,128)(2,1)S(1)} %get-tuple-element.57.qg, bf16[5120,640]{1,0:T(8,128)(2,1)S(1)} %bitcast.6), custom_call_target="tpu_custom_call" | custom-call | flops 1700000000 | bytes 9000000 | tf_op jit(solution)/shard_map/query_part/pallas_call | solution.py:310
  51.7 0.9 collective-permute-done.17.across
  52.6 2.2 %project.1 = bf16[5120,256]{1,0:T(8,128)(2,1)S(1)} custom-call(bf16[5120,256]{1,0:T(8,128)(2,1)S(1)} %query_part.1.part, f32[256,256]{1,0:T(8,128)S(1)} %get-tuple-element.62.own, bf16[256,256]{1,0:T(8,128)(2,1)S(1)} %collective-permute-done.17.across, bf16[256,256]{1,0:T(8,128)(2,1)S(1)} %collective-permute-done.14.near1, ...), custom_call_target="tpu_custom_call" | custom-call | flops 700000000 | bytes 6000000 | tf_op jit(solution)/shard_map/project/pallas_call | solution.py:344
  54.9 35.9 %all_to_all.5.parts = bf16[8,640,256]{2,1,0:T(8,128)(2,1)S(1)} all-to-all(bf16[8,640,256]{2,1,0:T(8,128)(2,1)S(1)} %bitcast.4), channel_id=1, replica_groups=mesh['y'=4,'zh'=2,'core'=2,'x'=4,'zl'=2] {'x','zl'}, dimensions={0} | all-to-all | bytes 5242880 | tf_op jit(solution)/shard_map/all_to_all | solution.py:417
  90.8 1.1 %last_sum.1 = bf16[640,256]{1,0:T(8,128)(2,1)} custom-call(bf16[8,640,256]{2,1,0:T(8,128)(2,1)S(1)} %all_to_all.5.parts), custom_call_target="tpu_custom_call" | custom-call | flops 1300000 | bytes 3000000 | tf_op jit(solution)/shard_map/last_sum/pallas_call | solution.py:371
  (31 shorter events, 0.2 us)
Async XLA Ops:
  2.2 5.3 %copy-start.7 = (bf16[256,256]{1,0:T(8,128)(2,1)S(1)}, bf16[256,256]{1,0:T(8,128)(2,1)}, u32[]{:S(2)}) copy-start(bf16[256,256]{1,0:T(8,128)(2,1)} %get-tuple-element.46) | copy-start | bytes 393220
  2.2 21.4 %copy-start.2 = (f32[256,128]{1,0:T(8,128)S(1)}, f32[256,128]{1,0:T(8,128)}, u32[]{:S(2)}) copy-start(f32[256,128]{1,0:T(8,128)} %get-tuple-element.39.cos) | copy-start | bytes 393220
  2.2 21.4 %copy-start.3 = (f32[256,128]{1,0:T(8,128)S(1)}, f32[256,128]{1,0:T(8,128)}, u32[]{:S(2)}) copy-start(f32[256,128]{1,0:T(8,128)} %get-tuple-element.40.sin) | copy-start | bytes 393220
  2.2 10.6 %collective-permute-start = (bf16[256,256]{1,0:T(8,128)(2,1)}, bf16[256,256]{1,0:T(8,128)(2,1)S(1)}, u32[]{:S(2)}, u32[]{:S(2)}) collective-permute-start(bf16[256,256]{1,0:T(8,128)(2,1)} %get-tuple-element.46), channel_id=1, source_target_pairs={{0,16},{16,0},{1,17},{17,1},{2,18},{18,2},{3,19},{19,3},{4,20},{20... | collective-permute-start | bytes 393224 | tf_op jit(solution)/shard_map/ppermute | solution.py:32
  7.5 17.8 %copy-start.4 = (s32[32,32]{1,0:T(8,128)S(1)}, s32[32,32]{1,0:T(8,128)}, u32[]{:S(2)}) copy-start(s32[32,32]{1,0:T(8,128)} %mask.1) | copy-start | bytes 12292
  7.5 17.8 %copy-start.5 = (s32[4096]{0:T(1024)S(1)}, s32[4096]{0:T(1024)}, u32[]{:S(2)}) copy-start(s32[4096]{0:T(1024)} %param.21) | copy-start | bytes 49156
  7.5 17.8 %copy-start.6 = (f32[5,256]{1,0:T(8,128)S(1)}, f32[5,256]{1,0:T(8,128)}, u32[]{:S(2)}) copy-start(f32[5,256]{1,0:T(8,128)} %lse.1) | copy-start | bytes 15364
  7.5 8.1 %collective-permute-start.1 = (bf16[256,256]{1,0:T(8,128)(2,1)S(1)}, bf16[256,256]{1,0:T(8,128)(2,1)S(1)}, u32[]{:S(2)}, u32[]{:S(2)}) collective-permute-start(bf16[256,256]{1,0:T(8,128)(2,1)S(1)} %copy-done.7), channel_id=1, source_target_pairs={{0,32},{32,64},{64,96},{96,0},{1,33},{33,65},{65,97},{97,1},{2,34}... | collective-permute-start | bytes 393224 | tf_op jit(solution)/shard_map/ppermute | solution.py:32
  9.2 9.8 %collective-permute-start.3 = (bf16[256,256]{1,0:T(8,128)(2,1)S(1)}, bf16[256,256]{1,0:T(8,128)(2,1)S(1)}, u32[]{:S(2)}, u32[]{:S(2)}) collective-permute-start(bf16[256,256]{1,0:T(8,128)(2,1)S(1)} %copy-done.7), channel_id=1, source_target_pairs={{0,96},{32,0},{64,32},{96,64},{1,97},{33,1},{65,33},{97,65},{2,98}... | collective-permute-start | bytes 393224 | tf_op jit(solution)/shard_map/ppermute | solution.py:32
  10.8 8.1 %collective-permute-start.2 = (bf16[256,256]{1,0:T(8,128)(2,1)S(1)}, bf16[256,256]{1,0:T(8,128)(2,1)S(1)}, u32[]{:S(2)}, u32[]{:S(2)}) collective-permute-start(bf16[256,256]{1,0:T(8,128)(2,1)S(1)} %copy-done.7), channel_id=1, source_target_pairs={{0,64},{32,96},{64,0},{96,32},{1,65},{33,97},{65,1},{97,33},{2,66}... | collective-permute-start | bytes 393224 | tf_op jit(solution)/shard_map/ppermute | solution.py:32
  12.8 10.6 %collective-permute-start.7 = (bf16[256,256]{1,0:T(8,128)(2,1)S(1)}, bf16[256,256]{1,0:T(8,128)(2,1)S(1)}, u32[]{:S(2)}, u32[]{:S(2)}) collective-permute-start(bf16[256,256]{1,0:T(8,128)(2,1)S(1)} %collective-permute-done), channel_id=1, source_target_pairs={{0,96},{32,0},{64,32},{96,64},{1,97},{33,1},{65,33},{97,65},{2,98}... | collective-permute-start | bytes 393224 | tf_op jit(solution)/shard_map/ppermute | solution.py:32
  14.0 9.5 %collective-permute-start.6 = (bf16[256,256]{1,0:T(8,128)(2,1)S(1)}, bf16[256,256]{1,0:T(8,128)(2,1)S(1)}, u32[]{:S(2)}, u32[]{:S(2)}) collective-permute-start(bf16[256,256]{1,0:T(8,128)(2,1)S(1)} %collective-permute-done), channel_id=1, source_target_pairs={{0,64},{32,96},{64,0},{96,32},{1,65},{33,97},{65,1},{97,33},{2,66}... | collective-permute-start | bytes 393224 | tf_op jit(solution)/shard_map/ppermute | solution.py:32
  15.7 7.8 %collective-permute-start.5 = (bf16[256,256]{1,0:T(8,128)(2,1)S(1)}, bf16[256,256]{1,0:T(8,128)(2,1)S(1)}, u32[]{:S(2)}, u32[]{:S(2)}) collective-permute-start(bf16[256,256]{1,0:T(8,128)(2,1)S(1)} %collective-permute-done), channel_id=1, source_target_pairs={{0,32},{32,64},{64,96},{96,0},{1,33},{33,65},{65,97},{97,1},{2,34}... | collective-permute-start | bytes 393224 | tf_op jit(solution)/shard_map/ppermute | solution.py:32
  19.0 6.3 %collective-permute-start.4 = (bf16[1280,256]{1,0:T(8,128)(2,1)S(1)}, bf16[1280,256]{1,0:T(8,128)(2,1)S(1)}, u32[]{:S(2)}, u32[]{:S(2)}) collective-permute-start(bf16[1280,256]{1,0:T(8,128)(2,1)S(1)} %constant_dynamic-update-slice_fusion.early_mine), channel_id=1, source_target_pairs={{0,8},{8,0},{1,9},{9,1},{2,10},{10,2},{3,11},{11,3},{4,12},{12,4},... | collective-permute-start | bytes 1966088 | tf_op jit(solution)/shard_map/ppermute | solution.py:32
  23.5 1.8 %collective-permute-start.8 = (bf16[768,256]{1,0:T(8,128)(2,1)S(1)}, bf16[768,256]{1,0:T(8,128)(2,1)S(1)}, u32[]{:S(2)}, u32[]{:S(2)}) collective-permute-start(bf16[768,256]{1,0:T(8,128)(2,1)S(1)} %constant_dynamic-update-slice_fusion.5.late_mine), channel_id=1, source_target_pairs={{0,8},{8,0},{1,9},{9,1},{2,10},{10,2},{3,11},{11,3},{4,12},{12,4},... | collective-permute-start | bytes 1179656 | tf_op jit(solution)/shard_map/ppermute | solution.py:32
  25.3 22.9 %slice-start = ((s8[6553600]{0:T(1024)(128)(4,1)}), s8[2359296]{0:T(1024)(128)(4,1)S(1)}, s32[]{:S(2)}) async-start(s8[6553600]{0:T(1024)(128)(4,1)} %bitcast.5), calls=%async_computation.1 | async-start | bytes 4718592
  29.1 2.6 %collective-permute-start.10 = (bf16[768,256]{1,0:T(8,128)(2,1)S(1)}, bf16[768,256]{1,0:T(8,128)(2,1)S(1)}, u32[]{:S(2)}, u32[]{:S(2)}) collective-permute-start(bf16[768,256]{1,0:T(8,128)(2,1)S(1)} %get-tuple-element.51), channel_id=1, source_target_pairs={{0,8},{8,0},{1,9},{9,1},{2,10},{10,2},{3,11},{11,3},{4,12},{12,4},... | collective-permute-start | bytes 1179656 | tf_op jit(solution)/shard_map/ppermute | solution.py:32
  30.4 2.3 %collective-permute-start.9 = (bf16[1280,256]{1,0:T(8,128)(2,1)S(1)}, bf16[1280,256]{1,0:T(8,128)(2,1)S(1)}, u32[]{:S(2)}, u32[]{:S(2)}) collective-permute-start(bf16[1280,256]{1,0:T(8,128)(2,1)S(1)} %get-tuple-element.49), channel_id=1, source_target_pairs={{0,8},{8,0},{1,9},{9,1},{2,10},{10,2},{3,11},{11,3},{4,12},{12,4},... | collective-permute-start | bytes 1966088 | tf_op jit(solution)/shard_map/ppermute | solution.py:32
  31.7 16.6 %slice-start.1 = ((s8[6553600]{0:T(1024)(128)(4,1)}), s8[4194304]{0:T(1024)(128)(4,1)S(1)}, s32[]{:S(2)}) async-start(s8[6553600]{0:T(1024)(128)(4,1)} %bitcast.5), calls=%async_computation.2 | async-start | bytes 8388608
  32.9 8.3 %collective-permute-start.11 = (bf16[256,256]{1,0:T(8,128)(2,1)S(1)}, bf16[256,256]{1,0:T(8,128)(2,1)S(1)}, u32[]{:S(2)}, u32[]{:S(2)}) collective-permute-start(bf16[256,256]{1,0:T(8,128)(2,1)S(1)} %get-tuple-element.53), channel_id=1, source_target_pairs={{0,96},{32,0},{64,32},{96,64},{1,97},{33,1},{65,33},{97,65},{2,98}... | collective-permute-start | bytes 393224 | tf_op jit(solution)/shard_map/ppermute | solution.py:32
  35.0 7.9 %collective-permute-start.12 = (bf16[256,256]{1,0:T(8,128)(2,1)S(1)}, bf16[256,256]{1,0:T(8,128)(2,1)S(1)}, u32[]{:S(2)}, u32[]{:S(2)}) collective-permute-start(bf16[256,256]{1,0:T(8,128)(2,1)S(1)} %get-tuple-element.54), channel_id=1, source_target_pairs={{0,64},{32,96},{64,0},{96,32},{1,65},{33,97},{65,1},{97,33},{2,66}... | collective-permute-start | bytes 393224 | tf_op jit(solution)/shard_map/ppermute | solution.py:32
  36.1 9.6 %collective-permute-start.13 = (bf16[256,256]{1,0:T(8,128)(2,1)S(1)}, bf16[256,256]{1,0:T(8,128)(2,1)S(1)}, u32[]{:S(2)}, u32[]{:S(2)}) collective-permute-start(bf16[256,256]{1,0:T(8,128)(2,1)S(1)} %get-tuple-element.55), channel_id=1, source_target_pairs={{0,32},{32,64},{64,96},{96,0},{1,33},{33,65},{65,97},{97,1},{2,34}... | collective-permute-start | bytes 393224 | tf_op jit(solution)/shard_map/ppermute | solution.py:32
  36.2 15.5 %collective-permute-start.14 = (bf16[256,256]{1,0:T(8,128)(2,1)S(1)}, bf16[256,256]{1,0:T(8,128)(2,1)S(1)}, u32[]{:S(2)}, u32[]{:S(2)}) collective-permute-start(bf16[256,256]{1,0:T(8,128)(2,1)S(1)} %get-tuple-element.58), channel_id=1, source_target_pairs={{0,96},{32,0},{64,32},{96,64},{1,97},{33,1},{65,33},{97,65},{2,98}... | collective-permute-start | bytes 393224 | tf_op jit(solution)/shard_map/ppermute | solution.py:32
  39.4 12.3 %collective-permute-start.15 = (bf16[256,256]{1,0:T(8,128)(2,1)S(1)}, bf16[256,256]{1,0:T(8,128)(2,1)S(1)}, u32[]{:S(2)}, u32[]{:S(2)}) collective-permute-start(bf16[256,256]{1,0:T(8,128)(2,1)S(1)} %get-tuple-element.59), channel_id=1, source_target_pairs={{0,64},{32,96},{64,0},{96,32},{1,65},{33,97},{65,1},{97,33},{2,66}... | collective-permute-start | bytes 393224 | tf_op jit(solution)/shard_map/ppermute | solution.py:32
  41.2 10.5 %collective-permute-start.16 = (bf16[256,256]{1,0:T(8,128)(2,1)S(1)}, bf16[256,256]{1,0:T(8,128)(2,1)S(1)}, u32[]{:S(2)}, u32[]{:S(2)}) collective-permute-start(bf16[256,256]{1,0:T(8,128)(2,1)S(1)} %get-tuple-element.60), channel_id=1, source_target_pairs={{0,32},{32,64},{64,96},{96,0},{1,33},{33,65},{65,97},{97,1},{2,34}... | collective-permute-start | bytes 393224 | tf_op jit(solution)/shard_map/ppermute | solution.py:32
  45.8 6.8 %copy-start = (bf16[5120,128]{1,0:T(8,128)(2,1)S(1)}, bf16[5120,128]{1,0:T(8,128)(2,1)}, u32[]{:S(2)}) copy-start(bf16[5120,128]{1,0:T(8,128)(2,1)} %wk.1) | copy-start | bytes 3932164
  45.8 6.8 %copy-start.1 = (bf16[5120,128]{1,0:T(8,128)(2,1)S(1)}, bf16[5120,128]{1,0:T(8,128)(2,1)}, u32[]{:S(2)}) copy-start(bf16[5120,128]{1,0:T(8,128)(2,1)} %wv.1) | copy-start | bytes 3932164
  45.8 6.8 %collective-permute-start.17 = (bf16[256,256]{1,0:T(8,128)(2,1)S(1)}, bf16[256,256]{1,0:T(8,128)(2,1)S(1)}, u32[]{:S(2)}, u32[]{:S(2)}) collective-permute-start(bf16[256,256]{1,0:T(8,128)(2,1)S(1)} %add_convert_fusion.1), channel_id=1, source_target_pairs={{0,16},{16,0},{1,17},{17,1},{2,18},{18,2},{3,19},{19,3},{4,20},{20... | collective-permute-start | bytes 393224 | tf_op jit(solution)/shard_map/ppermute | solution.py:32

commit v11 on v10

--- a/solution.py
+++ b/solution.py
@@ -53,11 +53,15 @@
 
 def block_kernel(key, value, positions, inverse, cos, sin, block):
     sign = half_sign((TILE, HEAD), 1)
+    low = lax.broadcasted_iota(jnp.int32, (TILE, HEAD), 1) < HEAD // 2
+    places = [jnp.broadcast_to(positions[t].astype(f32), (TILE, TILE)).T for t in range(2)]
+    angles = jnp.where(low, places[0], places[1]) * inverse[...]
+    both_cos, both_sin = jnp.cos(angles), jnp.sin(angles)
     for t in range(2):
         tok = pl.ds(t * TILE, TILE)
-        place = jnp.broadcast_to(positions[t].astype(f32), (TILE, TILE)).T
-        angles = place * inverse[...]
-        c, s = jnp.cos(angles), jnp.sin(angles)
+        mine = low if t == 0 else jnp.logical_not(low)
+        c = jnp.where(mine, both_cos, pltpu.roll(both_cos, HEAD // 2, 1))
+        s = jnp.where(mine, both_sin, pltpu.roll(both_sin, HEAD // 2, 1))
         cos[tok, :] = c
         sin[tok, :] = s
         x = key[tok, :].astype(f32)
@@ -65,7 +69,7 @@
         block[tok, HEAD:] = value[tok, :]
 
 
-def prep_kernel(joined, cos, sin, q_rows, q_cols, g_rows, g_cols, delta):
+def prep_kernel(query, grad, att, cos, sin, q_rows, q_cols, g_rows, g_cols, delta):
     sign = half_sign((TILE, HEAD), 1)
     for t in range(2):
         tok = pl.ds(t * TILE, TILE)
@@ -73,14 +77,14 @@
         for h in range(GROUPS):
             feat = pl.ds(h * HEAD, HEAD)
             lane = pl.ds(h * TILE, TILE)
-            x = joined[tok, feat].astype(f32)
+            x = query[tok, feat].astype(f32)
             rot = (x * c + pltpu.roll(x, HEAD // 2, 1) * s).astype(bf16)
             q_rows[t, lane, :] = rot
             q_cols[t, :, lane] = rot.T
-            g = joined[tok, pl.ds(ROWS + h * HEAD, HEAD)]
+            g = grad[tok, feat]
             g_rows[t, lane, :] = g
             g_cols[t, :, lane] = g.T
-            prod = g.astype(f32) * joined[tok, pl.ds(2 * ROWS + h * HEAD, HEAD)].astype(f32)
+            prod = g.astype(f32) * att[tok, feat].astype(f32)
             delta[t, :, lane] = jnp.sum(prod.T, axis=0, keepdims=True)
 
 
@@ -225,7 +229,7 @@
         tok = pl.ds(t * TILE, TILE)
         c, s = cos[tok, :].T, sin[tok, :].T
         for h in range(GROUPS):
-            g = dq[t, :, pl.ds(h * TILE, TILE)] * SCALE
+            g = dq[t, :, pl.ds(h * TILE, TILE)]
             u = g * s
             half = HEAD // 2
             turned = jnp.concatenate([u[half:], -u[:half]], 0)
@@ -236,7 +240,7 @@
     return [pl.BlockSpec(memory_space=pltpu.VMEM)] * n
 
 
-def prep(joined, cos, sin):
+def prep(query, grad, att, cos, sin):
     s = jax.ShapeDtypeStruct
     return pl.pallas_call(
         prep_kernel,
@@ -247,12 +251,12 @@
             s((2, HEAD, ROWS), bf16),
             s((2, 1, ROWS), f32),
         ),
-        in_specs=vmem(3),
+        in_specs=vmem(5),
         out_specs=tuple(vmem(5)),
         compiler_params=pltpu.CompilerParams(vmem_limit_bytes=12 << 20),
         cost_estimate=pl.CostEstimate(flops=1000000, bytes_accessed=10000, transcendentals=0),
         name="prep",
-    )(joined, cos, sin)
+    )(query, grad, att, cos, sin)
 
 
 def attention(mask, info, *operands):
@@ -387,17 +391,16 @@
     cos, sin, block = make_block(key, value, positions)
 
     across = swap_zh(block)
-    joined = jnp.concatenate([query, grad, att], 1)
-    joined, again = lax.optimization_barrier((joined, block))
+    scaled, again = lax.optimization_barrier(((cos * SCALE, sin * SCALE), block))
     near = [shift_y(again, k) for k in (1, 2, 3)]
-    across, joined = lax.optimization_barrier((across, joined))
+    across, query, grad, att = lax.optimization_barrier((across, query, grad, att))
     far = [shift_y(across, k) for k in (1, 2, 3)]
-    q_rows, q_cols, g_rows, g_cols, delta = prep(joined, cos, sin)
+    q_rows, q_cols, g_rows, g_cols, delta = prep(query, grad, att, cos, sin)
     early = jnp.concatenate([block] + near + [across], 0)
     late = jnp.concatenate(far, 0)
 
     early_mine, early_other, late_mine, late_other, query_grad = attention(
-        block_mask, me.reshape(1), segments.reshape(TILES, 1, TILE), lse, delta, cos, sin, q_rows,
+        block_mask, me.reshape(1), segments.reshape(TILES, 1, TILE), lse, delta, *scaled, q_rows,
         q_cols, g_rows, g_cols, early, swap_core(early), late, swap_core(late),
     )
 

time: 92 us -> 92.3 us (level)
  local copies, waits for them, and re-layouts: 0.23 us -> 1.18 us
    concatenate x1 -> x0, other arithmetic: 1.25 us -> none  [local(): joined = jnp.concatenate([query, grad, att], 1)]
    mul x0 -> x1, other arithmetic: none -> 1.09 us  [local(): sin * SCALE]
    unnamed x26 -> x30, local copies, waits for them, and re-layouts: 0.11 us -> 1.06 us
  transfers between devices with their start and end apart: 18 -> 18, of which waited for: 9 -> 9; matrix products, arithmetic and copies ran while one was open for 2% -> 3% of each run, Pallas kernels for 5% -> 5%
where the time goes in v11:
time: 92.3 us; the launch traced here: 92 us
  blocking collectives  35.9 us (39%)
  starting transfers between devices  23.8 us (26%)
  waiting for transfers between devices  15.9 us (17%)
  Pallas kernels  13.5 us (15%)
  other arithmetic  1.42 us (2%)
  local copies, waits for them, and re-layouts  1.18 us (1%)
    all_to_all x1, blocking collectives, local(): return last_sum(lax.all_to_all(send.reshape(8, 640, TOK), TP, 0, 0))  35.9 us
    ppermute x18, starting transfers between devices, shift(): return lax.ppermute(x, axes, perm)  23.8 us
    ppermute x18, waiting for transfers between devices, shift(): return lax.ppermute(x, axes, perm)  15.9 us
    pallas_call x1, Pallas kernels, attention(): pl.pallas_call(attention_kernel, out_shape=(early, early, late, late, s((...  4.05 us
    pallas_call x1, Pallas kernels, query_part(): pl.pallas_call(query_part_kernel, out_shape=jax.ShapeDtypeStruct((WIDTH,...  3.4 us
    pallas_call x1, Pallas kernels, project(): pl.pallas_call(project_kernel, out_shape=jax.ShapeDtypeStruct((WIDTH, TOK...  2.21 us
    pallas_call x1, Pallas kernels, make_block(): pl.pallas_call(block_kernel, out_shape=(s((TOK, HEAD), f32), s((TOK, HEAD...  1.99 us
  transfers between devices with their start and end apart: 18, of which 9 were waited for; matrix products, arithmetic and copies ran while one was open for 3% of the time, Pallas kernels for 5%

profile of v11, /device:TPU:0, one launch (start us, length us, event | category | flops | bytes accessed | tf_op | source)
XLA Modules:
  0.0 92.0 jit_solution(3655657399988197703)
XLA Ops:
  0.0 2.0 %block.1 = (f32[256,128]{1,0:T(8,128)}, f32[256,128]{1,0:T(8,128)}, bf16[256,256]{1,0:T(8,128)(2,1)}) custom-call(bf16[256,128]{1,0:T(8,128)(2,1)} %key.1, bf16[256,128]{1,0:T(8,128)(2,1)} %value.1, s32[2,1,128]{2,1,0:T(1,128)} %bitcast.8, f32[1,128]{1,0:T(1,128)} %constant.23.clone.inverse), custom_call_target="tpu_custom_call" | custom-call | flops 5000000 | bytes 700000 | tf_op jit(solution)/shard_map/block/pallas_call | solution.py:290
  2.0 4.0 %collective-permute-start = (bf16[256,256]{1,0:T(8,128)(2,1)}, bf16[256,256]{1,0:T(8,128)(2,1)S(1)}, u32[]{:S(2)}, u32[]{:S(2)}) collective-permute-start(bf16[256,256]{1,0:T(8,128)(2,1)} %get-tuple-element.52), channel_id=1, source_target_pairs={{0,16},{16,0},{1,17},{17,1},{2,18},{18,2},{3,19},{19,3},{4,20},{20... | collective-permute-start | bytes 393224 | tf_op jit(solution)/shard_map/ppermute | solution.py:32
  6.0 0.0 copy-start.6
  6.0 1.1 %broadcast_multiply_fusion = (f32[256,128]{1,0:T(8,128)S(1)}, f32[256,128]{1,0:T(8,128)S(1)}) fusion(f32[256,128]{1,0:T(8,128)} %get-tuple-element.44.sin, f32[256,128]{1,0:T(8,128)} %get-tuple-element.43.cos), kind=kLoop, calls=%fused_computation.3 | loop fusion | flops 65536 | bytes 524288 | tf_op jit(solution)/shard_map/mul | solution.py:394
  7.1 1.6 %collective-permute-start.1 = (bf16[256,256]{1,0:T(8,128)(2,1)}, bf16[256,256]{1,0:T(8,128)(2,1)S(1)}, u32[]{:S(2)}, u32[]{:S(2)}) collective-permute-start(bf16[256,256]{1,0:T(8,128)(2,1)} %get-tuple-element.52), channel_id=1, source_target_pairs={{0,32},{32,64},{64,96},{96,0},{1,33},{33,65},{65,97},{97,1},{2,34}... | collective-permute-start | bytes 393224 | tf_op jit(solution)/shard_map/ppermute | solution.py:32
  8.7 1.7 %collective-permute-start.3 = (bf16[256,256]{1,0:T(8,128)(2,1)}, bf16[256,256]{1,0:T(8,128)(2,1)S(1)}, u32[]{:S(2)}, u32[]{:S(2)}) collective-permute-start(bf16[256,256]{1,0:T(8,128)(2,1)} %get-tuple-element.52), channel_id=1, source_target_pairs={{0,96},{32,0},{64,32},{96,64},{1,97},{33,1},{65,33},{97,65},{2,98}... | collective-permute-start | bytes 393224 | tf_op jit(solution)/shard_map/ppermute | solution.py:32
  10.4 2.0 %collective-permute-start.2 = (bf16[256,256]{1,0:T(8,128)(2,1)}, bf16[256,256]{1,0:T(8,128)(2,1)S(1)}, u32[]{:S(2)}, u32[]{:S(2)}) collective-permute-start(bf16[256,256]{1,0:T(8,128)(2,1)} %get-tuple-element.52), channel_id=1, source_target_pairs={{0,64},{32,96},{64,0},{96,32},{1,65},{33,97},{65,1},{97,33},{2,66}... | collective-permute-start | bytes 393224 | tf_op jit(solution)/shard_map/ppermute | solution.py:32
  12.4 0.9 %constant_dynamic-update-slice_fusion.4 = bf16[1280,256]{1,0:T(8,128)(2,1)S(1)} fusion(bf16[256,256]{1,0:T(8,128)(2,1)} %get-tuple-element.52), kind=kLoop, calls=%fused_computation.9 | loop fusion | bytes 262144
  13.3 0.0 collective-permute-done
  13.3 1.1 %collective-permute-start.7 = (bf16[256,256]{1,0:T(8,128)(2,1)S(1)}, bf16[256,256]{1,0:T(8,128)(2,1)S(1)}, u32[]{:S(2)}, u32[]{:S(2)}) collective-permute-start(bf16[256,256]{1,0:T(8,128)(2,1)S(1)} %collective-permute-done), channel_id=1, source_target_pairs={{0,96},{32,0},{64,32},{96,64},{1,97},{33,1},{65,33},{97,65},{2,98}... | collective-permute-start | bytes 393224 | tf_op jit(solution)/shard_map/ppermute | solution.py:32
  14.4 1.7 %collective-permute-start.6 = (bf16[256,256]{1,0:T(8,128)(2,1)S(1)}, bf16[256,256]{1,0:T(8,128)(2,1)S(1)}, u32[]{:S(2)}, u32[]{:S(2)}) collective-permute-start(bf16[256,256]{1,0:T(8,128)(2,1)S(1)} %collective-permute-done), channel_id=1, source_target_pairs={{0,64},{32,96},{64,0},{96,32},{1,65},{33,97},{65,1},{97,33},{2,66}... | collective-permute-start | bytes 393224 | tf_op jit(solution)/shard_map/ppermute | solution.py:32
  16.1 0.2 collective-permute-start.5
  16.4 1.7 %collective-permute-done.2 = bf16[256,256]{1,0:T(8,128)(2,1)S(1)} collective-permute-done((bf16[256,256]{1,0:T(8,128)(2,1)}, bf16[256,256]{1,0:T(8,128)(2,1)S(1)}, u32[]{:S(2)}, u32[]{:S(2)}) %collective-permute-start.2) | collective-permute-done | bytes 131104 | tf_op jit(solution)/shard_map/ppermute | solution.py:32
  18.1 0.0 copy-start.7
  18.1 0.0 copy-start.8
  18.1 0.0 copy-start.9
  18.2 0.0 collective-permute-done.3
  18.2 0.1 collective-permute-start.4
  18.3 4.9 %collective-permute-done.5 = bf16[256,256]{1,0:T(8,128)(2,1)S(1)} collective-permute-done((bf16[256,256]{1,0:T(8,128)(2,1)S(1)}, bf16[256,256]{1,0:T(8,128)(2,1)S(1)}, u32[]{:S(2)}, u32[]{:S(2)}) %collective-permute-start.5) | collective-permute-done | bytes 131104 | tf_op jit(solution)/shard_map/ppermute | solution.py:32
  23.2 0.0 collective-permute-done.6
  23.2 0.0 collective-permute-done.7
  23.3 0.1 collective-permute-start.8
  23.4 0.8 prep.1
  24.2 1.0 %collective-permute-done.8.late_other = bf16[768,256]{1,0:T(8,128)(2,1)} collective-permute-done((bf16[768,256]{1,0:T(8,128)(2,1)S(1)}, bf16[768,256]{1,0:T(8,128)(2,1)}, u32[]{:S(2)}, u32[]{:S(2)}) %collective-permute-start.8) | collective-permute-done | bytes 393248 | tf_op jit(solution)/shard_map/ppermute | solution.py:32
  25.2 0.0 slice-start
  25.2 4.0 %attention.1 = (bf16[1280,256]{1,0:T(8,128)(2,1)S(1)}, bf16[1280,256]{1,0:T(8,128)(2,1)S(1)}, bf16[768,256]{1,0:T(8,128)(2,1)S(1)}, bf16[768,256]{1,0:T(8,128)(2,1)S(1)}, bf16[640,256]{1,0:T(8,128)(2,1)S(1)}) custom-call(s32[32,32]{1,0:T(8,128)S(1)} %copy-done.7, s32[1]{0:T(128)} %bitcast.info, s32[32,1,128]{2,1,0:T(1,128)S(1)} %bitcast.7, ...), custom_call_target="tpu_custom_call" | custom-call | flops 2000000000 | bytes 8000000 | tf_op jit(solution)/shard_map/attention/pallas_call | solution.py:265
  29.3 1.3 %collective-permute-start.10 = (bf16[768,256]{1,0:T(8,128)(2,1)S(1)}, bf16[768,256]{1,0:T(8,128)(2,1)S(1)}, u32[]{:S(2)}, u32[]{:S(2)}) collective-permute-start(bf16[768,256]{1,0:T(8,128)(2,1)S(1)} %get-tuple-element.57), channel_id=1, source_target_pairs={{0,8},{8,0},{1,9},{9,1},{2,10},{10,2},{3,11},{11,3},{4,12},{12,4},... | collective-permute-start | bytes 1179656 | tf_op jit(solution)/shard_map/ppermute | solution.py:32
  30.6 0.1 collective-permute-start.9
  30.7 1.3 %collective-permute-done.10 = bf16[768,256]{1,0:T(8,128)(2,1)S(1)} collective-permute-done((bf16[768,256]{1,0:T(8,128)(2,1)S(1)}, bf16[768,256]{1,0:T(8,128)(2,1)S(1)}, u32[]{:S(2)}, u32[]{:S(2)}) %collective-permute-start.10) | collective-permute-done | bytes 393248 | tf_op jit(solution)/shard_map/ppermute | solution.py:32
  31.9 0.1 add_convert_fusion
  32.1 0.8 collective-permute-done.9
  32.9 0.2 fusion
  33.1 2.0 %collective-permute-start.11 = (bf16[256,256]{1,0:T(8,128)(2,1)S(1)}, bf16[256,256]{1,0:T(8,128)(2,1)S(1)}, u32[]{:S(2)}, u32[]{:S(2)}) collective-permute-start(bf16[256,256]{1,0:T(8,128)(2,1)S(1)} %get-tuple-element.59), channel_id=1, source_target_pairs={{0,96},{32,0},{64,32},{96,64},{1,97},{33,1},{65,33},{97,65},{2,98}... | collective-permute-start | bytes 393224 | tf_op jit(solution)/shard_map/ppermute | solution.py:32
  35.1 1.2 %collective-permute-start.12 = (bf16[256,256]{1,0:T(8,128)(2,1)S(1)}, bf16[256,256]{1,0:T(8,128)(2,1)S(1)}, u32[]{:S(2)}, u32[]{:S(2)}) collective-permute-start(bf16[256,256]{1,0:T(8,128)(2,1)S(1)} %get-tuple-element.60), channel_id=1, source_target_pairs={{0,64},{32,96},{64,0},{96,32},{1,65},{33,97},{65,1},{97,33},{2,66}... | collective-permute-start | bytes 393224 | tf_op jit(solution)/shard_map/ppermute | solution.py:32
  36.4 3.2 %collective-permute-start.14 = (bf16[256,256]{1,0:T(8,128)(2,1)S(1)}, bf16[256,256]{1,0:T(8,128)(2,1)S(1)}, u32[]{:S(2)}, u32[]{:S(2)}) collective-permute-start(bf16[256,256]{1,0:T(8,128)(2,1)S(1)} %get-tuple-element.64), channel_id=1, source_target_pairs={{0,96},{32,0},{64,32},{96,64},{1,97},{33,1},{65,33},{97,65},{2,98}... | collective-permute-start | bytes 393224 | tf_op jit(solution)/shard_map/ppermute | solution.py:32
  39.6 1.1 %collective-permute-start.15 = (bf16[256,256]{1,0:T(8,128)(2,1)S(1)}, bf16[256,256]{1,0:T(8,128)(2,1)S(1)}, u32[]{:S(2)}, u32[]{:S(2)}) collective-permute-start(bf16[256,256]{1,0:T(8,128)(2,1)S(1)} %get-tuple-element.65), channel_id=1, source_target_pairs={{0,64},{32,96},{64,0},{96,32},{1,65},{33,97},{65,1},{97,33},{2,66}... | collective-permute-start | bytes 393224 | tf_op jit(solution)/shard_map/ppermute | solution.py:32
  40.7 0.5 collective-permute-done.11
  41.2 1.8 %collective-permute-done.12 = bf16[256,256]{1,0:T(8,128)(2,1)S(1)} collective-permute-done((bf16[256,256]{1,0:T(8,128)(2,1)S(1)}, bf16[256,256]{1,0:T(8,128)(2,1)S(1)}, u32[]{:S(2)}, u32[]{:S(2)}) %collective-permute-start.12) | collective-permute-done | bytes 131104 | tf_op jit(solution)/shard_map/ppermute | solution.py:32
  43.0 2.9 %collective-permute-done.13 = bf16[256,256]{1,0:T(8,128)(2,1)S(1)} collective-permute-done((bf16[256,256]{1,0:T(8,128)(2,1)S(1)}, bf16[256,256]{1,0:T(8,128)(2,1)S(1)}, u32[]{:S(2)}, u32[]{:S(2)}) %collective-permute-start.13) | collective-permute-done | bytes 131104 | tf_op jit(solution)/shard_map/ppermute | solution.py:32
  45.9 0.1 add_convert_fusion.1
  46.0 0.0 copy-start
  46.0 0.0 copy-start.1
  46.0 2.4 %collective-permute-start.17 = (bf16[256,256]{1,0:T(8,128)(2,1)S(1)}, bf16[256,256]{1,0:T(8,128)(2,1)S(1)}, u32[]{:S(2)}, u32[]{:S(2)}) collective-permute-start(bf16[256,256]{1,0:T(8,128)(2,1)S(1)} %add_convert_fusion.1), channel_id=1, source_target_pairs={{0,16},{16,0},{1,17},{17,1},{2,18},{18,2},{3,19},{19,3},{4,20},{20... | collective-permute-start | bytes 393224 | tf_op jit(solution)/shard_map/ppermute | solution.py:32
  48.4 3.4 %query_part.1.part = bf16[5120,256]{1,0:T(8,128)(2,1)S(1)} custom-call(bf16[640,256]{1,0:T(8,128)(2,1)S(1)} %get-tuple-element.63.qg, bf16[5120,640]{1,0:T(8,128)(2,1)S(1)} %bitcast.6), custom_call_target="tpu_custom_call" | custom-call | flops 1700000000 | bytes 9000000 | tf_op jit(solution)/shard_map/query_part/pallas_call | solution.py:314
  51.8 1.0 %collective-permute-done.17.across = bf16[256,256]{1,0:T(8,128)(2,1)S(1)} collective-permute-done((bf16[256,256]{1,0:T(8,128)(2,1)S(1)}, bf16[256,256]{1,0:T(8,128)(2,1)S(1)}, u32[]{:S(2)}, u32[]{:S(2)}) %collective-permute-start.17) | collective-permute-done | bytes 131104 | tf_op jit(solution)/shard_map/ppermute | solution.py:32
  52.8 2.2 %project.1 = bf16[5120,256]{1,0:T(8,128)(2,1)S(1)} custom-call(bf16[5120,256]{1,0:T(8,128)(2,1)S(1)} %query_part.1.part, f32[256,256]{1,0:T(8,128)S(1)} %get-tuple-element.68.own, bf16[256,256]{1,0:T(8,128)(2,1)S(1)} %collective-permute-done.17.across, bf16[256,256]{1,0:T(8,128)(2,1)S(1)} %collective-permute-done.14.near1, ...), custom_call_target="tpu_custom_call" | custom-call | flops 700000000 | bytes 6000000 | tf_op jit(solution)/shard_map/project/pallas_call | solution.py:348
  55.0 35.9 %all_to_all.5.parts = bf16[8,640,256]{2,1,0:T(8,128)(2,1)S(1)} all-to-all(bf16[8,640,256]{2,1,0:T(8,128)(2,1)S(1)} %bitcast.4), channel_id=1, replica_groups=mesh['y'=4,'zh'=2,'core'=2,'x'=4,'zl'=2] {'x','zl'}, dimensions={0} | all-to-all | bytes 5242880 | tf_op jit(solution)/shard_map/all_to_all | solution.py:420
  90.9 1.1 %last_sum.1 = bf16[640,256]{1,0:T(8,128)(2,1)} custom-call(bf16[8,640,256]{2,1,0:T(8,128)(2,1)S(1)} %all_to_all.5.parts), custom_call_target="tpu_custom_call" | custom-call | flops 1300000 | bytes 3000000 | tf_op jit(solution)/shard_map/last_sum/pallas_call | solution.py:375
  (35 shorter events, 0.2 us)
Async XLA Ops:
  2.0 11.3 %collective-permute-start = (bf16[256,256]{1,0:T(8,128)(2,1)}, bf16[256,256]{1,0:T(8,128)(2,1)S(1)}, u32[]{:S(2)}, u32[]{:S(2)}) collective-permute-start(bf16[256,256]{1,0:T(8,128)(2,1)} %get-tuple-element.52), channel_id=1, source_target_pairs={{0,16},{16,0},{1,17},{17,1},{2,18},{18,2},{3,19},{19,3},{4,20},{20... | collective-permute-start | bytes 393224 | tf_op jit(solution)/shard_map/ppermute | solution.py:32
  6.0 17.4 %copy-start.2 = (f32[256,128]{1,0:T(8,128)S(1)}, f32[256,128]{1,0:T(8,128)}, u32[]{:S(2)}) copy-start(f32[256,128]{1,0:T(8,128)} %get-tuple-element.43.cos) | copy-start | bytes 393220
  6.0 17.4 %copy-start.3 = (f32[256,128]{1,0:T(8,128)S(1)}, f32[256,128]{1,0:T(8,128)}, u32[]{:S(2)}) copy-start(f32[256,128]{1,0:T(8,128)} %get-tuple-element.44.sin) | copy-start | bytes 393220
  6.0 17.4 %copy-start.4 = (bf16[256,640]{1,0:T(8,128)(2,1)S(1)}, bf16[256,640]{1,0:T(8,128)(2,1)}, u32[]{:S(2)}) copy-start(bf16[256,640]{1,0:T(8,128)(2,1)} %query) | copy-start | bytes 983044
  6.0 17.4 %copy-start.5 = (bf16[256,640]{1,0:T(8,128)(2,1)S(1)}, bf16[256,640]{1,0:T(8,128)(2,1)}, u32[]{:S(2)}) copy-start(bf16[256,640]{1,0:T(8,128)(2,1)} %grad) | copy-start | bytes 983044
  6.0 17.4 %copy-start.6 = (bf16[256,640]{1,0:T(8,128)(2,1)S(1)}, bf16[256,640]{1,0:T(8,128)(2,1)}, u32[]{:S(2)}) copy-start(bf16[256,640]{1,0:T(8,128)(2,1)} %att) | copy-start | bytes 983044
  7.1 9.1 %collective-permute-start.1 = (bf16[256,256]{1,0:T(8,128)(2,1)}, bf16[256,256]{1,0:T(8,128)(2,1)S(1)}, u32[]{:S(2)}, u32[]{:S(2)}) collective-permute-start(bf16[256,256]{1,0:T(8,128)(2,1)} %get-tuple-element.52), channel_id=1, source_target_pairs={{0,32},{32,64},{64,96},{96,0},{1,33},{33,65},{65,97},{97,1},{2,34}... | collective-permute-start | bytes 393224 | tf_op jit(solution)/shard_map/ppermute | solution.py:32
  8.7 9.4 %collective-permute-start.3 = (bf16[256,256]{1,0:T(8,128)(2,1)}, bf16[256,256]{1,0:T(8,128)(2,1)S(1)}, u32[]{:S(2)}, u32[]{:S(2)}) collective-permute-start(bf16[256,256]{1,0:T(8,128)(2,1)} %get-tuple-element.52), channel_id=1, source_target_pairs={{0,96},{32,0},{64,32},{96,64},{1,97},{33,1},{65,33},{97,65},{2,98}... | collective-permute-start | bytes 393224 | tf_op jit(solution)/shard_map/ppermute | solution.py:32
  10.4 7.7 %collective-permute-start.2 = (bf16[256,256]{1,0:T(8,128)(2,1)}, bf16[256,256]{1,0:T(8,128)(2,1)S(1)}, u32[]{:S(2)}, u32[]{:S(2)}) collective-permute-start(bf16[256,256]{1,0:T(8,128)(2,1)} %get-tuple-element.52), channel_id=1, source_target_pairs={{0,64},{32,96},{64,0},{96,32},{1,65},{33,97},{65,1},{97,33},{2,66}... | collective-permute-start | bytes 393224 | tf_op jit(solution)/shard_map/ppermute | solution.py:32
  13.3 9.9 %collective-permute-start.7 = (bf16[256,256]{1,0:T(8,128)(2,1)S(1)}, bf16[256,256]{1,0:T(8,128)(2,1)S(1)}, u32[]{:S(2)}, u32[]{:S(2)}) collective-permute-start(bf16[256,256]{1,0:T(8,128)(2,1)S(1)} %collective-permute-done), channel_id=1, source_target_pairs={{0,96},{32,0},{64,32},{96,64},{1,97},{33,1},{65,33},{97,65},{2,98}... | collective-permute-start | bytes 393224 | tf_op jit(solution)/shard_map/ppermute | solution.py:32
  14.4 8.8 %collective-permute-start.6 = (bf16[256,256]{1,0:T(8,128)(2,1)S(1)}, bf16[256,256]{1,0:T(8,128)(2,1)S(1)}, u32[]{:S(2)}, u32[]{:S(2)}) collective-permute-start(bf16[256,256]{1,0:T(8,128)(2,1)S(1)} %collective-permute-done), channel_id=1, source_target_pairs={{0,64},{32,96},{64,0},{96,32},{1,65},{33,97},{65,1},{97,33},{2,66}... | collective-permute-start | bytes 393224 | tf_op jit(solution)/shard_map/ppermute | solution.py:32
  16.1 7.1 %collective-permute-start.5 = (bf16[256,256]{1,0:T(8,128)(2,1)S(1)}, bf16[256,256]{1,0:T(8,128)(2,1)S(1)}, u32[]{:S(2)}, u32[]{:S(2)}) collective-permute-start(bf16[256,256]{1,0:T(8,128)(2,1)S(1)} %collective-permute-done), channel_id=1, source_target_pairs={{0,32},{32,64},{64,96},{96,0},{1,33},{33,65},{65,97},{97,1},{2,34}... | collective-permute-start | bytes 393224 | tf_op jit(solution)/shard_map/ppermute | solution.py:32
  18.1 7.1 %copy-start.7 = (s32[32,32]{1,0:T(8,128)S(1)}, s32[32,32]{1,0:T(8,128)}, u32[]{:S(2)}) copy-start(s32[32,32]{1,0:T(8,128)} %mask.1) | copy-start | bytes 12292
  18.1 7.1 %copy-start.8 = (s32[4096]{0:T(1024)S(1)}, s32[4096]{0:T(1024)}, u32[]{:S(2)}) copy-start(s32[4096]{0:T(1024)} %param.21) | copy-start | bytes 49156
  18.1 7.1 %copy-start.9 = (f32[5,256]{1,0:T(8,128)S(1)}, f32[5,256]{1,0:T(8,128)}, u32[]{:S(2)}) copy-start(f32[5,256]{1,0:T(8,128)} %lse.1) | copy-start | bytes 15364
  18.2 7.0 %collective-permute-start.4 = (bf16[1280,256]{1,0:T(8,128)(2,1)S(1)}, bf16[1280,256]{1,0:T(8,128)(2,1)S(1)}, u32[]{:S(2)}, u32[]{:S(2)}) collective-permute-start(bf16[1280,256]{1,0:T(8,128)(2,1)S(1)} %constant_dynamic-update-slice_fusion.early_mine), channel_id=1, source_target_pairs={{0,8},{8,0},{1,9},{9,1},{2,10},{10,2},{3,11},{11,3},{4,12},{12,4},... | collective-permute-start | bytes 1966088 | tf_op jit(solution)/shard_map/ppermute | solution.py:32
  23.3 1.9 %collective-permute-start.8 = (bf16[768,256]{1,0:T(8,128)(2,1)S(1)}, bf16[768,256]{1,0:T(8,128)(2,1)}, u32[]{:S(2)}, u32[]{:S(2)}) collective-permute-start(bf16[768,256]{1,0:T(8,128)(2,1)S(1)} %constant_dynamic-update-slice_fusion.5.late_mine), channel_id=1, source_target_pairs={{0,8},{8,0},{1,9},{9,1},{2,10},{10,2},{3,11},{11,3},{4,12},{12,4},... | collective-permute-start | bytes 1179656 | tf_op jit(solution)/shard_map/ppermute | solution.py:32
  25.2 23.2 %slice-start = ((s8[6553600]{0:T(1024)(128)(4,1)}), s8[2359296]{0:T(1024)(128)(4,1)S(1)}, s32[]{:S(2)}) async-start(s8[6553600]{0:T(1024)(128)(4,1)} %bitcast.5), calls=%async_computation.1 | async-start | bytes 4718592
  29.3 2.6 %collective-permute-start.10 = (bf16[768,256]{1,0:T(8,128)(2,1)S(1)}, bf16[768,256]{1,0:T(8,128)(2,1)S(1)}, u32[]{:S(2)}, u32[]{:S(2)}) collective-permute-start(bf16[768,256]{1,0:T(8,128)(2,1)S(1)} %get-tuple-element.57), channel_id=1, source_target_pairs={{0,8},{8,0},{1,9},{9,1},{2,10},{10,2},{3,11},{11,3},{4,12},{12,4},... | collective-permute-start | bytes 1179656 | tf_op jit(solution)/shard_map/ppermute | solution.py:32
  30.6 2.3 %collective-permute-start.9 = (bf16[1280,256]{1,0:T(8,128)(2,1)S(1)}, bf16[1280,256]{1,0:T(8,128)(2,1)S(1)}, u32[]{:S(2)}, u32[]{:S(2)}) collective-permute-start(bf16[1280,256]{1,0:T(8,128)(2,1)S(1)} %get-tuple-element.55), channel_id=1, source_target_pairs={{0,8},{8,0},{1,9},{9,1},{2,10},{10,2},{3,11},{11,3},{4,12},{12,4},... | collective-permute-start | bytes 1966088 | tf_op jit(solution)/shard_map/ppermute | solution.py:32
  31.9 16.5 %slice-start.1 = ((s8[6553600]{0:T(1024)(128)(4,1)}), s8[4194304]{0:T(1024)(128)(4,1)S(1)}, s32[]{:S(2)}) async-start(s8[6553600]{0:T(1024)(128)(4,1)} %bitcast.5), calls=%async_computation.2 | async-start | bytes 8388608
  33.1 8.1 %collective-permute-start.11 = (bf16[256,256]{1,0:T(8,128)(2,1)S(1)}, bf16[256,256]{1,0:T(8,128)(2,1)S(1)}, u32[]{:S(2)}, u32[]{:S(2)}) collective-permute-start(bf16[256,256]{1,0:T(8,128)(2,1)S(1)} %get-tuple-element.59), channel_id=1, source_target_pairs={{0,96},{32,0},{64,32},{96,64},{1,97},{33,1},{65,33},{97,65},{2,98}... | collective-permute-start | bytes 393224 | tf_op jit(solution)/shard_map/ppermute | solution.py:32
  35.1 7.9 %collective-permute-start.12 = (bf16[256,256]{1,0:T(8,128)(2,1)S(1)}, bf16[256,256]{1,0:T(8,128)(2,1)S(1)}, u32[]{:S(2)}, u32[]{:S(2)}) collective-permute-start(bf16[256,256]{1,0:T(8,128)(2,1)S(1)} %get-tuple-element.60), channel_id=1, source_target_pairs={{0,64},{32,96},{64,0},{96,32},{1,65},{33,97},{65,1},{97,33},{2,66}... | collective-permute-start | bytes 393224 | tf_op jit(solution)/shard_map/ppermute | solution.py:32
  36.4 9.5 %collective-permute-start.13 = (bf16[256,256]{1,0:T(8,128)(2,1)S(1)}, bf16[256,256]{1,0:T(8,128)(2,1)S(1)}, u32[]{:S(2)}, u32[]{:S(2)}) collective-permute-start(bf16[256,256]{1,0:T(8,128)(2,1)S(1)} %get-tuple-element.61), channel_id=1, source_target_pairs={{0,32},{32,64},{64,96},{96,0},{1,33},{33,65},{65,97},{97,1},{2,34}... | collective-permute-start | bytes 393224 | tf_op jit(solution)/shard_map/ppermute | solution.py:32
  36.4 15.4 %collective-permute-start.14 = (bf16[256,256]{1,0:T(8,128)(2,1)S(1)}, bf16[256,256]{1,0:T(8,128)(2,1)S(1)}, u32[]{:S(2)}, u32[]{:S(2)}) collective-permute-start(bf16[256,256]{1,0:T(8,128)(2,1)S(1)} %get-tuple-element.64), channel_id=1, source_target_pairs={{0,96},{32,0},{64,32},{96,64},{1,97},{33,1},{65,33},{97,65},{2,98}... | collective-permute-start | bytes 393224 | tf_op jit(solution)/shard_map/ppermute | solution.py:32
  39.6 12.2 %collective-permute-start.15 = (bf16[256,256]{1,0:T(8,128)(2,1)S(1)}, bf16[256,256]{1,0:T(8,128)(2,1)S(1)}, u32[]{:S(2)}, u32[]{:S(2)}) collective-permute-start(bf16[256,256]{1,0:T(8,128)(2,1)S(1)} %get-tuple-element.65), channel_id=1, source_target_pairs={{0,64},{32,96},{64,0},{96,32},{1,65},{33,97},{65,1},{97,33},{2,66}... | collective-permute-start | bytes 393224 | tf_op jit(solution)/shard_map/ppermute | solution.py:32
  41.2 10.6 %collective-permute-start.16 = (bf16[256,256]{1,0:T(8,128)(2,1)S(1)}, bf16[256,256]{1,0:T(8,128)(2,1)S(1)}, u32[]{:S(2)}, u32[]{:S(2)}) collective-permute-start(bf16[256,256]{1,0:T(8,128)(2,1)S(1)} %get-tuple-element.66), channel_id=1, source_target_pairs={{0,32},{32,64},{64,96},{96,0},{1,33},{33,65},{65,97},{97,1},{2,34}... | collective-permute-start | bytes 393224 | tf_op jit(solution)/shard_map/ppermute | solution.py:32
  46.0 6.8 %copy-start = (bf16[5120,128]{1,0:T(8,128)(2,1)S(1)}, bf16[5120,128]{1,0:T(8,128)(2,1)}, u32[]{:S(2)}) copy-start(bf16[5120,128]{1,0:T(8,128)(2,1)} %wk.1) | copy-start | bytes 3932164
  46.0 6.8 %copy-start.1 = (bf16[5120,128]{1,0:T(8,128)(2,1)S(1)}, bf16[5120,128]{1,0:T(8,128)(2,1)}, u32[]{:S(2)}) copy-start(bf16[5120,128]{1,0:T(8,128)(2,1)} %wv.1) | copy-start | bytes 3932164
  46.0 6.8 %collective-permute-start.17 = (bf16[256,256]{1,0:T(8,128)(2,1)S(1)}, bf16[256,256]{1,0:T(8,128)(2,1)S(1)}, u32[]{:S(2)}, u32[]{:S(2)}) collective-permute-start(bf16[256,256]{1,0:T(8,128)(2,1)S(1)} %add_convert_fusion.1), channel_id=1, source_target_pairs={{0,16},{16,0},{1,17},{17,1},{2,18},{18,2},{3,19},{19,3},{4,20},{20... | collective-permute-start | bytes 393224 | tf_op jit(solution)/shard_map/ppermute | solution.py:32

commit v12 on v11

--- a/solution.py
+++ b/solution.py
@@ -69,7 +69,7 @@
         block[tok, HEAD:] = value[tok, :]
 
 
-def prep_kernel(query, grad, att, cos, sin, q_rows, q_cols, g_rows, g_cols, delta):
+def prep_kernel(query, grad, att, cos, sin, small, q_rows, q_cols, g_rows, g_cols, delta):
     sign = half_sign((TILE, HEAD), 1)
     for t in range(2):
         tok = pl.ds(t * TILE, TILE)
@@ -229,7 +229,7 @@
         tok = pl.ds(t * TILE, TILE)
         c, s = cos[tok, :].T, sin[tok, :].T
         for h in range(GROUPS):
-            g = dq[t, :, pl.ds(h * TILE, TILE)]
+            g = dq[t, :, pl.ds(h * TILE, TILE)] * SCALE
             u = g * s
             half = HEAD // 2
             turned = jnp.concatenate([u[half:], -u[:half]], 0)
@@ -240,7 +240,7 @@
     return [pl.BlockSpec(memory_space=pltpu.VMEM)] * n
 
 
-def prep(query, grad, att, cos, sin):
+def prep(query, grad, att, cos, sin, small):
     s = jax.ShapeDtypeStruct
     return pl.pallas_call(
         prep_kernel,
@@ -251,12 +251,12 @@
             s((2, HEAD, ROWS), bf16),
             s((2, 1, ROWS), f32),
         ),
-        in_specs=vmem(5),
+        in_specs=vmem(6),
         out_specs=tuple(vmem(5)),
         compiler_params=pltpu.CompilerParams(vmem_limit_bytes=12 << 20),
         cost_estimate=pl.CostEstimate(flops=1000000, bytes_accessed=10000, transcendentals=0),
         name="prep",
-    )(query, grad, att, cos, sin)
+    )(query, grad, att, cos, sin, small)
 
 
 def attention(mask, info, *operands):
@@ -391,16 +391,16 @@
     cos, sin, block = make_block(key, value, positions)
 
     across = swap_zh(block)
-    scaled, again = lax.optimization_barrier(((cos * SCALE, sin * SCALE), block))
+    small, again = lax.optimization_barrier((cos[:8] * SCALE, block))
     near = [shift_y(again, k) for k in (1, 2, 3)]
     across, query, grad, att = lax.optimization_barrier((across, query, grad, att))
     far = [shift_y(across, k) for k in (1, 2, 3)]
-    q_rows, q_cols, g_rows, g_cols, delta = prep(query, grad, att, cos, sin)
+    q_rows, q_cols, g_rows, g_cols, delta = prep(query, grad, att, cos, sin, small)
     early = jnp.concatenate([block] + near + [across], 0)
     late = jnp.concatenate(far, 0)
 
     early_mine, early_other, late_mine, late_other, query_grad = attention(
-        block_mask, me.reshape(1), segments.reshape(TILES, 1, TILE), lse, delta, *scaled, q_rows,
+        block_mask, me.reshape(1), segments.reshape(TILES, 1, TILE), lse, delta, cos, sin, q_rows,
         q_cols, g_rows, g_cols, early, swap_core(early), late, swap_core(late),
     )
 

time: 92.3 us -> 91.4 us (level)
  transfers between devices with their start and end apart: 18 -> 18, of which waited for: 9 -> 9; matrix products, arithmetic and copies ran while one was open for 3% -> 2% of each run, Pallas kernels for 5% -> 5%
where the time goes in v12:
time: 91.4 us; the launch traced here: 91.2 us
  blocking collectives  35.9 us (39%)
  starting transfers between devices  23.9 us (26%)
  waiting for transfers between devices  15.6 us (17%)
  Pallas kernels  13.3 us (15%)
  local copies, waits for them, and re-layouts  1.17 us (1%)
  other arithmetic  1.02 us (1%)
    all_to_all x1, blocking collectives, local(): return last_sum(lax.all_to_all(send.reshape(8, 640, TOK), TP, 0, 0))  35.9 us
    ppermute x18, starting transfers between devices, shift(): return lax.ppermute(x, axes, perm)  23.9 us
    ppermute x18, waiting for transfers between devices, shift(): return lax.ppermute(x, axes, perm)  15.6 us
    pallas_call x1, Pallas kernels, attention(): pl.pallas_call(attention_kernel, out_shape=(early, early, late, late, s((...  3.72 us
    pallas_call x1, Pallas kernels, query_part(): pl.pallas_call(query_part_kernel, out_shape=jax.ShapeDtypeStruct((WIDTH,...  3.4 us
    pallas_call x1, Pallas kernels, project(): pl.pallas_call(project_kernel, out_shape=jax.ShapeDtypeStruct((WIDTH, TOK...  2.22 us
    pallas_call x1, Pallas kernels, make_block(): pl.pallas_call(block_kernel, out_shape=(s((TOK, HEAD), f32), s((TOK, HEAD...  2.09 us
  transfers between devices with their start and end apart: 18, of which 9 were waited for; matrix products, arithmetic and copies ran while one was open for 2% of the time, Pallas kernels for 5%

profile of v12, /device:TPU:0, one launch (start us, length us, event | category | flops | bytes accessed | tf_op | source)
XLA Modules:
  0.0 91.2 jit_solution(1082809314623863197)
XLA Ops:
  0.0 2.1 %block.1 = (f32[256,128]{1,0:T(8,128)}, f32[256,128]{1,0:T(8,128)}, bf16[256,256]{1,0:T(8,128)(2,1)}) custom-call(bf16[256,128]{1,0:T(8,128)(2,1)} %key.1, bf16[256,128]{1,0:T(8,128)(2,1)} %value.1, s32[2,1,128]{2,1,0:T(1,128)} %bitcast.8, f32[1,128]{1,0:T(1,128)} %constant.23.clone.inverse), custom_call_target="tpu_custom_call" | custom-call | flops 5000000 | bytes 700000 | tf_op jit(solution)/shard_map/block/pallas_call | solution.py:290
  2.1 4.0 %collective-permute-start = (bf16[256,256]{1,0:T(8,128)(2,1)}, bf16[256,256]{1,0:T(8,128)(2,1)S(1)}, u32[]{:S(2)}, u32[]{:S(2)}) collective-permute-start(bf16[256,256]{1,0:T(8,128)(2,1)} %get-tuple-element.50), channel_id=1, source_target_pairs={{0,16},{16,0},{1,17},{17,1},{2,18},{18,2},{3,19},{19,3},{4,20},{20... | collective-permute-start | bytes 393224 | tf_op jit(solution)/shard_map/ppermute | solution.py:32
  6.1 0.7 slice_multiply_fusion.small
  6.8 1.6 %collective-permute-start.1 = (bf16[256,256]{1,0:T(8,128)(2,1)}, bf16[256,256]{1,0:T(8,128)(2,1)S(1)}, u32[]{:S(2)}, u32[]{:S(2)}) collective-permute-start(bf16[256,256]{1,0:T(8,128)(2,1)} %get-tuple-element.50), channel_id=1, source_target_pairs={{0,32},{32,64},{64,96},{96,0},{1,33},{33,65},{65,97},{97,1},{2,34}... | collective-permute-start | bytes 393224 | tf_op jit(solution)/shard_map/ppermute | solution.py:32
  8.3 1.7 %collective-permute-start.3 = (bf16[256,256]{1,0:T(8,128)(2,1)}, bf16[256,256]{1,0:T(8,128)(2,1)S(1)}, u32[]{:S(2)}, u32[]{:S(2)}) collective-permute-start(bf16[256,256]{1,0:T(8,128)(2,1)} %get-tuple-element.50), channel_id=1, source_target_pairs={{0,96},{32,0},{64,32},{96,64},{1,97},{33,1},{65,33},{97,65},{2,98}... | collective-permute-start | bytes 393224 | tf_op jit(solution)/shard_map/ppermute | solution.py:32
  10.0 2.0 %collective-permute-start.2 = (bf16[256,256]{1,0:T(8,128)(2,1)}, bf16[256,256]{1,0:T(8,128)(2,1)S(1)}, u32[]{:S(2)}, u32[]{:S(2)}) collective-permute-start(bf16[256,256]{1,0:T(8,128)(2,1)} %get-tuple-element.50), channel_id=1, source_target_pairs={{0,64},{32,96},{64,0},{96,32},{1,65},{33,97},{65,1},{97,33},{2,66}... | collective-permute-start | bytes 393224 | tf_op jit(solution)/shard_map/ppermute | solution.py:32
  12.0 0.9 %constant_dynamic-update-slice_fusion.4 = bf16[1280,256]{1,0:T(8,128)(2,1)S(1)} fusion(bf16[256,256]{1,0:T(8,128)(2,1)} %get-tuple-element.50), kind=kLoop, calls=%fused_computation.7 | loop fusion | bytes 262144
  12.9 0.0 collective-permute-done
  12.9 1.1 %collective-permute-start.7 = (bf16[256,256]{1,0:T(8,128)(2,1)S(1)}, bf16[256,256]{1,0:T(8,128)(2,1)S(1)}, u32[]{:S(2)}, u32[]{:S(2)}) collective-permute-start(bf16[256,256]{1,0:T(8,128)(2,1)S(1)} %collective-permute-done), channel_id=1, source_target_pairs={{0,96},{32,0},{64,32},{96,64},{1,97},{33,1},{65,33},{97,65},{2,98}... | collective-permute-start | bytes 393224 | tf_op jit(solution)/shard_map/ppermute | solution.py:32
  14.1 1.7 %collective-permute-start.6 = (bf16[256,256]{1,0:T(8,128)(2,1)S(1)}, bf16[256,256]{1,0:T(8,128)(2,1)S(1)}, u32[]{:S(2)}, u32[]{:S(2)}) collective-permute-start(bf16[256,256]{1,0:T(8,128)(2,1)S(1)} %collective-permute-done), channel_id=1, source_target_pairs={{0,64},{32,96},{64,0},{96,32},{1,65},{33,97},{65,1},{97,33},{2,66}... | collective-permute-start | bytes 393224 | tf_op jit(solution)/shard_map/ppermute | solution.py:32
  15.8 0.2 collective-permute-start.5
  16.0 1.7 %collective-permute-done.2 = bf16[256,256]{1,0:T(8,128)(2,1)S(1)} collective-permute-done((bf16[256,256]{1,0:T(8,128)(2,1)}, bf16[256,256]{1,0:T(8,128)(2,1)S(1)}, u32[]{:S(2)}, u32[]{:S(2)}) %collective-permute-start.2) | collective-permute-done | bytes 131104 | tf_op jit(solution)/shard_map/ppermute | solution.py:32
  17.7 0.0 copy-start.7
  17.8 0.0 copy-start.8
  17.8 0.0 copy-start.9
  17.8 0.0 collective-permute-done.3
  17.8 0.1 collective-permute-start.4
  17.9 4.9 %collective-permute-done.5 = bf16[256,256]{1,0:T(8,128)(2,1)S(1)} collective-permute-done((bf16[256,256]{1,0:T(8,128)(2,1)S(1)}, bf16[256,256]{1,0:T(8,128)(2,1)S(1)}, u32[]{:S(2)}, u32[]{:S(2)}) %collective-permute-start.5) | collective-permute-done | bytes 131104 | tf_op jit(solution)/shard_map/ppermute | solution.py:32
  22.9 0.0 collective-permute-done.7
  22.9 0.1 collective-permute-start.8
  23.0 0.8 prep.1
  23.9 0.8 collective-permute-done.8.late_other
  24.7 0.0 collective-permute-done.4.early_other
  24.7 0.0 slice-start
  24.7 3.7 %attention.1 = (bf16[1280,256]{1,0:T(8,128)(2,1)S(1)}, bf16[1280,256]{1,0:T(8,128)(2,1)S(1)}, bf16[768,256]{1,0:T(8,128)(2,1)S(1)}, bf16[768,256]{1,0:T(8,128)(2,1)S(1)}, bf16[640,256]{1,0:T(8,128)(2,1)S(1)}) custom-call(s32[32,32]{1,0:T(8,128)S(1)} %copy-done.7, s32[1]{0:T(128)} %bitcast.info, s32[32,1,128]{2,1,0:T(1,128)S(1)} %bitcast.7, ...), custom_call_target="tpu_custom_call" | custom-call | flops 2000000000 | bytes 8000000 | tf_op jit(solution)/shard_map/attention/pallas_call | solution.py:265
  28.5 1.3 %collective-permute-start.10 = (bf16[768,256]{1,0:T(8,128)(2,1)S(1)}, bf16[768,256]{1,0:T(8,128)(2,1)S(1)}, u32[]{:S(2)}, u32[]{:S(2)}) collective-permute-start(bf16[768,256]{1,0:T(8,128)(2,1)S(1)} %get-tuple-element.55), channel_id=1, source_target_pairs={{0,8},{8,0},{1,9},{9,1},{2,10},{10,2},{3,11},{11,3},{4,12},{12,4},... | collective-permute-start | bytes 1179656 | tf_op jit(solution)/shard_map/ppermute | solution.py:32
  29.7 0.1 collective-permute-start.9
  29.8 1.3 %collective-permute-done.10 = bf16[768,256]{1,0:T(8,128)(2,1)S(1)} collective-permute-done((bf16[768,256]{1,0:T(8,128)(2,1)S(1)}, bf16[768,256]{1,0:T(8,128)(2,1)S(1)}, u32[]{:S(2)}, u32[]{:S(2)}) %collective-permute-start.10) | collective-permute-done | bytes 393248 | tf_op jit(solution)/shard_map/ppermute | solution.py:32
  31.1 0.1 add_convert_fusion
  31.2 0.8 collective-permute-done.9
  32.0 0.2 fusion
  32.3 2.1 %collective-permute-start.11 = (bf16[256,256]{1,0:T(8,128)(2,1)S(1)}, bf16[256,256]{1,0:T(8,128)(2,1)S(1)}, u32[]{:S(2)}, u32[]{:S(2)}) collective-permute-start(bf16[256,256]{1,0:T(8,128)(2,1)S(1)} %get-tuple-element.57), channel_id=1, source_target_pairs={{0,96},{32,0},{64,32},{96,64},{1,97},{33,1},{65,33},{97,65},{2,98}... | collective-permute-start | bytes 393224 | tf_op jit(solution)/shard_map/ppermute | solution.py:32
  34.3 1.2 %collective-permute-start.12 = (bf16[256,256]{1,0:T(8,128)(2,1)S(1)}, bf16[256,256]{1,0:T(8,128)(2,1)S(1)}, u32[]{:S(2)}, u32[]{:S(2)}) collective-permute-start(bf16[256,256]{1,0:T(8,128)(2,1)S(1)} %get-tuple-element.58), channel_id=1, source_target_pairs={{0,64},{32,96},{64,0},{96,32},{1,65},{33,97},{65,1},{97,33},{2,66}... | collective-permute-start | bytes 393224 | tf_op jit(solution)/shard_map/ppermute | solution.py:32
  35.6 3.2 %collective-permute-start.14 = (bf16[256,256]{1,0:T(8,128)(2,1)S(1)}, bf16[256,256]{1,0:T(8,128)(2,1)S(1)}, u32[]{:S(2)}, u32[]{:S(2)}) collective-permute-start(bf16[256,256]{1,0:T(8,128)(2,1)S(1)} %get-tuple-element.62), channel_id=1, source_target_pairs={{0,96},{32,0},{64,32},{96,64},{1,97},{33,1},{65,33},{97,65},{2,98}... | collective-permute-start | bytes 393224 | tf_op jit(solution)/shard_map/ppermute | solution.py:32
  38.8 1.1 %collective-permute-start.15 = (bf16[256,256]{1,0:T(8,128)(2,1)S(1)}, bf16[256,256]{1,0:T(8,128)(2,1)S(1)}, u32[]{:S(2)}, u32[]{:S(2)}) collective-permute-start(bf16[256,256]{1,0:T(8,128)(2,1)S(1)} %get-tuple-element.63), channel_id=1, source_target_pairs={{0,64},{32,96},{64,0},{96,32},{1,65},{33,97},{65,1},{97,33},{2,66}... | collective-permute-start | bytes 393224 | tf_op jit(solution)/shard_map/ppermute | solution.py:32
  39.9 0.7 collective-permute-done.11
  40.5 1.6 %collective-permute-done.12 = bf16[256,256]{1,0:T(8,128)(2,1)S(1)} collective-permute-done((bf16[256,256]{1,0:T(8,128)(2,1)S(1)}, bf16[256,256]{1,0:T(8,128)(2,1)S(1)}, u32[]{:S(2)}, u32[]{:S(2)}) %collective-permute-start.12) | collective-permute-done | bytes 131104 | tf_op jit(solution)/shard_map/ppermute | solution.py:32
  42.2 2.9 %collective-permute-done.13 = bf16[256,256]{1,0:T(8,128)(2,1)S(1)} collective-permute-done((bf16[256,256]{1,0:T(8,128)(2,1)S(1)}, bf16[256,256]{1,0:T(8,128)(2,1)S(1)}, u32[]{:S(2)}, u32[]{:S(2)}) %collective-permute-start.13) | collective-permute-done | bytes 131104 | tf_op jit(solution)/shard_map/ppermute | solution.py:32
  45.1 0.1 add_convert_fusion.1
  45.2 0.0 copy-start
  45.2 0.0 copy-start.1
  45.2 2.5 %collective-permute-start.17 = (bf16[256,256]{1,0:T(8,128)(2,1)S(1)}, bf16[256,256]{1,0:T(8,128)(2,1)S(1)}, u32[]{:S(2)}, u32[]{:S(2)}) collective-permute-start(bf16[256,256]{1,0:T(8,128)(2,1)S(1)} %add_convert_fusion.1), channel_id=1, source_target_pairs={{0,16},{16,0},{1,17},{17,1},{2,18},{18,2},{3,19},{19,3},{4,20},{20... | collective-permute-start | bytes 393224 | tf_op jit(solution)/shard_map/ppermute | solution.py:32
  47.7 3.4 %query_part.1.part = bf16[5120,256]{1,0:T(8,128)(2,1)S(1)} custom-call(bf16[640,256]{1,0:T(8,128)(2,1)S(1)} %get-tuple-element.61.qg, bf16[5120,640]{1,0:T(8,128)(2,1)S(1)} %bitcast.6), custom_call_target="tpu_custom_call" | custom-call | flops 1700000000 | bytes 9000000 | tf_op jit(solution)/shard_map/query_part/pallas_call | solution.py:314
  51.1 0.0 collective-permute-done.16.near3
  51.1 0.9 collective-permute-done.17.across
  52.0 2.2 %project.1 = bf16[5120,256]{1,0:T(8,128)(2,1)S(1)} custom-call(bf16[5120,256]{1,0:T(8,128)(2,1)S(1)} %query_part.1.part, f32[256,256]{1,0:T(8,128)S(1)} %get-tuple-element.66.own, bf16[256,256]{1,0:T(8,128)(2,1)S(1)} %collective-permute-done.17.across, bf16[256,256]{1,0:T(8,128)(2,1)S(1)} %collective-permute-done.14.near1, ...), custom_call_target="tpu_custom_call" | custom-call | flops 700000000 | bytes 6000000 | tf_op jit(solution)/shard_map/project/pallas_call | solution.py:348
  54.2 35.9 %all_to_all.5.parts = bf16[8,640,256]{2,1,0:T(8,128)(2,1)S(1)} all-to-all(bf16[8,640,256]{2,1,0:T(8,128)(2,1)S(1)} %bitcast.4), channel_id=1, replica_groups=mesh['y'=4,'zh'=2,'core'=2,'x'=4,'zl'=2] {'x','zl'}, dimensions={0} | all-to-all | bytes 5242880 | tf_op jit(solution)/shard_map/all_to_all | solution.py:420
  90.1 1.1 %last_sum.1 = bf16[640,256]{1,0:T(8,128)(2,1)} custom-call(bf16[8,640,256]{2,1,0:T(8,128)(2,1)S(1)} %all_to_all.5.parts), custom_call_target="tpu_custom_call" | custom-call | flops 1300000 | bytes 3000000 | tf_op jit(solution)/shard_map/last_sum/pallas_call | solution.py:375
  (35 shorter events, 0.2 us)
Async XLA Ops:
  0.0 23.0 %copy-start.5 = (bf16[256,640]{1,0:T(8,128)(2,1)S(1)}, bf16[256,640]{1,0:T(8,128)(2,1)}, u32[]{:S(2)}) copy-start(bf16[256,640]{1,0:T(8,128)(2,1)} %grad) | copy-start | bytes 983044
  0.0 23.0 %copy-start.6 = (bf16[256,640]{1,0:T(8,128)(2,1)S(1)}, bf16[256,640]{1,0:T(8,128)(2,1)}, u32[]{:S(2)}) copy-start(bf16[256,640]{1,0:T(8,128)(2,1)} %att) | copy-start | bytes 983044
  0.0 23.0 %copy-start.4 = (bf16[256,640]{1,0:T(8,128)(2,1)S(1)}, bf16[256,640]{1,0:T(8,128)(2,1)}, u32[]{:S(2)}) copy-start(bf16[256,640]{1,0:T(8,128)(2,1)} %query) | copy-start | bytes 983044
  2.1 20.9 %copy-start.2 = (f32[256,128]{1,0:T(8,128)S(1)}, f32[256,128]{1,0:T(8,128)}, u32[]{:S(2)}) copy-start(f32[256,128]{1,0:T(8,128)} %get-tuple-element.42.cos) | copy-start | bytes 393220
  2.1 20.9 %copy-start.3 = (f32[256,128]{1,0:T(8,128)S(1)}, f32[256,128]{1,0:T(8,128)}, u32[]{:S(2)}) copy-start(f32[256,128]{1,0:T(8,128)} %get-tuple-element.43.sin) | copy-start | bytes 393220
  2.1 10.8 %collective-permute-start = (bf16[256,256]{1,0:T(8,128)(2,1)}, bf16[256,256]{1,0:T(8,128)(2,1)S(1)}, u32[]{:S(2)}, u32[]{:S(2)}) collective-permute-start(bf16[256,256]{1,0:T(8,128)(2,1)} %get-tuple-element.50), channel_id=1, source_target_pairs={{0,16},{16,0},{1,17},{17,1},{2,18},{18,2},{3,19},{19,3},{4,20},{20... | collective-permute-start | bytes 393224 | tf_op jit(solution)/shard_map/ppermute | solution.py:32
  6.8 9.0 %collective-permute-start.1 = (bf16[256,256]{1,0:T(8,128)(2,1)}, bf16[256,256]{1,0:T(8,128)(2,1)S(1)}, u32[]{:S(2)}, u32[]{:S(2)}) collective-permute-start(bf16[256,256]{1,0:T(8,128)(2,1)} %get-tuple-element.50), channel_id=1, source_target_pairs={{0,32},{32,64},{64,96},{96,0},{1,33},{33,65},{65,97},{97,1},{2,34}... | collective-permute-start | bytes 393224 | tf_op jit(solution)/shard_map/ppermute | solution.py:32
  8.3 9.4 %collective-permute-start.3 = (bf16[256,256]{1,0:T(8,128)(2,1)}, bf16[256,256]{1,0:T(8,128)(2,1)S(1)}, u32[]{:S(2)}, u32[]{:S(2)}) collective-permute-start(bf16[256,256]{1,0:T(8,128)(2,1)} %get-tuple-element.50), channel_id=1, source_target_pairs={{0,96},{32,0},{64,32},{96,64},{1,97},{33,1},{65,33},{97,65},{2,98}... | collective-permute-start | bytes 393224 | tf_op jit(solution)/shard_map/ppermute | solution.py:32
  10.0 7.7 %collective-permute-start.2 = (bf16[256,256]{1,0:T(8,128)(2,1)}, bf16[256,256]{1,0:T(8,128)(2,1)S(1)}, u32[]{:S(2)}, u32[]{:S(2)}) collective-permute-start(bf16[256,256]{1,0:T(8,128)(2,1)} %get-tuple-element.50), channel_id=1, source_target_pairs={{0,64},{32,96},{64,0},{96,32},{1,65},{33,97},{65,1},{97,33},{2,66}... | collective-permute-start | bytes 393224 | tf_op jit(solution)/shard_map/ppermute | solution.py:32
  12.9 9.9 %collective-permute-start.7 = (bf16[256,256]{1,0:T(8,128)(2,1)S(1)}, bf16[256,256]{1,0:T(8,128)(2,1)S(1)}, u32[]{:S(2)}, u32[]{:S(2)}) collective-permute-start(bf16[256,256]{1,0:T(8,128)(2,1)S(1)} %collective-permute-done), channel_id=1, source_target_pairs={{0,96},{32,0},{64,32},{96,64},{1,97},{33,1},{65,33},{97,65},{2,98}... | collective-permute-start | bytes 393224 | tf_op jit(solution)/shard_map/ppermute | solution.py:32
  14.1 8.8 %collective-permute-start.6 = (bf16[256,256]{1,0:T(8,128)(2,1)S(1)}, bf16[256,256]{1,0:T(8,128)(2,1)S(1)}, u32[]{:S(2)}, u32[]{:S(2)}) collective-permute-start(bf16[256,256]{1,0:T(8,128)(2,1)S(1)} %collective-permute-done), channel_id=1, source_target_pairs={{0,64},{32,96},{64,0},{96,32},{1,65},{33,97},{65,1},{97,33},{2,66}... | collective-permute-start | bytes 393224 | tf_op jit(solution)/shard_map/ppermute | solution.py:32
  15.8 7.1 %collective-permute-start.5 = (bf16[256,256]{1,0:T(8,128)(2,1)S(1)}, bf16[256,256]{1,0:T(8,128)(2,1)S(1)}, u32[]{:S(2)}, u32[]{:S(2)}) collective-permute-start(bf16[256,256]{1,0:T(8,128)(2,1)S(1)} %collective-permute-done), channel_id=1, source_target_pairs={{0,32},{32,64},{64,96},{96,0},{1,33},{33,65},{65,97},{97,1},{2,34}... | collective-permute-start | bytes 393224 | tf_op jit(solution)/shard_map/ppermute | solution.py:32
  17.7 7.0 %copy-start.7 = (s32[32,32]{1,0:T(8,128)S(1)}, s32[32,32]{1,0:T(8,128)}, u32[]{:S(2)}) copy-start(s32[32,32]{1,0:T(8,128)} %mask.1) | copy-start | bytes 12292
  17.8 6.9 %copy-start.8 = (s32[4096]{0:T(1024)S(1)}, s32[4096]{0:T(1024)}, u32[]{:S(2)}) copy-start(s32[4096]{0:T(1024)} %param.21) | copy-start | bytes 49156
  17.8 6.9 %copy-start.9 = (f32[5,256]{1,0:T(8,128)S(1)}, f32[5,256]{1,0:T(8,128)}, u32[]{:S(2)}) copy-start(f32[5,256]{1,0:T(8,128)} %lse.1) | copy-start | bytes 15364
  17.8 6.9 %collective-permute-start.4 = (bf16[1280,256]{1,0:T(8,128)(2,1)S(1)}, bf16[1280,256]{1,0:T(8,128)(2,1)S(1)}, u32[]{:S(2)}, u32[]{:S(2)}) collective-permute-start(bf16[1280,256]{1,0:T(8,128)(2,1)S(1)} %constant_dynamic-update-slice_fusion.early_mine), channel_id=1, source_target_pairs={{0,8},{8,0},{1,9},{9,1},{2,10},{10,2},{3,11},{11,3},{4,12},{12,4},... | collective-permute-start | bytes 1966088 | tf_op jit(solution)/shard_map/ppermute | solution.py:32
  22.9 1.8 %collective-permute-start.8 = (bf16[768,256]{1,0:T(8,128)(2,1)S(1)}, bf16[768,256]{1,0:T(8,128)(2,1)S(1)}, u32[]{:S(2)}, u32[]{:S(2)}) collective-permute-start(bf16[768,256]{1,0:T(8,128)(2,1)S(1)} %constant_dynamic-update-slice_fusion.5.late_mine), channel_id=1, source_target_pairs={{0,8},{8,0},{1,9},{9,1},{2,10},{10,2},{3,11},{11,3},{4,12},{12,4},... | collective-permute-start | bytes 1179656 | tf_op jit(solution)/shard_map/ppermute | solution.py:32
  24.7 23.0 %slice-start = ((s8[6553600]{0:T(1024)(128)(4,1)}), s8[2359296]{0:T(1024)(128)(4,1)S(1)}, s32[]{:S(2)}) async-start(s8[6553600]{0:T(1024)(128)(4,1)} %bitcast.5), calls=%async_computation.1 | async-start | bytes 4718592
  28.5 2.6 %collective-permute-start.10 = (bf16[768,256]{1,0:T(8,128)(2,1)S(1)}, bf16[768,256]{1,0:T(8,128)(2,1)S(1)}, u32[]{:S(2)}, u32[]{:S(2)}) collective-permute-start(bf16[768,256]{1,0:T(8,128)(2,1)S(1)} %get-tuple-element.55), channel_id=1, source_target_pairs={{0,8},{8,0},{1,9},{9,1},{2,10},{10,2},{3,11},{11,3},{4,12},{12,4},... | collective-permute-start | bytes 1179656 | tf_op jit(solution)/shard_map/ppermute | solution.py:32
  29.7 2.3 %collective-permute-start.9 = (bf16[1280,256]{1,0:T(8,128)(2,1)S(1)}, bf16[1280,256]{1,0:T(8,128)(2,1)S(1)}, u32[]{:S(2)}, u32[]{:S(2)}) collective-permute-start(bf16[1280,256]{1,0:T(8,128)(2,1)S(1)} %get-tuple-element.53), channel_id=1, source_target_pairs={{0,8},{8,0},{1,9},{9,1},{2,10},{10,2},{3,11},{11,3},{4,12},{12,4},... | collective-permute-start | bytes 1966088 | tf_op jit(solution)/shard_map/ppermute | solution.py:32
  31.1 16.6 %slice-start.1 = ((s8[6553600]{0:T(1024)(128)(4,1)}), s8[4194304]{0:T(1024)(128)(4,1)S(1)}, s32[]{:S(2)}) async-start(s8[6553600]{0:T(1024)(128)(4,1)} %bitcast.5), calls=%async_computation.2 | async-start | bytes 8388608
  32.3 8.3 %collective-permute-start.11 = (bf16[256,256]{1,0:T(8,128)(2,1)S(1)}, bf16[256,256]{1,0:T(8,128)(2,1)S(1)}, u32[]{:S(2)}, u32[]{:S(2)}) collective-permute-start(bf16[256,256]{1,0:T(8,128)(2,1)S(1)} %get-tuple-element.57), channel_id=1, source_target_pairs={{0,96},{32,0},{64,32},{96,64},{1,97},{33,1},{65,33},{97,65},{2,98}... | collective-permute-start | bytes 393224 | tf_op jit(solution)/shard_map/ppermute | solution.py:32
  34.3 7.9 %collective-permute-start.12 = (bf16[256,256]{1,0:T(8,128)(2,1)S(1)}, bf16[256,256]{1,0:T(8,128)(2,1)S(1)}, u32[]{:S(2)}, u32[]{:S(2)}) collective-permute-start(bf16[256,256]{1,0:T(8,128)(2,1)S(1)} %get-tuple-element.58), channel_id=1, source_target_pairs={{0,64},{32,96},{64,0},{96,32},{1,65},{33,97},{65,1},{97,33},{2,66}... | collective-permute-start | bytes 393224 | tf_op jit(solution)/shard_map/ppermute | solution.py:32
  35.6 9.5 %collective-permute-start.13 = (bf16[256,256]{1,0:T(8,128)(2,1)S(1)}, bf16[256,256]{1,0:T(8,128)(2,1)S(1)}, u32[]{:S(2)}, u32[]{:S(2)}) collective-permute-start(bf16[256,256]{1,0:T(8,128)(2,1)S(1)} %get-tuple-element.59), channel_id=1, source_target_pairs={{0,32},{32,64},{64,96},{96,0},{1,33},{33,65},{65,97},{97,1},{2,34}... | collective-permute-start | bytes 393224 | tf_op jit(solution)/shard_map/ppermute | solution.py:32
  35.6 15.5 %collective-permute-start.14 = (bf16[256,256]{1,0:T(8,128)(2,1)S(1)}, bf16[256,256]{1,0:T(8,128)(2,1)S(1)}, u32[]{:S(2)}, u32[]{:S(2)}) collective-permute-start(bf16[256,256]{1,0:T(8,128)(2,1)S(1)} %get-tuple-element.62), channel_id=1, source_target_pairs={{0,96},{32,0},{64,32},{96,64},{1,97},{33,1},{65,33},{97,65},{2,98}... | collective-permute-start | bytes 393224 | tf_op jit(solution)/shard_map/ppermute | solution.py:32
  38.8 12.3 %collective-permute-start.15 = (bf16[256,256]{1,0:T(8,128)(2,1)S(1)}, bf16[256,256]{1,0:T(8,128)(2,1)S(1)}, u32[]{:S(2)}, u32[]{:S(2)}) collective-permute-start(bf16[256,256]{1,0:T(8,128)(2,1)S(1)} %get-tuple-element.63), channel_id=1, source_target_pairs={{0,64},{32,96},{64,0},{96,32},{1,65},{33,97},{65,1},{97,33},{2,66}... | collective-permute-start | bytes 393224 | tf_op jit(solution)/shard_map/ppermute | solution.py:32
  40.5 10.6 %collective-permute-start.16 = (bf16[256,256]{1,0:T(8,128)(2,1)S(1)}, bf16[256,256]{1,0:T(8,128)(2,1)S(1)}, u32[]{:S(2)}, u32[]{:S(2)}) collective-permute-start(bf16[256,256]{1,0:T(8,128)(2,1)S(1)} %get-tuple-element.64), channel_id=1, source_target_pairs={{0,32},{32,64},{64,96},{96,0},{1,33},{33,65},{65,97},{97,1},{2,34}... | collective-permute-start | bytes 393224 | tf_op jit(solution)/shard_map/ppermute | solution.py:32
  45.2 6.8 %copy-start = (bf16[5120,128]{1,0:T(8,128)(2,1)S(1)}, bf16[5120,128]{1,0:T(8,128)(2,1)}, u32[]{:S(2)}) copy-start(bf16[5120,128]{1,0:T(8,128)(2,1)} %wk.1) | copy-start | bytes 3932164
  45.2 6.8 %copy-start.1 = (bf16[5120,128]{1,0:T(8,128)(2,1)S(1)}, bf16[5120,128]{1,0:T(8,128)(2,1)}, u32[]{:S(2)}) copy-start(bf16[5120,128]{1,0:T(8,128)(2,1)} %wv.1) | copy-start | bytes 3932164
  45.2 6.8 %collective-permute-start.17 = (bf16[256,256]{1,0:T(8,128)(2,1)S(1)}, bf16[256,256]{1,0:T(8,128)(2,1)S(1)}, u32[]{:S(2)}, u32[]{:S(2)}) collective-permute-start(bf16[256,256]{1,0:T(8,128)(2,1)S(1)} %add_convert_fusion.1), channel_id=1, source_target_pairs={{0,16},{16,0},{1,17},{17,1},{2,18},{18,2},{3,19},{19,3},{4,20},{20... | collective-permute-start | bytes 393224 | tf_op jit(solution)/shard_map/ppermute | solution.py:32

commit v13 on v12

--- a/solution.py
+++ b/solution.py
@@ -154,7 +154,7 @@
 
             return carry
 
-        lax.fori_loop(0, 2 * slots, collect, 0)
+        lax.fori_loop(0, 2 * slots, collect, 0, unroll=True)
 
     def two_tiles(t, first, second, allowed):
         ones = pl.ds(pl.multiple_of(first * TILE, TILE), TILE)
@@ -223,7 +223,7 @@
 
             return carry
 
-        lax.fori_loop(0, 2 * slots, give, 0)
+        lax.fori_loop(0, 2 * slots, give, 0, unroll=True)
 
     for t in range(2):
         tok = pl.ds(t * TILE, TILE)

time: 91.4 us -> 90.8 us (level)
  no operation moved by 1% of the time
where the time goes in v13:
time: 90.8 us; the launch traced here: 90.6 us
  blocking collectives  35.9 us (40%)
  starting transfers between devices  23.8 us (26%)
  waiting for transfers between devices  15.6 us (17%)
  Pallas kernels  12.7 us (14%)
  local copies, waits for them, and re-layouts  1.17 us (1%)
  other arithmetic  1.02 us (1%)
    all_to_all x1, blocking collectives, local(): return last_sum(lax.all_to_all(send.reshape(8, 640, TOK), TP, 0, 0))  35.9 us
    ppermute x18, starting transfers between devices, shift(): return lax.ppermute(x, axes, perm)  23.8 us
    ppermute x18, waiting for transfers between devices, shift(): return lax.ppermute(x, axes, perm)  15.6 us
    pallas_call x1, Pallas kernels, query_part(): pl.pallas_call(query_part_kernel, out_shape=jax.ShapeDtypeStruct((WIDTH,...  3.4 us
    pallas_call x1, Pallas kernels, attention(): pl.pallas_call(attention_kernel, out_shape=(early, early, late, late, s((...  3.12 us
    pallas_call x1, Pallas kernels, project(): pl.pallas_call(project_kernel, out_shape=jax.ShapeDtypeStruct((WIDTH, TOK...  2.21 us
    pallas_call x1, Pallas kernels, make_block(): pl.pallas_call(block_kernel, out_shape=(s((TOK, HEAD), f32), s((TOK, HEAD...  2.09 us
  transfers between devices with their start and end apart: 18, of which 9 were waited for; matrix products, arithmetic and copies ran while one was open for 2% of the time, Pallas kernels for 5%

profile of v13, /device:TPU:0, one launch (start us, length us, event | category | flops | bytes accessed | tf_op | source)
XLA Modules:
  0.0 90.6 jit_solution(12214433743638432073)
XLA Ops:
  0.0 2.1 %block.1 = (f32[256,128]{1,0:T(8,128)}, f32[256,128]{1,0:T(8,128)}, bf16[256,256]{1,0:T(8,128)(2,1)}) custom-call(bf16[256,128]{1,0:T(8,128)(2,1)} %key.1, bf16[256,128]{1,0:T(8,128)(2,1)} %value.1, s32[2,1,128]{2,1,0:T(1,128)} %bitcast.8, f32[1,128]{1,0:T(1,128)} %constant.23.clone.inverse), custom_call_target="tpu_custom_call" | custom-call | flops 5000000 | bytes 700000 | tf_op jit(solution)/shard_map/block/pallas_call | solution.py:290
  2.1 4.0 %collective-permute-start = (bf16[256,256]{1,0:T(8,128)(2,1)}, bf16[256,256]{1,0:T(8,128)(2,1)S(1)}, u32[]{:S(2)}, u32[]{:S(2)}) collective-permute-start(bf16[256,256]{1,0:T(8,128)(2,1)} %get-tuple-element.50), channel_id=1, source_target_pairs={{0,16},{16,0},{1,17},{17,1},{2,18},{18,2},{3,19},{19,3},{4,20},{20... | collective-permute-start | bytes 393224 | tf_op jit(solution)/shard_map/ppermute | solution.py:32
  6.1 0.7 slice_multiply_fusion.small
  6.8 1.6 %collective-permute-start.1 = (bf16[256,256]{1,0:T(8,128)(2,1)}, bf16[256,256]{1,0:T(8,128)(2,1)S(1)}, u32[]{:S(2)}, u32[]{:S(2)}) collective-permute-start(bf16[256,256]{1,0:T(8,128)(2,1)} %get-tuple-element.50), channel_id=1, source_target_pairs={{0,32},{32,64},{64,96},{96,0},{1,33},{33,65},{65,97},{97,1},{2,34}... | collective-permute-start | bytes 393224 | tf_op jit(solution)/shard_map/ppermute | solution.py:32
  8.3 1.7 %collective-permute-start.3 = (bf16[256,256]{1,0:T(8,128)(2,1)}, bf16[256,256]{1,0:T(8,128)(2,1)S(1)}, u32[]{:S(2)}, u32[]{:S(2)}) collective-permute-start(bf16[256,256]{1,0:T(8,128)(2,1)} %get-tuple-element.50), channel_id=1, source_target_pairs={{0,96},{32,0},{64,32},{96,64},{1,97},{33,1},{65,33},{97,65},{2,98}... | collective-permute-start | bytes 393224 | tf_op jit(solution)/shard_map/ppermute | solution.py:32
  10.0 2.0 %collective-permute-start.2 = (bf16[256,256]{1,0:T(8,128)(2,1)}, bf16[256,256]{1,0:T(8,128)(2,1)S(1)}, u32[]{:S(2)}, u32[]{:S(2)}) collective-permute-start(bf16[256,256]{1,0:T(8,128)(2,1)} %get-tuple-element.50), channel_id=1, source_target_pairs={{0,64},{32,96},{64,0},{96,32},{1,65},{33,97},{65,1},{97,33},{2,66}... | collective-permute-start | bytes 393224 | tf_op jit(solution)/shard_map/ppermute | solution.py:32
  12.0 0.9 %constant_dynamic-update-slice_fusion.4 = bf16[1280,256]{1,0:T(8,128)(2,1)S(1)} fusion(bf16[256,256]{1,0:T(8,128)(2,1)} %get-tuple-element.50), kind=kLoop, calls=%fused_computation.7 | loop fusion | bytes 262144
  12.9 1.1 %collective-permute-start.7 = (bf16[256,256]{1,0:T(8,128)(2,1)S(1)}, bf16[256,256]{1,0:T(8,128)(2,1)S(1)}, u32[]{:S(2)}, u32[]{:S(2)}) collective-permute-start(bf16[256,256]{1,0:T(8,128)(2,1)S(1)} %collective-permute-done), channel_id=1, source_target_pairs={{0,96},{32,0},{64,32},{96,64},{1,97},{33,1},{65,33},{97,65},{2,98}... | collective-permute-start | bytes 393224 | tf_op jit(solution)/shard_map/ppermute | solution.py:32
  14.1 1.7 %collective-permute-start.6 = (bf16[256,256]{1,0:T(8,128)(2,1)S(1)}, bf16[256,256]{1,0:T(8,128)(2,1)S(1)}, u32[]{:S(2)}, u32[]{:S(2)}) collective-permute-start(bf16[256,256]{1,0:T(8,128)(2,1)S(1)} %collective-permute-done), channel_id=1, source_target_pairs={{0,64},{32,96},{64,0},{96,32},{1,65},{33,97},{65,1},{97,33},{2,66}... | collective-permute-start | bytes 393224 | tf_op jit(solution)/shard_map/ppermute | solution.py:32
  15.8 0.0 collective-permute-done.1
  15.8 0.2 collective-permute-start.5
  16.0 1.7 %collective-permute-done.2 = bf16[256,256]{1,0:T(8,128)(2,1)S(1)} collective-permute-done((bf16[256,256]{1,0:T(8,128)(2,1)}, bf16[256,256]{1,0:T(8,128)(2,1)S(1)}, u32[]{:S(2)}, u32[]{:S(2)}) %collective-permute-start.2) | collective-permute-done | bytes 131104 | tf_op jit(solution)/shard_map/ppermute | solution.py:32
  17.7 0.0 copy-start.7
  17.8 0.0 copy-start.8
  17.8 0.0 copy-start.9
  17.8 0.1 collective-permute-start.4
  17.9 4.9 %collective-permute-done.5 = bf16[256,256]{1,0:T(8,128)(2,1)S(1)} collective-permute-done((bf16[256,256]{1,0:T(8,128)(2,1)S(1)}, bf16[256,256]{1,0:T(8,128)(2,1)S(1)}, u32[]{:S(2)}, u32[]{:S(2)}) %collective-permute-start.5) | collective-permute-done | bytes 131104 | tf_op jit(solution)/shard_map/ppermute | solution.py:32
  22.8 0.0 collective-permute-done.6
  22.9 0.1 collective-permute-start.8
  23.0 0.8 prep.1
  23.9 0.8 collective-permute-done.8.late_other
  24.7 0.0 collective-permute-done.4.early_other
  24.7 0.0 slice-start
  24.7 3.1 %attention.1 = (bf16[1280,256]{1,0:T(8,128)(2,1)S(1)}, bf16[1280,256]{1,0:T(8,128)(2,1)S(1)}, bf16[768,256]{1,0:T(8,128)(2,1)S(1)}, bf16[768,256]{1,0:T(8,128)(2,1)S(1)}, bf16[640,256]{1,0:T(8,128)(2,1)S(1)}) custom-call(s32[32,32]{1,0:T(8,128)S(1)} %copy-done.7, s32[1]{0:T(128)} %bitcast.info, s32[32,1,128]{2,1,0:T(1,128)S(1)} %bitcast.7, ...), custom_call_target="tpu_custom_call" | custom-call | flops 2000000000 | bytes 8000000 | tf_op jit(solution)/shard_map/attention/pallas_call | solution.py:265
  27.9 1.3 %collective-permute-start.10 = (bf16[768,256]{1,0:T(8,128)(2,1)S(1)}, bf16[768,256]{1,0:T(8,128)(2,1)S(1)}, u32[]{:S(2)}, u32[]{:S(2)}) collective-permute-start(bf16[768,256]{1,0:T(8,128)(2,1)S(1)} %get-tuple-element.55), channel_id=1, source_target_pairs={{0,8},{8,0},{1,9},{9,1},{2,10},{10,2},{3,11},{11,3},{4,12},{12,4},... | collective-permute-start | bytes 1179656 | tf_op jit(solution)/shard_map/ppermute | solution.py:32
  29.1 0.1 collective-permute-start.9
  29.2 1.3 %collective-permute-done.10 = bf16[768,256]{1,0:T(8,128)(2,1)S(1)} collective-permute-done((bf16[768,256]{1,0:T(8,128)(2,1)S(1)}, bf16[768,256]{1,0:T(8,128)(2,1)S(1)}, u32[]{:S(2)}, u32[]{:S(2)}) %collective-permute-start.10) | collective-permute-done | bytes 393248 | tf_op jit(solution)/shard_map/ppermute | solution.py:32
  30.5 0.1 add_convert_fusion
  30.6 0.8 collective-permute-done.9
  31.4 0.2 fusion
  31.7 2.0 %collective-permute-start.11 = (bf16[256,256]{1,0:T(8,128)(2,1)S(1)}, bf16[256,256]{1,0:T(8,128)(2,1)S(1)}, u32[]{:S(2)}, u32[]{:S(2)}) collective-permute-start(bf16[256,256]{1,0:T(8,128)(2,1)S(1)} %get-tuple-element.57), channel_id=1, source_target_pairs={{0,96},{32,0},{64,32},{96,64},{1,97},{33,1},{65,33},{97,65},{2,98}... | collective-permute-start | bytes 393224 | tf_op jit(solution)/shard_map/ppermute | solution.py:32
  33.7 1.2 %collective-permute-start.12 = (bf16[256,256]{1,0:T(8,128)(2,1)S(1)}, bf16[256,256]{1,0:T(8,128)(2,1)S(1)}, u32[]{:S(2)}, u32[]{:S(2)}) collective-permute-start(bf16[256,256]{1,0:T(8,128)(2,1)S(1)} %get-tuple-element.58), channel_id=1, source_target_pairs={{0,64},{32,96},{64,0},{96,32},{1,65},{33,97},{65,1},{97,33},{2,66}... | collective-permute-start | bytes 393224 | tf_op jit(solution)/shard_map/ppermute | solution.py:32
  34.9 3.2 %collective-permute-start.14 = (bf16[256,256]{1,0:T(8,128)(2,1)S(1)}, bf16[256,256]{1,0:T(8,128)(2,1)S(1)}, u32[]{:S(2)}, u32[]{:S(2)}) collective-permute-start(bf16[256,256]{1,0:T(8,128)(2,1)S(1)} %get-tuple-element.62), channel_id=1, source_target_pairs={{0,96},{32,0},{64,32},{96,64},{1,97},{33,1},{65,33},{97,65},{2,98}... | collective-permute-start | bytes 393224 | tf_op jit(solution)/shard_map/ppermute | solution.py:32
  38.1 1.1 %collective-permute-start.15 = (bf16[256,256]{1,0:T(8,128)(2,1)S(1)}, bf16[256,256]{1,0:T(8,128)(2,1)S(1)}, u32[]{:S(2)}, u32[]{:S(2)}) collective-permute-start(bf16[256,256]{1,0:T(8,128)(2,1)S(1)} %get-tuple-element.63), channel_id=1, source_target_pairs={{0,64},{32,96},{64,0},{96,32},{1,65},{33,97},{65,1},{97,33},{2,66}... | collective-permute-start | bytes 393224 | tf_op jit(solution)/shard_map/ppermute | solution.py:32
  39.2 0.5 collective-permute-done.11
  39.8 1.8 %collective-permute-done.12 = bf16[256,256]{1,0:T(8,128)(2,1)S(1)} collective-permute-done((bf16[256,256]{1,0:T(8,128)(2,1)S(1)}, bf16[256,256]{1,0:T(8,128)(2,1)S(1)}, u32[]{:S(2)}, u32[]{:S(2)}) %collective-permute-start.12) | collective-permute-done | bytes 131104 | tf_op jit(solution)/shard_map/ppermute | solution.py:32
  41.5 2.9 %collective-permute-done.13 = bf16[256,256]{1,0:T(8,128)(2,1)S(1)} collective-permute-done((bf16[256,256]{1,0:T(8,128)(2,1)S(1)}, bf16[256,256]{1,0:T(8,128)(2,1)S(1)}, u32[]{:S(2)}, u32[]{:S(2)}) %collective-permute-start.13) | collective-permute-done | bytes 131104 | tf_op jit(solution)/shard_map/ppermute | solution.py:32
  44.5 0.1 add_convert_fusion.1
  44.5 0.0 copy-start
  44.5 0.0 copy-start.1
  44.6 2.5 %collective-permute-start.17 = (bf16[256,256]{1,0:T(8,128)(2,1)S(1)}, bf16[256,256]{1,0:T(8,128)(2,1)S(1)}, u32[]{:S(2)}, u32[]{:S(2)}) collective-permute-start(bf16[256,256]{1,0:T(8,128)(2,1)S(1)} %add_convert_fusion.1), channel_id=1, source_target_pairs={{0,16},{16,0},{1,17},{17,1},{2,18},{18,2},{3,19},{19,3},{4,20},{20... | collective-permute-start | bytes 393224 | tf_op jit(solution)/shard_map/ppermute | solution.py:32
  47.0 3.4 %query_part.1.part = bf16[5120,256]{1,0:T(8,128)(2,1)S(1)} custom-call(bf16[640,256]{1,0:T(8,128)(2,1)S(1)} %get-tuple-element.61.qg, bf16[5120,640]{1,0:T(8,128)(2,1)S(1)} %bitcast.6), custom_call_target="tpu_custom_call" | custom-call | flops 1700000000 | bytes 9000000 | tf_op jit(solution)/shard_map/query_part/pallas_call | solution.py:314
  50.5 0.0 collective-permute-done.14.near1
  50.5 0.0 collective-permute-done.16.near3
  50.5 0.9 collective-permute-done.17.across
  51.4 2.2 %project.1 = bf16[5120,256]{1,0:T(8,128)(2,1)S(1)} custom-call(bf16[5120,256]{1,0:T(8,128)(2,1)S(1)} %query_part.1.part, f32[256,256]{1,0:T(8,128)S(1)} %get-tuple-element.66.own, bf16[256,256]{1,0:T(8,128)(2,1)S(1)} %collective-permute-done.17.across, bf16[256,256]{1,0:T(8,128)(2,1)S(1)} %collective-permute-done.14.near1, ...), custom_call_target="tpu_custom_call" | custom-call | flops 700000000 | bytes 6000000 | tf_op jit(solution)/shard_map/project/pallas_call | solution.py:348
  53.6 35.9 %all_to_all.5.parts = bf16[8,640,256]{2,1,0:T(8,128)(2,1)S(1)} all-to-all(bf16[8,640,256]{2,1,0:T(8,128)(2,1)S(1)} %bitcast.4), channel_id=1, replica_groups=mesh['y'=4,'zh'=2,'core'=2,'x'=4,'zl'=2] {'x','zl'}, dimensions={0} | all-to-all | bytes 5242880 | tf_op jit(solution)/shard_map/all_to_all | solution.py:420
  89.5 1.1 %last_sum.1 = bf16[640,256]{1,0:T(8,128)(2,1)} custom-call(bf16[8,640,256]{2,1,0:T(8,128)(2,1)S(1)} %all_to_all.5.parts), custom_call_target="tpu_custom_call" | custom-call | flops 1300000 | bytes 3000000 | tf_op jit(solution)/shard_map/last_sum/pallas_call | solution.py:375
  (35 shorter events, 0.2 us)
Async XLA Ops:
  0.0 23.0 %copy-start.5 = (bf16[256,640]{1,0:T(8,128)(2,1)S(1)}, bf16[256,640]{1,0:T(8,128)(2,1)}, u32[]{:S(2)}) copy-start(bf16[256,640]{1,0:T(8,128)(2,1)} %grad) | copy-start | bytes 983044
  0.0 23.0 %copy-start.6 = (bf16[256,640]{1,0:T(8,128)(2,1)S(1)}, bf16[256,640]{1,0:T(8,128)(2,1)}, u32[]{:S(2)}) copy-start(bf16[256,640]{1,0:T(8,128)(2,1)} %att) | copy-start | bytes 983044
  0.0 23.0 %copy-start.4 = (bf16[256,640]{1,0:T(8,128)(2,1)S(1)}, bf16[256,640]{1,0:T(8,128)(2,1)}, u32[]{:S(2)}) copy-start(bf16[256,640]{1,0:T(8,128)(2,1)} %query) | copy-start | bytes 983044
  2.1 20.9 %copy-start.2 = (f32[256,128]{1,0:T(8,128)S(1)}, f32[256,128]{1,0:T(8,128)}, u32[]{:S(2)}) copy-start(f32[256,128]{1,0:T(8,128)} %get-tuple-element.42.cos) | copy-start | bytes 393220
  2.1 20.9 %copy-start.3 = (f32[256,128]{1,0:T(8,128)S(1)}, f32[256,128]{1,0:T(8,128)}, u32[]{:S(2)}) copy-start(f32[256,128]{1,0:T(8,128)} %get-tuple-element.43.sin) | copy-start | bytes 393220
  2.1 10.8 %collective-permute-start = (bf16[256,256]{1,0:T(8,128)(2,1)}, bf16[256,256]{1,0:T(8,128)(2,1)S(1)}, u32[]{:S(2)}, u32[]{:S(2)}) collective-permute-start(bf16[256,256]{1,0:T(8,128)(2,1)} %get-tuple-element.50), channel_id=1, source_target_pairs={{0,16},{16,0},{1,17},{17,1},{2,18},{18,2},{3,19},{19,3},{4,20},{20... | collective-permute-start | bytes 393224 | tf_op jit(solution)/shard_map/ppermute | solution.py:32
  6.8 9.0 %collective-permute-start.1 = (bf16[256,256]{1,0:T(8,128)(2,1)}, bf16[256,256]{1,0:T(8,128)(2,1)S(1)}, u32[]{:S(2)}, u32[]{:S(2)}) collective-permute-start(bf16[256,256]{1,0:T(8,128)(2,1)} %get-tuple-element.50), channel_id=1, source_target_pairs={{0,32},{32,64},{64,96},{96,0},{1,33},{33,65},{65,97},{97,1},{2,34}... | collective-permute-start | bytes 393224 | tf_op jit(solution)/shard_map/ppermute | solution.py:32
  8.3 9.4 %collective-permute-start.3 = (bf16[256,256]{1,0:T(8,128)(2,1)}, bf16[256,256]{1,0:T(8,128)(2,1)S(1)}, u32[]{:S(2)}, u32[]{:S(2)}) collective-permute-start(bf16[256,256]{1,0:T(8,128)(2,1)} %get-tuple-element.50), channel_id=1, source_target_pairs={{0,96},{32,0},{64,32},{96,64},{1,97},{33,1},{65,33},{97,65},{2,98}... | collective-permute-start | bytes 393224 | tf_op jit(solution)/shard_map/ppermute | solution.py:32
  10.0 7.7 %collective-permute-start.2 = (bf16[256,256]{1,0:T(8,128)(2,1)}, bf16[256,256]{1,0:T(8,128)(2,1)S(1)}, u32[]{:S(2)}, u32[]{:S(2)}) collective-permute-start(bf16[256,256]{1,0:T(8,128)(2,1)} %get-tuple-element.50), channel_id=1, source_target_pairs={{0,64},{32,96},{64,0},{96,32},{1,65},{33,97},{65,1},{97,33},{2,66}... | collective-permute-start | bytes 393224 | tf_op jit(solution)/shard_map/ppermute | solution.py:32
  12.9 9.9 %collective-permute-start.7 = (bf16[256,256]{1,0:T(8,128)(2,1)S(1)}, bf16[256,256]{1,0:T(8,128)(2,1)S(1)}, u32[]{:S(2)}, u32[]{:S(2)}) collective-permute-start(bf16[256,256]{1,0:T(8,128)(2,1)S(1)} %collective-permute-done), channel_id=1, source_target_pairs={{0,96},{32,0},{64,32},{96,64},{1,97},{33,1},{65,33},{97,65},{2,98}... | collective-permute-start | bytes 393224 | tf_op jit(solution)/shard_map/ppermute | solution.py:32
  14.1 8.8 %collective-permute-start.6 = (bf16[256,256]{1,0:T(8,128)(2,1)S(1)}, bf16[256,256]{1,0:T(8,128)(2,1)S(1)}, u32[]{:S(2)}, u32[]{:S(2)}) collective-permute-start(bf16[256,256]{1,0:T(8,128)(2,1)S(1)} %collective-permute-done), channel_id=1, source_target_pairs={{0,64},{32,96},{64,0},{96,32},{1,65},{33,97},{65,1},{97,33},{2,66}... | collective-permute-start | bytes 393224 | tf_op jit(solution)/shard_map/ppermute | solution.py:32
  15.8 7.1 %collective-permute-start.5 = (bf16[256,256]{1,0:T(8,128)(2,1)S(1)}, bf16[256,256]{1,0:T(8,128)(2,1)S(1)}, u32[]{:S(2)}, u32[]{:S(2)}) collective-permute-start(bf16[256,256]{1,0:T(8,128)(2,1)S(1)} %collective-permute-done), channel_id=1, source_target_pairs={{0,32},{32,64},{64,96},{96,0},{1,33},{33,65},{65,97},{97,1},{2,34}... | collective-permute-start | bytes 393224 | tf_op jit(solution)/shard_map/ppermute | solution.py:32
  17.7 7.0 %copy-start.7 = (s32[32,32]{1,0:T(8,128)S(1)}, s32[32,32]{1,0:T(8,128)}, u32[]{:S(2)}) copy-start(s32[32,32]{1,0:T(8,128)} %mask.1) | copy-start | bytes 12292
  17.8 6.9 %copy-start.8 = (s32[4096]{0:T(1024)S(1)}, s32[4096]{0:T(1024)}, u32[]{:S(2)}) copy-start(s32[4096]{0:T(1024)} %param.21) | copy-start | bytes 49156
  17.8 6.9 %copy-start.9 = (f32[5,256]{1,0:T(8,128)S(1)}, f32[5,256]{1,0:T(8,128)}, u32[]{:S(2)}) copy-start(f32[5,256]{1,0:T(8,128)} %lse.1) | copy-start | bytes 15364
  17.8 6.9 %collective-permute-start.4 = (bf16[1280,256]{1,0:T(8,128)(2,1)S(1)}, bf16[1280,256]{1,0:T(8,128)(2,1)S(1)}, u32[]{:S(2)}, u32[]{:S(2)}) collective-permute-start(bf16[1280,256]{1,0:T(8,128)(2,1)S(1)} %constant_dynamic-update-slice_fusion.early_mine), channel_id=1, source_target_pairs={{0,8},{8,0},{1,9},{9,1},{2,10},{10,2},{3,11},{11,3},{4,12},{12,4},... | collective-permute-start | bytes 1966088 | tf_op jit(solution)/shard_map/ppermute | solution.py:32
  22.9 1.8 %collective-permute-start.8 = (bf16[768,256]{1,0:T(8,128)(2,1)S(1)}, bf16[768,256]{1,0:T(8,128)(2,1)S(1)}, u32[]{:S(2)}, u32[]{:S(2)}) collective-permute-start(bf16[768,256]{1,0:T(8,128)(2,1)S(1)} %constant_dynamic-update-slice_fusion.5.late_mine), channel_id=1, source_target_pairs={{0,8},{8,0},{1,9},{9,1},{2,10},{10,2},{3,11},{11,3},{4,12},{12,4},... | collective-permute-start | bytes 1179656 | tf_op jit(solution)/shard_map/ppermute | solution.py:32
  24.7 22.3 %slice-start = ((s8[6553600]{0:T(1024)(128)(4,1)}), s8[2359296]{0:T(1024)(128)(4,1)S(1)}, s32[]{:S(2)}) async-start(s8[6553600]{0:T(1024)(128)(4,1)} %bitcast.5), calls=%async_computation.1 | async-start | bytes 4718592
  27.9 2.6 %collective-permute-start.10 = (bf16[768,256]{1,0:T(8,128)(2,1)S(1)}, bf16[768,256]{1,0:T(8,128)(2,1)S(1)}, u32[]{:S(2)}, u32[]{:S(2)}) collective-permute-start(bf16[768,256]{1,0:T(8,128)(2,1)S(1)} %get-tuple-element.55), channel_id=1, source_target_pairs={{0,8},{8,0},{1,9},{9,1},{2,10},{10,2},{3,11},{11,3},{4,12},{12,4},... | collective-permute-start | bytes 1179656 | tf_op jit(solution)/shard_map/ppermute | solution.py:32
  29.1 2.3 %collective-permute-start.9 = (bf16[1280,256]{1,0:T(8,128)(2,1)S(1)}, bf16[1280,256]{1,0:T(8,128)(2,1)S(1)}, u32[]{:S(2)}, u32[]{:S(2)}) collective-permute-start(bf16[1280,256]{1,0:T(8,128)(2,1)S(1)} %get-tuple-element.53), channel_id=1, source_target_pairs={{0,8},{8,0},{1,9},{9,1},{2,10},{10,2},{3,11},{11,3},{4,12},{12,4},... | collective-permute-start | bytes 1966088 | tf_op jit(solution)/shard_map/ppermute | solution.py:32
  30.5 16.6 %slice-start.1 = ((s8[6553600]{0:T(1024)(128)(4,1)}), s8[4194304]{0:T(1024)(128)(4,1)S(1)}, s32[]{:S(2)}) async-start(s8[6553600]{0:T(1024)(128)(4,1)} %bitcast.5), calls=%async_computation.2 | async-start | bytes 8388608
  31.7 8.1 %collective-permute-start.11 = (bf16[256,256]{1,0:T(8,128)(2,1)S(1)}, bf16[256,256]{1,0:T(8,128)(2,1)S(1)}, u32[]{:S(2)}, u32[]{:S(2)}) collective-permute-start(bf16[256,256]{1,0:T(8,128)(2,1)S(1)} %get-tuple-element.57), channel_id=1, source_target_pairs={{0,96},{32,0},{64,32},{96,64},{1,97},{33,1},{65,33},{97,65},{2,98}... | collective-permute-start | bytes 393224 | tf_op jit(solution)/shard_map/ppermute | solution.py:32
  33.7 7.9 %collective-permute-start.12 = (bf16[256,256]{1,0:T(8,128)(2,1)S(1)}, bf16[256,256]{1,0:T(8,128)(2,1)S(1)}, u32[]{:S(2)}, u32[]{:S(2)}) collective-permute-start(bf16[256,256]{1,0:T(8,128)(2,1)S(1)} %get-tuple-element.58), channel_id=1, source_target_pairs={{0,64},{32,96},{64,0},{96,32},{1,65},{33,97},{65,1},{97,33},{2,66}... | collective-permute-start | bytes 393224 | tf_op jit(solution)/shard_map/ppermute | solution.py:32
  34.9 9.5 %collective-permute-start.13 = (bf16[256,256]{1,0:T(8,128)(2,1)S(1)}, bf16[256,256]{1,0:T(8,128)(2,1)S(1)}, u32[]{:S(2)}, u32[]{:S(2)}) collective-permute-start(bf16[256,256]{1,0:T(8,128)(2,1)S(1)} %get-tuple-element.59), channel_id=1, source_target_pairs={{0,32},{32,64},{64,96},{96,0},{1,33},{33,65},{65,97},{97,1},{2,34}... | collective-permute-start | bytes 393224 | tf_op jit(solution)/shard_map/ppermute | solution.py:32
  34.9 15.5 %collective-permute-start.14 = (bf16[256,256]{1,0:T(8,128)(2,1)S(1)}, bf16[256,256]{1,0:T(8,128)(2,1)S(1)}, u32[]{:S(2)}, u32[]{:S(2)}) collective-permute-start(bf16[256,256]{1,0:T(8,128)(2,1)S(1)} %get-tuple-element.62), channel_id=1, source_target_pairs={{0,96},{32,0},{64,32},{96,64},{1,97},{33,1},{65,33},{97,65},{2,98}... | collective-permute-start | bytes 393224 | tf_op jit(solution)/shard_map/ppermute | solution.py:32
  38.1 12.3 %collective-permute-start.15 = (bf16[256,256]{1,0:T(8,128)(2,1)S(1)}, bf16[256,256]{1,0:T(8,128)(2,1)S(1)}, u32[]{:S(2)}, u32[]{:S(2)}) collective-permute-start(bf16[256,256]{1,0:T(8,128)(2,1)S(1)} %get-tuple-element.63), channel_id=1, source_target_pairs={{0,64},{32,96},{64,0},{96,32},{1,65},{33,97},{65,1},{97,33},{2,66}... | collective-permute-start | bytes 393224 | tf_op jit(solution)/shard_map/ppermute | solution.py:32
  39.8 10.7 %collective-permute-start.16 = (bf16[256,256]{1,0:T(8,128)(2,1)S(1)}, bf16[256,256]{1,0:T(8,128)(2,1)S(1)}, u32[]{:S(2)}, u32[]{:S(2)}) collective-permute-start(bf16[256,256]{1,0:T(8,128)(2,1)S(1)} %get-tuple-element.64), channel_id=1, source_target_pairs={{0,32},{32,64},{64,96},{96,0},{1,33},{33,65},{65,97},{97,1},{2,34}... | collective-permute-start | bytes 393224 | tf_op jit(solution)/shard_map/ppermute | solution.py:32
  44.5 6.8 %copy-start = (bf16[5120,128]{1,0:T(8,128)(2,1)S(1)}, bf16[5120,128]{1,0:T(8,128)(2,1)}, u32[]{:S(2)}) copy-start(bf16[5120,128]{1,0:T(8,128)(2,1)} %wk.1) | copy-start | bytes 3932164
  44.5 6.8 %copy-start.1 = (bf16[5120,128]{1,0:T(8,128)(2,1)S(1)}, bf16[5120,128]{1,0:T(8,128)(2,1)}, u32[]{:S(2)}) copy-start(bf16[5120,128]{1,0:T(8,128)(2,1)} %wv.1) | copy-start | bytes 3932164
  44.6 6.8 %collective-permute-start.17 = (bf16[256,256]{1,0:T(8,128)(2,1)S(1)}, bf16[256,256]{1,0:T(8,128)(2,1)S(1)}, u32[]{:S(2)}, u32[]{:S(2)}) collective-permute-start(bf16[256,256]{1,0:T(8,128)(2,1)S(1)} %add_convert_fusion.1), channel_id=1, source_target_pairs={{0,16},{16,0},{1,17},{17,1},{2,18},{18,2},{3,19},{19,3},{4,20},{20... | collective-permute-start | bytes 393224 | tf_op jit(solution)/shard_map/ppermute | solution.py:32

commit v14 on v13

--- a/solution.py
+++ b/solution.py
@@ -341,7 +341,7 @@
         out[rows, :] = (part[rows, :].astype(f32) + result).astype(bf16)
         return carry
 
-    lax.fori_loop(0, WIDTH // STEP_ROWS, step, 0)
+    lax.fori_loop(0, WIDTH // STEP_ROWS, step, 0, unroll=True)
 
 
 def project(part, own, across, near, cos, sin, wk, wv):
@@ -368,7 +368,7 @@
         out[rows, :] = total.astype(bf16)
         return carry
 
-    lax.fori_loop(0, 5, step, 0)
+    lax.fori_loop(0, 5, step, 0, unroll=True)
 
 
 def last_sum(parts):

time: 90.8 us -> 89.5 us (0.986)
  Pallas kernels: 12.7 us -> 11.5 us
    pallas_call x1, Pallas kernels: 2.21 us -> 1.02 us  [project(): pl.pallas_call(project_kernel, out_shape=jax.ShapeDtypeStruct((WIDTH, TOK...]
where the time goes in v14:
time: 89.5 us; the launch traced here: 89.3 us
  blocking collectives  35.9 us (40%)
  starting transfers between devices  23.8 us (27%)
  waiting for transfers between devices  15.6 us (17%)
  Pallas kernels  11.5 us (13%)
  local copies, waits for them, and re-layouts  1.17 us (1%)
  other arithmetic  1.02 us (1%)
    all_to_all x1, blocking collectives, local(): return last_sum(lax.all_to_all(send.reshape(8, 640, TOK), TP, 0, 0))  35.9 us
    ppermute x18, starting transfers between devices, shift(): return lax.ppermute(x, axes, perm)  23.8 us
    ppermute x18, waiting for transfers between devices, shift(): return lax.ppermute(x, axes, perm)  15.6 us
    pallas_call x1, Pallas kernels, query_part(): pl.pallas_call(query_part_kernel, out_shape=jax.ShapeDtypeStruct((WIDTH,...  3.4 us
    pallas_call x1, Pallas kernels, attention(): pl.pallas_call(attention_kernel, out_shape=(early, early, late, late, s((...  3.12 us
    pallas_call x1, Pallas kernels, make_block(): pl.pallas_call(block_kernel, out_shape=(s((TOK, HEAD), f32), s((TOK, HEAD...  2.09 us
  transfers between devices with their start and end apart: 18, of which 9 were waited for; matrix products, arithmetic and copies ran while one was open for 2% of the time, Pallas kernels for 5%

profile of v14, /device:TPU:0, one launch (start us, length us, event | category | flops | bytes accessed | tf_op | source)
XLA Modules:
  0.0 89.3 jit_solution(9024799050149609696)
XLA Ops:
  0.0 2.1 %block.1 = (f32[256,128]{1,0:T(8,128)}, f32[256,128]{1,0:T(8,128)}, bf16[256,256]{1,0:T(8,128)(2,1)}) custom-call(bf16[256,128]{1,0:T(8,128)(2,1)} %key.1, bf16[256,128]{1,0:T(8,128)(2,1)} %value.1, s32[2,1,128]{2,1,0:T(1,128)} %bitcast.8, f32[1,128]{1,0:T(1,128)} %constant.23.clone.inverse), custom_call_target="tpu_custom_call" | custom-call | flops 5000000 | bytes 700000 | tf_op jit(solution)/shard_map/block/pallas_call | solution.py:290
  2.1 4.0 %collective-permute-start = (bf16[256,256]{1,0:T(8,128)(2,1)}, bf16[256,256]{1,0:T(8,128)(2,1)S(1)}, u32[]{:S(2)}, u32[]{:S(2)}) collective-permute-start(bf16[256,256]{1,0:T(8,128)(2,1)} %get-tuple-element.50), channel_id=1, source_target_pairs={{0,16},{16,0},{1,17},{17,1},{2,18},{18,2},{3,19},{19,3},{4,20},{20... | collective-permute-start | bytes 393224 | tf_op jit(solution)/shard_map/ppermute | solution.py:32
  6.1 0.7 slice_multiply_fusion.small
  6.8 1.6 %collective-permute-start.1 = (bf16[256,256]{1,0:T(8,128)(2,1)}, bf16[256,256]{1,0:T(8,128)(2,1)S(1)}, u32[]{:S(2)}, u32[]{:S(2)}) collective-permute-start(bf16[256,256]{1,0:T(8,128)(2,1)} %get-tuple-element.50), channel_id=1, source_target_pairs={{0,32},{32,64},{64,96},{96,0},{1,33},{33,65},{65,97},{97,1},{2,34}... | collective-permute-start | bytes 393224 | tf_op jit(solution)/shard_map/ppermute | solution.py:32
  8.3 1.7 %collective-permute-start.3 = (bf16[256,256]{1,0:T(8,128)(2,1)}, bf16[256,256]{1,0:T(8,128)(2,1)S(1)}, u32[]{:S(2)}, u32[]{:S(2)}) collective-permute-start(bf16[256,256]{1,0:T(8,128)(2,1)} %get-tuple-element.50), channel_id=1, source_target_pairs={{0,96},{32,0},{64,32},{96,64},{1,97},{33,1},{65,33},{97,65},{2,98}... | collective-permute-start | bytes 393224 | tf_op jit(solution)/shard_map/ppermute | solution.py:32
  10.0 2.0 %collective-permute-start.2 = (bf16[256,256]{1,0:T(8,128)(2,1)}, bf16[256,256]{1,0:T(8,128)(2,1)S(1)}, u32[]{:S(2)}, u32[]{:S(2)}) collective-permute-start(bf16[256,256]{1,0:T(8,128)(2,1)} %get-tuple-element.50), channel_id=1, source_target_pairs={{0,64},{32,96},{64,0},{96,32},{1,65},{33,97},{65,1},{97,33},{2,66}... | collective-permute-start | bytes 393224 | tf_op jit(solution)/shard_map/ppermute | solution.py:32
  12.0 0.9 %constant_dynamic-update-slice_fusion.4 = bf16[1280,256]{1,0:T(8,128)(2,1)S(1)} fusion(bf16[256,256]{1,0:T(8,128)(2,1)} %get-tuple-element.50), kind=kLoop, calls=%fused_computation.7 | loop fusion | bytes 262144
  12.9 1.1 %collective-permute-start.7 = (bf16[256,256]{1,0:T(8,128)(2,1)S(1)}, bf16[256,256]{1,0:T(8,128)(2,1)S(1)}, u32[]{:S(2)}, u32[]{:S(2)}) collective-permute-start(bf16[256,256]{1,0:T(8,128)(2,1)S(1)} %collective-permute-done), channel_id=1, source_target_pairs={{0,96},{32,0},{64,32},{96,64},{1,97},{33,1},{65,33},{97,65},{2,98}... | collective-permute-start | bytes 393224 | tf_op jit(solution)/shard_map/ppermute | solution.py:32
  14.1 1.7 %collective-permute-start.6 = (bf16[256,256]{1,0:T(8,128)(2,1)S(1)}, bf16[256,256]{1,0:T(8,128)(2,1)S(1)}, u32[]{:S(2)}, u32[]{:S(2)}) collective-permute-start(bf16[256,256]{1,0:T(8,128)(2,1)S(1)} %collective-permute-done), channel_id=1, source_target_pairs={{0,64},{32,96},{64,0},{96,32},{1,65},{33,97},{65,1},{97,33},{2,66}... | collective-permute-start | bytes 393224 | tf_op jit(solution)/shard_map/ppermute | solution.py:32
  15.8 0.2 collective-permute-start.5
  16.0 1.7 %collective-permute-done.2 = bf16[256,256]{1,0:T(8,128)(2,1)S(1)} collective-permute-done((bf16[256,256]{1,0:T(8,128)(2,1)}, bf16[256,256]{1,0:T(8,128)(2,1)S(1)}, u32[]{:S(2)}, u32[]{:S(2)}) %collective-permute-start.2) | collective-permute-done | bytes 131104 | tf_op jit(solution)/shard_map/ppermute | solution.py:32
  17.7 0.0 copy-start.7
  17.8 0.0 copy-start.8
  17.8 0.0 copy-start.9
  17.8 0.0 collective-permute-done.3
  17.8 0.1 collective-permute-start.4
  17.9 4.9 %collective-permute-done.5 = bf16[256,256]{1,0:T(8,128)(2,1)S(1)} collective-permute-done((bf16[256,256]{1,0:T(8,128)(2,1)S(1)}, bf16[256,256]{1,0:T(8,128)(2,1)S(1)}, u32[]{:S(2)}, u32[]{:S(2)}) %collective-permute-start.5) | collective-permute-done | bytes 131104 | tf_op jit(solution)/shard_map/ppermute | solution.py:32
  22.9 0.0 collective-permute-done.7
  22.9 0.1 collective-permute-start.8
  23.0 0.8 prep.1
  23.9 0.8 collective-permute-done.8.late_other
  24.7 0.0 collective-permute-done.4.early_other
  24.7 0.0 slice-start
  24.7 3.1 %attention.1 = (bf16[1280,256]{1,0:T(8,128)(2,1)S(1)}, bf16[1280,256]{1,0:T(8,128)(2,1)S(1)}, bf16[768,256]{1,0:T(8,128)(2,1)S(1)}, bf16[768,256]{1,0:T(8,128)(2,1)S(1)}, bf16[640,256]{1,0:T(8,128)(2,1)S(1)}) custom-call(s32[32,32]{1,0:T(8,128)S(1)} %copy-done.7, s32[1]{0:T(128)} %bitcast.info, s32[32,1,128]{2,1,0:T(1,128)S(1)} %bitcast.7, ...), custom_call_target="tpu_custom_call" | custom-call | flops 2000000000 | bytes 8000000 | tf_op jit(solution)/shard_map/attention/pallas_call | solution.py:265
  27.9 1.3 %collective-permute-start.10 = (bf16[768,256]{1,0:T(8,128)(2,1)S(1)}, bf16[768,256]{1,0:T(8,128)(2,1)S(1)}, u32[]{:S(2)}, u32[]{:S(2)}) collective-permute-start(bf16[768,256]{1,0:T(8,128)(2,1)S(1)} %get-tuple-element.55), channel_id=1, source_target_pairs={{0,8},{8,0},{1,9},{9,1},{2,10},{10,2},{3,11},{11,3},{4,12},{12,4},... | collective-permute-start | bytes 1179656 | tf_op jit(solution)/shard_map/ppermute | solution.py:32
  29.1 0.1 collective-permute-start.9
  29.2 1.3 %collective-permute-done.10 = bf16[768,256]{1,0:T(8,128)(2,1)S(1)} collective-permute-done((bf16[768,256]{1,0:T(8,128)(2,1)S(1)}, bf16[768,256]{1,0:T(8,128)(2,1)S(1)}, u32[]{:S(2)}, u32[]{:S(2)}) %collective-permute-start.10) | collective-permute-done | bytes 393248 | tf_op jit(solution)/shard_map/ppermute | solution.py:32
  30.5 0.1 add_convert_fusion
  30.6 0.8 collective-permute-done.9
  31.4 0.2 fusion
  31.7 2.0 %collective-permute-start.11 = (bf16[256,256]{1,0:T(8,128)(2,1)S(1)}, bf16[256,256]{1,0:T(8,128)(2,1)S(1)}, u32[]{:S(2)}, u32[]{:S(2)}) collective-permute-start(bf16[256,256]{1,0:T(8,128)(2,1)S(1)} %get-tuple-element.57), channel_id=1, source_target_pairs={{0,96},{32,0},{64,32},{96,64},{1,97},{33,1},{65,33},{97,65},{2,98}... | collective-permute-start | bytes 393224 | tf_op jit(solution)/shard_map/ppermute | solution.py:32
  33.7 1.2 %collective-permute-start.12 = (bf16[256,256]{1,0:T(8,128)(2,1)S(1)}, bf16[256,256]{1,0:T(8,128)(2,1)S(1)}, u32[]{:S(2)}, u32[]{:S(2)}) collective-permute-start(bf16[256,256]{1,0:T(8,128)(2,1)S(1)} %get-tuple-element.58), channel_id=1, source_target_pairs={{0,64},{32,96},{64,0},{96,32},{1,65},{33,97},{65,1},{97,33},{2,66}... | collective-permute-start | bytes 393224 | tf_op jit(solution)/shard_map/ppermute | solution.py:32
  34.9 3.2 %collective-permute-start.14 = (bf16[256,256]{1,0:T(8,128)(2,1)S(1)}, bf16[256,256]{1,0:T(8,128)(2,1)S(1)}, u32[]{:S(2)}, u32[]{:S(2)}) collective-permute-start(bf16[256,256]{1,0:T(8,128)(2,1)S(1)} %get-tuple-element.62), channel_id=1, source_target_pairs={{0,96},{32,0},{64,32},{96,64},{1,97},{33,1},{65,33},{97,65},{2,98}... | collective-permute-start | bytes 393224 | tf_op jit(solution)/shard_map/ppermute | solution.py:32
  38.2 1.1 %collective-permute-start.15 = (bf16[256,256]{1,0:T(8,128)(2,1)S(1)}, bf16[256,256]{1,0:T(8,128)(2,1)S(1)}, u32[]{:S(2)}, u32[]{:S(2)}) collective-permute-start(bf16[256,256]{1,0:T(8,128)(2,1)S(1)} %get-tuple-element.63), channel_id=1, source_target_pairs={{0,64},{32,96},{64,0},{96,32},{1,65},{33,97},{65,1},{97,33},{2,66}... | collective-permute-start | bytes 393224 | tf_op jit(solution)/shard_map/ppermute | solution.py:32
  39.2 0.5 collective-permute-done.11
  39.8 0.0 collective-permute-start.16
  39.8 1.8 %collective-permute-done.12 = bf16[256,256]{1,0:T(8,128)(2,1)S(1)} collective-permute-done((bf16[256,256]{1,0:T(8,128)(2,1)S(1)}, bf16[256,256]{1,0:T(8,128)(2,1)S(1)}, u32[]{:S(2)}, u32[]{:S(2)}) %collective-permute-start.12) | collective-permute-done | bytes 131104 | tf_op jit(solution)/shard_map/ppermute | solution.py:32
  41.5 2.9 %collective-permute-done.13 = bf16[256,256]{1,0:T(8,128)(2,1)S(1)} collective-permute-done((bf16[256,256]{1,0:T(8,128)(2,1)S(1)}, bf16[256,256]{1,0:T(8,128)(2,1)S(1)}, u32[]{:S(2)}, u32[]{:S(2)}) %collective-permute-start.13) | collective-permute-done | bytes 131104 | tf_op jit(solution)/shard_map/ppermute | solution.py:32
  44.5 0.1 add_convert_fusion.1
  44.5 0.0 copy-start
  44.5 0.0 copy-start.1
  44.6 2.5 %collective-permute-start.17 = (bf16[256,256]{1,0:T(8,128)(2,1)S(1)}, bf16[256,256]{1,0:T(8,128)(2,1)S(1)}, u32[]{:S(2)}, u32[]{:S(2)}) collective-permute-start(bf16[256,256]{1,0:T(8,128)(2,1)S(1)} %add_convert_fusion.1), channel_id=1, source_target_pairs={{0,16},{16,0},{1,17},{17,1},{2,18},{18,2},{3,19},{19,3},{4,20},{20... | collective-permute-start | bytes 393224 | tf_op jit(solution)/shard_map/ppermute | solution.py:32
  47.0 3.4 %query_part.1.part = bf16[5120,256]{1,0:T(8,128)(2,1)S(1)} custom-call(bf16[640,256]{1,0:T(8,128)(2,1)S(1)} %get-tuple-element.61.qg, bf16[5120,640]{1,0:T(8,128)(2,1)S(1)} %bitcast.6), custom_call_target="tpu_custom_call" | custom-call | flops 1700000000 | bytes 9000000 | tf_op jit(solution)/shard_map/query_part/pallas_call | solution.py:314
  50.4 0.0 collective-permute-done.14.near1
  50.5 0.9 %collective-permute-done.17.across = bf16[256,256]{1,0:T(8,128)(2,1)S(1)} collective-permute-done((bf16[256,256]{1,0:T(8,128)(2,1)S(1)}, bf16[256,256]{1,0:T(8,128)(2,1)S(1)}, u32[]{:S(2)}, u32[]{:S(2)}) %collective-permute-start.17) | collective-permute-done | bytes 131104 | tf_op jit(solution)/shard_map/ppermute | solution.py:32
  51.4 1.0 %project.1 = bf16[5120,256]{1,0:T(8,128)(2,1)S(1)} custom-call(bf16[5120,256]{1,0:T(8,128)(2,1)S(1)} %query_part.1.part, f32[256,256]{1,0:T(8,128)S(1)} %get-tuple-element.66.own, bf16[256,256]{1,0:T(8,128)(2,1)S(1)} %collective-permute-done.17.across, bf16[256,256]{1,0:T(8,128)(2,1)S(1)} %collective-permute-done.14.near1, ...), custom_call_target="tpu_custom_call" | custom-call | flops 700000000 | bytes 6000000 | tf_op jit(solution)/shard_map/project/pallas_call | solution.py:348
  52.4 35.9 %all_to_all.5.parts = bf16[8,640,256]{2,1,0:T(8,128)(2,1)S(1)} all-to-all(bf16[8,640,256]{2,1,0:T(8,128)(2,1)S(1)} %bitcast.4), channel_id=1, replica_groups=mesh['y'=4,'zh'=2,'core'=2,'x'=4,'zl'=2] {'x','zl'}, dimensions={0} | all-to-all | bytes 5242880 | tf_op jit(solution)/shard_map/all_to_all | solution.py:420
  88.3 1.1 %last_sum.1 = bf16[640,256]{1,0:T(8,128)(2,1)} custom-call(bf16[8,640,256]{2,1,0:T(8,128)(2,1)S(1)} %all_to_all.5.parts), custom_call_target="tpu_custom_call" | custom-call | flops 1300000 | bytes 3000000 | tf_op jit(solution)/shard_map/last_sum/pallas_call | solution.py:375
  (35 shorter events, 0.2 us)
Async XLA Ops:
  0.0 23.0 %copy-start.5 = (bf16[256,640]{1,0:T(8,128)(2,1)S(1)}, bf16[256,640]{1,0:T(8,128)(2,1)}, u32[]{:S(2)}) copy-start(bf16[256,640]{1,0:T(8,128)(2,1)} %grad) | copy-start | bytes 983044
  0.0 23.0 %copy-start.6 = (bf16[256,640]{1,0:T(8,128)(2,1)S(1)}, bf16[256,640]{1,0:T(8,128)(2,1)}, u32[]{:S(2)}) copy-start(bf16[256,640]{1,0:T(8,128)(2,1)} %att) | copy-start | bytes 983044
  0.0 23.0 %copy-start.4 = (bf16[256,640]{1,0:T(8,128)(2,1)S(1)}, bf16[256,640]{1,0:T(8,128)(2,1)}, u32[]{:S(2)}) copy-start(bf16[256,640]{1,0:T(8,128)(2,1)} %query) | copy-start | bytes 983044
  2.1 20.9 %copy-start.2 = (f32[256,128]{1,0:T(8,128)S(1)}, f32[256,128]{1,0:T(8,128)}, u32[]{:S(2)}) copy-start(f32[256,128]{1,0:T(8,128)} %get-tuple-element.42.cos) | copy-start | bytes 393220
  2.1 20.9 %copy-start.3 = (f32[256,128]{1,0:T(8,128)S(1)}, f32[256,128]{1,0:T(8,128)}, u32[]{:S(2)}) copy-start(f32[256,128]{1,0:T(8,128)} %get-tuple-element.43.sin) | copy-start | bytes 393220
  2.1 10.8 %collective-permute-start = (bf16[256,256]{1,0:T(8,128)(2,1)}, bf16[256,256]{1,0:T(8,128)(2,1)S(1)}, u32[]{:S(2)}, u32[]{:S(2)}) collective-permute-start(bf16[256,256]{1,0:T(8,128)(2,1)} %get-tuple-element.50), channel_id=1, source_target_pairs={{0,16},{16,0},{1,17},{17,1},{2,18},{18,2},{3,19},{19,3},{4,20},{20... | collective-permute-start | bytes 393224 | tf_op jit(solution)/shard_map/ppermute | solution.py:32
  6.8 9.0 %collective-permute-start.1 = (bf16[256,256]{1,0:T(8,128)(2,1)}, bf16[256,256]{1,0:T(8,128)(2,1)S(1)}, u32[]{:S(2)}, u32[]{:S(2)}) collective-permute-start(bf16[256,256]{1,0:T(8,128)(2,1)} %get-tuple-element.50), channel_id=1, source_target_pairs={{0,32},{32,64},{64,96},{96,0},{1,33},{33,65},{65,97},{97,1},{2,34}... | collective-permute-start | bytes 393224 | tf_op jit(solution)/shard_map/ppermute | solution.py:32
  8.3 9.4 %collective-permute-start.3 = (bf16[256,256]{1,0:T(8,128)(2,1)}, bf16[256,256]{1,0:T(8,128)(2,1)S(1)}, u32[]{:S(2)}, u32[]{:S(2)}) collective-permute-start(bf16[256,256]{1,0:T(8,128)(2,1)} %get-tuple-element.50), channel_id=1, source_target_pairs={{0,96},{32,0},{64,32},{96,64},{1,97},{33,1},{65,33},{97,65},{2,98}... | collective-permute-start | bytes 393224 | tf_op jit(solution)/shard_map/ppermute | solution.py:32
  10.0 7.7 %collective-permute-start.2 = (bf16[256,256]{1,0:T(8,128)(2,1)}, bf16[256,256]{1,0:T(8,128)(2,1)S(1)}, u32[]{:S(2)}, u32[]{:S(2)}) collective-permute-start(bf16[256,256]{1,0:T(8,128)(2,1)} %get-tuple-element.50), channel_id=1, source_target_pairs={{0,64},{32,96},{64,0},{96,32},{1,65},{33,97},{65,1},{97,33},{2,66}... | collective-permute-start | bytes 393224 | tf_op jit(solution)/shard_map/ppermute | solution.py:32
  12.9 9.9 %collective-permute-start.7 = (bf16[256,256]{1,0:T(8,128)(2,1)S(1)}, bf16[256,256]{1,0:T(8,128)(2,1)S(1)}, u32[]{:S(2)}, u32[]{:S(2)}) collective-permute-start(bf16[256,256]{1,0:T(8,128)(2,1)S(1)} %collective-permute-done), channel_id=1, source_target_pairs={{0,96},{32,0},{64,32},{96,64},{1,97},{33,1},{65,33},{97,65},{2,98}... | collective-permute-start | bytes 393224 | tf_op jit(solution)/shard_map/ppermute | solution.py:32
  14.1 8.8 %collective-permute-start.6 = (bf16[256,256]{1,0:T(8,128)(2,1)S(1)}, bf16[256,256]{1,0:T(8,128)(2,1)S(1)}, u32[]{:S(2)}, u32[]{:S(2)}) collective-permute-start(bf16[256,256]{1,0:T(8,128)(2,1)S(1)} %collective-permute-done), channel_id=1, source_target_pairs={{0,64},{32,96},{64,0},{96,32},{1,65},{33,97},{65,1},{97,33},{2,66}... | collective-permute-start | bytes 393224 | tf_op jit(solution)/shard_map/ppermute | solution.py:32
  15.8 7.1 %collective-permute-start.5 = (bf16[256,256]{1,0:T(8,128)(2,1)S(1)}, bf16[256,256]{1,0:T(8,128)(2,1)S(1)}, u32[]{:S(2)}, u32[]{:S(2)}) collective-permute-start(bf16[256,256]{1,0:T(8,128)(2,1)S(1)} %collective-permute-done), channel_id=1, source_target_pairs={{0,32},{32,64},{64,96},{96,0},{1,33},{33,65},{65,97},{97,1},{2,34}... | collective-permute-start | bytes 393224 | tf_op jit(solution)/shard_map/ppermute | solution.py:32
  17.7 7.0 %copy-start.7 = (s32[32,32]{1,0:T(8,128)S(1)}, s32[32,32]{1,0:T(8,128)}, u32[]{:S(2)}) copy-start(s32[32,32]{1,0:T(8,128)} %mask.1) | copy-start | bytes 12292
  17.8 6.9 %copy-start.8 = (s32[4096]{0:T(1024)S(1)}, s32[4096]{0:T(1024)}, u32[]{:S(2)}) copy-start(s32[4096]{0:T(1024)} %param.21) | copy-start | bytes 49156
  17.8 6.9 %copy-start.9 = (f32[5,256]{1,0:T(8,128)S(1)}, f32[5,256]{1,0:T(8,128)}, u32[]{:S(2)}) copy-start(f32[5,256]{1,0:T(8,128)} %lse.1) | copy-start | bytes 15364
  17.8 6.9 %collective-permute-start.4 = (bf16[1280,256]{1,0:T(8,128)(2,1)S(1)}, bf16[1280,256]{1,0:T(8,128)(2,1)S(1)}, u32[]{:S(2)}, u32[]{:S(2)}) collective-permute-start(bf16[1280,256]{1,0:T(8,128)(2,1)S(1)} %constant_dynamic-update-slice_fusion.early_mine), channel_id=1, source_target_pairs={{0,8},{8,0},{1,9},{9,1},{2,10},{10,2},{3,11},{11,3},{4,12},{12,4},... | collective-permute-start | bytes 1966088 | tf_op jit(solution)/shard_map/ppermute | solution.py:32
  22.9 1.8 %collective-permute-start.8 = (bf16[768,256]{1,0:T(8,128)(2,1)S(1)}, bf16[768,256]{1,0:T(8,128)(2,1)S(1)}, u32[]{:S(2)}, u32[]{:S(2)}) collective-permute-start(bf16[768,256]{1,0:T(8,128)(2,1)S(1)} %constant_dynamic-update-slice_fusion.5.late_mine), channel_id=1, source_target_pairs={{0,8},{8,0},{1,9},{9,1},{2,10},{10,2},{3,11},{11,3},{4,12},{12,4},... | collective-permute-start | bytes 1179656 | tf_op jit(solution)/shard_map/ppermute | solution.py:32
  24.7 22.3 %slice-start = ((s8[6553600]{0:T(1024)(128)(4,1)}), s8[2359296]{0:T(1024)(128)(4,1)S(1)}, s32[]{:S(2)}) async-start(s8[6553600]{0:T(1024)(128)(4,1)} %bitcast.5), calls=%async_computation.1 | async-start | bytes 4718592
  27.9 2.6 %collective-permute-start.10 = (bf16[768,256]{1,0:T(8,128)(2,1)S(1)}, bf16[768,256]{1,0:T(8,128)(2,1)S(1)}, u32[]{:S(2)}, u32[]{:S(2)}) collective-permute-start(bf16[768,256]{1,0:T(8,128)(2,1)S(1)} %get-tuple-element.55), channel_id=1, source_target_pairs={{0,8},{8,0},{1,9},{9,1},{2,10},{10,2},{3,11},{11,3},{4,12},{12,4},... | collective-permute-start | bytes 1179656 | tf_op jit(solution)/shard_map/ppermute | solution.py:32
  29.1 2.3 %collective-permute-start.9 = (bf16[1280,256]{1,0:T(8,128)(2,1)S(1)}, bf16[1280,256]{1,0:T(8,128)(2,1)S(1)}, u32[]{:S(2)}, u32[]{:S(2)}) collective-permute-start(bf16[1280,256]{1,0:T(8,128)(2,1)S(1)} %get-tuple-element.53), channel_id=1, source_target_pairs={{0,8},{8,0},{1,9},{9,1},{2,10},{10,2},{3,11},{11,3},{4,12},{12,4},... | collective-permute-start | bytes 1966088 | tf_op jit(solution)/shard_map/ppermute | solution.py:32
  30.5 16.5 %slice-start.1 = ((s8[6553600]{0:T(1024)(128)(4,1)}), s8[4194304]{0:T(1024)(128)(4,1)S(1)}, s32[]{:S(2)}) async-start(s8[6553600]{0:T(1024)(128)(4,1)} %bitcast.5), calls=%async_computation.2 | async-start | bytes 8388608
  31.7 8.1 %collective-permute-start.11 = (bf16[256,256]{1,0:T(8,128)(2,1)S(1)}, bf16[256,256]{1,0:T(8,128)(2,1)S(1)}, u32[]{:S(2)}, u32[]{:S(2)}) collective-permute-start(bf16[256,256]{1,0:T(8,128)(2,1)S(1)} %get-tuple-element.57), channel_id=1, source_target_pairs={{0,96},{32,0},{64,32},{96,64},{1,97},{33,1},{65,33},{97,65},{2,98}... | collective-permute-start | bytes 393224 | tf_op jit(solution)/shard_map/ppermute | solution.py:32
  33.7 7.9 %collective-permute-start.12 = (bf16[256,256]{1,0:T(8,128)(2,1)S(1)}, bf16[256,256]{1,0:T(8,128)(2,1)S(1)}, u32[]{:S(2)}, u32[]{:S(2)}) collective-permute-start(bf16[256,256]{1,0:T(8,128)(2,1)S(1)} %get-tuple-element.58), channel_id=1, source_target_pairs={{0,64},{32,96},{64,0},{96,32},{1,65},{33,97},{65,1},{97,33},{2,66}... | collective-permute-start | bytes 393224 | tf_op jit(solution)/shard_map/ppermute | solution.py:32
  34.9 9.5 %collective-permute-start.13 = (bf16[256,256]{1,0:T(8,128)(2,1)S(1)}, bf16[256,256]{1,0:T(8,128)(2,1)S(1)}, u32[]{:S(2)}, u32[]{:S(2)}) collective-permute-start(bf16[256,256]{1,0:T(8,128)(2,1)S(1)} %get-tuple-element.59), channel_id=1, source_target_pairs={{0,32},{32,64},{64,96},{96,0},{1,33},{33,65},{65,97},{97,1},{2,34}... | collective-permute-start | bytes 393224 | tf_op jit(solution)/shard_map/ppermute | solution.py:32
  34.9 15.5 %collective-permute-start.14 = (bf16[256,256]{1,0:T(8,128)(2,1)S(1)}, bf16[256,256]{1,0:T(8,128)(2,1)S(1)}, u32[]{:S(2)}, u32[]{:S(2)}) collective-permute-start(bf16[256,256]{1,0:T(8,128)(2,1)S(1)} %get-tuple-element.62), channel_id=1, source_target_pairs={{0,96},{32,0},{64,32},{96,64},{1,97},{33,1},{65,33},{97,65},{2,98}... | collective-permute-start | bytes 393224 | tf_op jit(solution)/shard_map/ppermute | solution.py:32
  38.2 12.3 %collective-permute-start.15 = (bf16[256,256]{1,0:T(8,128)(2,1)S(1)}, bf16[256,256]{1,0:T(8,128)(2,1)S(1)}, u32[]{:S(2)}, u32[]{:S(2)}) collective-permute-start(bf16[256,256]{1,0:T(8,128)(2,1)S(1)} %get-tuple-element.63), channel_id=1, source_target_pairs={{0,64},{32,96},{64,0},{96,32},{1,65},{33,97},{65,1},{97,33},{2,66}... | collective-permute-start | bytes 393224 | tf_op jit(solution)/shard_map/ppermute | solution.py:32
  39.8 10.7 %collective-permute-start.16 = (bf16[256,256]{1,0:T(8,128)(2,1)S(1)}, bf16[256,256]{1,0:T(8,128)(2,1)S(1)}, u32[]{:S(2)}, u32[]{:S(2)}) collective-permute-start(bf16[256,256]{1,0:T(8,128)(2,1)S(1)} %get-tuple-element.64), channel_id=1, source_target_pairs={{0,32},{32,64},{64,96},{96,0},{1,33},{33,65},{65,97},{97,1},{2,34}... | collective-permute-start | bytes 393224 | tf_op jit(solution)/shard_map/ppermute | solution.py:32
  44.5 6.8 %copy-start = (bf16[5120,128]{1,0:T(8,128)(2,1)S(1)}, bf16[5120,128]{1,0:T(8,128)(2,1)}, u32[]{:S(2)}) copy-start(bf16[5120,128]{1,0:T(8,128)(2,1)} %wk.1) | copy-start | bytes 3932164
  44.5 6.8 %copy-start.1 = (bf16[5120,128]{1,0:T(8,128)(2,1)S(1)}, bf16[5120,128]{1,0:T(8,128)(2,1)}, u32[]{:S(2)}) copy-start(bf16[5120,128]{1,0:T(8,128)(2,1)} %wv.1) | copy-start | bytes 3932164
  44.6 6.8 %collective-permute-start.17 = (bf16[256,256]{1,0:T(8,128)(2,1)S(1)}, bf16[256,256]{1,0:T(8,128)(2,1)S(1)}, u32[]{:S(2)}, u32[]{:S(2)}) collective-permute-start(bf16[256,256]{1,0:T(8,128)(2,1)S(1)} %add_convert_fusion.1), channel_id=1, source_target_pairs={{0,16},{16,0},{1,17},{17,1},{2,18},{18,2},{3,19},{19,3},{4,20},{20... | collective-permute-start | bytes 393224 | tf_op jit(solution)/shard_map/ppermute | solution.py:32

commit v15 on v14

--- a/solution.py
+++ b/solution.py
@@ -307,7 +307,7 @@
         out[rows, :] = jnp.dot(wq[rows, :], qg[...], preferred_element_type=f32).astype(bf16)
         return carry
 
-    lax.fori_loop(0, WIDTH // STEP_ROWS, step, 0)
+    lax.fori_loop(0, WIDTH // STEP_ROWS, step, 0, unroll=True)
 
 
 def query_part(qg, wq):

time: 89.5 us -> 89.7 us (level)
  waiting for transfers between devices: 15.6 us -> 16.9 us
  Pallas kernels: 11.5 us -> 10.3 us
    ppermute x18, waiting for transfers between devices: 15.6 us -> 16.9 us  [shift(): return lax.ppermute(x, axes, perm)]
    pallas_call x1, Pallas kernels: 3.4 us -> 2.2 us  [query_part(): pl.pallas_call(query_part_kernel, out_shape=jax.ShapeDtypeStruct((WIDTH,...]
  transfers between devices with their start and end apart: 18 -> 18, of which waited for: 9 -> 9; matrix products, arithmetic and copies ran while one was open for 2% -> 2% of each run, Pallas kernels for 5% -> 3%
where the time goes in v15:
time: 89.7 us; the launch traced here: 89.5 us
  blocking collectives  35.9 us (40%)
  starting transfers between devices  24 us (27%)
  waiting for transfers between devices  16.9 us (19%)
  Pallas kernels  10.3 us (11%)
  local copies, waits for them, and re-layouts  1.17 us (1%)
  other arithmetic  1.02 us (1%)
    all_to_all x1, blocking collectives, local(): return last_sum(lax.all_to_all(send.reshape(8, 640, TOK), TP, 0, 0))  35.9 us
    ppermute x18, starting transfers between devices, shift(): return lax.ppermute(x, axes, perm)  24 us
    ppermute x18, waiting for transfers between devices, shift(): return lax.ppermute(x, axes, perm)  16.9 us
    pallas_call x1, Pallas kernels, attention(): pl.pallas_call(attention_kernel, out_shape=(early, early, late, late, s((...  3.12 us
    pallas_call x1, Pallas kernels, query_part(): pl.pallas_call(query_part_kernel, out_shape=jax.ShapeDtypeStruct((WIDTH,...  2.2 us
    pallas_call x1, Pallas kernels, make_block(): pl.pallas_call(block_kernel, out_shape=(s((TOK, HEAD), f32), s((TOK, HEAD...  2.09 us
  transfers between devices with their start and end apart: 18, of which 9 were waited for; matrix products, arithmetic and copies ran while one was open for 2% of the time, Pallas kernels for 3%

profile of v15, /device:TPU:0, one launch (start us, length us, event | category | flops | bytes accessed | tf_op | source)
XLA Modules:
  0.0 89.5 jit_solution(7808331038677727924)
XLA Ops:
  0.0 2.1 %block.1 = (f32[256,128]{1,0:T(8,128)}, f32[256,128]{1,0:T(8,128)}, bf16[256,256]{1,0:T(8,128)(2,1)}) custom-call(bf16[256,128]{1,0:T(8,128)(2,1)} %key.1, bf16[256,128]{1,0:T(8,128)(2,1)} %value.1, s32[2,1,128]{2,1,0:T(1,128)} %bitcast.8, f32[1,128]{1,0:T(1,128)} %constant.23.clone.inverse), custom_call_target="tpu_custom_call" | custom-call | flops 5000000 | bytes 700000 | tf_op jit(solution)/shard_map/block/pallas_call | solution.py:290
  2.1 4.0 %collective-permute-start = (bf16[256,256]{1,0:T(8,128)(2,1)}, bf16[256,256]{1,0:T(8,128)(2,1)S(1)}, u32[]{:S(2)}, u32[]{:S(2)}) collective-permute-start(bf16[256,256]{1,0:T(8,128)(2,1)} %get-tuple-element.50), channel_id=1, source_target_pairs={{0,16},{16,0},{1,17},{17,1},{2,18},{18,2},{3,19},{19,3},{4,20},{20... | collective-permute-start | bytes 393224 | tf_op jit(solution)/shard_map/ppermute | solution.py:32
  6.1 0.7 slice_multiply_fusion.small
  6.8 1.6 %collective-permute-start.1 = (bf16[256,256]{1,0:T(8,128)(2,1)}, bf16[256,256]{1,0:T(8,128)(2,1)S(1)}, u32[]{:S(2)}, u32[]{:S(2)}) collective-permute-start(bf16[256,256]{1,0:T(8,128)(2,1)} %get-tuple-element.50), channel_id=1, source_target_pairs={{0,32},{32,64},{64,96},{96,0},{1,33},{33,65},{65,97},{97,1},{2,34}... | collective-permute-start | bytes 393224 | tf_op jit(solution)/shard_map/ppermute | solution.py:32
  8.3 1.7 %collective-permute-start.3 = (bf16[256,256]{1,0:T(8,128)(2,1)}, bf16[256,256]{1,0:T(8,128)(2,1)S(1)}, u32[]{:S(2)}, u32[]{:S(2)}) collective-permute-start(bf16[256,256]{1,0:T(8,128)(2,1)} %get-tuple-element.50), channel_id=1, source_target_pairs={{0,96},{32,0},{64,32},{96,64},{1,97},{33,1},{65,33},{97,65},{2,98}... | collective-permute-start | bytes 393224 | tf_op jit(solution)/shard_map/ppermute | solution.py:32
  10.0 2.0 %collective-permute-start.2 = (bf16[256,256]{1,0:T(8,128)(2,1)}, bf16[256,256]{1,0:T(8,128)(2,1)S(1)}, u32[]{:S(2)}, u32[]{:S(2)}) collective-permute-start(bf16[256,256]{1,0:T(8,128)(2,1)} %get-tuple-element.50), channel_id=1, source_target_pairs={{0,64},{32,96},{64,0},{96,32},{1,65},{33,97},{65,1},{97,33},{2,66}... | collective-permute-start | bytes 393224 | tf_op jit(solution)/shard_map/ppermute | solution.py:32
  12.0 0.9 %constant_dynamic-update-slice_fusion.4 = bf16[1280,256]{1,0:T(8,128)(2,1)S(1)} fusion(bf16[256,256]{1,0:T(8,128)(2,1)} %get-tuple-element.50), kind=kLoop, calls=%fused_computation.7 | loop fusion | bytes 262144
  12.9 0.0 collective-permute-done
  12.9 1.1 %collective-permute-start.7 = (bf16[256,256]{1,0:T(8,128)(2,1)S(1)}, bf16[256,256]{1,0:T(8,128)(2,1)S(1)}, u32[]{:S(2)}, u32[]{:S(2)}) collective-permute-start(bf16[256,256]{1,0:T(8,128)(2,1)S(1)} %collective-permute-done), channel_id=1, source_target_pairs={{0,96},{32,0},{64,32},{96,64},{1,97},{33,1},{65,33},{97,65},{2,98}... | collective-permute-start | bytes 393224 | tf_op jit(solution)/shard_map/ppermute | solution.py:32
  14.1 1.7 %collective-permute-start.6 = (bf16[256,256]{1,0:T(8,128)(2,1)S(1)}, bf16[256,256]{1,0:T(8,128)(2,1)S(1)}, u32[]{:S(2)}, u32[]{:S(2)}) collective-permute-start(bf16[256,256]{1,0:T(8,128)(2,1)S(1)} %collective-permute-done), channel_id=1, source_target_pairs={{0,64},{32,96},{64,0},{96,32},{1,65},{33,97},{65,1},{97,33},{2,66}... | collective-permute-start | bytes 393224 | tf_op jit(solution)/shard_map/ppermute | solution.py:32
  15.8 0.0 collective-permute-done.1
  15.8 0.2 collective-permute-start.5
  16.0 1.7 %collective-permute-done.2 = bf16[256,256]{1,0:T(8,128)(2,1)S(1)} collective-permute-done((bf16[256,256]{1,0:T(8,128)(2,1)}, bf16[256,256]{1,0:T(8,128)(2,1)S(1)}, u32[]{:S(2)}, u32[]{:S(2)}) %collective-permute-start.2) | collective-permute-done | bytes 131104 | tf_op jit(solution)/shard_map/ppermute | solution.py:32
  17.7 0.0 copy-start.7
  17.8 0.0 copy-start.8
  17.8 0.0 copy-start.9
  17.8 0.1 collective-permute-start.4
  17.9 4.9 %collective-permute-done.5 = bf16[256,256]{1,0:T(8,128)(2,1)S(1)} collective-permute-done((bf16[256,256]{1,0:T(8,128)(2,1)S(1)}, bf16[256,256]{1,0:T(8,128)(2,1)S(1)}, u32[]{:S(2)}, u32[]{:S(2)}) %collective-permute-start.5) | collective-permute-done | bytes 131104 | tf_op jit(solution)/shard_map/ppermute | solution.py:32
  22.8 0.0 collective-permute-done.6
  22.9 0.0 collective-permute-done.7
  22.9 0.1 collective-permute-start.8
  23.0 0.8 prep.1
  23.9 0.8 collective-permute-done.8.late_other
  24.7 0.0 slice-start
  24.7 3.1 %attention.1 = (bf16[1280,256]{1,0:T(8,128)(2,1)S(1)}, bf16[1280,256]{1,0:T(8,128)(2,1)S(1)}, bf16[768,256]{1,0:T(8,128)(2,1)S(1)}, bf16[768,256]{1,0:T(8,128)(2,1)S(1)}, bf16[640,256]{1,0:T(8,128)(2,1)S(1)}) custom-call(s32[32,32]{1,0:T(8,128)S(1)} %copy-done.7, s32[1]{0:T(128)} %bitcast.info, s32[32,1,128]{2,1,0:T(1,128)S(1)} %bitcast.7, ...), custom_call_target="tpu_custom_call" | custom-call | flops 2000000000 | bytes 8000000 | tf_op jit(solution)/shard_map/attention/pallas_call | solution.py:265
  27.9 1.3 %collective-permute-start.10 = (bf16[768,256]{1,0:T(8,128)(2,1)S(1)}, bf16[768,256]{1,0:T(8,128)(2,1)S(1)}, u32[]{:S(2)}, u32[]{:S(2)}) collective-permute-start(bf16[768,256]{1,0:T(8,128)(2,1)S(1)} %get-tuple-element.55), channel_id=1, source_target_pairs={{0,8},{8,0},{1,9},{9,1},{2,10},{10,2},{3,11},{11,3},{4,12},{12,4},... | collective-permute-start | bytes 1179656 | tf_op jit(solution)/shard_map/ppermute | solution.py:32
  29.1 0.1 collective-permute-start.9
  29.2 1.3 %collective-permute-done.10 = bf16[768,256]{1,0:T(8,128)(2,1)S(1)} collective-permute-done((bf16[768,256]{1,0:T(8,128)(2,1)S(1)}, bf16[768,256]{1,0:T(8,128)(2,1)S(1)}, u32[]{:S(2)}, u32[]{:S(2)}) %collective-permute-start.10) | collective-permute-done | bytes 393248 | tf_op jit(solution)/shard_map/ppermute | solution.py:32
  30.5 0.1 add_convert_fusion
  30.6 0.8 collective-permute-done.9
  31.4 0.2 fusion
  31.7 2.1 %collective-permute-start.11 = (bf16[256,256]{1,0:T(8,128)(2,1)S(1)}, bf16[256,256]{1,0:T(8,128)(2,1)S(1)}, u32[]{:S(2)}, u32[]{:S(2)}) collective-permute-start(bf16[256,256]{1,0:T(8,128)(2,1)S(1)} %get-tuple-element.57), channel_id=1, source_target_pairs={{0,96},{32,0},{64,32},{96,64},{1,97},{33,1},{65,33},{97,65},{2,98}... | collective-permute-start | bytes 393224 | tf_op jit(solution)/shard_map/ppermute | solution.py:32
  33.7 1.2 %collective-permute-start.12 = (bf16[256,256]{1,0:T(8,128)(2,1)S(1)}, bf16[256,256]{1,0:T(8,128)(2,1)S(1)}, u32[]{:S(2)}, u32[]{:S(2)}) collective-permute-start(bf16[256,256]{1,0:T(8,128)(2,1)S(1)} %get-tuple-element.58), channel_id=1, source_target_pairs={{0,64},{32,96},{64,0},{96,32},{1,65},{33,97},{65,1},{97,33},{2,66}... | collective-permute-start | bytes 393224 | tf_op jit(solution)/shard_map/ppermute | solution.py:32
  34.9 0.0 collective-permute-start.13
  34.9 3.2 %collective-permute-start.14 = (bf16[256,256]{1,0:T(8,128)(2,1)S(1)}, bf16[256,256]{1,0:T(8,128)(2,1)S(1)}, u32[]{:S(2)}, u32[]{:S(2)}) collective-permute-start(bf16[256,256]{1,0:T(8,128)(2,1)S(1)} %get-tuple-element.62), channel_id=1, source_target_pairs={{0,96},{32,0},{64,32},{96,64},{1,97},{33,1},{65,33},{97,65},{2,98}... | collective-permute-start | bytes 393224 | tf_op jit(solution)/shard_map/ppermute | solution.py:32
  38.2 1.1 %collective-permute-start.15 = (bf16[256,256]{1,0:T(8,128)(2,1)S(1)}, bf16[256,256]{1,0:T(8,128)(2,1)S(1)}, u32[]{:S(2)}, u32[]{:S(2)}) collective-permute-start(bf16[256,256]{1,0:T(8,128)(2,1)S(1)} %get-tuple-element.63), channel_id=1, source_target_pairs={{0,64},{32,96},{64,0},{96,32},{1,65},{33,97},{65,1},{97,33},{2,66}... | collective-permute-start | bytes 393224 | tf_op jit(solution)/shard_map/ppermute | solution.py:32
  39.3 0.6 collective-permute-done.11
  39.9 1.7 %collective-permute-done.12 = bf16[256,256]{1,0:T(8,128)(2,1)S(1)} collective-permute-done((bf16[256,256]{1,0:T(8,128)(2,1)S(1)}, bf16[256,256]{1,0:T(8,128)(2,1)S(1)}, u32[]{:S(2)}, u32[]{:S(2)}) %collective-permute-start.12) | collective-permute-done | bytes 131104 | tf_op jit(solution)/shard_map/ppermute | solution.py:32
  41.6 2.9 %collective-permute-done.13 = bf16[256,256]{1,0:T(8,128)(2,1)S(1)} collective-permute-done((bf16[256,256]{1,0:T(8,128)(2,1)S(1)}, bf16[256,256]{1,0:T(8,128)(2,1)S(1)}, u32[]{:S(2)}, u32[]{:S(2)}) %collective-permute-start.13) | collective-permute-done | bytes 131104 | tf_op jit(solution)/shard_map/ppermute | solution.py:32
  44.5 0.1 add_convert_fusion.1
  44.6 0.0 copy-start
  44.6 0.0 copy-start.1
  44.6 2.6 %collective-permute-start.17 = (bf16[256,256]{1,0:T(8,128)(2,1)S(1)}, bf16[256,256]{1,0:T(8,128)(2,1)S(1)}, u32[]{:S(2)}, u32[]{:S(2)}) collective-permute-start(bf16[256,256]{1,0:T(8,128)(2,1)S(1)} %add_convert_fusion.1), channel_id=1, source_target_pairs={{0,16},{16,0},{1,17},{17,1},{2,18},{18,2},{3,19},{19,3},{4,20},{20... | collective-permute-start | bytes 393224 | tf_op jit(solution)/shard_map/ppermute | solution.py:32
  47.2 2.2 %query_part.1.part = bf16[5120,256]{1,0:T(8,128)(2,1)S(1)} custom-call(bf16[640,256]{1,0:T(8,128)(2,1)S(1)} %get-tuple-element.61.qg, bf16[5120,640]{1,0:T(8,128)(2,1)S(1)} %bitcast.6), custom_call_target="tpu_custom_call" | custom-call | flops 1700000000 | bytes 9000000 | tf_op jit(solution)/shard_map/query_part/pallas_call | solution.py:314
  49.5 2.1 %collective-permute-done.17.across = bf16[256,256]{1,0:T(8,128)(2,1)S(1)} collective-permute-done((bf16[256,256]{1,0:T(8,128)(2,1)S(1)}, bf16[256,256]{1,0:T(8,128)(2,1)S(1)}, u32[]{:S(2)}, u32[]{:S(2)}) %collective-permute-start.17) | collective-permute-done | bytes 131104 | tf_op jit(solution)/shard_map/ppermute | solution.py:32
  51.6 1.0 %project.1 = bf16[5120,256]{1,0:T(8,128)(2,1)S(1)} custom-call(bf16[5120,256]{1,0:T(8,128)(2,1)S(1)} %query_part.1.part, f32[256,256]{1,0:T(8,128)S(1)} %get-tuple-element.66.own, bf16[256,256]{1,0:T(8,128)(2,1)S(1)} %collective-permute-done.17.across, bf16[256,256]{1,0:T(8,128)(2,1)S(1)} %collective-permute-done.14.near1, ...), custom_call_target="tpu_custom_call" | custom-call | flops 700000000 | bytes 6000000 | tf_op jit(solution)/shard_map/project/pallas_call | solution.py:348
  52.6 35.9 %all_to_all.5.parts = bf16[8,640,256]{2,1,0:T(8,128)(2,1)S(1)} all-to-all(bf16[8,640,256]{2,1,0:T(8,128)(2,1)S(1)} %bitcast.4), channel_id=1, replica_groups=mesh['y'=4,'zh'=2,'core'=2,'x'=4,'zl'=2] {'x','zl'}, dimensions={0} | all-to-all | bytes 5242880 | tf_op jit(solution)/shard_map/all_to_all | solution.py:420
  88.5 1.1 %last_sum.1 = bf16[640,256]{1,0:T(8,128)(2,1)} custom-call(bf16[8,640,256]{2,1,0:T(8,128)(2,1)S(1)} %all_to_all.5.parts), custom_call_target="tpu_custom_call" | custom-call | flops 1300000 | bytes 3000000 | tf_op jit(solution)/shard_map/last_sum/pallas_call | solution.py:375
  (35 shorter events, 0.2 us)
Async XLA Ops:
  0.0 23.0 %copy-start.5 = (bf16[256,640]{1,0:T(8,128)(2,1)S(1)}, bf16[256,640]{1,0:T(8,128)(2,1)}, u32[]{:S(2)}) copy-start(bf16[256,640]{1,0:T(8,128)(2,1)} %grad) | copy-start | bytes 983044
  0.0 23.0 %copy-start.6 = (bf16[256,640]{1,0:T(8,128)(2,1)S(1)}, bf16[256,640]{1,0:T(8,128)(2,1)}, u32[]{:S(2)}) copy-start(bf16[256,640]{1,0:T(8,128)(2,1)} %att) | copy-start | bytes 983044
  0.0 23.0 %copy-start.4 = (bf16[256,640]{1,0:T(8,128)(2,1)S(1)}, bf16[256,640]{1,0:T(8,128)(2,1)}, u32[]{:S(2)}) copy-start(bf16[256,640]{1,0:T(8,128)(2,1)} %query) | copy-start | bytes 983044
  2.1 20.9 %copy-start.2 = (f32[256,128]{1,0:T(8,128)S(1)}, f32[256,128]{1,0:T(8,128)}, u32[]{:S(2)}) copy-start(f32[256,128]{1,0:T(8,128)} %get-tuple-element.42.cos) | copy-start | bytes 393220
  2.1 20.9 %copy-start.3 = (f32[256,128]{1,0:T(8,128)S(1)}, f32[256,128]{1,0:T(8,128)}, u32[]{:S(2)}) copy-start(f32[256,128]{1,0:T(8,128)} %get-tuple-element.43.sin) | copy-start | bytes 393220
  2.1 10.8 %collective-permute-start = (bf16[256,256]{1,0:T(8,128)(2,1)}, bf16[256,256]{1,0:T(8,128)(2,1)S(1)}, u32[]{:S(2)}, u32[]{:S(2)}) collective-permute-start(bf16[256,256]{1,0:T(8,128)(2,1)} %get-tuple-element.50), channel_id=1, source_target_pairs={{0,16},{16,0},{1,17},{17,1},{2,18},{18,2},{3,19},{19,3},{4,20},{20... | collective-permute-start | bytes 393224 | tf_op jit(solution)/shard_map/ppermute | solution.py:32
  6.8 9.0 %collective-permute-start.1 = (bf16[256,256]{1,0:T(8,128)(2,1)}, bf16[256,256]{1,0:T(8,128)(2,1)S(1)}, u32[]{:S(2)}, u32[]{:S(2)}) collective-permute-start(bf16[256,256]{1,0:T(8,128)(2,1)} %get-tuple-element.50), channel_id=1, source_target_pairs={{0,32},{32,64},{64,96},{96,0},{1,33},{33,65},{65,97},{97,1},{2,34}... | collective-permute-start | bytes 393224 | tf_op jit(solution)/shard_map/ppermute | solution.py:32
  8.3 9.4 %collective-permute-start.3 = (bf16[256,256]{1,0:T(8,128)(2,1)}, bf16[256,256]{1,0:T(8,128)(2,1)S(1)}, u32[]{:S(2)}, u32[]{:S(2)}) collective-permute-start(bf16[256,256]{1,0:T(8,128)(2,1)} %get-tuple-element.50), channel_id=1, source_target_pairs={{0,96},{32,0},{64,32},{96,64},{1,97},{33,1},{65,33},{97,65},{2,98}... | collective-permute-start | bytes 393224 | tf_op jit(solution)/shard_map/ppermute | solution.py:32
  10.0 7.7 %collective-permute-start.2 = (bf16[256,256]{1,0:T(8,128)(2,1)}, bf16[256,256]{1,0:T(8,128)(2,1)S(1)}, u32[]{:S(2)}, u32[]{:S(2)}) collective-permute-start(bf16[256,256]{1,0:T(8,128)(2,1)} %get-tuple-element.50), channel_id=1, source_target_pairs={{0,64},{32,96},{64,0},{96,32},{1,65},{33,97},{65,1},{97,33},{2,66}... | collective-permute-start | bytes 393224 | tf_op jit(solution)/shard_map/ppermute | solution.py:32
  12.9 9.9 %collective-permute-start.7 = (bf16[256,256]{1,0:T(8,128)(2,1)S(1)}, bf16[256,256]{1,0:T(8,128)(2,1)S(1)}, u32[]{:S(2)}, u32[]{:S(2)}) collective-permute-start(bf16[256,256]{1,0:T(8,128)(2,1)S(1)} %collective-permute-done), channel_id=1, source_target_pairs={{0,96},{32,0},{64,32},{96,64},{1,97},{33,1},{65,33},{97,65},{2,98}... | collective-permute-start | bytes 393224 | tf_op jit(solution)/shard_map/ppermute | solution.py:32
  14.1 8.8 %collective-permute-start.6 = (bf16[256,256]{1,0:T(8,128)(2,1)S(1)}, bf16[256,256]{1,0:T(8,128)(2,1)S(1)}, u32[]{:S(2)}, u32[]{:S(2)}) collective-permute-start(bf16[256,256]{1,0:T(8,128)(2,1)S(1)} %collective-permute-done), channel_id=1, source_target_pairs={{0,64},{32,96},{64,0},{96,32},{1,65},{33,97},{65,1},{97,33},{2,66}... | collective-permute-start | bytes 393224 | tf_op jit(solution)/shard_map/ppermute | solution.py:32
  15.8 7.1 %collective-permute-start.5 = (bf16[256,256]{1,0:T(8,128)(2,1)S(1)}, bf16[256,256]{1,0:T(8,128)(2,1)S(1)}, u32[]{:S(2)}, u32[]{:S(2)}) collective-permute-start(bf16[256,256]{1,0:T(8,128)(2,1)S(1)} %collective-permute-done), channel_id=1, source_target_pairs={{0,32},{32,64},{64,96},{96,0},{1,33},{33,65},{65,97},{97,1},{2,34}... | collective-permute-start | bytes 393224 | tf_op jit(solution)/shard_map/ppermute | solution.py:32
  17.7 7.0 %copy-start.7 = (s32[32,32]{1,0:T(8,128)S(1)}, s32[32,32]{1,0:T(8,128)}, u32[]{:S(2)}) copy-start(s32[32,32]{1,0:T(8,128)} %mask.1) | copy-start | bytes 12292
  17.8 6.9 %copy-start.8 = (s32[4096]{0:T(1024)S(1)}, s32[4096]{0:T(1024)}, u32[]{:S(2)}) copy-start(s32[4096]{0:T(1024)} %param.21) | copy-start | bytes 49156
  17.8 6.9 %copy-start.9 = (f32[5,256]{1,0:T(8,128)S(1)}, f32[5,256]{1,0:T(8,128)}, u32[]{:S(2)}) copy-start(f32[5,256]{1,0:T(8,128)} %lse.1) | copy-start | bytes 15364
  17.8 6.9 %collective-permute-start.4 = (bf16[1280,256]{1,0:T(8,128)(2,1)S(1)}, bf16[1280,256]{1,0:T(8,128)(2,1)S(1)}, u32[]{:S(2)}, u32[]{:S(2)}) collective-permute-start(bf16[1280,256]{1,0:T(8,128)(2,1)S(1)} %constant_dynamic-update-slice_fusion.early_mine), channel_id=1, source_target_pairs={{0,8},{8,0},{1,9},{9,1},{2,10},{10,2},{3,11},{11,3},{4,12},{12,4},... | collective-permute-start | bytes 1966088 | tf_op jit(solution)/shard_map/ppermute | solution.py:32
  22.9 1.8 %collective-permute-start.8 = (bf16[768,256]{1,0:T(8,128)(2,1)S(1)}, bf16[768,256]{1,0:T(8,128)(2,1)S(1)}, u32[]{:S(2)}, u32[]{:S(2)}) collective-permute-start(bf16[768,256]{1,0:T(8,128)(2,1)S(1)} %constant_dynamic-update-slice_fusion.5.late_mine), channel_id=1, source_target_pairs={{0,8},{8,0},{1,9},{9,1},{2,10},{10,2},{3,11},{11,3},{4,12},{12,4},... | collective-permute-start | bytes 1179656 | tf_op jit(solution)/shard_map/ppermute | solution.py:32
  24.7 22.5 %slice-start = ((s8[6553600]{0:T(1024)(128)(4,1)}), s8[2359296]{0:T(1024)(128)(4,1)S(1)}, s32[]{:S(2)}) async-start(s8[6553600]{0:T(1024)(128)(4,1)} %bitcast.5), calls=%async_computation.1 | async-start | bytes 4718592
  27.9 2.6 %collective-permute-start.10 = (bf16[768,256]{1,0:T(8,128)(2,1)S(1)}, bf16[768,256]{1,0:T(8,128)(2,1)S(1)}, u32[]{:S(2)}, u32[]{:S(2)}) collective-permute-start(bf16[768,256]{1,0:T(8,128)(2,1)S(1)} %get-tuple-element.55), channel_id=1, source_target_pairs={{0,8},{8,0},{1,9},{9,1},{2,10},{10,2},{3,11},{11,3},{4,12},{12,4},... | collective-permute-start | bytes 1179656 | tf_op jit(solution)/shard_map/ppermute | solution.py:32
  29.1 2.3 %collective-permute-start.9 = (bf16[1280,256]{1,0:T(8,128)(2,1)S(1)}, bf16[1280,256]{1,0:T(8,128)(2,1)S(1)}, u32[]{:S(2)}, u32[]{:S(2)}) collective-permute-start(bf16[1280,256]{1,0:T(8,128)(2,1)S(1)} %get-tuple-element.53), channel_id=1, source_target_pairs={{0,8},{8,0},{1,9},{9,1},{2,10},{10,2},{3,11},{11,3},{4,12},{12,4},... | collective-permute-start | bytes 1966088 | tf_op jit(solution)/shard_map/ppermute | solution.py:32
  30.5 16.7 %slice-start.1 = ((s8[6553600]{0:T(1024)(128)(4,1)}), s8[4194304]{0:T(1024)(128)(4,1)S(1)}, s32[]{:S(2)}) async-start(s8[6553600]{0:T(1024)(128)(4,1)} %bitcast.5), calls=%async_computation.2 | async-start | bytes 8388608
  31.7 8.2 %collective-permute-start.11 = (bf16[256,256]{1,0:T(8,128)(2,1)S(1)}, bf16[256,256]{1,0:T(8,128)(2,1)S(1)}, u32[]{:S(2)}, u32[]{:S(2)}) collective-permute-start(bf16[256,256]{1,0:T(8,128)(2,1)S(1)} %get-tuple-element.57), channel_id=1, source_target_pairs={{0,96},{32,0},{64,32},{96,64},{1,97},{33,1},{65,33},{97,65},{2,98}... | collective-permute-start | bytes 393224 | tf_op jit(solution)/shard_map/ppermute | solution.py:32
  33.7 7.9 %collective-permute-start.12 = (bf16[256,256]{1,0:T(8,128)(2,1)S(1)}, bf16[256,256]{1,0:T(8,128)(2,1)S(1)}, u32[]{:S(2)}, u32[]{:S(2)}) collective-permute-start(bf16[256,256]{1,0:T(8,128)(2,1)S(1)} %get-tuple-element.58), channel_id=1, source_target_pairs={{0,64},{32,96},{64,0},{96,32},{1,65},{33,97},{65,1},{97,33},{2,66}... | collective-permute-start | bytes 393224 | tf_op jit(solution)/shard_map/ppermute | solution.py:32
  34.9 9.5 %collective-permute-start.13 = (bf16[256,256]{1,0:T(8,128)(2,1)S(1)}, bf16[256,256]{1,0:T(8,128)(2,1)S(1)}, u32[]{:S(2)}, u32[]{:S(2)}) collective-permute-start(bf16[256,256]{1,0:T(8,128)(2,1)S(1)} %get-tuple-element.59), channel_id=1, source_target_pairs={{0,32},{32,64},{64,96},{96,0},{1,33},{33,65},{65,97},{97,1},{2,34}... | collective-permute-start | bytes 393224 | tf_op jit(solution)/shard_map/ppermute | solution.py:32
  34.9 14.5 %collective-permute-start.14 = (bf16[256,256]{1,0:T(8,128)(2,1)S(1)}, bf16[256,256]{1,0:T(8,128)(2,1)S(1)}, u32[]{:S(2)}, u32[]{:S(2)}) collective-permute-start(bf16[256,256]{1,0:T(8,128)(2,1)S(1)} %get-tuple-element.62), channel_id=1, source_target_pairs={{0,96},{32,0},{64,32},{96,64},{1,97},{33,1},{65,33},{97,65},{2,98}... | collective-permute-start | bytes 393224 | tf_op jit(solution)/shard_map/ppermute | solution.py:32
  38.2 11.3 %collective-permute-start.15 = (bf16[256,256]{1,0:T(8,128)(2,1)S(1)}, bf16[256,256]{1,0:T(8,128)(2,1)S(1)}, u32[]{:S(2)}, u32[]{:S(2)}) collective-permute-start(bf16[256,256]{1,0:T(8,128)(2,1)S(1)} %get-tuple-element.63), channel_id=1, source_target_pairs={{0,64},{32,96},{64,0},{96,32},{1,65},{33,97},{65,1},{97,33},{2,66}... | collective-permute-start | bytes 393224 | tf_op jit(solution)/shard_map/ppermute | solution.py:32
  39.9 9.6 %collective-permute-start.16 = (bf16[256,256]{1,0:T(8,128)(2,1)S(1)}, bf16[256,256]{1,0:T(8,128)(2,1)S(1)}, u32[]{:S(2)}, u32[]{:S(2)}) collective-permute-start(bf16[256,256]{1,0:T(8,128)(2,1)S(1)} %get-tuple-element.64), channel_id=1, source_target_pairs={{0,32},{32,64},{64,96},{96,0},{1,33},{33,65},{65,97},{97,1},{2,34}... | collective-permute-start | bytes 393224 | tf_op jit(solution)/shard_map/ppermute | solution.py:32
  44.6 7.0 %copy-start = (bf16[5120,128]{1,0:T(8,128)(2,1)S(1)}, bf16[5120,128]{1,0:T(8,128)(2,1)}, u32[]{:S(2)}) copy-start(bf16[5120,128]{1,0:T(8,128)(2,1)} %wk.1) | copy-start | bytes 3932164
  44.6 7.0 %copy-start.1 = (bf16[5120,128]{1,0:T(8,128)(2,1)S(1)}, bf16[5120,128]{1,0:T(8,128)(2,1)}, u32[]{:S(2)}) copy-start(bf16[5120,128]{1,0:T(8,128)(2,1)} %wv.1) | copy-start | bytes 3932164
  44.6 7.0 %collective-permute-start.17 = (bf16[256,256]{1,0:T(8,128)(2,1)S(1)}, bf16[256,256]{1,0:T(8,128)(2,1)S(1)}, u32[]{:S(2)}, u32[]{:S(2)}) collective-permute-start(bf16[256,256]{1,0:T(8,128)(2,1)S(1)} %add_convert_fusion.1), channel_id=1, source_target_pairs={{0,16},{16,0},{1,17},{17,1},{2,18},{18,2},{3,19},{19,3},{4,20},{20... | collective-permute-start | bytes 393224 | tf_op jit(solution)/shard_map/ppermute | solution.py:32

commit v16 on v14

--- a/solution.py
+++ b/solution.py
@@ -362,9 +362,10 @@
 def last_kernel(parts, out):
     def step(i, carry):
         rows = pl.ds(pl.multiple_of(i * TILE, TILE), TILE)
-        total = parts[0, rows, :].astype(f32)
-        for k in range(1, 8):
-            total += parts[k, rows, :].astype(f32)
+        terms = [parts[k, rows, :].astype(f32) for k in range(8)]
+        while len(terms) > 1:
+            terms = [p + q for p, q in zip(terms[::2], terms[1::2])]
+        total = terms[0]
         out[rows, :] = total.astype(bf16)
         return carry
 

time: 89.5 us -> 89.6 us (level)
  no operation moved by 1% of the time
where the time goes in v16:
time: 89.6 us; the launch traced here: 89.3 us
  blocking collectives  35.9 us (40%)
  starting transfers between devices  23.8 us (27%)
  waiting for transfers between devices  15.7 us (18%)
  Pallas kernels  11.5 us (13%)
  local copies, waits for them, and re-layouts  1.17 us (1%)
  other arithmetic  1.02 us (1%)
    all_to_all x1, blocking collectives, local(): return last_sum(lax.all_to_all(send.reshape(8, 640, TOK), TP, 0, 0))  35.9 us
    ppermute x18, starting transfers between devices, shift(): return lax.ppermute(x, axes, perm)  23.8 us
    ppermute x18, waiting for transfers between devices, shift(): return lax.ppermute(x, axes, perm)  15.7 us
    pallas_call x1, Pallas kernels, query_part(): pl.pallas_call(query_part_kernel, out_shape=jax.ShapeDtypeStruct((WIDTH,...  3.4 us
    pallas_call x1, Pallas kernels, attention(): pl.pallas_call(attention_kernel, out_shape=(early, early, late, late, s((...  3.12 us
    pallas_call x1, Pallas kernels, make_block(): pl.pallas_call(block_kernel, out_shape=(s((TOK, HEAD), f32), s((TOK, HEAD...  2.09 us
  transfers between devices with their start and end apart: 18, of which 9 were waited for; matrix products, arithmetic and copies ran while one was open for 2% of the time, Pallas kernels for 5%

profile of v16, /device:TPU:0, one launch (start us, length us, event | category | flops | bytes accessed | tf_op | source)
XLA Modules:
  0.0 89.3 jit_solution(15347646280491006351)
XLA Ops:
  0.0 2.1 %block.1 = (f32[256,128]{1,0:T(8,128)}, f32[256,128]{1,0:T(8,128)}, bf16[256,256]{1,0:T(8,128)(2,1)}) custom-call(bf16[256,128]{1,0:T(8,128)(2,1)} %key.1, bf16[256,128]{1,0:T(8,128)(2,1)} %value.1, s32[2,1,128]{2,1,0:T(1,128)} %bitcast.8, f32[1,128]{1,0:T(1,128)} %constant.23.clone.inverse), custom_call_target="tpu_custom_call" | custom-call | flops 5000000 | bytes 700000 | tf_op jit(solution)/shard_map/block/pallas_call | solution.py:290
  2.1 4.0 %collective-permute-start = (bf16[256,256]{1,0:T(8,128)(2,1)}, bf16[256,256]{1,0:T(8,128)(2,1)S(1)}, u32[]{:S(2)}, u32[]{:S(2)}) collective-permute-start(bf16[256,256]{1,0:T(8,128)(2,1)} %get-tuple-element.50), channel_id=1, source_target_pairs={{0,16},{16,0},{1,17},{17,1},{2,18},{18,2},{3,19},{19,3},{4,20},{20... | collective-permute-start | bytes 393224 | tf_op jit(solution)/shard_map/ppermute | solution.py:32
  6.1 0.7 slice_multiply_fusion.small
  6.8 1.6 %collective-permute-start.1 = (bf16[256,256]{1,0:T(8,128)(2,1)}, bf16[256,256]{1,0:T(8,128)(2,1)S(1)}, u32[]{:S(2)}, u32[]{:S(2)}) collective-permute-start(bf16[256,256]{1,0:T(8,128)(2,1)} %get-tuple-element.50), channel_id=1, source_target_pairs={{0,32},{32,64},{64,96},{96,0},{1,33},{33,65},{65,97},{97,1},{2,34}... | collective-permute-start | bytes 393224 | tf_op jit(solution)/shard_map/ppermute | solution.py:32
  8.3 1.7 %collective-permute-start.3 = (bf16[256,256]{1,0:T(8,128)(2,1)}, bf16[256,256]{1,0:T(8,128)(2,1)S(1)}, u32[]{:S(2)}, u32[]{:S(2)}) collective-permute-start(bf16[256,256]{1,0:T(8,128)(2,1)} %get-tuple-element.50), channel_id=1, source_target_pairs={{0,96},{32,0},{64,32},{96,64},{1,97},{33,1},{65,33},{97,65},{2,98}... | collective-permute-start | bytes 393224 | tf_op jit(solution)/shard_map/ppermute | solution.py:32
  10.0 2.0 %collective-permute-start.2 = (bf16[256,256]{1,0:T(8,128)(2,1)}, bf16[256,256]{1,0:T(8,128)(2,1)S(1)}, u32[]{:S(2)}, u32[]{:S(2)}) collective-permute-start(bf16[256,256]{1,0:T(8,128)(2,1)} %get-tuple-element.50), channel_id=1, source_target_pairs={{0,64},{32,96},{64,0},{96,32},{1,65},{33,97},{65,1},{97,33},{2,66}... | collective-permute-start | bytes 393224 | tf_op jit(solution)/shard_map/ppermute | solution.py:32
  12.0 0.9 %constant_dynamic-update-slice_fusion.4 = bf16[1280,256]{1,0:T(8,128)(2,1)S(1)} fusion(bf16[256,256]{1,0:T(8,128)(2,1)} %get-tuple-element.50), kind=kLoop, calls=%fused_computation.7 | loop fusion | bytes 262144
  12.9 1.1 %collective-permute-start.7 = (bf16[256,256]{1,0:T(8,128)(2,1)S(1)}, bf16[256,256]{1,0:T(8,128)(2,1)S(1)}, u32[]{:S(2)}, u32[]{:S(2)}) collective-permute-start(bf16[256,256]{1,0:T(8,128)(2,1)S(1)} %collective-permute-done), channel_id=1, source_target_pairs={{0,96},{32,0},{64,32},{96,64},{1,97},{33,1},{65,33},{97,65},{2,98}... | collective-permute-start | bytes 393224 | tf_op jit(solution)/shard_map/ppermute | solution.py:32
  14.1 1.7 %collective-permute-start.6 = (bf16[256,256]{1,0:T(8,128)(2,1)S(1)}, bf16[256,256]{1,0:T(8,128)(2,1)S(1)}, u32[]{:S(2)}, u32[]{:S(2)}) collective-permute-start(bf16[256,256]{1,0:T(8,128)(2,1)S(1)} %collective-permute-done), channel_id=1, source_target_pairs={{0,64},{32,96},{64,0},{96,32},{1,65},{33,97},{65,1},{97,33},{2,66}... | collective-permute-start | bytes 393224 | tf_op jit(solution)/shard_map/ppermute | solution.py:32
  15.8 0.2 collective-permute-start.5
  16.0 1.7 %collective-permute-done.2 = bf16[256,256]{1,0:T(8,128)(2,1)S(1)} collective-permute-done((bf16[256,256]{1,0:T(8,128)(2,1)}, bf16[256,256]{1,0:T(8,128)(2,1)S(1)}, u32[]{:S(2)}, u32[]{:S(2)}) %collective-permute-start.2) | collective-permute-done | bytes 131104 | tf_op jit(solution)/shard_map/ppermute | solution.py:32
  17.7 0.0 copy-start.7
  17.8 0.0 copy-start.8
  17.8 0.0 copy-start.9
  17.8 0.0 collective-permute-done.3
  17.8 0.1 collective-permute-start.4
  17.9 4.9 %collective-permute-done.5 = bf16[256,256]{1,0:T(8,128)(2,1)S(1)} collective-permute-done((bf16[256,256]{1,0:T(8,128)(2,1)S(1)}, bf16[256,256]{1,0:T(8,128)(2,1)S(1)}, u32[]{:S(2)}, u32[]{:S(2)}) %collective-permute-start.5) | collective-permute-done | bytes 131104 | tf_op jit(solution)/shard_map/ppermute | solution.py:32
  22.9 0.0 collective-permute-done.7
  22.9 0.1 collective-permute-start.8
  23.0 0.8 prep.1
  23.9 0.8 collective-permute-done.8.late_other
  24.7 0.0 collective-permute-done.4.early_other
  24.7 0.0 slice-start
  24.7 3.1 %attention.1 = (bf16[1280,256]{1,0:T(8,128)(2,1)S(1)}, bf16[1280,256]{1,0:T(8,128)(2,1)S(1)}, bf16[768,256]{1,0:T(8,128)(2,1)S(1)}, bf16[768,256]{1,0:T(8,128)(2,1)S(1)}, bf16[640,256]{1,0:T(8,128)(2,1)S(1)}) custom-call(s32[32,32]{1,0:T(8,128)S(1)} %copy-done.7, s32[1]{0:T(128)} %bitcast.info, s32[32,1,128]{2,1,0:T(1,128)S(1)} %bitcast.7, ...), custom_call_target="tpu_custom_call" | custom-call | flops 2000000000 | bytes 8000000 | tf_op jit(solution)/shard_map/attention/pallas_call | solution.py:265
  27.9 1.3 %collective-permute-start.10 = (bf16[768,256]{1,0:T(8,128)(2,1)S(1)}, bf16[768,256]{1,0:T(8,128)(2,1)S(1)}, u32[]{:S(2)}, u32[]{:S(2)}) collective-permute-start(bf16[768,256]{1,0:T(8,128)(2,1)S(1)} %get-tuple-element.55), channel_id=1, source_target_pairs={{0,8},{8,0},{1,9},{9,1},{2,10},{10,2},{3,11},{11,3},{4,12},{12,4},... | collective-permute-start | bytes 1179656 | tf_op jit(solution)/shard_map/ppermute | solution.py:32
  29.1 0.1 collective-permute-start.9
  29.2 1.3 %collective-permute-done.10 = bf16[768,256]{1,0:T(8,128)(2,1)S(1)} collective-permute-done((bf16[768,256]{1,0:T(8,128)(2,1)S(1)}, bf16[768,256]{1,0:T(8,128)(2,1)S(1)}, u32[]{:S(2)}, u32[]{:S(2)}) %collective-permute-start.10) | collective-permute-done | bytes 393248 | tf_op jit(solution)/shard_map/ppermute | solution.py:32
  30.5 0.1 add_convert_fusion
  30.6 0.8 collective-permute-done.9
  31.4 0.2 fusion
  31.7 2.1 %collective-permute-start.11 = (bf16[256,256]{1,0:T(8,128)(2,1)S(1)}, bf16[256,256]{1,0:T(8,128)(2,1)S(1)}, u32[]{:S(2)}, u32[]{:S(2)}) collective-permute-start(bf16[256,256]{1,0:T(8,128)(2,1)S(1)} %get-tuple-element.57), channel_id=1, source_target_pairs={{0,96},{32,0},{64,32},{96,64},{1,97},{33,1},{65,33},{97,65},{2,98}... | collective-permute-start | bytes 393224 | tf_op jit(solution)/shard_map/ppermute | solution.py:32
  33.7 1.2 %collective-permute-start.12 = (bf16[256,256]{1,0:T(8,128)(2,1)S(1)}, bf16[256,256]{1,0:T(8,128)(2,1)S(1)}, u32[]{:S(2)}, u32[]{:S(2)}) collective-permute-start(bf16[256,256]{1,0:T(8,128)(2,1)S(1)} %get-tuple-element.58), channel_id=1, source_target_pairs={{0,64},{32,96},{64,0},{96,32},{1,65},{33,97},{65,1},{97,33},{2,66}... | collective-permute-start | bytes 393224 | tf_op jit(solution)/shard_map/ppermute | solution.py:32
  34.9 3.2 %collective-permute-start.14 = (bf16[256,256]{1,0:T(8,128)(2,1)S(1)}, bf16[256,256]{1,0:T(8,128)(2,1)S(1)}, u32[]{:S(2)}, u32[]{:S(2)}) collective-permute-start(bf16[256,256]{1,0:T(8,128)(2,1)S(1)} %get-tuple-element.62), channel_id=1, source_target_pairs={{0,96},{32,0},{64,32},{96,64},{1,97},{33,1},{65,33},{97,65},{2,98}... | collective-permute-start | bytes 393224 | tf_op jit(solution)/shard_map/ppermute | solution.py:32
  38.1 1.1 %collective-permute-start.15 = (bf16[256,256]{1,0:T(8,128)(2,1)S(1)}, bf16[256,256]{1,0:T(8,128)(2,1)S(1)}, u32[]{:S(2)}, u32[]{:S(2)}) collective-permute-start(bf16[256,256]{1,0:T(8,128)(2,1)S(1)} %get-tuple-element.63), channel_id=1, source_target_pairs={{0,64},{32,96},{64,0},{96,32},{1,65},{33,97},{65,1},{97,33},{2,66}... | collective-permute-start | bytes 393224 | tf_op jit(solution)/shard_map/ppermute | solution.py:32
  39.3 0.6 collective-permute-done.11
  39.9 0.0 collective-permute-start.16
  39.9 1.7 %collective-permute-done.12 = bf16[256,256]{1,0:T(8,128)(2,1)S(1)} collective-permute-done((bf16[256,256]{1,0:T(8,128)(2,1)S(1)}, bf16[256,256]{1,0:T(8,128)(2,1)S(1)}, u32[]{:S(2)}, u32[]{:S(2)}) %collective-permute-start.12) | collective-permute-done | bytes 131104 | tf_op jit(solution)/shard_map/ppermute | solution.py:32
  41.6 2.9 %collective-permute-done.13 = bf16[256,256]{1,0:T(8,128)(2,1)S(1)} collective-permute-done((bf16[256,256]{1,0:T(8,128)(2,1)S(1)}, bf16[256,256]{1,0:T(8,128)(2,1)S(1)}, u32[]{:S(2)}, u32[]{:S(2)}) %collective-permute-start.13) | collective-permute-done | bytes 131104 | tf_op jit(solution)/shard_map/ppermute | solution.py:32
  44.5 0.1 add_convert_fusion.1
  44.6 0.0 copy-start
  44.6 0.0 copy-start.1
  44.6 2.4 %collective-permute-start.17 = (bf16[256,256]{1,0:T(8,128)(2,1)S(1)}, bf16[256,256]{1,0:T(8,128)(2,1)S(1)}, u32[]{:S(2)}, u32[]{:S(2)}) collective-permute-start(bf16[256,256]{1,0:T(8,128)(2,1)S(1)} %add_convert_fusion.1), channel_id=1, source_target_pairs={{0,16},{16,0},{1,17},{17,1},{2,18},{18,2},{3,19},{19,3},{4,20},{20... | collective-permute-start | bytes 393224 | tf_op jit(solution)/shard_map/ppermute | solution.py:32
  47.0 3.4 %query_part.1.part = bf16[5120,256]{1,0:T(8,128)(2,1)S(1)} custom-call(bf16[640,256]{1,0:T(8,128)(2,1)S(1)} %get-tuple-element.61.qg, bf16[5120,640]{1,0:T(8,128)(2,1)S(1)} %bitcast.6), custom_call_target="tpu_custom_call" | custom-call | flops 1700000000 | bytes 9000000 | tf_op jit(solution)/shard_map/query_part/pallas_call | solution.py:314
  50.4 0.0 collective-permute-done.14.near1
  50.5 0.9 %collective-permute-done.17.across = bf16[256,256]{1,0:T(8,128)(2,1)S(1)} collective-permute-done((bf16[256,256]{1,0:T(8,128)(2,1)S(1)}, bf16[256,256]{1,0:T(8,128)(2,1)S(1)}, u32[]{:S(2)}, u32[]{:S(2)}) %collective-permute-start.17) | collective-permute-done | bytes 131104 | tf_op jit(solution)/shard_map/ppermute | solution.py:32
  51.4 1.0 %project.1 = bf16[5120,256]{1,0:T(8,128)(2,1)S(1)} custom-call(bf16[5120,256]{1,0:T(8,128)(2,1)S(1)} %query_part.1.part, f32[256,256]{1,0:T(8,128)S(1)} %get-tuple-element.66.own, bf16[256,256]{1,0:T(8,128)(2,1)S(1)} %collective-permute-done.17.across, bf16[256,256]{1,0:T(8,128)(2,1)S(1)} %collective-permute-done.14.near1, ...), custom_call_target="tpu_custom_call" | custom-call | flops 700000000 | bytes 6000000 | tf_op jit(solution)/shard_map/project/pallas_call | solution.py:348
  52.4 35.9 %all_to_all.5.parts = bf16[8,640,256]{2,1,0:T(8,128)(2,1)S(1)} all-to-all(bf16[8,640,256]{2,1,0:T(8,128)(2,1)S(1)} %bitcast.4), channel_id=1, replica_groups=mesh['y'=4,'zh'=2,'core'=2,'x'=4,'zl'=2] {'x','zl'}, dimensions={0} | all-to-all | bytes 5242880 | tf_op jit(solution)/shard_map/all_to_all | solution.py:421
  88.3 1.1 %last_sum.1 = bf16[640,256]{1,0:T(8,128)(2,1)} custom-call(bf16[8,640,256]{2,1,0:T(8,128)(2,1)S(1)} %all_to_all.5.parts), custom_call_target="tpu_custom_call" | custom-call | flops 1300000 | bytes 3000000 | tf_op jit(solution)/shard_map/last_sum/pallas_call | solution.py:376
  (35 shorter events, 0.2 us)
Async XLA Ops:
  0.0 23.0 %copy-start.5 = (bf16[256,640]{1,0:T(8,128)(2,1)S(1)}, bf16[256,640]{1,0:T(8,128)(2,1)}, u32[]{:S(2)}) copy-start(bf16[256,640]{1,0:T(8,128)(2,1)} %grad) | copy-start | bytes 983044
  0.0 23.0 %copy-start.6 = (bf16[256,640]{1,0:T(8,128)(2,1)S(1)}, bf16[256,640]{1,0:T(8,128)(2,1)}, u32[]{:S(2)}) copy-start(bf16[256,640]{1,0:T(8,128)(2,1)} %att) | copy-start | bytes 983044
  0.0 23.0 %copy-start.4 = (bf16[256,640]{1,0:T(8,128)(2,1)S(1)}, bf16[256,640]{1,0:T(8,128)(2,1)}, u32[]{:S(2)}) copy-start(bf16[256,640]{1,0:T(8,128)(2,1)} %query) | copy-start | bytes 983044
  2.1 20.9 %copy-start.2 = (f32[256,128]{1,0:T(8,128)S(1)}, f32[256,128]{1,0:T(8,128)}, u32[]{:S(2)}) copy-start(f32[256,128]{1,0:T(8,128)} %get-tuple-element.42.cos) | copy-start | bytes 393220
  2.1 20.9 %copy-start.3 = (f32[256,128]{1,0:T(8,128)S(1)}, f32[256,128]{1,0:T(8,128)}, u32[]{:S(2)}) copy-start(f32[256,128]{1,0:T(8,128)} %get-tuple-element.43.sin) | copy-start | bytes 393220
  2.1 10.8 %collective-permute-start = (bf16[256,256]{1,0:T(8,128)(2,1)}, bf16[256,256]{1,0:T(8,128)(2,1)S(1)}, u32[]{:S(2)}, u32[]{:S(2)}) collective-permute-start(bf16[256,256]{1,0:T(8,128)(2,1)} %get-tuple-element.50), channel_id=1, source_target_pairs={{0,16},{16,0},{1,17},{17,1},{2,18},{18,2},{3,19},{19,3},{4,20},{20... | collective-permute-start | bytes 393224 | tf_op jit(solution)/shard_map/ppermute | solution.py:32
  6.8 9.0 %collective-permute-start.1 = (bf16[256,256]{1,0:T(8,128)(2,1)}, bf16[256,256]{1,0:T(8,128)(2,1)S(1)}, u32[]{:S(2)}, u32[]{:S(2)}) collective-permute-start(bf16[256,256]{1,0:T(8,128)(2,1)} %get-tuple-element.50), channel_id=1, source_target_pairs={{0,32},{32,64},{64,96},{96,0},{1,33},{33,65},{65,97},{97,1},{2,34}... | collective-permute-start | bytes 393224 | tf_op jit(solution)/shard_map/ppermute | solution.py:32
  8.3 9.4 %collective-permute-start.3 = (bf16[256,256]{1,0:T(8,128)(2,1)}, bf16[256,256]{1,0:T(8,128)(2,1)S(1)}, u32[]{:S(2)}, u32[]{:S(2)}) collective-permute-start(bf16[256,256]{1,0:T(8,128)(2,1)} %get-tuple-element.50), channel_id=1, source_target_pairs={{0,96},{32,0},{64,32},{96,64},{1,97},{33,1},{65,33},{97,65},{2,98}... | collective-permute-start | bytes 393224 | tf_op jit(solution)/shard_map/ppermute | solution.py:32
  10.0 7.7 %collective-permute-start.2 = (bf16[256,256]{1,0:T(8,128)(2,1)}, bf16[256,256]{1,0:T(8,128)(2,1)S(1)}, u32[]{:S(2)}, u32[]{:S(2)}) collective-permute-start(bf16[256,256]{1,0:T(8,128)(2,1)} %get-tuple-element.50), channel_id=1, source_target_pairs={{0,64},{32,96},{64,0},{96,32},{1,65},{33,97},{65,1},{97,33},{2,66}... | collective-permute-start | bytes 393224 | tf_op jit(solution)/shard_map/ppermute | solution.py:32
  12.9 9.9 %collective-permute-start.7 = (bf16[256,256]{1,0:T(8,128)(2,1)S(1)}, bf16[256,256]{1,0:T(8,128)(2,1)S(1)}, u32[]{:S(2)}, u32[]{:S(2)}) collective-permute-start(bf16[256,256]{1,0:T(8,128)(2,1)S(1)} %collective-permute-done), channel_id=1, source_target_pairs={{0,96},{32,0},{64,32},{96,64},{1,97},{33,1},{65,33},{97,65},{2,98}... | collective-permute-start | bytes 393224 | tf_op jit(solution)/shard_map/ppermute | solution.py:32
  14.1 8.8 %collective-permute-start.6 = (bf16[256,256]{1,0:T(8,128)(2,1)S(1)}, bf16[256,256]{1,0:T(8,128)(2,1)S(1)}, u32[]{:S(2)}, u32[]{:S(2)}) collective-permute-start(bf16[256,256]{1,0:T(8,128)(2,1)S(1)} %collective-permute-done), channel_id=1, source_target_pairs={{0,64},{32,96},{64,0},{96,32},{1,65},{33,97},{65,1},{97,33},{2,66}... | collective-permute-start | bytes 393224 | tf_op jit(solution)/shard_map/ppermute | solution.py:32
  15.8 7.1 %collective-permute-start.5 = (bf16[256,256]{1,0:T(8,128)(2,1)S(1)}, bf16[256,256]{1,0:T(8,128)(2,1)S(1)}, u32[]{:S(2)}, u32[]{:S(2)}) collective-permute-start(bf16[256,256]{1,0:T(8,128)(2,1)S(1)} %collective-permute-done), channel_id=1, source_target_pairs={{0,32},{32,64},{64,96},{96,0},{1,33},{33,65},{65,97},{97,1},{2,34}... | collective-permute-start | bytes 393224 | tf_op jit(solution)/shard_map/ppermute | solution.py:32
  17.7 7.0 %copy-start.7 = (s32[32,32]{1,0:T(8,128)S(1)}, s32[32,32]{1,0:T(8,128)}, u32[]{:S(2)}) copy-start(s32[32,32]{1,0:T(8,128)} %mask.1) | copy-start | bytes 12292
  17.8 6.9 %copy-start.8 = (s32[4096]{0:T(1024)S(1)}, s32[4096]{0:T(1024)}, u32[]{:S(2)}) copy-start(s32[4096]{0:T(1024)} %param.21) | copy-start | bytes 49156
  17.8 6.9 %copy-start.9 = (f32[5,256]{1,0:T(8,128)S(1)}, f32[5,256]{1,0:T(8,128)}, u32[]{:S(2)}) copy-start(f32[5,256]{1,0:T(8,128)} %lse.1) | copy-start | bytes 15364
  17.8 6.9 %collective-permute-start.4 = (bf16[1280,256]{1,0:T(8,128)(2,1)S(1)}, bf16[1280,256]{1,0:T(8,128)(2,1)S(1)}, u32[]{:S(2)}, u32[]{:S(2)}) collective-permute-start(bf16[1280,256]{1,0:T(8,128)(2,1)S(1)} %constant_dynamic-update-slice_fusion.early_mine), channel_id=1, source_target_pairs={{0,8},{8,0},{1,9},{9,1},{2,10},{10,2},{3,11},{11,3},{4,12},{12,4},... | collective-permute-start | bytes 1966088 | tf_op jit(solution)/shard_map/ppermute | solution.py:32
  22.9 1.8 %collective-permute-start.8 = (bf16[768,256]{1,0:T(8,128)(2,1)S(1)}, bf16[768,256]{1,0:T(8,128)(2,1)S(1)}, u32[]{:S(2)}, u32[]{:S(2)}) collective-permute-start(bf16[768,256]{1,0:T(8,128)(2,1)S(1)} %constant_dynamic-update-slice_fusion.5.late_mine), channel_id=1, source_target_pairs={{0,8},{8,0},{1,9},{9,1},{2,10},{10,2},{3,11},{11,3},{4,12},{12,4},... | collective-permute-start | bytes 1179656 | tf_op jit(solution)/shard_map/ppermute | solution.py:32
  24.7 22.3 %slice-start = ((s8[6553600]{0:T(1024)(128)(4,1)}), s8[2359296]{0:T(1024)(128)(4,1)S(1)}, s32[]{:S(2)}) async-start(s8[6553600]{0:T(1024)(128)(4,1)} %bitcast.5), calls=%async_computation.1 | async-start | bytes 4718592
  27.9 2.6 %collective-permute-start.10 = (bf16[768,256]{1,0:T(8,128)(2,1)S(1)}, bf16[768,256]{1,0:T(8,128)(2,1)S(1)}, u32[]{:S(2)}, u32[]{:S(2)}) collective-permute-start(bf16[768,256]{1,0:T(8,128)(2,1)S(1)} %get-tuple-element.55), channel_id=1, source_target_pairs={{0,8},{8,0},{1,9},{9,1},{2,10},{10,2},{3,11},{11,3},{4,12},{12,4},... | collective-permute-start | bytes 1179656 | tf_op jit(solution)/shard_map/ppermute | solution.py:32
  29.1 2.3 %collective-permute-start.9 = (bf16[1280,256]{1,0:T(8,128)(2,1)S(1)}, bf16[1280,256]{1,0:T(8,128)(2,1)S(1)}, u32[]{:S(2)}, u32[]{:S(2)}) collective-permute-start(bf16[1280,256]{1,0:T(8,128)(2,1)S(1)} %get-tuple-element.53), channel_id=1, source_target_pairs={{0,8},{8,0},{1,9},{9,1},{2,10},{10,2},{3,11},{11,3},{4,12},{12,4},... | collective-permute-start | bytes 1966088 | tf_op jit(solution)/shard_map/ppermute | solution.py:32
  30.5 16.6 %slice-start.1 = ((s8[6553600]{0:T(1024)(128)(4,1)}), s8[4194304]{0:T(1024)(128)(4,1)S(1)}, s32[]{:S(2)}) async-start(s8[6553600]{0:T(1024)(128)(4,1)} %bitcast.5), calls=%async_computation.2 | async-start | bytes 8388608
  31.7 8.2 %collective-permute-start.11 = (bf16[256,256]{1,0:T(8,128)(2,1)S(1)}, bf16[256,256]{1,0:T(8,128)(2,1)S(1)}, u32[]{:S(2)}, u32[]{:S(2)}) collective-permute-start(bf16[256,256]{1,0:T(8,128)(2,1)S(1)} %get-tuple-element.57), channel_id=1, source_target_pairs={{0,96},{32,0},{64,32},{96,64},{1,97},{33,1},{65,33},{97,65},{2,98}... | collective-permute-start | bytes 393224 | tf_op jit(solution)/shard_map/ppermute | solution.py:32
  33.7 7.9 %collective-permute-start.12 = (bf16[256,256]{1,0:T(8,128)(2,1)S(1)}, bf16[256,256]{1,0:T(8,128)(2,1)S(1)}, u32[]{:S(2)}, u32[]{:S(2)}) collective-permute-start(bf16[256,256]{1,0:T(8,128)(2,1)S(1)} %get-tuple-element.58), channel_id=1, source_target_pairs={{0,64},{32,96},{64,0},{96,32},{1,65},{33,97},{65,1},{97,33},{2,66}... | collective-permute-start | bytes 393224 | tf_op jit(solution)/shard_map/ppermute | solution.py:32
  34.9 9.6 %collective-permute-start.13 = (bf16[256,256]{1,0:T(8,128)(2,1)S(1)}, bf16[256,256]{1,0:T(8,128)(2,1)S(1)}, u32[]{:S(2)}, u32[]{:S(2)}) collective-permute-start(bf16[256,256]{1,0:T(8,128)(2,1)S(1)} %get-tuple-element.59), channel_id=1, source_target_pairs={{0,32},{32,64},{64,96},{96,0},{1,33},{33,65},{65,97},{97,1},{2,34}... | collective-permute-start | bytes 393224 | tf_op jit(solution)/shard_map/ppermute | solution.py:32
  34.9 15.5 %collective-permute-start.14 = (bf16[256,256]{1,0:T(8,128)(2,1)S(1)}, bf16[256,256]{1,0:T(8,128)(2,1)S(1)}, u32[]{:S(2)}, u32[]{:S(2)}) collective-permute-start(bf16[256,256]{1,0:T(8,128)(2,1)S(1)} %get-tuple-element.62), channel_id=1, source_target_pairs={{0,96},{32,0},{64,32},{96,64},{1,97},{33,1},{65,33},{97,65},{2,98}... | collective-permute-start | bytes 393224 | tf_op jit(solution)/shard_map/ppermute | solution.py:32
  38.1 12.3 %collective-permute-start.15 = (bf16[256,256]{1,0:T(8,128)(2,1)S(1)}, bf16[256,256]{1,0:T(8,128)(2,1)S(1)}, u32[]{:S(2)}, u32[]{:S(2)}) collective-permute-start(bf16[256,256]{1,0:T(8,128)(2,1)S(1)} %get-tuple-element.63), channel_id=1, source_target_pairs={{0,64},{32,96},{64,0},{96,32},{1,65},{33,97},{65,1},{97,33},{2,66}... | collective-permute-start | bytes 393224 | tf_op jit(solution)/shard_map/ppermute | solution.py:32
  39.9 10.6 %collective-permute-start.16 = (bf16[256,256]{1,0:T(8,128)(2,1)S(1)}, bf16[256,256]{1,0:T(8,128)(2,1)S(1)}, u32[]{:S(2)}, u32[]{:S(2)}) collective-permute-start(bf16[256,256]{1,0:T(8,128)(2,1)S(1)} %get-tuple-element.64), channel_id=1, source_target_pairs={{0,32},{32,64},{64,96},{96,0},{1,33},{33,65},{65,97},{97,1},{2,34}... | collective-permute-start | bytes 393224 | tf_op jit(solution)/shard_map/ppermute | solution.py:32
  44.6 6.8 %copy-start = (bf16[5120,128]{1,0:T(8,128)(2,1)S(1)}, bf16[5120,128]{1,0:T(8,128)(2,1)}, u32[]{:S(2)}) copy-start(bf16[5120,128]{1,0:T(8,128)(2,1)} %wk.1) | copy-start | bytes 3932164
  44.6 6.8 %copy-start.1 = (bf16[5120,128]{1,0:T(8,128)(2,1)S(1)}, bf16[5120,128]{1,0:T(8,128)(2,1)}, u32[]{:S(2)}) copy-start(bf16[5120,128]{1,0:T(8,128)(2,1)} %wv.1) | copy-start | bytes 3932164
  44.6 6.8 %collective-permute-start.17 = (bf16[256,256]{1,0:T(8,128)(2,1)S(1)}, bf16[256,256]{1,0:T(8,128)(2,1)S(1)}, u32[]{:S(2)}, u32[]{:S(2)}) collective-permute-start(bf16[256,256]{1,0:T(8,128)(2,1)S(1)} %add_convert_fusion.1), channel_id=1, source_target_pairs={{0,16},{16,0},{1,17},{17,1},{2,18},{18,2},{3,19},{19,3},{4,20},{20... | collective-permute-start | bytes 393224 | tf_op jit(solution)/shard_map/ppermute | solution.py:32
